TPU v7x, 32 devices: a whole 2x2x4 slice. The times are simulated.
32 devices in a mesh: ka: 16 (over z, x, core), ga: 2 (over y).
Axes of the slice: x: 2, y: 2, z: 4, core: 2. Of those that a mesh axis runs over, the one named last changes fastest.
Arguments:
- orbitals: bfloat16 [32, 1024, 256], P('ka', 'ga'), may hold values from -1.5 to 1.5
- minus_table: int32 [2, 32], replicated, may hold values from 0 to 31, as said below
- points: int32 [512], replicated, may hold values from 0 to 1023, as said below
Outputs:
- pair_matrix: float32 [512, 2, 2, 1024], P('ka', None, None, 'ga')
Inputs may be any that keep to these rules, and one draw needn't show every extreme that they name: `minus_table`: row q holds (k - s) mod 32 for every k, with one shift s for the row that is a nonzero multiple of 2; the two rows have different shifts. `points`: distinct grid indices; 0 and 1023 are among them.
All inputs are finite; a program needn't handle non-finite values.
Results may differ from a plain program's by a relative error of at most 0.0012.
Values may be sent and summed in bfloat16 or wider, within the bound.
No kernel may reach another device: no remote copies, remote signals or barrier semaphores. Data moves between devices by JAX's collectives and lax.ppermute only.
A program may use at most 64 MiB of HBM per device.

v0:
```python
import math

import jax
import jax.numpy as jnp
from jax import lax
from jax.sharding import PartitionSpec as P


def from_behind(block, axis, distance):
    devices = range(lax.axis_size(axis))
    route = [((i - distance) % len(devices), i) for i in devices]
    return lax.ppermute(block, axis, route)


def pair_block(field_rows, collected):
    halfway = collected.shape[-1] // 2
    rotated = jnp.concatenate([-collected[:, :, halfway:], collected[:, :, :halfway]], axis=2)
    stacked = jnp.concatenate([collected, rotated], axis=1)
    product = jnp.einsum("kpc,kgc->kpg", stacked, field_rows, preferred_element_type=jnp.float32)
    rounded = lax.optimization_barrier(product.astype(jnp.bfloat16))
    return rounded.astype(jnp.float32)


def hadamard(own_field, other_field, length):
    real_part = jnp.sum(
        own_field[:, :length] * other_field[:, :length]
        + own_field[:, length:] * other_field[:, length:],
        axis=0,
    )
    imag_part = jnp.sum(
        own_field[:, length:] * other_field[:, :length]
        - own_field[:, :length] * other_field[:, length:],
        axis=0,
    )
    return jnp.stack([real_part, imag_part], axis=1)


def on_device(orbitals, minus_table, points):
    kdevice, slab_size, channels = orbitals.shape
    cycle_size = lax.axis_size("ka")
    total_k = kdevice * cycle_size
    transfers = minus_table.shape[0]
    first_kpoint = lax.axis_index("ka") * kdevice
    local_rows = points - lax.axis_index("ga") * slab_size
    inside = (local_rows >= 0) & (local_rows < slab_size)
    clipped = jnp.clip(local_rows, 0, slab_size - 1)

    def collect(fields):
        picked = jnp.take(fields, clipped, axis=-2).astype(jnp.float32)
        return jnp.where(inside[:, None], picked, 0.0)

    own_rows = lax.psum(collect(orbitals).astype(jnp.bfloat16), "ga")
    targets = lax.dynamic_slice_in_dim(minus_table, first_kpoint, 1, 1)[:, 0]
    offsets = (first_kpoint - targets) % total_k // kdevice
    sections = (cycle_size - 1).bit_length()
    series = []
    for transfer in range(transfers):
        current = orbitals
        for section in range(sections):
            arrived = from_behind(current, "ka", 1 << section)
            current = jnp.where(offsets[transfer] >> section & 1 == 1, arrived, current)
        series.append(current)
    moving = jnp.stack(series)
    shifted_rows = lax.psum(collect(moving).astype(jnp.bfloat16), "ga")
    factor = 1.0 / math.sqrt(total_k)
    length = lax.axis_size("ka") * (points.shape[0] // cycle_size)
    own_field = pair_block(orbitals, own_rows)
    pieces = []
    for transfer in range(transfers):
        other_field = pair_block(moving[transfer], shifted_rows[transfer])
        pieces.append(hadamard(own_field, other_field, length))
    summed = lax.psum_scatter(jnp.stack(pieces, axis=1), "ka", scatter_dimension=0, tiled=True)
    return summed * factor


def solution(mesh):
    placed = (P("ka", "ga", None), P(), P())
    return jax.shard_map(
        on_device, mesh=mesh, in_specs=placed, out_specs=P("ka", None, None, "ga"), check_vma=False
    )
```

profile of v0, /device:TPU:1, one launch (start us, length us, event | category | flops | bytes accessed | tf_op | source)
XLA Modules:
  0.0 310.1 jit_solution(997486530758725940)
XLA Ops:
  6.5 0.0 all-reduce.7.cloned.1.call-start
  6.5 1.6 copy.10
  8.1 2.7 collective-permute-start
  10.8 0.9 subtract_reduce_fusion.2
  11.7 0.6 fusion.23
  13.5 3.4 %collective-permute-done = bf16[2,512,256]{2,0,1:T(2,128)(2,1)S(1)} collective-permute-done((bf16[2,512,256]{2,0,1:T(2,128)(2,1)S(1)}, bf16[2,512,256]{2,0,1:T(2,128)(2,1)S(1)}, u32[]{:S(2)}, u32[]{:S(2)}) %collective-permute-start) | collective-permute-done | bytes 524320 | tf_op jit(solution)/shard_map/ppermute | solution.py:12
  16.9 2.1 broadcast_select_fusion.4
  19.0 0.0 copy-start.4
  19.0 1.3 collective-permute-start.1
  20.3 1.2 collective-permute-start.4
  22.8 8.7 %collective-permute-done.1 = bf16[2,512,256]{2,0,1:T(2,128)(2,1)S(1)} collective-permute-done((bf16[2,512,256]{2,0,1:T(2,128)(2,1)S(1)}, bf16[2,512,256]{2,0,1:T(2,128)(2,1)S(1)}, u32[]{:S(2)}, u32[]{:S(2)}) %collective-permute-start.1) | collective-permute-done | bytes 524320 | tf_op jit(solution)/shard_map/ppermute | solution.py:12
  31.6 0.1 broadcast_select_fusion.5
  31.6 0.9 collective-permute-start.2
  32.5 10.3 %collective-permute-done.4 = bf16[2,512,256]{2,0,1:T(2,128)(2,1)S(1)} collective-permute-done((bf16[2,512,256]{2,0,1:T(2,128)(2,1)S(1)}, bf16[2,512,256]{2,0,1:T(2,128)(2,1)S(1)}, u32[]{:S(2)}, u32[]{:S(2)}) %collective-permute-start.4) | collective-permute-done | bytes 524320 | tf_op jit(solution)/shard_map/ppermute | solution.py:12
  42.8 0.0 copy-start
  42.8 0.1 broadcast_select_fusion.1
  42.9 0.9 collective-permute-start.5
  45.0 0.0 copy-done.4
  45.0 0.0 collective-permute-done.2
  45.1 0.1 broadcast_select_fusion.6
  45.1 2.4 collective-permute-start.3
  47.5 8.9 %collective-permute-done.5 = bf16[2,512,256]{2,0,1:T(2,128)(2,1)S(1)} collective-permute-done((bf16[2,512,256]{2,0,1:T(2,128)(2,1)S(1)}, bf16[2,512,256]{2,0,1:T(2,128)(2,1)S(1)}, u32[]{:S(2)}, u32[]{:S(2)}) %collective-permute-start.5) | collective-permute-done | bytes 524320 | tf_op jit(solution)/shard_map/ppermute | solution.py:12
  56.4 0.1 broadcast_select_fusion.2
  56.4 0.1 collective-permute-start.6
  57.8 0.0 copy-done
  57.8 3.0 gather_fusion
  60.7 1.0 fusion.16
  61.8 34.1 %collective-permute-done.3 = bf16[2,512,256]{2,0,1:T(2,128)(2,1)} collective-permute-done((bf16[2,512,256]{2,0,1:T(2,128)(2,1)S(1)}, bf16[2,512,256]{2,0,1:T(2,128)(2,1)}, u32[]{:S(2)}, u32[]{:S(2)}) %collective-permute-start.3) | collective-permute-done | bytes 524320 | tf_op jit(solution)/shard_map/ppermute | solution.py:12
  95.9 0.1 broadcast_select_fusion.7
  95.9 11.1 %collective-permute-done.6 = bf16[2,512,256]{2,0,1:T(2,128)(2,1)S(1)} collective-permute-done((bf16[2,512,256]{2,0,1:T(2,128)(2,1)S(1)}, bf16[2,512,256]{2,0,1:T(2,128)(2,1)S(1)}, u32[]{:S(2)}, u32[]{:S(2)}) %collective-permute-start.6) | collective-permute-done | bytes 524320 | tf_op jit(solution)/shard_map/ppermute | solution.py:12
  107.0 0.1 broadcast_select_fusion.3
  107.1 0.0 copy-start.1
  107.1 0.8 copy-done.1
  107.9 1.5 pad_maximum_fusion.1
  109.4 3.8 %gather_fusion.1 = bf16[512,2,2,256]{3,2,1,0:T(2,128)(2,1)S(1)} fusion(bf16[2,2,512,256]{3,1,2,0:T(2,128)(2,1)S(1)} %pad_maximum_fusion.1, s32[1024]{0:T(1024)S(1)} %pad_clamp_fusion), kind=kCustom, calls=%fused_computation.1 | custom fusion | bytes 2099200 | tf_op jit(solution)/shard_map/jit(_take)/gather | solution.py:49
  113.1 1.4 fusion
  114.5 0.0 all-reduce.7.cloned.1.call-update
  114.5 0.0 all-reduce.5.cloned.1.call-start
  114.6 57.2 %all-reduce.7.cloned.1.call-done = (bf16[2,2,512,256]{3,2,1,0:T(8,128)(2,1)}, bf16[2,512,256]{2,1,0:T(8,128)(2,1)}) async-done(((bf16[2,2,512,256]{3,2,1,0:T(8,128)(2,1)}, bf16[2,512,256]{2,1,0:T(8,128)(2,1)}), (bf16[2,2,512,256]{3,2,1,0:T(8,128)(2,1)}, bf16[2,512,256]{2,1,0:T(8,128)(2,1)})) %all-reduce.7.cloned.1.call-update) | async-done | bytes 1572880 | tf_op jit(solution)/shard_map/psum | solution.py:64
  171.8 1.3 slice_bitcast_fusion
  173.1 0.1 slice_negate_fusion
  173.3 0.0 copy-done.2
  173.3 0.7 convolution_convert_fusion
  174.0 0.0 copy-start.3
  174.0 0.6 convert_element_type.39
  174.6 0.4 copy-done.3
  175.1 0.1 slice_negate_fusion.2
  175.1 0.7 convolution_convert_fusion.2
  175.9 0.6 convert_element_type.33
  176.5 0.8 convolution_convert_fusion.1
  177.2 0.6 convert_element_type.37
  177.8 2.6 add_reduce_fusion.1
  180.4 0.7 stack.39
  181.1 0.7 stack.40
  181.9 0.7 stack.43
  182.6 0.7 stack.44
  183.3 1.9 maximum_bitcast_fusion
  185.2 1.9 maximum_bitcast_fusion.1
  187.1 3.9 %pad_maximum_fusion = f32[512,2,2,512]{3,2,1,0:T(2,128)} fusion(f32[512,1,2,512]{3,2,1,0:T(2,128)S(1)} %maximum_bitcast_fusion.1, f32[512,1,2,512]{3,2,1,0:T(2,128)S(1)} %maximum_bitcast_fusion), kind=kLoop, calls=%fused_computation.2 | loop fusion | flops 1048576 | bytes 8388608 | tf_op jit(solution)/shard_map/stack | solution.py:72
  191.0 0.0 all-reduce.5.cloned.1.call-update
  191.0 0.6 copy-done.5
  191.6 0.6 dynamic-slice
  192.9 108.6 %all-reduce.5.cloned.1.call-done = f32[512,2,2,512]{3,2,1,0:T(2,128)} async-done(((f32[512,2,2,512]{3,2,1,0:T(2,128)}), f32[512,2,2,512]{3,2,1,0:T(2,128)}) %all-reduce.5.cloned.1.call-update) | async-done | bytes 4194320
  301.5 1.8 dynamic-slice_multiply_fusion
  (5 shorter events, 0.0 us)
Async XLA Ops:
  6.5 165.3 %all-reduce.7.cloned.1.call-start = ((), (), s32[]{:S(2)}) async-start(), calls=%async_computation.1 | async-start | bytes 3145728 | tf_op jit(solution)/shard_map/psum | solution.py:64
  8.1 8.8 %collective-permute-start = (bf16[2,512,256]{2,0,1:T(2,128)(2,1)S(1)}, bf16[2,512,256]{2,0,1:T(2,128)(2,1)S(1)}, u32[]{:S(2)}, u32[]{:S(2)}) collective-permute-start(bf16[2,512,256]{2,0,1:T(2,128)(2,1)S(1)} %copy.10), channel_id=1, source_target_pairs={{30,0},{0,2},{2,4},{4,6},{6,8},{8,10},{10,12},{12,14},{14,16},{16,... | collective-permute-start | bytes 1572872 | tf_op jit(solution)/shard_map/ppermute | solution.py:12
  19.0 26.0 %copy-start.4 = (s32[512]{0:T(512)S(1)}, s32[512]{0:T(512)}, u32[]{:S(2)}) copy-start(s32[512]{0:T(512)} %param.5) | copy-start | bytes 6148
  19.0 12.6 %collective-permute-start.1 = (bf16[2,512,256]{2,0,1:T(2,128)(2,1)S(1)}, bf16[2,512,256]{2,0,1:T(2,128)(2,1)S(1)}, u32[]{:S(2)}, u32[]{:S(2)}) collective-permute-start(bf16[2,512,256]{2,0,1:T(2,128)(2,1)S(1)} %get-tuple-element.17), channel_id=1, source_target_pairs={{28,0},{30,2},{0,4},{2,6},{4,8},{6,10},{8,12},{10,14},{12,16},{14,... | collective-permute-start | bytes 1572872 | tf_op jit(solution)/shard_map/ppermute | solution.py:12
  20.3 22.5 %collective-permute-start.4 = (bf16[2,512,256]{2,0,1:T(2,128)(2,1)S(1)}, bf16[2,512,256]{2,0,1:T(2,128)(2,1)S(1)}, u32[]{:S(2)}, u32[]{:S(2)}) collective-permute-start(bf16[2,512,256]{2,0,1:T(2,128)(2,1)S(1)} %get-tuple-element.18), channel_id=1, source_target_pairs={{28,0},{30,2},{0,4},{2,6},{4,8},{6,10},{8,12},{10,14},{12,16},{14,... | collective-permute-start | bytes 1572872 | tf_op jit(solution)/shard_map/ppermute | solution.py:12
  31.6 13.4 %collective-permute-start.2 = (bf16[2,512,256]{2,0,1:T(2,128)(2,1)S(1)}, bf16[2,512,256]{2,0,1:T(2,128)(2,1)S(1)}, u32[]{:S(2)}, u32[]{:S(2)}) collective-permute-start(bf16[2,512,256]{2,0,1:T(2,128)(2,1)S(1)} %bitcast.42), channel_id=1, source_target_pairs={{24,0},{26,2},{28,4},{30,6},{0,8},{2,10},{4,12},{6,14},{8,16},{10,... | collective-permute-start | bytes 1572872 | tf_op jit(solution)/shard_map/ppermute | solution.py:12
  42.8 15.0 %copy-start = (bf16[2,512,256]{2,1,0:T(8,128)(2,1)S(1)}, bf16[2,512,256]{2,1,0:T(8,128)(2,1)}, u32[]{:S(2)}) copy-start(bf16[2,512,256]{2,1,0:T(8,128)(2,1)} %param.3) | copy-start | bytes 1572868
  42.9 13.5 %collective-permute-start.5 = (bf16[2,512,256]{2,0,1:T(2,128)(2,1)S(1)}, bf16[2,512,256]{2,0,1:T(2,128)(2,1)S(1)}, u32[]{:S(2)}, u32[]{:S(2)}) collective-permute-start(bf16[2,512,256]{2,0,1:T(2,128)(2,1)S(1)} %bitcast.43), channel_id=1, source_target_pairs={{24,0},{26,2},{28,4},{30,6},{0,8},{2,10},{4,12},{6,14},{8,16},{10,... | collective-permute-start | bytes 1572872 | tf_op jit(solution)/shard_map/ppermute | solution.py:12
  45.1 50.8 %collective-permute-start.3 = (bf16[2,512,256]{2,0,1:T(2,128)(2,1)S(1)}, bf16[2,512,256]{2,0,1:T(2,128)(2,1)}, u32[]{:S(2)}, u32[]{:S(2)}) collective-permute-start(bf16[2,512,256]{2,0,1:T(2,128)(2,1)S(1)} %bitcast.44), channel_id=1, source_target_pairs={{16,0},{18,2},{20,4},{22,6},{24,8},{26,10},{28,12},{30,14},{0,16},... | collective-permute-start | bytes 1572872 | tf_op jit(solution)/shard_map/ppermute | solution.py:12
  56.4 50.6 %collective-permute-start.6 = (bf16[2,512,256]{2,0,1:T(2,128)(2,1)S(1)}, bf16[2,512,256]{2,0,1:T(2,128)(2,1)S(1)}, u32[]{:S(2)}, u32[]{:S(2)}) collective-permute-start(bf16[2,512,256]{2,0,1:T(2,128)(2,1)S(1)} %bitcast.45), channel_id=1, source_target_pairs={{16,0},{18,2},{20,4},{22,6},{24,8},{26,10},{28,12},{30,14},{0,16},... | collective-permute-start | bytes 1572872 | tf_op jit(solution)/shard_map/ppermute | solution.py:12
  107.1 0.8 copy-start.1
  114.5 186.9 %all-reduce.5.cloned.1.call-start = ((), (), s32[]{:S(2)}) async-start(), calls=%async_computation | async-start | bytes 8388608
  171.8 1.5 copy-start.2
  174.0 1.0 copy-start.3
  191.0 0.7 copy-start.5
Sparse Core Ops, SparseCore 0:
  114.6 57.1 all-reduce.6
  191.1 110.3 all-reduce.4
where the time goes:
time: 312 us; the launch traced here: 310 us
  waiting for transfers between devices  242 us (78%)
  other arithmetic  21.1 us (7%)
  between operations  19.4 us (6%)
  local copies, waits for them, and re-layouts  15.6 us (5%)
  starting transfers between devices  9.43 us (3%)
    unnamed x3, waiting for transfers between devices  109 us
    ppermute x7, waiting for transfers between devices, from_behind(): return lax.ppermute(block, axis, route)  76.5 us
    psum x1, waiting for transfers between devices, on_device(): shifted_rows = lax.psum(collect(moving).astype(jnp.bfloat16), 'ga')  57.2 us
    ppermute x7, starting transfers between devices, from_behind(): return lax.ppermute(block, axis, route)  9.39 us
    another operation x3, other arithmetic, on_device(): jnp.stack(pieces, axis=1)  7.64 us
    gather x2, local copies, waits for them, and re-layouts, collect(): picked = jnp.take(fields, clipped, axis=-2).astype(jnp.float32)  6.73 us
  transfers between devices with their start and end apart: 9, of which 8 were waited for; matrix products, arithmetic and copies ran while one was open for 2% of the time, Pallas kernels for 0%

commit v1 on v0

v1 whole, which is shorter than its diff:
```python
import functools
import math

import jax
import jax.numpy as jnp
from jax import lax
from jax.experimental import pallas as pl
from jax.experimental.pallas import tpu as pltpu
from jax.sharding import Mesh
from jax.sharding import PartitionSpec as P

VMEM_LIMIT = 40 * 1024 * 1024
SPLIT = 2
ALL = ("half", "inner", "hi", "lo")


def swap(block, cut, other):
    half, inner, hi, lo = (lax.axis_size(name) for name in ALL)
    slabs = hi * lo
    size = half * inner * slabs
    route = []
    for place in range(size):
        kplace, slab = divmod(place, slabs)
        kplace = (kplace + cut * inner) % (half * inner)
        route.append((place, kplace * slabs + (slab ^ other)))
    return lax.ppermute(block, ALL, route)


def field_kernel(count, lo_ref, rows_ref, *refs):
    slab_refs, (out_ref, picked_ref) = refs[:count], refs[count:]
    slab_size, channels = slab_refs[0].shape
    npoints = rows_ref.shape[0]
    half = channels // 2
    groups, _, _, length, _ = out_ref.shape
    place = pl.program_id(0)

    @pl.when(place == 0)
    def _():
        spot = lax.broadcasted_iota(jnp.int32, (npoints, slab_size), 1)
        picked = jnp.zeros((npoints, channels), jnp.float32)
        for number, slab_ref in enumerate(slab_refs):
            chosen = (rows_ref[:, number : number + 1] == spot).astype(jnp.float32)
            picked += jnp.dot(
                chosen.astype(jnp.bfloat16), slab_ref[...], preferred_element_type=jnp.float32
            )
        rotated = jnp.concatenate([-picked[:, half:], picked[:, :half]], axis=1)
        picked_ref[0] = picked.astype(jnp.bfloat16)
        picked_ref[1] = rotated.astype(jnp.bfloat16)

    for number in range(SPLIT):

        @pl.when(place == number)
        def _(number=number):
            for part in range(2):
                product = lax.dot_general(
                    picked_ref[part],
                    slab_refs[number][...],
                    (((1,), (1,)), ((), ())),
                    preferred_element_type=jnp.float32,
                )
                pieces = product.reshape(groups, length, slab_size)
                out_ref[:, 0, part] = pieces.astype(jnp.bfloat16)


def make_fields(slabs, rows, groups, lo):
    slab_size, channels = slabs[0].shape
    npoints = rows.shape[0]
    length = npoints // groups
    whole = lambda place, lo: (0, 0)
    return pl.pallas_call(
        functools.partial(field_kernel, len(slabs)),
        grid_spec=pltpu.PrefetchScalarGridSpec(
            num_scalar_prefetch=1,
            grid=(SPLIT,),
            in_specs=[pl.BlockSpec(rows.shape, whole)]
            + [pl.BlockSpec((slab_size, channels), whole) for _ in slabs],
            out_specs=pl.BlockSpec(
                (groups, 1, 2, length, slab_size), lambda place, lo: (0, lo[0] ^ place, 0, 0, 0)
            ),
            scratch_shapes=[pltpu.VMEM((2, npoints, channels), jnp.bfloat16)],
        ),
        out_shape=jax.ShapeDtypeStruct((groups, SPLIT, 2, length, slab_size), jnp.bfloat16),
        compiler_params=pltpu.CompilerParams(vmem_limit_bytes=VMEM_LIMIT),
        name="fields",
    )(lo, rows, *slabs)


def pair_kernel(scale, table_ref, near_ref, far_ref, out_ref, held_ref):
    total_k, _, length, width = held_ref.shape
    transfers = table_ref.shape[0]
    held_ref[: total_k // 2] = near_ref[...].astype(jnp.float32)
    held_ref[total_k // 2 :] = far_ref[...].astype(jnp.float32)

    def load(k, part, start, count):
        return held_ref[k, part, pl.ds(start, count), :]

    count = min(16, length)
    for start in range(0, length, count):

        def step(k, sums):
            real, imag = load(k, 0, start, count), load(k, 1, start, count)
            after = []
            for transfer in range(transfers):
                other = table_ref[transfer, k]
                other_real = load(other, 0, start, count)
                other_imag = load(other, 1, start, count)
                after.append(sums[2 * transfer] + (real * other_real + imag * other_imag))
                after.append(sums[2 * transfer + 1] + (imag * other_real - real * other_imag))
            return tuple(after)

        zero = jnp.zeros((count, width), jnp.float32)
        sums = lax.fori_loop(0, total_k, step, (zero,) * (2 * transfers), unroll=4)
        for place, value in enumerate(sums):
            out_ref[pl.ds(start, count), place // 2, place % 2, :] = value * scale


def make_pairs(near, far, table):
    half_k, _, length, slab_size = near.shape
    transfers = table.shape[0]
    width = 256
    fields = pl.BlockSpec((half_k, 2, length, width), lambda r, table: (0, 0, 0, r))
    return pl.pallas_call(
        functools.partial(pair_kernel, 1.0 / math.sqrt(2 * half_k)),
        grid_spec=pltpu.PrefetchScalarGridSpec(
            num_scalar_prefetch=1,
            grid=(slab_size // width,),
            in_specs=[fields, fields],
            out_specs=pl.BlockSpec((length, transfers, 2, width), lambda r, table: (0, 0, 0, r)),
            scratch_shapes=[pltpu.VMEM((2 * half_k, 2, length, width), jnp.float32)],
        ),
        out_shape=jax.ShapeDtypeStruct((length, transfers, 2, slab_size), jnp.float32),
        compiler_params=pltpu.CompilerParams(vmem_limit_bytes=VMEM_LIMIT),
        name="pairs",
    )(table, near, far)


def on_device(orbitals, minus_table, points):
    kdevice, slab_size, channels = orbitals.shape
    half = lax.axis_index("half")
    groups = lax.axis_size("inner")
    slabs = lax.axis_size("hi") * lax.axis_size("lo")
    lo = lax.axis_index("lo")
    here = lax.axis_index("hi") * SPLIT + lo
    total_k = 2 * groups * kdevice

    mine = lax.dynamic_index_in_dim(orbitals, lo, 0, keepdims=False)
    other = lax.dynamic_index_in_dim(orbitals, 1 - lo, 0, keepdims=False)
    near = [mine] + [swap(other if x & 1 else mine, 0, x) for x in range(1, slabs)]
    far = [swap(other if x & 1 else mine, 1, x) for x in range(slabs)]

    half_points = points.shape[0] // 2
    wanted = lax.dynamic_slice_in_dim(points, half * half_points, half_points)
    starts = jnp.stack([(here ^ x) * slab_size for x in range(slabs)])
    rows = wanted[:, None] - starts[None, :]

    def share(held):
        fields = make_fields(held, rows, groups, lo.reshape(1))
        fields = fields.reshape((groups * SPLIT,) + fields.shape[2:])
        return lax.all_to_all(fields, ("inner", "lo"), split_axis=0, concat_axis=0, tiled=True)

    near_fields = share(near)
    far_fields = share(far)

    turn = half * (total_k // 2)
    table = (jnp.roll(minus_table, -turn, axis=1) - turn) % total_k
    return make_pairs(near_fields, far_fields, table)


def solution(mesh):
    kplaces, slabs = mesh.shape["ka"], mesh.shape["ga"]
    devices = mesh.devices.reshape(2, kplaces // 2, slabs // SPLIT, SPLIT)
    finer = Mesh(devices, ALL)
    return jax.shard_map(
        on_device,
        mesh=finer,
        in_specs=(P(("half", "inner"), ("hi", "lo"), None), P(), P()),
        out_specs=P(("half", "inner"), None, None, ("hi", "lo")),
        check_vma=False,
    )
```

time: 312 us -> 80.5 us (0.26)
  waiting for transfers between devices: 242 us -> 55.2 us
  other arithmetic: 21.1 us -> 0.33 us
  between operations: 19.4 us -> 0.03 us
  local copies, waits for them, and re-layouts: 15.6 us -> 2.49 us
  Pallas kernels: 0 us -> 6.95 us
  starting transfers between devices: 9.43 us -> 15.2 us
    unnamed x3 -> x0, waiting for transfers between devices: 109 us -> none
    psum x1 -> x0, waiting for transfers between devices: 57.2 us -> none  [on_device(): shifted_rows = lax.psum(collect(moving).astype(jnp.bfloat16), 'ga')]
    ppermute x7 -> x3, waiting for transfers between devices: 76.5 us -> 39.4 us  [swap(): return lax.ppermute(block, ALL, route)]
    all_to_all x0 -> x2, waiting for transfers between devices: none -> 15.7 us  [share(): lax.all_to_all(fields, ('inner', 'lo'), split_axis=0, concat_axis=0, tile...]
    all_to_all x0 -> x2, starting transfers between devices: none -> 9.59 us  [share(): lax.all_to_all(fields, ('inner', 'lo'), split_axis=0, concat_axis=0, tile...]
    another operation x4 -> x1, other arithmetic: 9.12 us -> 0.07 us  [on_device(): starts = jnp.stack([(here ^ x) * slab_size for x in range(slabs)])]
    pallas_call x0 -> x3, Pallas kernels: none -> 6.95 us  [the longest x2 3.84 us: make_fields(): pl.pallas_call(functools.partial(field_kernel, len(slabs)), grid_spec=plt...]
    gather x2 -> x0, local copies, waits for them, and re-layouts: 6.73 us -> none  [collect(): picked = jnp.take(fields, clipped, axis=-2).astype(jnp.float32)]
  transfers between devices with their start and end apart: 9 -> 5, of which waited for: 8 -> 4; matrix products, arithmetic and copies ran while one was open for 2% -> 1% of each run, Pallas kernels for 0% -> 2%
where the time goes in v1:
time: 80.5 us; the launch traced here: 80.2 us
  waiting for transfers between devices  55.2 us (69%)
  starting transfers between devices  15.2 us (19%)
  Pallas kernels  6.95 us (9%)
  local copies, waits for them, and re-layouts  2.49 us (3%)
    ppermute x3, waiting for transfers between devices, swap(): return lax.ppermute(block, ALL, route)  39.4 us
    all_to_all x2, waiting for transfers between devices, share(): lax.all_to_all(fields, ('inner', 'lo'), split_axis=0, concat_axis=0, tile...  15.7 us
    all_to_all x2, starting transfers between devices, share(): lax.all_to_all(fields, ('inner', 'lo'), split_axis=0, concat_axis=0, tile...  9.59 us
    ppermute x3, starting transfers between devices, swap(): return lax.ppermute(block, ALL, route)  5.62 us
    pallas_call x2, Pallas kernels, make_fields(): pl.pallas_call(functools.partial(field_kernel, len(slabs)), grid_spec=plt...  3.84 us
    pallas_call x1, Pallas kernels, make_pairs(): pl.pallas_call(functools.partial(pair_kernel, 1.0 / math.sqrt(2 * half_k)...  3.12 us
  transfers between devices with their start and end apart: 5, of which 4 were waited for; matrix products, arithmetic and copies ran while one was open for 1% of the time, Pallas kernels for 2%

profile of v1, /device:TPU:1, one launch (start us, length us, event | category | flops | bytes accessed | tf_op | source)
XLA Modules:
  0.0 80.2 jit_solution(9037645222047153714)
XLA Ops:
  0.0 1.1 %dynamic-slice_bitcast_fusion = (bf16[512,256]{1,0:T(8,128)(2,1)S(1)}, bf16[512,256]{1,0:T(8,128)(2,1)S(1)}) fusion(bf16[2,512,256]{2,1,0:T(8,128)(2,1)} %param.3, s32[]{:T(128)S(6)} %select_n.34, s32[]{:T(128)S(6)} %select_n.33), kind=kLoop, calls=%fused_computation | loop fusion | bytes 1048584 | tf_op jit(solution)/shard_map/jit(dynamic_index_in_dim)/squeeze | solution.py:147
  1.1 3.2 %collective-permute-start.1 = (bf16[512,256]{1,0:T(8,128)(2,1)S(1)}, bf16[512,256]{1,0:T(8,128)(2,1)S(1)}, u32[]{:S(2)}, u32[]{:S(2)}) collective-permute-start(bf16[512,256]{1,0:T(8,128)(2,1)S(1)} %get-tuple-element.6.refs_0_), channel_id=1, source_target_pairs={{0,16},{1,17},{2,18},{3,19},{4,20},{5,21},{6,22},{7,23},{8,24},{9,... | collective-permute-start | bytes 786440 | tf_op jit(solution)/shard_map/ppermute | solution.py:26
  4.3 1.0 %collective-permute-start.2 = (bf16[512,256]{1,0:T(8,128)(2,1)S(1)}, bf16[512,256]{1,0:T(8,128)(2,1)S(1)}, u32[]{:S(2)}, u32[]{:S(2)}) collective-permute-start(bf16[512,256]{1,0:T(8,128)(2,1)S(1)} %get-tuple-element.5), channel_id=1, source_target_pairs={{0,17},{1,16},{2,19},{3,18},{4,21},{5,20},{6,23},{7,22},{8,25},{9,... | collective-permute-start | bytes 786440 | tf_op jit(solution)/shard_map/ppermute | solution.py:26
  5.3 0.1 pad_add_fusion.1
  5.4 0.0 copy-start.1
  5.4 0.7 copy-done.1
  6.1 0.1 dynamic_slice.15
  6.1 0.1 broadcast_subtract_fusion.rows_ref
  6.2 15.3 %collective-permute-done.1.refs_0_ = bf16[512,256]{1,0:T(8,128)(2,1)S(1)} collective-permute-done((bf16[512,256]{1,0:T(8,128)(2,1)S(1)}, bf16[512,256]{1,0:T(8,128)(2,1)S(1)}, u32[]{:S(2)}, u32[]{:S(2)}) %collective-permute-start.1) | collective-permute-done | bytes 262176 | tf_op jit(solution)/shard_map/ppermute | solution.py:26
  21.5 6.3 %collective-permute-done.2.refs_1_ = bf16[512,256]{1,0:T(8,128)(2,1)S(1)} collective-permute-done((bf16[512,256]{1,0:T(8,128)(2,1)S(1)}, bf16[512,256]{1,0:T(8,128)(2,1)S(1)}, u32[]{:S(2)}, u32[]{:S(2)}) %collective-permute-start.2) | collective-permute-done | bytes 262176 | tf_op jit(solution)/shard_map/ppermute | solution.py:26
  27.9 1.9 %fields.3 = bf16[8,2,2,32,512]{4,3,2,1,0:T(8,128)(2,1)} custom-call(s32[1]{0:T(128)} %bitcast.lo_ref, s32[256,2]{1,0:T(8,128)S(1)} %broadcast_subtract_fusion.rows_ref, bf16[512,256]{1,0:T(8,128)(2,1)S(1)} %collective-permute-done.1.refs_0_, bf16[512,256]{1,0:T(8,128)(2,1)S(1)} %collective-permute-done.2.refs_1_), custom_call_target="tpu_custom_call" | custom-call | tf_op jit(solution)/shard_map/fields/pallas_call | solution.py:70
  29.8 5.0 %all-to-all-start.1 = ((bf16[16,2,32,512]{3,2,1,0:T(8,128)(2,1)}), bf16[16,2,32,512]{3,2,1,0:T(8,128)(2,1)S(1)}, u32[]{:S(2)}, u32[]{:S(2)}) async-start(bf16[16,2,32,512]{3,2,1,0:T(8,128)(2,1)} %bitcast.6), calls=%async_computation.1 | async-start | bytes 2097152 | tf_op jit(solution)/shard_map/all_to_all | solution.py:159
  34.8 1.4 %collective-permute-start = (bf16[512,256]{1,0:T(8,128)(2,1)S(1)}, bf16[512,256]{1,0:T(8,128)(2,1)S(1)}, u32[]{:S(2)}, u32[]{:S(2)}) collective-permute-start(bf16[512,256]{1,0:T(8,128)(2,1)S(1)} %get-tuple-element.5), channel_id=1, source_target_pairs={{0,1},{1,0},{2,3},{3,2},{4,5},{5,4},{6,7},{7,6},{8,9},{9,8},{10,11... | collective-permute-start | bytes 786440 | tf_op jit(solution)/shard_map/ppermute | solution.py:26
  36.1 17.8 %collective-permute-done.refs_1_ = bf16[512,256]{1,0:T(8,128)(2,1)S(1)} collective-permute-done((bf16[512,256]{1,0:T(8,128)(2,1)S(1)}, bf16[512,256]{1,0:T(8,128)(2,1)S(1)}, u32[]{:S(2)}, u32[]{:S(2)}) %collective-permute-start) | collective-permute-done | bytes 262176 | tf_op jit(solution)/shard_map/ppermute | solution.py:26
  54.0 1.9 %fields.2 = bf16[8,2,2,32,512]{4,3,2,1,0:T(8,128)(2,1)} custom-call(s32[1]{0:T(128)} %bitcast.lo_ref, s32[256,2]{1,0:T(8,128)S(1)} %broadcast_subtract_fusion.rows_ref, bf16[512,256]{1,0:T(8,128)(2,1)S(1)} %get-tuple-element.6.refs_0_, bf16[512,256]{1,0:T(8,128)(2,1)S(1)} %collective-permute-done.refs_1_), custom_call_target="tpu_custom_call" | custom-call | tf_op jit(solution)/shard_map/fields/pallas_call | solution.py:70
  55.9 0.0 all-to-all-done.1.far_ref
  55.9 4.6 %all-to-all-start = ((bf16[16,2,32,512]{3,2,1,0:T(8,128)(2,1)}), bf16[16,2,32,512]{3,2,1,0:T(8,128)(2,1)S(1)}, u32[]{:S(2)}, u32[]{:S(2)}) async-start(bf16[16,2,32,512]{3,2,1,0:T(8,128)(2,1)} %bitcast.5), calls=%async_computation | async-start | bytes 2097152 | tf_op jit(solution)/shard_map/all_to_all | solution.py:159
  60.5 0.0 copy-start
  60.5 0.7 copy-done
  61.2 0.1 pad_add_fusion
  61.3 0.1 and_select_fusion.table_ref
  61.3 15.7 %all-to-all-done.near_ref = bf16[16,2,32,512]{3,2,1,0:T(8,128)(2,1)S(1)} async-done(((bf16[16,2,32,512]{3,2,1,0:T(8,128)(2,1)}), bf16[16,2,32,512]{3,2,1,0:T(8,128)(2,1)S(1)}, u32[]{:S(2)}, u32[]{:S(2)}) %all-to-all-start) | async-done | bytes 1048608 | tf_op jit(solution)/shard_map/all_to_all | solution.py:159
  77.0 3.1 %pairs.1 = f32[32,2,2,512]{3,2,1,0:T(2,128)} custom-call(s32[2,32]{1,0:T(2,128)S(1)} %and_select_fusion.table_ref, bf16[16,2,32,512]{3,2,1,0:T(8,128)(2,1)S(1)} %all-to-all-done.near_ref, bf16[16,2,32,512]{3,2,1,0:T(8,128)(2,1)S(1)} %all-to-all-done.1.far_ref), custom_call_target="tpu_custom_call" | custom-call | tf_op jit(solution)/shard_map/pairs/pallas_call | solution.py:122
Async XLA Ops:
  1.1 20.5 %collective-permute-start.1 = (bf16[512,256]{1,0:T(8,128)(2,1)S(1)}, bf16[512,256]{1,0:T(8,128)(2,1)S(1)}, u32[]{:S(2)}, u32[]{:S(2)}) collective-permute-start(bf16[512,256]{1,0:T(8,128)(2,1)S(1)} %get-tuple-element.6.refs_0_), channel_id=1, source_target_pairs={{0,16},{1,17},{2,18},{3,19},{4,20},{5,21},{6,22},{7,23},{8,24},{9,... | collective-permute-start | bytes 786440 | tf_op jit(solution)/shard_map/ppermute | solution.py:26
  4.3 23.6 %collective-permute-start.2 = (bf16[512,256]{1,0:T(8,128)(2,1)S(1)}, bf16[512,256]{1,0:T(8,128)(2,1)S(1)}, u32[]{:S(2)}, u32[]{:S(2)}) collective-permute-start(bf16[512,256]{1,0:T(8,128)(2,1)S(1)} %get-tuple-element.5), channel_id=1, source_target_pairs={{0,17},{1,16},{2,19},{3,18},{4,21},{5,20},{6,23},{7,22},{8,25},{9,... | collective-permute-start | bytes 786440 | tf_op jit(solution)/shard_map/ppermute | solution.py:26
  5.4 0.7 copy-start.1
  29.8 26.1 %all-to-all-start.1 = ((bf16[16,2,32,512]{3,2,1,0:T(8,128)(2,1)}), bf16[16,2,32,512]{3,2,1,0:T(8,128)(2,1)S(1)}, u32[]{:S(2)}, u32[]{:S(2)}) async-start(bf16[16,2,32,512]{3,2,1,0:T(8,128)(2,1)} %bitcast.6), calls=%async_computation.1 | async-start | bytes 2097152 | tf_op jit(solution)/shard_map/all_to_all | solution.py:159
  34.8 19.2 %collective-permute-start = (bf16[512,256]{1,0:T(8,128)(2,1)S(1)}, bf16[512,256]{1,0:T(8,128)(2,1)S(1)}, u32[]{:S(2)}, u32[]{:S(2)}) collective-permute-start(bf16[512,256]{1,0:T(8,128)(2,1)S(1)} %get-tuple-element.5), channel_id=1, source_target_pairs={{0,1},{1,0},{2,3},{3,2},{4,5},{5,4},{6,7},{7,6},{8,9},{9,8},{10,11... | collective-permute-start | bytes 786440 | tf_op jit(solution)/shard_map/ppermute | solution.py:26
  55.9 21.2 %all-to-all-start = ((bf16[16,2,32,512]{3,2,1,0:T(8,128)(2,1)}), bf16[16,2,32,512]{3,2,1,0:T(8,128)(2,1)S(1)}, u32[]{:S(2)}, u32[]{:S(2)}) async-start(bf16[16,2,32,512]{3,2,1,0:T(8,128)(2,1)} %bitcast.5), calls=%async_computation | async-start | bytes 2097152 | tf_op jit(solution)/shard_map/all_to_all | solution.py:159
  60.5 0.7 copy-start

commit v2 on v1

--- a/solution.py
+++ b/solution.py
@@ -153,13 +153,14 @@
     starts = jnp.stack([(here ^ x) * slab_size for x in range(slabs)])
     rows = wanted[:, None] - starts[None, :]
 
-    def share(held):
-        fields = make_fields(held, rows, groups, lo.reshape(1))
+    def share(fields):
         fields = fields.reshape((groups * SPLIT,) + fields.shape[2:])
         return lax.all_to_all(fields, ("inner", "lo"), split_axis=0, concat_axis=0, tiled=True)
 
-    near_fields = share(near)
-    far_fields = share(far)
+    near_fields = make_fields(near, rows, groups, lo.reshape(1))
+    near_fields, rows = lax.optimization_barrier((near_fields, rows))
+    near_fields = share(near_fields)
+    far_fields = share(make_fields(far, rows, groups, lo.reshape(1)))
 
     turn = half * (total_k // 2)
     table = (jnp.roll(minus_table, -turn, axis=1) - turn) % total_k

time: 80.5 us -> 74.1 us (0.920)
  blocking collectives: 0 us -> 20.7 us
  waiting for transfers between devices: 55.2 us -> 35.4 us
  starting transfers between devices: 15.2 us -> 8.23 us
    all_to_all x0 -> x1, blocking collectives: none -> 20.7 us  [share(): lax.all_to_all(fields, ('inner', 'lo'), split_axis=0, concat_axis=0, tile...]
    ppermute x3, waiting for transfers between devices: 39.4 us -> 19.7 us  [swap(): return lax.ppermute(block, ALL, route)]
    all_to_all x2 -> x1, starting transfers between devices: 9.59 us -> 3.79 us  [share(): lax.all_to_all(fields, ('inner', 'lo'), split_axis=0, concat_axis=0, tile...]
    ppermute x3, starting transfers between devices: 5.62 us -> 4.45 us  [swap(): return lax.ppermute(block, ALL, route)]
    all_to_all x2 -> x1, waiting for transfers between devices: 15.7 us -> 15.7 us  [share(): lax.all_to_all(fields, ('inner', 'lo'), split_axis=0, concat_axis=0, tile...]
  transfers between devices with their start and end apart: 5 -> 4, of which waited for: 4 -> 3; matrix products, arithmetic and copies ran while one was open for 1% -> 1% of each run, Pallas kernels for 2% -> 3%
where the time goes in v2:
time: 74.1 us; the launch traced here: 73.6 us
  waiting for transfers between devices  35.4 us (48%)
  blocking collectives  20.7 us (28%)
  starting transfers between devices  8.23 us (11%)
  Pallas kernels  6.29 us (8%)
  local copies, waits for them, and re-layouts  2.49 us (3%)
    all_to_all x1, blocking collectives, share(): lax.all_to_all(fields, ('inner', 'lo'), split_axis=0, concat_axis=0, tile...  20.7 us
    ppermute x3, waiting for transfers between devices, swap(): return lax.ppermute(block, ALL, route)  19.7 us
    all_to_all x1, waiting for transfers between devices, share(): lax.all_to_all(fields, ('inner', 'lo'), split_axis=0, concat_axis=0, tile...  15.7 us
    ppermute x3, starting transfers between devices, swap(): return lax.ppermute(block, ALL, route)  4.45 us
    all_to_all x1, starting transfers between devices, share(): lax.all_to_all(fields, ('inner', 'lo'), split_axis=0, concat_axis=0, tile...  3.79 us
    pallas_call x2, Pallas kernels, make_fields(): pl.pallas_call(functools.partial(field_kernel, len(slabs)), grid_spec=plt...  3.18 us
    pallas_call x1, Pallas kernels, make_pairs(): pl.pallas_call(functools.partial(pair_kernel, 1.0 / math.sqrt(2 * half_k)...  3.12 us
  transfers between devices with their start and end apart: 4, of which 3 were waited for; matrix products, arithmetic and copies ran while one was open for 1% of the time, Pallas kernels for 3%

profile of v2, /device:TPU:1, one launch (start us, length us, event | category | flops | bytes accessed | tf_op | source)
XLA Modules:
  0.0 73.6 jit_solution(11110994187318454154)
XLA Ops:
  0.0 1.1 %dynamic-slice_bitcast_fusion = (bf16[512,256]{1,0:T(8,128)(2,1)S(1)}, bf16[512,256]{1,0:T(8,128)(2,1)S(1)}) fusion(bf16[2,512,256]{2,1,0:T(8,128)(2,1)} %param.3, s32[]{:T(128)S(6)} %select_n.34, s32[]{:T(128)S(6)} %select_n.33), kind=kLoop, calls=%fused_computation | loop fusion | bytes 1048584 | tf_op jit(solution)/shard_map/jit(dynamic_index_in_dim)/squeeze | solution.py:147
  1.1 2.1 %collective-permute-start = (bf16[512,256]{1,0:T(8,128)(2,1)S(1)}, bf16[512,256]{1,0:T(8,128)(2,1)S(1)}, u32[]{:S(2)}, u32[]{:S(2)}) collective-permute-start(bf16[512,256]{1,0:T(8,128)(2,1)S(1)} %get-tuple-element.9), channel_id=1, source_target_pairs={{0,1},{1,0},{2,3},{3,2},{4,5},{5,4},{6,7},{7,6},{8,9},{9,8},{10,11... | collective-permute-start | bytes 786440 | tf_op jit(solution)/shard_map/ppermute | solution.py:26
  3.2 2.3 %collective-permute-start.2 = (bf16[512,256]{1,0:T(8,128)(2,1)S(1)}, bf16[512,256]{1,0:T(8,128)(2,1)S(1)}, u32[]{:S(2)}, u32[]{:S(2)}) collective-permute-start(bf16[512,256]{1,0:T(8,128)(2,1)S(1)} %get-tuple-element.9), channel_id=1, source_target_pairs={{0,17},{1,16},{2,19},{3,18},{4,21},{5,20},{6,23},{7,22},{8,25},{9,... | collective-permute-start | bytes 786440 | tf_op jit(solution)/shard_map/ppermute | solution.py:26
  5.5 0.1 collective-permute-start.1
  5.5 0.1 pad_add_fusion.1
  5.6 0.0 copy-start.1
  5.6 0.7 copy-done.1
  6.3 0.1 dynamic_slice.15
  6.3 0.1 broadcast_subtract_fusion.rows_ref
  6.5 3.9 %collective-permute-done.refs_1_ = bf16[512,256]{1,0:T(8,128)(2,1)S(1)} collective-permute-done((bf16[512,256]{1,0:T(8,128)(2,1)S(1)}, bf16[512,256]{1,0:T(8,128)(2,1)S(1)}, u32[]{:S(2)}, u32[]{:S(2)}) %collective-permute-start) | collective-permute-done | bytes 262176 | tf_op jit(solution)/shard_map/ppermute | solution.py:26
  10.3 2.0 %fields.2 = bf16[8,2,2,32,512]{4,3,2,1,0:T(8,128)(2,1)} custom-call(s32[1]{0:T(128)} %bitcast.lo_ref, s32[256,2]{1,0:T(8,128)S(1)} %broadcast_subtract_fusion.rows_ref, bf16[512,256]{1,0:T(8,128)(2,1)S(1)} %get-tuple-element.10.refs_0_, bf16[512,256]{1,0:T(8,128)(2,1)S(1)} %collective-permute-done.refs_1_), custom_call_target="tpu_custom_call" | custom-call | tf_op jit(solution)/shard_map/fields/pallas_call | solution.py:70
  12.3 15.8 %collective-permute-done.1.refs_0_ = bf16[512,256]{1,0:T(8,128)(2,1)S(1)} collective-permute-done((bf16[512,256]{1,0:T(8,128)(2,1)S(1)}, bf16[512,256]{1,0:T(8,128)(2,1)S(1)}, u32[]{:S(2)}, u32[]{:S(2)}) %collective-permute-start.1) | collective-permute-done | bytes 262176 | tf_op jit(solution)/shard_map/ppermute | solution.py:26
  28.1 0.0 collective-permute-done.2.refs_1_
  28.1 1.2 %fields.3 = bf16[8,2,2,32,512]{4,3,2,1,0:T(8,128)(2,1)S(1)} custom-call(s32[1]{0:T(128)} %bitcast.lo_ref, s32[256,2]{1,0:T(8,128)S(1)} %broadcast_subtract_fusion.rows_ref, bf16[512,256]{1,0:T(8,128)(2,1)S(1)} %collective-permute-done.1.refs_0_, bf16[512,256]{1,0:T(8,128)(2,1)S(1)} %collective-permute-done.2.refs_1_), custom_call_target="tpu_custom_call" | custom-call | tf_op jit(solution)/shard_map/fields/pallas_call | solution.py:70
  29.3 20.7 %all_to_all.10.far_ref = bf16[16,2,32,512]{3,2,1,0:T(8,128)(2,1)S(1)} all-to-all(bf16[16,2,32,512]{3,2,1,0:T(8,128)(2,1)S(1)} %bitcast.9), channel_id=1, replica_groups=mesh['half'=2,'inner'=8,'hi'=1,'lo'=2] {'inner','lo'}, dimensions={0} | all-to-all | bytes 2097152 | tf_op jit(solution)/shard_map/all_to_all | solution.py:158
  50.1 3.8 %all-to-all-start = ((bf16[16,2,32,512]{3,2,1,0:T(8,128)(2,1)}), bf16[16,2,32,512]{3,2,1,0:T(8,128)(2,1)S(1)}, u32[]{:S(2)}, u32[]{:S(2)}) async-start(bf16[16,2,32,512]{3,2,1,0:T(8,128)(2,1)} %bitcast.5), calls=%async_computation | async-start | bytes 2097152 | tf_op jit(solution)/shard_map/all_to_all | solution.py:158
  53.9 0.0 copy-start
  53.9 0.7 copy-done
  54.5 0.1 pad_add_fusion
  54.6 0.1 and_select_fusion.table_ref
  54.7 15.7 %all-to-all-done.near_ref = bf16[16,2,32,512]{3,2,1,0:T(8,128)(2,1)S(1)} async-done(((bf16[16,2,32,512]{3,2,1,0:T(8,128)(2,1)}), bf16[16,2,32,512]{3,2,1,0:T(8,128)(2,1)S(1)}, u32[]{:S(2)}, u32[]{:S(2)}) %all-to-all-start) | async-done | bytes 1048608 | tf_op jit(solution)/shard_map/all_to_all | solution.py:158
  70.4 3.1 %pairs.1 = f32[32,2,2,512]{3,2,1,0:T(2,128)} custom-call(s32[2,32]{1,0:T(2,128)S(1)} %and_select_fusion.table_ref, bf16[16,2,32,512]{3,2,1,0:T(8,128)(2,1)S(1)} %all-to-all-done.near_ref, bf16[16,2,32,512]{3,2,1,0:T(8,128)(2,1)S(1)} %all_to_all.10.far_ref), custom_call_target="tpu_custom_call" | custom-call | tf_op jit(solution)/shard_map/pairs/pallas_call | solution.py:122
Async XLA Ops:
  1.1 9.3 %collective-permute-start = (bf16[512,256]{1,0:T(8,128)(2,1)S(1)}, bf16[512,256]{1,0:T(8,128)(2,1)S(1)}, u32[]{:S(2)}, u32[]{:S(2)}) collective-permute-start(bf16[512,256]{1,0:T(8,128)(2,1)S(1)} %get-tuple-element.9), channel_id=1, source_target_pairs={{0,1},{1,0},{2,3},{3,2},{4,5},{5,4},{6,7},{7,6},{8,9},{9,8},{10,11... | collective-permute-start | bytes 786440 | tf_op jit(solution)/shard_map/ppermute | solution.py:26
  3.2 24.9 %collective-permute-start.2 = (bf16[512,256]{1,0:T(8,128)(2,1)S(1)}, bf16[512,256]{1,0:T(8,128)(2,1)S(1)}, u32[]{:S(2)}, u32[]{:S(2)}) collective-permute-start(bf16[512,256]{1,0:T(8,128)(2,1)S(1)} %get-tuple-element.9), channel_id=1, source_target_pairs={{0,17},{1,16},{2,19},{3,18},{4,21},{5,20},{6,23},{7,22},{8,25},{9,... | collective-permute-start | bytes 786440 | tf_op jit(solution)/shard_map/ppermute | solution.py:26
  5.5 22.6 %collective-permute-start.1 = (bf16[512,256]{1,0:T(8,128)(2,1)S(1)}, bf16[512,256]{1,0:T(8,128)(2,1)S(1)}, u32[]{:S(2)}, u32[]{:S(2)}) collective-permute-start(bf16[512,256]{1,0:T(8,128)(2,1)S(1)} %get-tuple-element.10.refs_0_), channel_id=1, source_target_pairs={{0,16},{1,17},{2,18},{3,19},{4,20},{5,21},{6,22},{7,23},{8,24},{9,... | collective-permute-start | bytes 786440 | tf_op jit(solution)/shard_map/ppermute | solution.py:26
  5.6 0.7 copy-start.1
  50.1 20.4 %all-to-all-start = ((bf16[16,2,32,512]{3,2,1,0:T(8,128)(2,1)}), bf16[16,2,32,512]{3,2,1,0:T(8,128)(2,1)S(1)}, u32[]{:S(2)}, u32[]{:S(2)}) async-start(bf16[16,2,32,512]{3,2,1,0:T(8,128)(2,1)} %bitcast.5), calls=%async_computation | async-start | bytes 2097152 | tf_op jit(solution)/shard_map/all_to_all | solution.py:158
  53.9 0.7 copy-start

commit v3 on v2

--- a/solution.py
+++ b/solution.py
@@ -157,9 +157,8 @@
         fields = fields.reshape((groups * SPLIT,) + fields.shape[2:])
         return lax.all_to_all(fields, ("inner", "lo"), split_axis=0, concat_axis=0, tiled=True)
 
-    near_fields = make_fields(near, rows, groups, lo.reshape(1))
+    near_fields = share(make_fields(near, rows, groups, lo.reshape(1)))
     near_fields, rows = lax.optimization_barrier((near_fields, rows))
-    near_fields = share(near_fields)
     far_fields = share(make_fields(far, rows, groups, lo.reshape(1)))
 
     turn = half * (total_k // 2)

time: 74.1 us -> 71.1 us (0.960)
  blocking collectives: 20.7 us -> 0 us
  starting transfers between devices: 8.23 us -> 18.4 us
  waiting for transfers between devices: 35.4 us -> 42.5 us
    all_to_all x1 -> x2, waiting for transfers between devices: 15.7 us -> 37.4 us  [share(): lax.all_to_all(fields, ('inner', 'lo'), split_axis=0, concat_axis=0, tile...]
    all_to_all x1 -> x0, blocking collectives: 20.7 us -> none  [share(): lax.all_to_all(fields, ('inner', 'lo'), split_axis=0, concat_axis=0, tile...]
    ppermute x3, waiting for transfers between devices: 19.7 us -> 5.1 us  [swap(): return lax.ppermute(block, ALL, route)]
    all_to_all x1 -> x2, starting transfers between devices: 3.79 us -> 12.8 us  [share(): lax.all_to_all(fields, ('inner', 'lo'), split_axis=0, concat_axis=0, tile...]
    ppermute x3, starting transfers between devices: 4.45 us -> 5.62 us  [swap(): return lax.ppermute(block, ALL, route)]
  transfers between devices with their start and end apart: 4 -> 5, of which waited for: 3 -> 3; matrix products, arithmetic and copies ran while one was open for 1% -> 1% of each run, Pallas kernels for 3% -> 0%
where the time goes in v3:
time: 71.1 us; the launch traced here: 70.7 us
  waiting for transfers between devices  42.5 us (60%)
  starting transfers between devices  18.4 us (26%)
  Pallas kernels  6.97 us (10%)
  local copies, waits for them, and re-layouts  2.49 us (4%)
    all_to_all x2, waiting for transfers between devices, share(): lax.all_to_all(fields, ('inner', 'lo'), split_axis=0, concat_axis=0, tile...  37.4 us
    all_to_all x2, starting transfers between devices, share(): lax.all_to_all(fields, ('inner', 'lo'), split_axis=0, concat_axis=0, tile...  12.8 us
    ppermute x3, starting transfers between devices, swap(): return lax.ppermute(block, ALL, route)  5.62 us
    ppermute x3, waiting for transfers between devices, swap(): return lax.ppermute(block, ALL, route)  5.1 us
    pallas_call x2, Pallas kernels, make_fields(): pl.pallas_call(functools.partial(field_kernel, len(slabs)), grid_spec=plt...  3.85 us
    pallas_call x1, Pallas kernels, make_pairs(): pl.pallas_call(functools.partial(pair_kernel, 1.0 / math.sqrt(2 * half_k)...  3.12 us
  transfers between devices with their start and end apart: 5, of which 3 were waited for; matrix products, arithmetic and copies ran while one was open for 1% of the time, Pallas kernels for 0%

profile of v3, /device:TPU:1, one launch (start us, length us, event | category | flops | bytes accessed | tf_op | source)
XLA Modules:
  0.0 70.7 jit_solution(3108448915836357329)
XLA Ops:
  0.0 1.1 %dynamic-slice_bitcast_fusion = (bf16[512,256]{1,0:T(8,128)(2,1)S(1)}, bf16[512,256]{1,0:T(8,128)(2,1)S(1)}) fusion(bf16[2,512,256]{2,1,0:T(8,128)(2,1)} %param.3, s32[]{:T(128)S(6)} %select_n.34, s32[]{:T(128)S(6)} %select_n.33), kind=kLoop, calls=%fused_computation | loop fusion | bytes 1048584 | tf_op jit(solution)/shard_map/jit(dynamic_index_in_dim)/squeeze | solution.py:147
  1.1 2.1 %collective-permute-start = (bf16[512,256]{1,0:T(8,128)(2,1)S(1)}, bf16[512,256]{1,0:T(8,128)(2,1)S(1)}, u32[]{:S(2)}, u32[]{:S(2)}) collective-permute-start(bf16[512,256]{1,0:T(8,128)(2,1)S(1)} %get-tuple-element.9), channel_id=1, source_target_pairs={{0,1},{1,0},{2,3},{3,2},{4,5},{5,4},{6,7},{7,6},{8,9},{9,8},{10,11... | collective-permute-start | bytes 786440 | tf_op jit(solution)/shard_map/ppermute | solution.py:26
  3.2 0.1 pad_add_fusion.1
  3.3 0.0 copy-start.1
  3.3 0.7 copy-done.1
  4.0 0.1 dynamic_slice.15
  4.0 0.1 broadcast_subtract_fusion.rows_ref
  4.1 5.1 %collective-permute-done.refs_1_ = bf16[512,256]{1,0:T(8,128)(2,1)S(1)} collective-permute-done((bf16[512,256]{1,0:T(8,128)(2,1)S(1)}, bf16[512,256]{1,0:T(8,128)(2,1)S(1)}, u32[]{:S(2)}, u32[]{:S(2)}) %collective-permute-start) | collective-permute-done | bytes 262176 | tf_op jit(solution)/shard_map/ppermute | solution.py:26
  9.2 1.9 %fields.2 = bf16[8,2,2,32,512]{4,3,2,1,0:T(8,128)(2,1)} custom-call(s32[1]{0:T(128)} %bitcast.lo_ref, s32[256,2]{1,0:T(8,128)S(1)} %broadcast_subtract_fusion.rows_ref, bf16[512,256]{1,0:T(8,128)(2,1)S(1)} %get-tuple-element.10.refs_0_, bf16[512,256]{1,0:T(8,128)(2,1)S(1)} %collective-permute-done.refs_1_), custom_call_target="tpu_custom_call" | custom-call | tf_op jit(solution)/shard_map/fields/pallas_call | solution.py:70
  11.2 6.2 %all-to-all-start = ((bf16[16,2,32,512]{3,2,1,0:T(8,128)(2,1)}), bf16[16,2,32,512]{3,2,1,0:T(8,128)(2,1)S(1)}, u32[]{:S(2)}, u32[]{:S(2)}) async-start(bf16[16,2,32,512]{3,2,1,0:T(8,128)(2,1)} %bitcast.5), calls=%async_computation | async-start | bytes 2097152 | tf_op jit(solution)/shard_map/all_to_all | solution.py:158
  17.4 2.3 %collective-permute-start.1 = (bf16[512,256]{1,0:T(8,128)(2,1)S(1)}, bf16[512,256]{1,0:T(8,128)(2,1)S(1)}, u32[]{:S(2)}, u32[]{:S(2)}) collective-permute-start(bf16[512,256]{1,0:T(8,128)(2,1)S(1)} %get-tuple-element.10.refs_0_), channel_id=1, source_target_pairs={{0,16},{1,17},{2,18},{3,19},{4,20},{5,21},{6,22},{7,23},{8,24},{9,... | collective-permute-start | bytes 786440 | tf_op jit(solution)/shard_map/ppermute | solution.py:26
  19.7 1.2 %collective-permute-start.2 = (bf16[512,256]{1,0:T(8,128)(2,1)S(1)}, bf16[512,256]{1,0:T(8,128)(2,1)S(1)}, u32[]{:S(2)}, u32[]{:S(2)}) collective-permute-start(bf16[512,256]{1,0:T(8,128)(2,1)S(1)} %get-tuple-element.9), channel_id=1, source_target_pairs={{0,17},{1,16},{2,19},{3,18},{4,21},{5,20},{6,23},{7,22},{8,25},{9,... | collective-permute-start | bytes 786440 | tf_op jit(solution)/shard_map/ppermute | solution.py:26
  20.9 21.7 %all-to-all-done.near_ref = bf16[16,2,32,512]{3,2,1,0:T(8,128)(2,1)S(1)} async-done(((bf16[16,2,32,512]{3,2,1,0:T(8,128)(2,1)}), bf16[16,2,32,512]{3,2,1,0:T(8,128)(2,1)S(1)}, u32[]{:S(2)}, u32[]{:S(2)}) %all-to-all-start) | async-done | bytes 1048608 | tf_op jit(solution)/shard_map/all_to_all | solution.py:158
  42.6 0.0 collective-permute-done.1.refs_0_
  42.6 0.0 collective-permute-done.2.refs_1_
  42.6 1.9 %fields.3 = bf16[8,2,2,32,512]{4,3,2,1,0:T(8,128)(2,1)} custom-call(s32[1]{0:T(128)} %bitcast.lo_ref, s32[256,2]{1,0:T(8,128)S(1)} %broadcast_subtract_fusion.rows_ref, bf16[512,256]{1,0:T(8,128)(2,1)S(1)} %collective-permute-done.1.refs_0_, bf16[512,256]{1,0:T(8,128)(2,1)S(1)} %collective-permute-done.2.refs_1_), custom_call_target="tpu_custom_call" | custom-call | tf_op jit(solution)/shard_map/fields/pallas_call | solution.py:70
  44.5 6.6 %all-to-all-start.1 = ((bf16[16,2,32,512]{3,2,1,0:T(8,128)(2,1)}), bf16[16,2,32,512]{3,2,1,0:T(8,128)(2,1)S(1)}, u32[]{:S(2)}, u32[]{:S(2)}) async-start(bf16[16,2,32,512]{3,2,1,0:T(8,128)(2,1)} %bitcast.6), calls=%async_computation.1 | async-start | bytes 2097152 | tf_op jit(solution)/shard_map/all_to_all | solution.py:158
  51.1 0.0 copy-start
  51.1 0.7 copy-done
  51.7 0.1 pad_add_fusion
  51.8 0.1 and_select_fusion.table_ref
  51.9 15.7 %all-to-all-done.1.far_ref = bf16[16,2,32,512]{3,2,1,0:T(8,128)(2,1)S(1)} async-done(((bf16[16,2,32,512]{3,2,1,0:T(8,128)(2,1)}), bf16[16,2,32,512]{3,2,1,0:T(8,128)(2,1)S(1)}, u32[]{:S(2)}, u32[]{:S(2)}) %all-to-all-start.1) | async-done | bytes 1048608 | tf_op jit(solution)/shard_map/all_to_all | solution.py:158
  67.6 3.1 %pairs.1 = f32[32,2,2,512]{3,2,1,0:T(2,128)} custom-call(s32[2,32]{1,0:T(2,128)S(1)} %and_select_fusion.table_ref, bf16[16,2,32,512]{3,2,1,0:T(8,128)(2,1)S(1)} %all-to-all-done.near_ref, bf16[16,2,32,512]{3,2,1,0:T(8,128)(2,1)S(1)} %all-to-all-done.1.far_ref), custom_call_target="tpu_custom_call" | custom-call | tf_op jit(solution)/shard_map/pairs/pallas_call | solution.py:122
Async XLA Ops:
  1.1 8.2 %collective-permute-start = (bf16[512,256]{1,0:T(8,128)(2,1)S(1)}, bf16[512,256]{1,0:T(8,128)(2,1)S(1)}, u32[]{:S(2)}, u32[]{:S(2)}) collective-permute-start(bf16[512,256]{1,0:T(8,128)(2,1)S(1)} %get-tuple-element.9), channel_id=1, source_target_pairs={{0,1},{1,0},{2,3},{3,2},{4,5},{5,4},{6,7},{7,6},{8,9},{9,8},{10,11... | collective-permute-start | bytes 786440 | tf_op jit(solution)/shard_map/ppermute | solution.py:26
  3.3 0.7 copy-start.1
  11.2 31.4 %all-to-all-start = ((bf16[16,2,32,512]{3,2,1,0:T(8,128)(2,1)}), bf16[16,2,32,512]{3,2,1,0:T(8,128)(2,1)S(1)}, u32[]{:S(2)}, u32[]{:S(2)}) async-start(bf16[16,2,32,512]{3,2,1,0:T(8,128)(2,1)} %bitcast.5), calls=%async_computation | async-start | bytes 2097152 | tf_op jit(solution)/shard_map/all_to_all | solution.py:158
  17.4 25.2 %collective-permute-start.1 = (bf16[512,256]{1,0:T(8,128)(2,1)S(1)}, bf16[512,256]{1,0:T(8,128)(2,1)S(1)}, u32[]{:S(2)}, u32[]{:S(2)}) collective-permute-start(bf16[512,256]{1,0:T(8,128)(2,1)S(1)} %get-tuple-element.10.refs_0_), channel_id=1, source_target_pairs={{0,16},{1,17},{2,18},{3,19},{4,20},{5,21},{6,22},{7,23},{8,24},{9,... | collective-permute-start | bytes 786440 | tf_op jit(solution)/shard_map/ppermute | solution.py:26
  19.7 22.9 %collective-permute-start.2 = (bf16[512,256]{1,0:T(8,128)(2,1)S(1)}, bf16[512,256]{1,0:T(8,128)(2,1)S(1)}, u32[]{:S(2)}, u32[]{:S(2)}) collective-permute-start(bf16[512,256]{1,0:T(8,128)(2,1)S(1)} %get-tuple-element.9), channel_id=1, source_target_pairs={{0,17},{1,16},{2,19},{3,18},{4,21},{5,20},{6,23},{7,22},{8,25},{9,... | collective-permute-start | bytes 786440 | tf_op jit(solution)/shard_map/ppermute | solution.py:26
  44.5 23.1 %all-to-all-start.1 = ((bf16[16,2,32,512]{3,2,1,0:T(8,128)(2,1)}), bf16[16,2,32,512]{3,2,1,0:T(8,128)(2,1)S(1)}, u32[]{:S(2)}, u32[]{:S(2)}) async-start(bf16[16,2,32,512]{3,2,1,0:T(8,128)(2,1)} %bitcast.6), calls=%async_computation.1 | async-start | bytes 2097152 | tf_op jit(solution)/shard_map/all_to_all | solution.py:158
  51.1 0.7 copy-start

commit v4 on v2

--- a/solution.py
+++ b/solution.py
@@ -146,7 +146,7 @@
     mine = lax.dynamic_index_in_dim(orbitals, lo, 0, keepdims=False)
     other = lax.dynamic_index_in_dim(orbitals, 1 - lo, 0, keepdims=False)
     near = [mine] + [swap(other if x & 1 else mine, 0, x) for x in range(1, slabs)]
-    far = [swap(other if x & 1 else mine, 1, x) for x in range(slabs)]
+    far = [swap(slab, 1, 0) for slab in near]
 
     half_points = points.shape[0] // 2
     wanted = lax.dynamic_slice_in_dim(points, half * half_points, half_points)
@@ -159,8 +159,9 @@
 
     near_fields = make_fields(near, rows, groups, lo.reshape(1))
     near_fields, rows = lax.optimization_barrier((near_fields, rows))
-    near_fields = share(near_fields)
-    far_fields = share(make_fields(far, rows, groups, lo.reshape(1)))
+    far_fields = make_fields(far, rows, groups, lo.reshape(1))
+    near_fields, far_fields = lax.optimization_barrier((share(near_fields), far_fields))
+    far_fields = share(far_fields)
 
     turn = half * (total_k // 2)
     table = (jnp.roll(minus_table, -turn, axis=1) - turn) % total_k

time: 74.1 us -> 71.1 us (0.960)
  blocking collectives: 20.7 us -> 0 us
  starting transfers between devices: 8.23 us -> 18.1 us
  waiting for transfers between devices: 35.4 us -> 42.8 us
    all_to_all x1 -> x0, blocking collectives: 20.7 us -> none  [share(): lax.all_to_all(fields, ('inner', 'lo'), split_axis=0, concat_axis=0, tile...]
    all_to_all x1 -> x2, starting transfers between devices: 3.79 us -> 13.6 us  [share(): lax.all_to_all(fields, ('inner', 'lo'), split_axis=0, concat_axis=0, tile...]
    ppermute x3, waiting for transfers between devices: 19.7 us -> 27.1 us  [swap(): return lax.ppermute(block, ALL, route)]
    all_to_all x1 -> x2, waiting for transfers between devices: 15.7 us -> 15.7 us  [share(): lax.all_to_all(fields, ('inner', 'lo'), split_axis=0, concat_axis=0, tile...]
  transfers between devices with their start and end apart: 4 -> 5, of which waited for: 3 -> 4; matrix products, arithmetic and copies ran while one was open for 1% -> 1% of each run, Pallas kernels for 3% -> 3%
where the time goes in v4:
time: 71.1 us; the launch traced here: 70.7 us
  waiting for transfers between devices  42.8 us (60%)
  starting transfers between devices  18.1 us (25%)
  Pallas kernels  6.95 us (10%)
  local copies, waits for them, and re-layouts  2.49 us (4%)
    ppermute x3, waiting for transfers between devices, swap(): return lax.ppermute(block, ALL, route)  27.1 us
    all_to_all x2, waiting for transfers between devices, share(): lax.all_to_all(fields, ('inner', 'lo'), split_axis=0, concat_axis=0, tile...  15.7 us
    all_to_all x2, starting transfers between devices, share(): lax.all_to_all(fields, ('inner', 'lo'), split_axis=0, concat_axis=0, tile...  13.6 us
    ppermute x3, starting transfers between devices, swap(): return lax.ppermute(block, ALL, route)  4.53 us
    pallas_call x2, Pallas kernels, make_fields(): pl.pallas_call(functools.partial(field_kernel, len(slabs)), grid_spec=plt...  3.84 us
    pallas_call x1, Pallas kernels, make_pairs(): pl.pallas_call(functools.partial(pair_kernel, 1.0 / math.sqrt(2 * half_k)...  3.12 us
  transfers between devices with their start and end apart: 5, of which 4 were waited for; matrix products, arithmetic and copies ran while one was open for 1% of the time, Pallas kernels for 3%

profile of v4, /device:TPU:1, one launch (start us, length us, event | category | flops | bytes accessed | tf_op | source)
XLA Modules:
  0.0 70.7 jit_solution(5023335788801322327)
XLA Ops:
  0.0 1.1 %dynamic-slice_bitcast_fusion = (bf16[512,256]{1,0:T(8,128)(2,1)S(1)}, bf16[512,256]{1,0:T(8,128)(2,1)S(1)}) fusion(bf16[2,512,256]{2,1,0:T(8,128)(2,1)} %param.3, s32[]{:T(128)S(6)} %select_n.34, s32[]{:T(128)S(6)} %select_n.33), kind=kLoop, calls=%fused_computation | loop fusion | bytes 1048584 | tf_op jit(solution)/shard_map/jit(dynamic_index_in_dim)/squeeze | solution.py:147
  1.1 2.1 %collective-permute-start = (bf16[512,256]{1,0:T(8,128)(2,1)S(1)}, bf16[512,256]{1,0:T(8,128)(2,1)S(1)}, u32[]{:S(2)}, u32[]{:S(2)}) collective-permute-start(bf16[512,256]{1,0:T(8,128)(2,1)S(1)} %get-tuple-element.13), channel_id=1, source_target_pairs={{0,1},{1,0},{2,3},{3,2},{4,5},{5,4},{6,7},{7,6},{8,9},{9,8},{10,11... | collective-permute-start | bytes 786440 | tf_op jit(solution)/shard_map/ppermute | solution.py:26
  3.2 0.1 pad_add_fusion.1
  3.3 0.0 copy-start.1
  3.3 0.7 copy-done.1
  4.0 0.1 dynamic_slice.15
  4.0 0.1 broadcast_subtract_fusion.rows_ref
  4.1 5.1 %collective-permute-done.refs_1_ = bf16[512,256]{1,0:T(8,128)(2,1)S(1)} collective-permute-done((bf16[512,256]{1,0:T(8,128)(2,1)S(1)}, bf16[512,256]{1,0:T(8,128)(2,1)S(1)}, u32[]{:S(2)}, u32[]{:S(2)}) %collective-permute-start) | collective-permute-done | bytes 262176 | tf_op jit(solution)/shard_map/ppermute | solution.py:26
  9.2 1.9 %fields.2 = bf16[8,2,2,32,512]{4,3,2,1,0:T(8,128)(2,1)} custom-call(s32[1]{0:T(128)} %bitcast.lo_ref, s32[256,2]{1,0:T(8,128)S(1)} %broadcast_subtract_fusion.rows_ref, bf16[512,256]{1,0:T(8,128)(2,1)S(1)} %get-tuple-element.14.refs_0_, bf16[512,256]{1,0:T(8,128)(2,1)S(1)} %collective-permute-done.refs_1_), custom_call_target="tpu_custom_call" | custom-call | tf_op jit(solution)/shard_map/fields/pallas_call | solution.py:70
  11.2 6.2 %all-to-all-start = ((bf16[16,2,32,512]{3,2,1,0:T(8,128)(2,1)}), bf16[16,2,32,512]{3,2,1,0:T(8,128)(2,1)S(1)}, u32[]{:S(2)}, u32[]{:S(2)}) async-start(bf16[16,2,32,512]{3,2,1,0:T(8,128)(2,1)} %bitcast.5), calls=%async_computation | async-start | bytes 2097152 | tf_op jit(solution)/shard_map/all_to_all | solution.py:158
  17.4 2.3 %collective-permute-start.1 = (bf16[512,256]{1,0:T(8,128)(2,1)S(1)}, bf16[512,256]{1,0:T(8,128)(2,1)S(1)}, u32[]{:S(2)}, u32[]{:S(2)}) collective-permute-start(bf16[512,256]{1,0:T(8,128)(2,1)S(1)} %get-tuple-element.14.refs_0_), channel_id=1, source_target_pairs={{0,16},{1,17},{2,18},{3,19},{4,20},{5,21},{6,22},{7,23},{8,24},{9,... | collective-permute-start | bytes 786440 | tf_op jit(solution)/shard_map/ppermute | solution.py:26
  19.7 0.1 collective-permute-start.2
  19.8 16.4 %collective-permute-done.1.refs_0_ = bf16[512,256]{1,0:T(8,128)(2,1)S(1)} collective-permute-done((bf16[512,256]{1,0:T(8,128)(2,1)S(1)}, bf16[512,256]{1,0:T(8,128)(2,1)S(1)}, u32[]{:S(2)}, u32[]{:S(2)}) %collective-permute-start.1) | collective-permute-done | bytes 262176 | tf_op jit(solution)/shard_map/ppermute | solution.py:26
  36.2 5.6 %collective-permute-done.2.refs_1_ = bf16[512,256]{1,0:T(8,128)(2,1)S(1)} collective-permute-done((bf16[512,256]{1,0:T(8,128)(2,1)S(1)}, bf16[512,256]{1,0:T(8,128)(2,1)S(1)}, u32[]{:S(2)}, u32[]{:S(2)}) %collective-permute-start.2) | collective-permute-done | bytes 262176 | tf_op jit(solution)/shard_map/ppermute | solution.py:26
  41.8 1.9 %fields.3 = bf16[8,2,2,32,512]{4,3,2,1,0:T(8,128)(2,1)} custom-call(s32[1]{0:T(128)} %bitcast.lo_ref, s32[256,2]{1,0:T(8,128)S(1)} %broadcast_subtract_fusion.rows_ref, bf16[512,256]{1,0:T(8,128)(2,1)S(1)} %collective-permute-done.1.refs_0_, bf16[512,256]{1,0:T(8,128)(2,1)S(1)} %collective-permute-done.2.refs_1_), custom_call_target="tpu_custom_call" | custom-call | tf_op jit(solution)/shard_map/fields/pallas_call | solution.py:70
  43.7 0.0 all-to-all-done.near_ref
  43.7 7.4 %all-to-all-start.1 = ((bf16[16,2,32,512]{3,2,1,0:T(8,128)(2,1)}), bf16[16,2,32,512]{3,2,1,0:T(8,128)(2,1)S(1)}, u32[]{:S(2)}, u32[]{:S(2)}) async-start(bf16[16,2,32,512]{3,2,1,0:T(8,128)(2,1)} %bitcast.6), calls=%async_computation.1 | async-start | bytes 2097152 | tf_op jit(solution)/shard_map/all_to_all | solution.py:158
  51.1 0.0 copy-start
  51.1 0.7 copy-done
  51.8 0.1 pad_add_fusion
  51.8 0.1 and_select_fusion.table_ref
  51.9 15.7 %all-to-all-done.1.far_ref = bf16[16,2,32,512]{3,2,1,0:T(8,128)(2,1)S(1)} async-done(((bf16[16,2,32,512]{3,2,1,0:T(8,128)(2,1)}), bf16[16,2,32,512]{3,2,1,0:T(8,128)(2,1)S(1)}, u32[]{:S(2)}, u32[]{:S(2)}) %all-to-all-start.1) | async-done | bytes 1048608 | tf_op jit(solution)/shard_map/all_to_all | solution.py:158
  67.6 3.1 %pairs.1 = f32[32,2,2,512]{3,2,1,0:T(2,128)} custom-call(s32[2,32]{1,0:T(2,128)S(1)} %and_select_fusion.table_ref, bf16[16,2,32,512]{3,2,1,0:T(8,128)(2,1)S(1)} %all-to-all-done.near_ref, bf16[16,2,32,512]{3,2,1,0:T(8,128)(2,1)S(1)} %all-to-all-done.1.far_ref), custom_call_target="tpu_custom_call" | custom-call | tf_op jit(solution)/shard_map/pairs/pallas_call | solution.py:122
Async XLA Ops:
  1.1 8.2 %collective-permute-start = (bf16[512,256]{1,0:T(8,128)(2,1)S(1)}, bf16[512,256]{1,0:T(8,128)(2,1)S(1)}, u32[]{:S(2)}, u32[]{:S(2)}) collective-permute-start(bf16[512,256]{1,0:T(8,128)(2,1)S(1)} %get-tuple-element.13), channel_id=1, source_target_pairs={{0,1},{1,0},{2,3},{3,2},{4,5},{5,4},{6,7},{7,6},{8,9},{9,8},{10,11... | collective-permute-start | bytes 786440 | tf_op jit(solution)/shard_map/ppermute | solution.py:26
  3.3 0.7 copy-start.1
  11.2 32.5 %all-to-all-start = ((bf16[16,2,32,512]{3,2,1,0:T(8,128)(2,1)}), bf16[16,2,32,512]{3,2,1,0:T(8,128)(2,1)S(1)}, u32[]{:S(2)}, u32[]{:S(2)}) async-start(bf16[16,2,32,512]{3,2,1,0:T(8,128)(2,1)} %bitcast.5), calls=%async_computation | async-start | bytes 2097152 | tf_op jit(solution)/shard_map/all_to_all | solution.py:158
  17.4 18.8 %collective-permute-start.1 = (bf16[512,256]{1,0:T(8,128)(2,1)S(1)}, bf16[512,256]{1,0:T(8,128)(2,1)S(1)}, u32[]{:S(2)}, u32[]{:S(2)}) collective-permute-start(bf16[512,256]{1,0:T(8,128)(2,1)S(1)} %get-tuple-element.14.refs_0_), channel_id=1, source_target_pairs={{0,16},{1,17},{2,18},{3,19},{4,20},{5,21},{6,22},{7,23},{8,24},{9,... | collective-permute-start | bytes 786440 | tf_op jit(solution)/shard_map/ppermute | solution.py:26
  19.7 22.1 %collective-permute-start.2 = (bf16[512,256]{1,0:T(8,128)(2,1)S(1)}, bf16[512,256]{1,0:T(8,128)(2,1)S(1)}, u32[]{:S(2)}, u32[]{:S(2)}) collective-permute-start(bf16[512,256]{1,0:T(8,128)(2,1)S(1)} %collective-permute-done.refs_1_), channel_id=1, source_target_pairs={{0,16},{1,17},{2,18},{3,19},{4,20},{5,21},{6,22},{7,23},{8,24},{9,... | collective-permute-start | bytes 786440 | tf_op jit(solution)/shard_map/ppermute | solution.py:26
  43.7 23.9 %all-to-all-start.1 = ((bf16[16,2,32,512]{3,2,1,0:T(8,128)(2,1)}), bf16[16,2,32,512]{3,2,1,0:T(8,128)(2,1)S(1)}, u32[]{:S(2)}, u32[]{:S(2)}) async-start(bf16[16,2,32,512]{3,2,1,0:T(8,128)(2,1)} %bitcast.6), calls=%async_computation.1 | async-start | bytes 2097152 | tf_op jit(solution)/shard_map/all_to_all | solution.py:158
  51.1 0.7 copy-start

commit v5 on v4

--- a/solution.py
+++ b/solution.py
@@ -80,6 +80,9 @@
             scratch_shapes=[pltpu.VMEM((2, npoints, channels), jnp.bfloat16)],
         ),
         out_shape=jax.ShapeDtypeStruct((groups, SPLIT, 2, length, slab_size), jnp.bfloat16),
+        cost_estimate=pl.CostEstimate(
+            flops=7_000_000_000, bytes_accessed=22_000_000, transcendentals=0
+        ),
         compiler_params=pltpu.CompilerParams(vmem_limit_bytes=VMEM_LIMIT),
         name="fields",
     )(lo, rows, *slabs)

time: 71.1 us -> 71.1 us (level)
  no operation moved by 1% of the time
where the time goes in v5:
time: 71.1 us; the launch traced here: 70.7 us
  waiting for transfers between devices  42.8 us (60%)
  starting transfers between devices  18.1 us (25%)
  Pallas kernels  6.95 us (10%)
  local copies, waits for them, and re-layouts  2.49 us (4%)
    ppermute x3, waiting for transfers between devices, swap(): return lax.ppermute(block, ALL, route)  27.1 us
    all_to_all x2, waiting for transfers between devices, share(): lax.all_to_all(fields, ('inner', 'lo'), split_axis=0, concat_axis=0, tile...  15.7 us
    all_to_all x2, starting transfers between devices, share(): lax.all_to_all(fields, ('inner', 'lo'), split_axis=0, concat_axis=0, tile...  13.6 us
    ppermute x3, starting transfers between devices, swap(): return lax.ppermute(block, ALL, route)  4.53 us
    pallas_call x2, Pallas kernels, make_fields(): pl.pallas_call(functools.partial(field_kernel, len(slabs)), grid_spec=plt...  3.84 us
    pallas_call x1, Pallas kernels, make_pairs(): pl.pallas_call(functools.partial(pair_kernel, 1.0 / math.sqrt(2 * half_k)...  3.12 us
  transfers between devices with their start and end apart: 5, of which 4 were waited for; matrix products, arithmetic and copies ran while one was open for 1% of the time, Pallas kernels for 3%

profile of v5, /device:TPU:1, one launch (start us, length us, event | category | flops | bytes accessed | tf_op | source)
XLA Modules:
  0.0 70.7 jit_solution(4673641114042947534)
XLA Ops:
  0.0 1.1 %dynamic-slice_bitcast_fusion = (bf16[512,256]{1,0:T(8,128)(2,1)S(1)}, bf16[512,256]{1,0:T(8,128)(2,1)S(1)}) fusion(bf16[2,512,256]{2,1,0:T(8,128)(2,1)} %param.3, s32[]{:T(128)S(6)} %select_n.34, s32[]{:T(128)S(6)} %select_n.33), kind=kLoop, calls=%fused_computation | loop fusion | bytes 1048584 | tf_op jit(solution)/shard_map/jit(dynamic_index_in_dim)/squeeze | solution.py:150
  1.1 2.1 %collective-permute-start = (bf16[512,256]{1,0:T(8,128)(2,1)S(1)}, bf16[512,256]{1,0:T(8,128)(2,1)S(1)}, u32[]{:S(2)}, u32[]{:S(2)}) collective-permute-start(bf16[512,256]{1,0:T(8,128)(2,1)S(1)} %get-tuple-element.13), channel_id=1, source_target_pairs={{0,1},{1,0},{2,3},{3,2},{4,5},{5,4},{6,7},{7,6},{8,9},{9,8},{10,11... | collective-permute-start | bytes 786440 | tf_op jit(solution)/shard_map/ppermute | solution.py:26
  3.2 0.1 pad_add_fusion.1
  3.3 0.0 copy-start.1
  3.3 0.7 copy-done.1
  4.0 0.1 dynamic_slice.15
  4.0 0.1 broadcast_subtract_fusion.rows_ref
  4.1 5.1 %collective-permute-done.refs_1_ = bf16[512,256]{1,0:T(8,128)(2,1)S(1)} collective-permute-done((bf16[512,256]{1,0:T(8,128)(2,1)S(1)}, bf16[512,256]{1,0:T(8,128)(2,1)S(1)}, u32[]{:S(2)}, u32[]{:S(2)}) %collective-permute-start) | collective-permute-done | bytes 262176 | tf_op jit(solution)/shard_map/ppermute | solution.py:26
  9.2 1.9 %fields.2 = bf16[8,2,2,32,512]{4,3,2,1,0:T(8,128)(2,1)} custom-call(s32[1]{0:T(128)} %bitcast.lo_ref, s32[256,2]{1,0:T(8,128)S(1)} %broadcast_subtract_fusion.rows_ref, bf16[512,256]{1,0:T(8,128)(2,1)S(1)} %get-tuple-element.14.refs_0_, bf16[512,256]{1,0:T(8,128)(2,1)S(1)} %collective-permute-done.refs_1_), custom_call_target="tpu_custom_call" | custom-call | flops 7000000000 | bytes 22000000 | tf_op jit(solution)/shard_map/fields/pallas_call | solution.py:70
  11.2 6.2 %all-to-all-start = ((bf16[16,2,32,512]{3,2,1,0:T(8,128)(2,1)}), bf16[16,2,32,512]{3,2,1,0:T(8,128)(2,1)S(1)}, u32[]{:S(2)}, u32[]{:S(2)}) async-start(bf16[16,2,32,512]{3,2,1,0:T(8,128)(2,1)} %bitcast.5), calls=%async_computation | async-start | bytes 2097152 | tf_op jit(solution)/shard_map/all_to_all | solution.py:161
  17.4 2.3 %collective-permute-start.1 = (bf16[512,256]{1,0:T(8,128)(2,1)S(1)}, bf16[512,256]{1,0:T(8,128)(2,1)S(1)}, u32[]{:S(2)}, u32[]{:S(2)}) collective-permute-start(bf16[512,256]{1,0:T(8,128)(2,1)S(1)} %get-tuple-element.14.refs_0_), channel_id=1, source_target_pairs={{0,16},{1,17},{2,18},{3,19},{4,20},{5,21},{6,22},{7,23},{8,24},{9,... | collective-permute-start | bytes 786440 | tf_op jit(solution)/shard_map/ppermute | solution.py:26
  19.7 0.1 collective-permute-start.2
  19.8 16.4 %collective-permute-done.1.refs_0_ = bf16[512,256]{1,0:T(8,128)(2,1)S(1)} collective-permute-done((bf16[512,256]{1,0:T(8,128)(2,1)S(1)}, bf16[512,256]{1,0:T(8,128)(2,1)S(1)}, u32[]{:S(2)}, u32[]{:S(2)}) %collective-permute-start.1) | collective-permute-done | bytes 262176 | tf_op jit(solution)/shard_map/ppermute | solution.py:26
  36.2 5.6 %collective-permute-done.2.refs_1_ = bf16[512,256]{1,0:T(8,128)(2,1)S(1)} collective-permute-done((bf16[512,256]{1,0:T(8,128)(2,1)S(1)}, bf16[512,256]{1,0:T(8,128)(2,1)S(1)}, u32[]{:S(2)}, u32[]{:S(2)}) %collective-permute-start.2) | collective-permute-done | bytes 262176 | tf_op jit(solution)/shard_map/ppermute | solution.py:26
  41.8 1.9 %fields.3 = bf16[8,2,2,32,512]{4,3,2,1,0:T(8,128)(2,1)} custom-call(s32[1]{0:T(128)} %bitcast.lo_ref, s32[256,2]{1,0:T(8,128)S(1)} %broadcast_subtract_fusion.rows_ref, bf16[512,256]{1,0:T(8,128)(2,1)S(1)} %collective-permute-done.1.refs_0_, bf16[512,256]{1,0:T(8,128)(2,1)S(1)} %collective-permute-done.2.refs_1_), custom_call_target="tpu_custom_call" | custom-call | flops 7000000000 | bytes 22000000 | tf_op jit(solution)/shard_map/fields/pallas_call | solution.py:70
  43.7 0.0 all-to-all-done.near_ref
  43.7 7.4 %all-to-all-start.1 = ((bf16[16,2,32,512]{3,2,1,0:T(8,128)(2,1)}), bf16[16,2,32,512]{3,2,1,0:T(8,128)(2,1)S(1)}, u32[]{:S(2)}, u32[]{:S(2)}) async-start(bf16[16,2,32,512]{3,2,1,0:T(8,128)(2,1)} %bitcast.6), calls=%async_computation.1 | async-start | bytes 2097152 | tf_op jit(solution)/shard_map/all_to_all | solution.py:161
  51.1 0.0 copy-start
  51.1 0.7 copy-done
  51.8 0.1 pad_add_fusion
  51.8 0.1 and_select_fusion.table_ref
  51.9 15.7 %all-to-all-done.1.far_ref = bf16[16,2,32,512]{3,2,1,0:T(8,128)(2,1)S(1)} async-done(((bf16[16,2,32,512]{3,2,1,0:T(8,128)(2,1)}), bf16[16,2,32,512]{3,2,1,0:T(8,128)(2,1)S(1)}, u32[]{:S(2)}, u32[]{:S(2)}) %all-to-all-start.1) | async-done | bytes 1048608 | tf_op jit(solution)/shard_map/all_to_all | solution.py:161
  67.6 3.1 %pairs.1 = f32[32,2,2,512]{3,2,1,0:T(2,128)} custom-call(s32[2,32]{1,0:T(2,128)S(1)} %and_select_fusion.table_ref, bf16[16,2,32,512]{3,2,1,0:T(8,128)(2,1)S(1)} %all-to-all-done.near_ref, bf16[16,2,32,512]{3,2,1,0:T(8,128)(2,1)S(1)} %all-to-all-done.1.far_ref), custom_call_target="tpu_custom_call" | custom-call | tf_op jit(solution)/shard_map/pairs/pallas_call | solution.py:125
Async XLA Ops:
  1.1 8.2 %collective-permute-start = (bf16[512,256]{1,0:T(8,128)(2,1)S(1)}, bf16[512,256]{1,0:T(8,128)(2,1)S(1)}, u32[]{:S(2)}, u32[]{:S(2)}) collective-permute-start(bf16[512,256]{1,0:T(8,128)(2,1)S(1)} %get-tuple-element.13), channel_id=1, source_target_pairs={{0,1},{1,0},{2,3},{3,2},{4,5},{5,4},{6,7},{7,6},{8,9},{9,8},{10,11... | collective-permute-start | bytes 786440 | tf_op jit(solution)/shard_map/ppermute | solution.py:26
  3.3 0.7 copy-start.1
  11.2 32.5 %all-to-all-start = ((bf16[16,2,32,512]{3,2,1,0:T(8,128)(2,1)}), bf16[16,2,32,512]{3,2,1,0:T(8,128)(2,1)S(1)}, u32[]{:S(2)}, u32[]{:S(2)}) async-start(bf16[16,2,32,512]{3,2,1,0:T(8,128)(2,1)} %bitcast.5), calls=%async_computation | async-start | bytes 2097152 | tf_op jit(solution)/shard_map/all_to_all | solution.py:161
  17.4 18.8 %collective-permute-start.1 = (bf16[512,256]{1,0:T(8,128)(2,1)S(1)}, bf16[512,256]{1,0:T(8,128)(2,1)S(1)}, u32[]{:S(2)}, u32[]{:S(2)}) collective-permute-start(bf16[512,256]{1,0:T(8,128)(2,1)S(1)} %get-tuple-element.14.refs_0_), channel_id=1, source_target_pairs={{0,16},{1,17},{2,18},{3,19},{4,20},{5,21},{6,22},{7,23},{8,24},{9,... | collective-permute-start | bytes 786440 | tf_op jit(solution)/shard_map/ppermute | solution.py:26
  19.7 22.1 %collective-permute-start.2 = (bf16[512,256]{1,0:T(8,128)(2,1)S(1)}, bf16[512,256]{1,0:T(8,128)(2,1)S(1)}, u32[]{:S(2)}, u32[]{:S(2)}) collective-permute-start(bf16[512,256]{1,0:T(8,128)(2,1)S(1)} %collective-permute-done.refs_1_), channel_id=1, source_target_pairs={{0,16},{1,17},{2,18},{3,19},{4,20},{5,21},{6,22},{7,23},{8,24},{9,... | collective-permute-start | bytes 786440 | tf_op jit(solution)/shard_map/ppermute | solution.py:26
  43.7 23.9 %all-to-all-start.1 = ((bf16[16,2,32,512]{3,2,1,0:T(8,128)(2,1)}), bf16[16,2,32,512]{3,2,1,0:T(8,128)(2,1)S(1)}, u32[]{:S(2)}, u32[]{:S(2)}) async-start(bf16[16,2,32,512]{3,2,1,0:T(8,128)(2,1)} %bitcast.6), calls=%async_computation.1 | async-start | bytes 2097152 | tf_op jit(solution)/shard_map/all_to_all | solution.py:161
  51.1 0.7 copy-start

commit v6 on v4

--- a/solution.py
+++ b/solution.py
@@ -153,14 +153,17 @@
     starts = jnp.stack([(here ^ x) * slab_size for x in range(slabs)])
     rows = wanted[:, None] - starts[None, :]
 
+    def flat(fields):
+        return fields.reshape((groups * SPLIT,) + fields.shape[2:])
+
     def share(fields):
-        fields = fields.reshape((groups * SPLIT,) + fields.shape[2:])
         return lax.all_to_all(fields, ("inner", "lo"), split_axis=0, concat_axis=0, tiled=True)
 
-    near_fields = make_fields(near, rows, groups, lo.reshape(1))
+    near_fields = flat(make_fields(near, rows, groups, lo.reshape(1)))
     near_fields, rows = lax.optimization_barrier((near_fields, rows))
-    far_fields = make_fields(far, rows, groups, lo.reshape(1))
-    near_fields, far_fields = lax.optimization_barrier((share(near_fields), far_fields))
+    far_fields = flat(make_fields(far, rows, groups, lo.reshape(1)))
+    near_fields = lax.cond(minus_table[0, 0] >= 0, share, lambda fields: fields, near_fields)
+    near_fields, far_fields = lax.optimization_barrier((near_fields, far_fields))
     far_fields = share(far_fields)
 
     turn = half * (total_k // 2)

time: 71.1 us -> 67.3 us (0.947)
  blocking collectives: 0 us -> 24.8 us
  waiting for transfers between devices: 42.8 us -> 20.2 us
  starting transfers between devices: 18.1 us -> 11.5 us
    all_to_all x0 -> x1, blocking collectives: none -> 24.8 us  [share(): lax.all_to_all(fields, ('inner', 'lo'), split_axis=0, concat_axis=0, tile...]
    ppermute x3, waiting for transfers between devices: 27.1 us -> 3.73 us  [swap(): return lax.ppermute(block, ALL, route)]
    all_to_all x2 -> x1, starting transfers between devices: 13.6 us -> 4.85 us  [share(): lax.all_to_all(fields, ('inner', 'lo'), split_axis=0, concat_axis=0, tile...]
    ppermute x3, starting transfers between devices: 4.53 us -> 6.65 us  [swap(): return lax.ppermute(block, ALL, route)]
    all_to_all x2 -> x1, waiting for transfers between devices: 15.7 us -> 16.4 us  [share(): lax.all_to_all(fields, ('inner', 'lo'), split_axis=0, concat_axis=0, tile...]
  transfers between devices with their start and end apart: 5 -> 4, of which waited for: 4 -> 2; matrix products, arithmetic and copies ran while one was open for 1% -> 2% of each run, Pallas kernels for 3% -> 2%
where the time goes in v6:
time: 67.3 us; the launch traced here: 66.9 us
  blocking collectives  24.8 us (37%)
  waiting for transfers between devices  20.2 us (30%)
  starting transfers between devices  11.5 us (17%)
  Pallas kernels  6.37 us (9%)
  local copies, waits for them, and re-layouts  3.1 us (5%)
  between operations  0.69 us (1%)
    all_to_all x1, blocking collectives, share(): lax.all_to_all(fields, ('inner', 'lo'), split_axis=0, concat_axis=0, tile...  24.8 us
    all_to_all x1, waiting for transfers between devices, share(): lax.all_to_all(fields, ('inner', 'lo'), split_axis=0, concat_axis=0, tile...  16.4 us
    ppermute x3, starting transfers between devices, swap(): return lax.ppermute(block, ALL, route)  6.65 us
    all_to_all x1, starting transfers between devices, share(): lax.all_to_all(fields, ('inner', 'lo'), split_axis=0, concat_axis=0, tile...  4.85 us
    ppermute x3, waiting for transfers between devices, swap(): return lax.ppermute(block, ALL, route)  3.73 us
    pallas_call x2, Pallas kernels, make_fields(): pl.pallas_call(functools.partial(field_kernel, len(slabs)), grid_spec=plt...  3.25 us
    pallas_call x1, Pallas kernels, make_pairs(): pl.pallas_call(functools.partial(pair_kernel, 1.0 / math.sqrt(2 * half_k)...  3.12 us
    unnamed x4, local copies, waits for them, and re-layouts  1.36 us
  transfers between devices with their start and end apart: 4, of which 2 were waited for; matrix products, arithmetic and copies ran while one was open for 2% of the time, Pallas kernels for 2%

profile of v6, /device:TPU:1, one launch (start us, length us, event | category | flops | bytes accessed | tf_op | source)
XLA Modules:
  0.0 66.9 jit_solution(17696650134374964282)
XLA Ops:
  0.0 1.1 %dynamic-slice_bitcast_fusion = (bf16[512,256]{1,0:T(8,128)(2,1)S(1)}, bf16[512,256]{1,0:T(8,128)(2,1)S(1)}) fusion(bf16[2,512,256]{2,1,0:T(8,128)(2,1)} %param.5, s32[]{:T(128)S(6)} %select_n.34, s32[]{:T(128)S(6)} %select_n.33), kind=kLoop, calls=%fused_computation | loop fusion | bytes 1048584 | tf_op jit(solution)/shard_map/jit(dynamic_index_in_dim)/squeeze | solution.py:147
  1.1 2.1 %collective-permute-start = (bf16[512,256]{1,0:T(8,128)(2,1)S(1)}, bf16[512,256]{1,0:T(8,128)(2,1)S(1)}, u32[]{:S(2)}, u32[]{:S(2)}) collective-permute-start(bf16[512,256]{1,0:T(8,128)(2,1)S(1)} %get-tuple-element.18), channel_id=1, source_target_pairs={{0,1},{1,0},{2,3},{3,2},{4,5},{5,4},{6,7},{7,6},{8,9},{9,8},{10,11... | collective-permute-start | bytes 786440 | tf_op jit(solution)/shard_map/ppermute | solution.py:26
  3.2 2.3 %collective-permute-start.1 = (bf16[512,256]{1,0:T(8,128)(2,1)S(1)}, bf16[512,256]{1,0:T(8,128)(2,1)S(1)}, u32[]{:S(2)}, u32[]{:S(2)}) collective-permute-start(bf16[512,256]{1,0:T(8,128)(2,1)S(1)} %get-tuple-element.19.refs_0_), channel_id=1, source_target_pairs={{0,16},{1,17},{2,18},{3,19},{4,20},{5,21},{6,22},{7,23},{8,24},{9,... | collective-permute-start | bytes 786440 | tf_op jit(solution)/shard_map/ppermute | solution.py:26
  5.5 3.7 %collective-permute-done.refs_1_ = bf16[512,256]{1,0:T(8,128)(2,1)S(1)} collective-permute-done((bf16[512,256]{1,0:T(8,128)(2,1)S(1)}, bf16[512,256]{1,0:T(8,128)(2,1)S(1)}, u32[]{:S(2)}, u32[]{:S(2)}) %collective-permute-start) | collective-permute-done | bytes 262176 | tf_op jit(solution)/shard_map/ppermute | solution.py:26
  9.2 2.2 %collective-permute-start.2 = (bf16[512,256]{1,0:T(8,128)(2,1)S(1)}, bf16[512,256]{1,0:T(8,128)(2,1)S(1)}, u32[]{:S(2)}, u32[]{:S(2)}) collective-permute-start(bf16[512,256]{1,0:T(8,128)(2,1)S(1)} %collective-permute-done.refs_1_), channel_id=1, source_target_pairs={{0,16},{1,17},{2,18},{3,19},{4,20},{5,21},{6,22},{7,23},{8,24},{9,... | collective-permute-start | bytes 786440 | tf_op jit(solution)/shard_map/ppermute | solution.py:26
  11.4 0.1 pad_add_fusion.1
  11.5 0.0 copy-start
  11.5 0.7 %copy-done = s32[2,32]{1,0:T(2,128)S(1)} copy-done((s32[2,32]{1,0:T(2,128)S(1)}, s32[2,32]{1,0:T(2,128)}, u32[]{:S(2)}) %copy-start) | copy-done | bytes 280
  12.2 0.5 slice.3
  13.4 0.0 copy-start.1
  13.4 0.7 %copy-done.1 = s32[512]{0:T(512)S(1)} copy-done((s32[512]{0:T(512)S(1)}, s32[512]{0:T(512)}, u32[]{:S(2)}) %copy-start.1) | copy-done | bytes 2072
  14.1 0.1 dynamic_slice.15
  14.1 0.1 broadcast_subtract_fusion.rows_ref
  14.2 1.2 %fields.2 = bf16[8,2,2,32,512]{4,3,2,1,0:T(8,128)(2,1)S(1)} custom-call(s32[1]{0:T(128)} %bitcast.1.lo_ref, s32[256,2]{1,0:T(8,128)S(1)} %broadcast_subtract_fusion.rows_ref, bf16[512,256]{1,0:T(8,128)(2,1)S(1)} %get-tuple-element.19.refs_0_, bf16[512,256]{1,0:T(8,128)(2,1)S(1)} %collective-permute-done.refs_1_), custom_call_target="tpu_custom_call" | custom-call | tf_op jit(solution)/shard_map/fields/pallas_call | solution.py:70
  15.5 24.9 %conditional.1 = (bf16[16,2,32,512]{3,2,1,0:T(8,128)(2,1)S(1)}) conditional(s32[]{:T(128)} %bitcast, bf16[16,2,32,512]{3,2,1,0:T(8,128)(2,1)S(1)} %bitcast.10, bf16[16,2,32,512]{3,2,1,0:T(8,128)(2,1)S(1)} %bitcast.11), branch_computations={%region_0.1_spmd, %region_1.2_spmd} | conditional | bytes 4194312 | solution.py:165
  15.5 0.1 copy.6
  15.6 24.8 %all_to_all.9 = bf16[16,2,32,512]{3,2,1,0:T(8,128)(2,1)S(1)} all-to-all(bf16[16,2,32,512]{3,2,1,0:T(8,128)(2,1)S(1)} %copy.6), channel_id=1, replica_groups=mesh['half'=2,'inner'=8,'hi'=1,'lo'=2] {'inner','lo'}, dimensions={0} | all-to-all | bytes 2097152 | tf_op jit(solution)/shard_map/cond/branch_1_fun/all_to_all | solution.py:160
  40.4 0.0 collective-permute-done.1.refs_0_
  40.4 0.0 collective-permute-done.2.refs_1_
  40.4 2.0 %fields.3 = bf16[8,2,2,32,512]{4,3,2,1,0:T(8,128)(2,1)} custom-call(s32[1]{0:T(128)} %bitcast.1.lo_ref, s32[256,2]{1,0:T(8,128)S(1)} %broadcast_subtract_fusion.rows_ref, bf16[512,256]{1,0:T(8,128)(2,1)S(1)} %collective-permute-done.1.refs_0_, bf16[512,256]{1,0:T(8,128)(2,1)S(1)} %collective-permute-done.2.refs_1_), custom_call_target="tpu_custom_call" | custom-call | tf_op jit(solution)/shard_map/fields/pallas_call | solution.py:70
  42.4 4.9 %all-to-all-start.1 = ((bf16[16,2,32,512]{3,2,1,0:T(8,128)(2,1)}), bf16[16,2,32,512]{3,2,1,0:T(8,128)(2,1)S(1)}, u32[]{:S(2)}, u32[]{:S(2)}) async-start(bf16[16,2,32,512]{3,2,1,0:T(8,128)(2,1)} %bitcast.7), calls=%async_computation.1 | async-start | bytes 2097152 | tf_op jit(solution)/shard_map/all_to_all | solution.py:160
  47.2 0.1 pad_add_fusion
  47.3 0.1 and_select_fusion.table_ref
  47.4 16.4 %all-to-all-done.1.far_ref = bf16[16,2,32,512]{3,2,1,0:T(8,128)(2,1)S(1)} async-done(((bf16[16,2,32,512]{3,2,1,0:T(8,128)(2,1)}), bf16[16,2,32,512]{3,2,1,0:T(8,128)(2,1)S(1)}, u32[]{:S(2)}, u32[]{:S(2)}) %all-to-all-start.1) | async-done | bytes 1048608 | tf_op jit(solution)/shard_map/all_to_all | solution.py:160
  63.8 3.1 %pairs.1 = f32[32,2,2,512]{3,2,1,0:T(2,128)} custom-call(s32[2,32]{1,0:T(2,128)S(1)} %and_select_fusion.table_ref, bf16[16,2,32,512]{3,2,1,0:T(8,128)(2,1)S(1)} %get-tuple-element.20.near_ref, bf16[16,2,32,512]{3,2,1,0:T(8,128)(2,1)S(1)} %all-to-all-done.1.far_ref), custom_call_target="tpu_custom_call" | custom-call | tf_op jit(solution)/shard_map/pairs/pallas_call | solution.py:122
Async XLA Ops:
  1.1 8.2 %collective-permute-start = (bf16[512,256]{1,0:T(8,128)(2,1)S(1)}, bf16[512,256]{1,0:T(8,128)(2,1)S(1)}, u32[]{:S(2)}, u32[]{:S(2)}) collective-permute-start(bf16[512,256]{1,0:T(8,128)(2,1)S(1)} %get-tuple-element.18), channel_id=1, source_target_pairs={{0,1},{1,0},{2,3},{3,2},{4,5},{5,4},{6,7},{7,6},{8,9},{9,8},{10,11... | collective-permute-start | bytes 786440 | tf_op jit(solution)/shard_map/ppermute | solution.py:26
  3.2 37.2 %collective-permute-start.1 = (bf16[512,256]{1,0:T(8,128)(2,1)S(1)}, bf16[512,256]{1,0:T(8,128)(2,1)S(1)}, u32[]{:S(2)}, u32[]{:S(2)}) collective-permute-start(bf16[512,256]{1,0:T(8,128)(2,1)S(1)} %get-tuple-element.19.refs_0_), channel_id=1, source_target_pairs={{0,16},{1,17},{2,18},{3,19},{4,20},{5,21},{6,22},{7,23},{8,24},{9,... | collective-permute-start | bytes 786440 | tf_op jit(solution)/shard_map/ppermute | solution.py:26
  9.2 31.1 %collective-permute-start.2 = (bf16[512,256]{1,0:T(8,128)(2,1)S(1)}, bf16[512,256]{1,0:T(8,128)(2,1)S(1)}, u32[]{:S(2)}, u32[]{:S(2)}) collective-permute-start(bf16[512,256]{1,0:T(8,128)(2,1)S(1)} %collective-permute-done.refs_1_), channel_id=1, source_target_pairs={{0,16},{1,17},{2,18},{3,19},{4,20},{5,21},{6,22},{7,23},{8,24},{9,... | collective-permute-start | bytes 786440 | tf_op jit(solution)/shard_map/ppermute | solution.py:26
  11.5 0.7 %copy-start = (s32[2,32]{1,0:T(2,128)S(1)}, s32[2,32]{1,0:T(2,128)}, u32[]{:S(2)}) copy-start(s32[2,32]{1,0:T(2,128)} %param.6) | copy-start | bytes 772
  13.4 0.7 %copy-start.1 = (s32[512]{0:T(512)S(1)}, s32[512]{0:T(512)}, u32[]{:S(2)}) copy-start(s32[512]{0:T(512)} %param.7) | copy-start | bytes 6148
  42.4 21.4 %all-to-all-start.1 = ((bf16[16,2,32,512]{3,2,1,0:T(8,128)(2,1)}), bf16[16,2,32,512]{3,2,1,0:T(8,128)(2,1)S(1)}, u32[]{:S(2)}, u32[]{:S(2)}) async-start(bf16[16,2,32,512]{3,2,1,0:T(8,128)(2,1)} %bitcast.7), calls=%async_computation.1 | async-start | bytes 2097152 | tf_op jit(solution)/shard_map/all_to_all | solution.py:160

commit v7 on v6

v7 whole, which is shorter than its diff:
```python
import functools
import math

import jax
import jax.numpy as jnp
from jax import lax
from jax.experimental import pallas as pl
from jax.experimental.pallas import tpu as pltpu
from jax.sharding import Mesh
from jax.sharding import PartitionSpec as P

VMEM_LIMIT = 40 * 1024 * 1024
SPLIT = 2
KA, GA = ("half", "inner"), ("hi", "lo")


def field_kernel(place_ref, points_ref, held_ref, out_ref, picked_ref):
    slabs, slab_size, channels = held_ref.shape
    npoints = points_ref.shape[1] // 2
    middle = channels // 2
    groups, _, _, length, _ = out_ref.shape
    step = pl.program_id(0)

    @pl.when(step == 0)
    def _():
        first = pl.multiple_of(place_ref[0] * npoints, npoints)
        wanted = points_ref[:, pl.ds(first, npoints)]
        spot = lax.broadcasted_iota(jnp.int32, (slab_size, npoints), 0)
        picked = jnp.zeros((npoints, channels), jnp.float32)
        for slab in range(slabs):
            chosen = (spot == wanted - slab * slab_size).astype(jnp.float32)
            picked += lax.dot_general(
                chosen.astype(jnp.bfloat16),
                held_ref[slab],
                (((0,), (0,)), ((), ())),
                preferred_element_type=jnp.float32,
            )
        rotated = jnp.concatenate([-picked[:, middle:], picked[:, :middle]], axis=1)
        picked_ref[0] = picked.astype(jnp.bfloat16)
        picked_ref[1] = rotated.astype(jnp.bfloat16)

    for part in range(2):
        product = lax.dot_general(
            picked_ref[part],
            held_ref[place_ref[1] * SPLIT + step],
            (((1,), (1,)), ((), ())),
            preferred_element_type=jnp.float32,
        )
        pieces = product.reshape(groups, length, slab_size)
        out_ref[:, 0, part] = pieces.astype(jnp.bfloat16)


def make_fields(held, points, groups, place):
    slabs, slab_size, channels = held.shape
    npoints = points.shape[1] // 2
    length = npoints // groups
    return pl.pallas_call(
        field_kernel,
        grid_spec=pltpu.PrefetchScalarGridSpec(
            num_scalar_prefetch=1,
            grid=(SPLIT,),
            in_specs=[
                pl.BlockSpec(points.shape, lambda step, place: (0, 0)),
                pl.BlockSpec(held.shape, lambda step, place: (0, 0, 0)),
            ],
            out_specs=pl.BlockSpec(
                (groups, 1, 2, length, slab_size), lambda step, place: (0, step, 0, 0, 0)
            ),
            scratch_shapes=[pltpu.VMEM((2, npoints, channels), jnp.bfloat16)],
        ),
        out_shape=jax.ShapeDtypeStruct((groups, SPLIT, 2, length, slab_size), jnp.bfloat16),
        compiler_params=pltpu.CompilerParams(vmem_limit_bytes=VMEM_LIMIT),
        name="fields",
    )(place, points, held)


def pair_kernel(scale, table_ref, near_ref, far_ref, out_ref, held_ref):
    total_k, _, length, width = held_ref.shape
    transfers = table_ref.shape[0]
    held_ref[: total_k // 2] = near_ref[...].astype(jnp.float32)
    held_ref[total_k // 2 :] = far_ref[...].astype(jnp.float32)

    def load(k, part, start, count):
        return held_ref[k, part, pl.ds(start, count), :]

    count = min(16, length)
    for start in range(0, length, count):

        def step(k, sums):
            real, imag = load(k, 0, start, count), load(k, 1, start, count)
            after = []
            for transfer in range(transfers):
                other = table_ref[transfer, k]
                other_real = load(other, 0, start, count)
                other_imag = load(other, 1, start, count)
                after.append(sums[2 * transfer] + (real * other_real + imag * other_imag))
                after.append(sums[2 * transfer + 1] + (imag * other_real - real * other_imag))
            return tuple(after)

        zero = jnp.zeros((count, width), jnp.float32)
        sums = lax.fori_loop(0, total_k, step, (zero,) * (2 * transfers), unroll=4)
        for place, value in enumerate(sums):
            out_ref[pl.ds(start, count), place // 2, place % 2, :] = value * scale


def make_pairs(near, far, table):
    half_k, _, length, slab_size = near.shape
    transfers = table.shape[0]
    width = 256
    fields = pl.BlockSpec((half_k, 2, length, width), lambda r, table: (0, 0, 0, r))
    return pl.pallas_call(
        functools.partial(pair_kernel, 1.0 / math.sqrt(2 * half_k)),
        grid_spec=pltpu.PrefetchScalarGridSpec(
            num_scalar_prefetch=1,
            grid=(slab_size // width,),
            in_specs=[fields, fields],
            out_specs=pl.BlockSpec((length, transfers, 2, width), lambda r, table: (0, 0, 0, r)),
            scratch_shapes=[pltpu.VMEM((2 * half_k, 2, length, width), jnp.float32)],
        ),
        out_shape=jax.ShapeDtypeStruct((length, transfers, 2, slab_size), jnp.float32),
        compiler_params=pltpu.CompilerParams(vmem_limit_bytes=VMEM_LIMIT),
        name="pairs",
    )(table, near, far)


def on_device(orbitals, minus_table, points):
    kdevice, slab_size, channels = orbitals.shape
    half = lax.axis_index("half")
    groups = lax.axis_size("inner")
    total_k = 2 * groups * kdevice

    near = lax.all_to_all(orbitals, "lo", split_axis=0, concat_axis=0, tiled=True)
    if lax.axis_size("hi") > 1:
        near = lax.all_gather(near, "hi", axis=0, tiled=True)
    far = lax.ppermute(near, "half", [(0, 1), (1, 0)])

    points = points.reshape(1, -1)
    place = jnp.stack([half, lax.axis_index("hi")])

    def flat(fields):
        return fields.reshape((groups * SPLIT,) + fields.shape[2:])

    def share(fields):
        return lax.all_to_all(fields, ("inner", "lo"), split_axis=0, concat_axis=0, tiled=True)

    near_fields = flat(make_fields(near, points, groups, place))
    near_fields, points = lax.optimization_barrier((near_fields, points))
    far_fields = flat(make_fields(far, points, groups, place))
    near_fields = lax.cond(half >= 0, share, lambda fields: fields, near_fields)
    near_fields, far_fields = lax.optimization_barrier((near_fields, far_fields))
    far_fields = share(far_fields)

    turn = half * (total_k // 2)
    table = (jnp.roll(minus_table, -turn, axis=1) - turn) % total_k
    return make_pairs(near_fields, far_fields, table)


def solution(mesh):
    kplaces, slabs = mesh.shape["ka"], mesh.shape["ga"]
    devices = mesh.devices.reshape(2, kplaces // 2, slabs // SPLIT, SPLIT)
    finer = Mesh(devices, KA + GA)
    return jax.shard_map(
        on_device,
        mesh=finer,
        in_specs=(P(KA, GA, None), P(), P()),
        out_specs=P(KA, None, None, GA),
        check_vma=False,
    )
```

time: 67.3 us -> 72.8 us (1.082)
  blocking collectives: 24.8 us -> 41.9 us
  starting transfers between devices: 11.5 us -> 5.94 us
  waiting for transfers between devices: 20.2 us -> 15.7 us
  local copies, waits for them, and re-layouts: 3.1 us -> 1.38 us
  Pallas kernels: 6.37 us -> 7.17 us
    all_to_all x0 -> x1, blocking collectives: none -> 11.8 us  [on_device(): lax.all_to_all(orbitals, 'lo', split_axis=0, concat_axis=0, tiled=True)]
    all_to_all x1, blocking collectives: 24.8 us -> 30.1 us  [share(): lax.all_to_all(fields, ('inner', 'lo'), split_axis=0, concat_axis=0, tile...]
    ppermute x3 -> x1, starting transfers between devices: 6.65 us -> 2.21 us  [on_device(): far = lax.ppermute(near, 'half', [(0, 1), (1, 0)])]
    ppermute x3 -> x1, waiting for transfers between devices: 3.73 us -> 0.01 us  [on_device(): far = lax.ppermute(near, 'half', [(0, 1), (1, 0)])]
    all_to_all x1, starting transfers between devices: 4.85 us -> 3.73 us  [share(): lax.all_to_all(fields, ('inner', 'lo'), split_axis=0, concat_axis=0, tile...]
    squeeze x1 -> x0, local copies, waits for them, and re-layouts: 1.06 us -> none  [on_device(): other = lax.dynamic_index_in_dim(orbitals, 1 - lo, 0, keepdims=False)]
    pallas_call x2, Pallas kernels: 3.25 us -> 4.06 us  [make_fields(): pl.pallas_call(field_kernel, grid_spec=pltpu.PrefetchScalarGridSpec(num_s...]
  transfers between devices with their start and end apart: 4 -> 2, of which waited for: 2 -> 1; matrix products, arithmetic and copies ran while one was open for 2% -> 0% of each run, Pallas kernels for 2% -> 2%
where the time goes in v7:
time: 72.8 us; the launch traced here: 72.4 us
  blocking collectives  41.9 us (58%)
  waiting for transfers between devices  15.7 us (22%)
  Pallas kernels  7.17 us (10%)
  starting transfers between devices  5.94 us (8%)
  local copies, waits for them, and re-layouts  1.38 us (2%)
    all_to_all x1, blocking collectives, share(): lax.all_to_all(fields, ('inner', 'lo'), split_axis=0, concat_axis=0, tile...  30.1 us
    all_to_all x1, waiting for transfers between devices, share(): lax.all_to_all(fields, ('inner', 'lo'), split_axis=0, concat_axis=0, tile...  15.7 us
    all_to_all x1, blocking collectives, on_device(): lax.all_to_all(orbitals, 'lo', split_axis=0, concat_axis=0, tiled=True)  11.8 us
    pallas_call x2, Pallas kernels, make_fields(): pl.pallas_call(field_kernel, grid_spec=pltpu.PrefetchScalarGridSpec(num_s...  4.06 us
    all_to_all x1, starting transfers between devices, share(): lax.all_to_all(fields, ('inner', 'lo'), split_axis=0, concat_axis=0, tile...  3.73 us
    pallas_call x1, Pallas kernels, make_pairs(): pl.pallas_call(functools.partial(pair_kernel, 1.0 / math.sqrt(2 * half_k)...  3.12 us
    ppermute x1, starting transfers between devices, on_device(): far = lax.ppermute(near, 'half', [(0, 1), (1, 0)])  2.21 us
  transfers between devices with their start and end apart: 2, of which 1 were waited for; matrix products, arithmetic and copies ran while one was open for 0% of the time, Pallas kernels for 2%

profile of v7, /device:TPU:1, one launch (start us, length us, event | category | flops | bytes accessed | tf_op | source)
XLA Modules:
  0.0 72.4 jit_solution(5074489319467800192)
XLA Ops:
  0.0 11.8 %all_to_all.15.held_ref = bf16[2,512,256]{2,1,0:T(8,128)(2,1)S(1)} all-to-all(bf16[2,512,256]{2,1,0:T(8,128)(2,1)} %param.5), channel_id=1, replica_groups=mesh['half'=2,'inner'=8,'hi'=1,'lo'=2] {'lo'}, dimensions={0} | all-to-all | bytes 1048576 | tf_op jit(solution)/shard_map/all_to_all | solution.py:132
  11.8 2.2 %collective-permute-start = (bf16[2,512,256]{2,1,0:T(8,128)(2,1)S(1)}, bf16[2,512,256]{2,1,0:T(8,128)(2,1)S(1)}, u32[]{:S(2)}, u32[]{:S(2)}) collective-permute-start(bf16[2,512,256]{2,1,0:T(8,128)(2,1)S(1)} %all_to_all.15.held_ref), channel_id=1, source_target_pairs={{0,16},{16,0},{1,17},{17,1},{2,18},{18,2},{3,19},{19,3},{4,20},{20... | collective-permute-start | bytes 1572872 | tf_op jit(solution)/shard_map/ppermute | solution.py:135
  14.0 0.0 copy-start
  14.0 0.1 pad_add_fusion.1.place_ref
  14.1 0.6 copy-done
  14.7 1.6 %fields.2 = bf16[8,2,2,32,512]{4,3,2,1,0:T(8,128)(2,1)S(1)} custom-call(s32[2]{0:T(128)S(1)} %pad_add_fusion.1.place_ref, s32[1,512]{1,0:T(1,128)S(1)} %bitcast.4, bf16[2,512,256]{2,1,0:T(8,128)(2,1)S(1)} %all_to_all.15.held_ref), custom_call_target="tpu_custom_call" | custom-call | tf_op jit(solution)/shard_map/fields/pallas_call | solution.py:57
  16.3 30.3 %conditional.1 = (bf16[16,2,32,512]{3,2,1,0:T(8,128)(2,1)S(1)}) conditional(s32[]{:T(128)} %convert_element_type.3, bf16[16,2,32,512]{3,2,1,0:T(8,128)(2,1)S(1)} %bitcast.6, bf16[16,2,32,512]{3,2,1,0:T(8,128)(2,1)S(1)} %bitcast.7), branch_computations={%region_0.0_spmd, %region_1.0_spmd} | conditional | bytes 4194312 | solution.py:149
  16.3 0.1 copy.6
  16.4 30.1 %all_to_all.14 = bf16[16,2,32,512]{3,2,1,0:T(8,128)(2,1)S(1)} all-to-all(bf16[16,2,32,512]{3,2,1,0:T(8,128)(2,1)S(1)} %copy.6), channel_id=1, replica_groups=mesh['half'=2,'inner'=8,'hi'=1,'lo'=2] {'inner','lo'}, dimensions={0} | all-to-all | bytes 2097152 | tf_op jit(solution)/shard_map/cond/branch_1_fun/all_to_all | solution.py:144
  46.6 0.0 collective-permute-done.held_ref
  46.6 2.4 %fields.3 = bf16[8,2,2,32,512]{4,3,2,1,0:T(8,128)(2,1)} custom-call(s32[2]{0:T(128)S(1)} %pad_add_fusion.1.place_ref, s32[1,512]{1,0:T(1,128)S(1)} %bitcast.5, bf16[2,512,256]{2,1,0:T(8,128)(2,1)S(1)} %collective-permute-done.held_ref), custom_call_target="tpu_custom_call" | custom-call | tf_op jit(solution)/shard_map/fields/pallas_call | solution.py:57
  49.0 3.7 %all-to-all-start.2 = ((bf16[16,2,32,512]{3,2,1,0:T(8,128)(2,1)}), bf16[16,2,32,512]{3,2,1,0:T(8,128)(2,1)S(1)}, u32[]{:S(2)}, u32[]{:S(2)}) async-start(bf16[16,2,32,512]{3,2,1,0:T(8,128)(2,1)} %bitcast.3), calls=%async_computation.2 | async-start | bytes 2097152 | tf_op jit(solution)/shard_map/all_to_all | solution.py:144
  52.7 0.0 copy-start.1
  52.7 0.7 copy-done.1
  53.4 0.1 pad_add_fusion
  53.5 0.1 and_select_fusion.table_ref
  53.6 15.7 %all-to-all-done.2.far_ref = bf16[16,2,32,512]{3,2,1,0:T(8,128)(2,1)S(1)} async-done(((bf16[16,2,32,512]{3,2,1,0:T(8,128)(2,1)}), bf16[16,2,32,512]{3,2,1,0:T(8,128)(2,1)S(1)}, u32[]{:S(2)}, u32[]{:S(2)}) %all-to-all-start.2) | async-done | bytes 1048608 | tf_op jit(solution)/shard_map/all_to_all | solution.py:144
  69.3 3.1 %pairs.1 = f32[32,2,2,512]{3,2,1,0:T(2,128)} custom-call(s32[2,32]{1,0:T(2,128)S(1)} %and_select_fusion.table_ref, bf16[16,2,32,512]{3,2,1,0:T(8,128)(2,1)S(1)} %get-tuple-element.18.near_ref, bf16[16,2,32,512]{3,2,1,0:T(8,128)(2,1)S(1)} %all-to-all-done.2.far_ref), custom_call_target="tpu_custom_call" | custom-call | tf_op jit(solution)/shard_map/pairs/pallas_call | solution.py:111
Async XLA Ops:
  11.8 34.8 %collective-permute-start = (bf16[2,512,256]{2,1,0:T(8,128)(2,1)S(1)}, bf16[2,512,256]{2,1,0:T(8,128)(2,1)S(1)}, u32[]{:S(2)}, u32[]{:S(2)}) collective-permute-start(bf16[2,512,256]{2,1,0:T(8,128)(2,1)S(1)} %all_to_all.15.held_ref), channel_id=1, source_target_pairs={{0,16},{16,0},{1,17},{17,1},{2,18},{18,2},{3,19},{19,3},{4,20},{20... | collective-permute-start | bytes 1572872 | tf_op jit(solution)/shard_map/ppermute | solution.py:135
  14.0 0.7 copy-start
  49.0 20.3 %all-to-all-start.2 = ((bf16[16,2,32,512]{3,2,1,0:T(8,128)(2,1)}), bf16[16,2,32,512]{3,2,1,0:T(8,128)(2,1)S(1)}, u32[]{:S(2)}, u32[]{:S(2)}) async-start(bf16[16,2,32,512]{3,2,1,0:T(8,128)(2,1)} %bitcast.3), calls=%async_computation.2 | async-start | bytes 2097152 | tf_op jit(solution)/shard_map/all_to_all | solution.py:144
  52.7 0.7 copy-start.1

commit v8 on v7

--- a/solution.py
+++ b/solution.py
@@ -14,8 +14,20 @@
 KA, GA = ("half", "inner"), ("hi", "lo")
 
 
-def field_kernel(place_ref, points_ref, held_ref, out_ref, picked_ref):
-    slabs, slab_size, channels = held_ref.shape
+def swap(block, cut, other):
+    half, inner, hi, lo = (lax.axis_size(name) for name in KA + GA)
+    slabs = hi * lo
+    route = []
+    for place in range(half * inner * slabs):
+        kplace, slab = divmod(place, slabs)
+        kplace = (kplace + cut * inner) % (half * inner)
+        route.append((place, kplace * slabs + (slab ^ other)))
+    return lax.ppermute(block, KA + GA, route)
+
+
+def field_kernel(count, place_ref, points_ref, *refs):
+    slab_refs, (out_ref, picked_ref) = refs[:count], refs[count:]
+    slab_size, channels = slab_refs[0].shape
     npoints = points_ref.shape[1] // 2
     middle = channels // 2
     groups, _, _, length, _ = out_ref.shape
@@ -27,11 +39,11 @@
         wanted = points_ref[:, pl.ds(first, npoints)]
         spot = lax.broadcasted_iota(jnp.int32, (slab_size, npoints), 0)
         picked = jnp.zeros((npoints, channels), jnp.float32)
-        for slab in range(slabs):
-            chosen = (spot == wanted - slab * slab_size).astype(jnp.float32)
+        for number, slab_ref in enumerate(slab_refs):
+            chosen = spot == wanted - (place_ref[1] ^ number) * slab_size
             picked += lax.dot_general(
-                chosen.astype(jnp.bfloat16),
-                held_ref[slab],
+                chosen.astype(jnp.float32).astype(jnp.bfloat16),
+                slab_ref[...],
                 (((0,), (0,)), ((), ())),
                 preferred_element_type=jnp.float32,
             )
@@ -39,39 +51,42 @@
         picked_ref[0] = picked.astype(jnp.bfloat16)
         picked_ref[1] = rotated.astype(jnp.bfloat16)
 
-    for part in range(2):
-        product = lax.dot_general(
-            picked_ref[part],
-            held_ref[place_ref[1] * SPLIT + step],
-            (((1,), (1,)), ((), ())),
-            preferred_element_type=jnp.float32,
-        )
-        pieces = product.reshape(groups, length, slab_size)
-        out_ref[:, 0, part] = pieces.astype(jnp.bfloat16)
+    for number in range(SPLIT):
+
+        @pl.when(step == number)
+        def _(number=number):
+            for part in range(2):
+                product = lax.dot_general(
+                    picked_ref[part],
+                    slab_refs[number][...],
+                    (((1,), (1,)), ((), ())),
+                    preferred_element_type=jnp.float32,
+                )
+                pieces = product.reshape(groups, length, slab_size)
+                out_ref[:, 0, part] = pieces.astype(jnp.bfloat16)
 
 
-def make_fields(held, points, groups, place):
-    slabs, slab_size, channels = held.shape
+def make_fields(slabs, points, groups, place):
+    slab_size, channels = slabs[0].shape
     npoints = points.shape[1] // 2
     length = npoints // groups
     return pl.pallas_call(
-        field_kernel,
+        functools.partial(field_kernel, len(slabs)),
         grid_spec=pltpu.PrefetchScalarGridSpec(
             num_scalar_prefetch=1,
             grid=(SPLIT,),
-            in_specs=[
-                pl.BlockSpec(points.shape, lambda step, place: (0, 0)),
-                pl.BlockSpec(held.shape, lambda step, place: (0, 0, 0)),
-            ],
+            in_specs=[pl.BlockSpec(points.shape, lambda step, place: (0, 0))]
+            + [pl.BlockSpec((slab_size, channels), lambda step, place: (0, 0)) for _ in slabs],
             out_specs=pl.BlockSpec(
-                (groups, 1, 2, length, slab_size), lambda step, place: (0, step, 0, 0, 0)
+                (groups, 1, 2, length, slab_size),
+                lambda step, place: (0, place[1] % SPLIT ^ step, 0, 0, 0),
             ),
             scratch_shapes=[pltpu.VMEM((2, npoints, channels), jnp.bfloat16)],
         ),
         out_shape=jax.ShapeDtypeStruct((groups, SPLIT, 2, length, slab_size), jnp.bfloat16),
         compiler_params=pltpu.CompilerParams(vmem_limit_bytes=VMEM_LIMIT),
         name="fields",
-    )(place, points, held)
+    )(place, points, *slabs)
 
 
 def pair_kernel(scale, table_ref, near_ref, far_ref, out_ref, held_ref):
@@ -129,13 +144,15 @@
     groups = lax.axis_size("inner")
     total_k = 2 * groups * kdevice
 
-    near = lax.all_to_all(orbitals, "lo", split_axis=0, concat_axis=0, tiled=True)
-    if lax.axis_size("hi") > 1:
-        near = lax.all_gather(near, "hi", axis=0, tiled=True)
-    far = lax.ppermute(near, "half", [(0, 1), (1, 0)])
+    lo = lax.axis_index("lo")
+    slabs = lax.axis_size("hi") * SPLIT
+    mine = lax.dynamic_index_in_dim(orbitals, lo, 0, keepdims=False)
+    other = lax.dynamic_index_in_dim(orbitals, 1 - lo, 0, keepdims=False)
+    near = [mine] + [swap(other if x & 1 else mine, 0, x) for x in range(1, slabs)]
+    far = [swap(other if x & 1 else mine, 1, x) for x in range(slabs)]
 
     points = points.reshape(1, -1)
-    place = jnp.stack([half, lax.axis_index("hi")])
+    place = jnp.stack([half, lax.axis_index("hi") * SPLIT + lo])
 
     def flat(fields):
         return fields.reshape((groups * SPLIT,) + fields.shape[2:])

time: 72.8 us -> 67.8 us (0.931)
  blocking collectives: 41.9 us -> 29 us
  waiting for transfers between devices: 15.7 us -> 20.5 us
  starting transfers between devices: 5.94 us -> 8.32 us
    all_to_all x1 -> x0, blocking collectives: 11.8 us -> none  [on_device(): lax.all_to_all(orbitals, 'lo', split_axis=0, concat_axis=0, tiled=True)]
    ppermute x1 -> x3, waiting for transfers between devices: 0.01 us -> 4.76 us  [swap(): return lax.ppermute(block, KA + GA, route)]
    ppermute x1 -> x3, starting transfers between devices: 2.21 us -> 4.45 us  [swap(): return lax.ppermute(block, KA + GA, route)]
    all_to_all x1, blocking collectives: 30.1 us -> 29 us  [share(): lax.all_to_all(fields, ('inner', 'lo'), split_axis=0, concat_axis=0, tile...]
    squeeze x0 -> x1, local copies, waits for them, and re-layouts: none -> 1.06 us  [on_device(): other = lax.dynamic_index_in_dim(orbitals, 1 - lo, 0, keepdims=False)]
  transfers between devices with their start and end apart: 2 -> 4, of which waited for: 1 -> 2; matrix products, arithmetic and copies ran while one was open for 0% -> 0% of each run, Pallas kernels for 2% -> 3%
where the time goes in v8:
time: 67.8 us; the launch traced here: 67.4 us
  blocking collectives  29 us (43%)
  waiting for transfers between devices  20.5 us (30%)
  starting transfers between devices  8.32 us (12%)
  Pallas kernels  7.46 us (11%)
  local copies, waits for them, and re-layouts  1.84 us (3%)
    all_to_all x1, blocking collectives, share(): lax.all_to_all(fields, ('inner', 'lo'), split_axis=0, concat_axis=0, tile...  29 us
    all_to_all x1, waiting for transfers between devices, share(): lax.all_to_all(fields, ('inner', 'lo'), split_axis=0, concat_axis=0, tile...  15.7 us
    ppermute x3, waiting for transfers between devices, swap(): return lax.ppermute(block, KA + GA, route)  4.76 us
    ppermute x3, starting transfers between devices, swap(): return lax.ppermute(block, KA + GA, route)  4.45 us
    pallas_call x2, Pallas kernels, make_fields(): pl.pallas_call(functools.partial(field_kernel, len(slabs)), grid_spec=plt...  4.34 us
    all_to_all x1, starting transfers between devices, share(): lax.all_to_all(fields, ('inner', 'lo'), split_axis=0, concat_axis=0, tile...  3.88 us
    pallas_call x1, Pallas kernels, make_pairs(): pl.pallas_call(functools.partial(pair_kernel, 1.0 / math.sqrt(2 * half_k)...  3.12 us
  transfers between devices with their start and end apart: 4, of which 2 were waited for; matrix products, arithmetic and copies ran while one was open for 0% of the time, Pallas kernels for 3%

profile of v8, /device:TPU:1, one launch (start us, length us, event | category | flops | bytes accessed | tf_op | source)
XLA Modules:
  0.0 67.4 jit_solution(10723105223718439930)
XLA Ops:
  0.0 1.1 %dynamic-slice_bitcast_fusion = (bf16[512,256]{1,0:T(8,128)(2,1)S(1)}, bf16[512,256]{1,0:T(8,128)(2,1)S(1)}) fusion(bf16[2,512,256]{2,1,0:T(8,128)(2,1)} %param.5, s32[]{:T(128)S(6)} %select_n.30, s32[]{:T(128)S(6)} %select_n.29), kind=kLoop, calls=%fused_computation | loop fusion | bytes 1048584 | tf_op jit(solution)/shard_map/jit(dynamic_index_in_dim)/squeeze | solution.py:150
  1.1 2.1 %collective-permute-start = (bf16[512,256]{1,0:T(8,128)(2,1)S(1)}, bf16[512,256]{1,0:T(8,128)(2,1)S(1)}, u32[]{:S(2)}, u32[]{:S(2)}) collective-permute-start(bf16[512,256]{1,0:T(8,128)(2,1)S(1)} %get-tuple-element.18), channel_id=1, source_target_pairs={{0,1},{1,0},{2,3},{3,2},{4,5},{5,4},{6,7},{7,6},{8,9},{9,8},{10,11... | collective-permute-start | bytes 786440 | tf_op jit(solution)/shard_map/ppermute | solution.py:25
  3.2 2.3 %collective-permute-start.2 = (bf16[512,256]{1,0:T(8,128)(2,1)S(1)}, bf16[512,256]{1,0:T(8,128)(2,1)S(1)}, u32[]{:S(2)}, u32[]{:S(2)}) collective-permute-start(bf16[512,256]{1,0:T(8,128)(2,1)S(1)} %get-tuple-element.18), channel_id=1, source_target_pairs={{0,17},{1,16},{2,19},{3,18},{4,21},{5,20},{6,23},{7,22},{8,25},{9,... | collective-permute-start | bytes 786440 | tf_op jit(solution)/shard_map/ppermute | solution.py:25
  5.5 0.1 collective-permute-start.1
  5.5 0.0 copy-start
  5.5 0.1 pad_add_fusion.1.place_ref
  5.6 4.8 %collective-permute-done.refs_1_ = bf16[512,256]{1,0:T(8,128)(2,1)S(1)} collective-permute-done((bf16[512,256]{1,0:T(8,128)(2,1)S(1)}, bf16[512,256]{1,0:T(8,128)(2,1)S(1)}, u32[]{:S(2)}, u32[]{:S(2)}) %collective-permute-start) | collective-permute-done | bytes 262176 | tf_op jit(solution)/shard_map/ppermute | solution.py:25
  10.3 0.0 copy-done
  10.4 1.8 %fields.2 = bf16[8,2,2,32,512]{4,3,2,1,0:T(8,128)(2,1)S(1)} custom-call(s32[2]{0:T(128)S(1)} %pad_add_fusion.1.place_ref, s32[1,512]{1,0:T(1,128)S(1)} %bitcast.9, bf16[512,256]{1,0:T(8,128)(2,1)S(1)} %get-tuple-element.19.refs_0_, bf16[512,256]{1,0:T(8,128)(2,1)S(1)} %collective-permute-done.refs_1_), custom_call_target="tpu_custom_call" | custom-call | tf_op jit(solution)/shard_map/fields/pallas_call | solution.py:73
  12.1 29.2 %conditional.1 = (bf16[16,2,32,512]{3,2,1,0:T(8,128)(2,1)S(1)}) conditional(s32[]{:T(128)} %convert_element_type.3, bf16[16,2,32,512]{3,2,1,0:T(8,128)(2,1)S(1)} %bitcast.11, bf16[16,2,32,512]{3,2,1,0:T(8,128)(2,1)S(1)} %bitcast.12), branch_computations={%region_0.1_spmd, %region_1.2_spmd} | conditional | bytes 4194312 | solution.py:166
  12.2 0.1 copy.6
  12.3 29.0 %all_to_all.9 = bf16[16,2,32,512]{3,2,1,0:T(8,128)(2,1)S(1)} all-to-all(bf16[16,2,32,512]{3,2,1,0:T(8,128)(2,1)S(1)} %copy.6), channel_id=1, replica_groups=mesh['half'=2,'inner'=8,'hi'=1,'lo'=2] {'inner','lo'}, dimensions={0} | all-to-all | bytes 2097152 | tf_op jit(solution)/shard_map/cond/branch_1_fun/all_to_all | solution.py:161
  41.3 0.0 collective-permute-done.2.refs_1_
  41.3 0.0 collective-permute-done.1.refs_0_
  41.3 2.6 %fields.3 = bf16[8,2,2,32,512]{4,3,2,1,0:T(8,128)(2,1)} custom-call(s32[2]{0:T(128)S(1)} %pad_add_fusion.1.place_ref, s32[1,512]{1,0:T(1,128)S(1)} %bitcast.10, bf16[512,256]{1,0:T(8,128)(2,1)S(1)} %collective-permute-done.1.refs_0_, bf16[512,256]{1,0:T(8,128)(2,1)S(1)} %collective-permute-done.2.refs_1_), custom_call_target="tpu_custom_call" | custom-call | tf_op jit(solution)/shard_map/fields/pallas_call | solution.py:73
  43.9 3.9 %all-to-all-start.1 = ((bf16[16,2,32,512]{3,2,1,0:T(8,128)(2,1)}), bf16[16,2,32,512]{3,2,1,0:T(8,128)(2,1)S(1)}, u32[]{:S(2)}, u32[]{:S(2)}) async-start(bf16[16,2,32,512]{3,2,1,0:T(8,128)(2,1)} %bitcast.6), calls=%async_computation.1 | async-start | bytes 2097152 | tf_op jit(solution)/shard_map/all_to_all | solution.py:161
  47.7 0.0 copy-start.1
  47.8 0.7 copy-done.1
  48.4 0.1 pad_add_fusion
  48.5 0.1 and_select_fusion.table_ref
  48.6 15.7 %all-to-all-done.1.far_ref = bf16[16,2,32,512]{3,2,1,0:T(8,128)(2,1)S(1)} async-done(((bf16[16,2,32,512]{3,2,1,0:T(8,128)(2,1)}), bf16[16,2,32,512]{3,2,1,0:T(8,128)(2,1)S(1)}, u32[]{:S(2)}, u32[]{:S(2)}) %all-to-all-start.1) | async-done | bytes 1048608 | tf_op jit(solution)/shard_map/all_to_all | solution.py:161
  64.3 3.1 %pairs.1 = f32[32,2,2,512]{3,2,1,0:T(2,128)} custom-call(s32[2,32]{1,0:T(2,128)S(1)} %and_select_fusion.table_ref, bf16[16,2,32,512]{3,2,1,0:T(8,128)(2,1)S(1)} %get-tuple-element.20.near_ref, bf16[16,2,32,512]{3,2,1,0:T(8,128)(2,1)S(1)} %all-to-all-done.1.far_ref), custom_call_target="tpu_custom_call" | custom-call | tf_op jit(solution)/shard_map/pairs/pallas_call | solution.py:126
Async XLA Ops:
  1.1 9.3 %collective-permute-start = (bf16[512,256]{1,0:T(8,128)(2,1)S(1)}, bf16[512,256]{1,0:T(8,128)(2,1)S(1)}, u32[]{:S(2)}, u32[]{:S(2)}) collective-permute-start(bf16[512,256]{1,0:T(8,128)(2,1)S(1)} %get-tuple-element.18), channel_id=1, source_target_pairs={{0,1},{1,0},{2,3},{3,2},{4,5},{5,4},{6,7},{7,6},{8,9},{9,8},{10,11... | collective-permute-start | bytes 786440 | tf_op jit(solution)/shard_map/ppermute | solution.py:25
  3.2 38.1 %collective-permute-start.2 = (bf16[512,256]{1,0:T(8,128)(2,1)S(1)}, bf16[512,256]{1,0:T(8,128)(2,1)S(1)}, u32[]{:S(2)}, u32[]{:S(2)}) collective-permute-start(bf16[512,256]{1,0:T(8,128)(2,1)S(1)} %get-tuple-element.18), channel_id=1, source_target_pairs={{0,17},{1,16},{2,19},{3,18},{4,21},{5,20},{6,23},{7,22},{8,25},{9,... | collective-permute-start | bytes 786440 | tf_op jit(solution)/shard_map/ppermute | solution.py:25
  5.5 35.9 %collective-permute-start.1 = (bf16[512,256]{1,0:T(8,128)(2,1)S(1)}, bf16[512,256]{1,0:T(8,128)(2,1)S(1)}, u32[]{:S(2)}, u32[]{:S(2)}) collective-permute-start(bf16[512,256]{1,0:T(8,128)(2,1)S(1)} %get-tuple-element.19.refs_0_), channel_id=1, source_target_pairs={{0,16},{1,17},{2,18},{3,19},{4,20},{5,21},{6,22},{7,23},{8,24},{9,... | collective-permute-start | bytes 786440 | tf_op jit(solution)/shard_map/ppermute | solution.py:25
  5.5 4.8 %copy-start = (s32[512]{0:T(512)S(1)}, s32[512]{0:T(512)}, u32[]{:S(2)}) copy-start(s32[512]{0:T(512)} %param.7) | copy-start | bytes 6148
  43.9 20.5 %all-to-all-start.1 = ((bf16[16,2,32,512]{3,2,1,0:T(8,128)(2,1)}), bf16[16,2,32,512]{3,2,1,0:T(8,128)(2,1)S(1)}, u32[]{:S(2)}, u32[]{:S(2)}) async-start(bf16[16,2,32,512]{3,2,1,0:T(8,128)(2,1)} %bitcast.6), calls=%async_computation.1 | async-start | bytes 2097152 | tf_op jit(solution)/shard_map/all_to_all | solution.py:161
  47.7 0.7 %copy-start.1 = (s32[2,32]{1,0:T(2,128)S(1)}, s32[2,32]{1,0:T(2,128)}, u32[]{:S(2)}) copy-start(s32[2,32]{1,0:T(2,128)} %param.6) | copy-start | bytes 772

commit v9 on v8

--- a/solution.py
+++ b/solution.py
@@ -11,23 +11,30 @@
 
 VMEM_LIMIT = 40 * 1024 * 1024
 SPLIT = 2
-KA, GA = ("half", "inner"), ("hi", "lo")
-
-
-def swap(block, cut, other):
-    half, inner, hi, lo = (lax.axis_size(name) for name in KA + GA)
+KA, GA = ("half", "quarter", "inner"), ("hi", "lo")
+OUTER, MIDDLE = (0, 3), (1, 2)
+
+
+def swap(block, other, quarters=None):
+    half, quarter, inner, hi, lo = (lax.axis_size(name) for name in KA + GA)
     slabs = hi * lo
     route = []
-    for place in range(half * inner * slabs):
+    for place in range(half * quarter * inner * slabs):
         kplace, slab = divmod(place, slabs)
-        kplace = (kplace + cut * inner) % (half * inner)
-        route.append((place, kplace * slabs + (slab ^ other)))
+        part, within = divmod(kplace, inner)
+        if quarters is not None and part not in quarters:
+            continue
+        part = part if quarters is None else half * quarter - 1 - part
+        route.append((place, (part * inner + within) * slabs + (slab ^ other)))
     return lax.ppermute(block, KA + GA, route)
 
 
-def field_kernel(count, place_ref, points_ref, *refs):
-    slab_refs, (out_ref, picked_ref) = refs[:count], refs[count:]
-    slab_size, channels = slab_refs[0].shape
+def field_kernel(sets, place_ref, points_ref, *refs):
+    *source_refs, out_ref, picked_ref, held_ref = refs
+    slabs, slab_size, channels = held_ref.shape
+    slab_refs = [held_ref.at[number] for number in range(slabs)]
+    if sets == 1:
+        slab_refs = source_refs
     npoints = points_ref.shape[1] // 2
     middle = channels // 2
     groups, _, _, length, _ = out_ref.shape
@@ -35,6 +42,13 @@
 
     @pl.when(step == 0)
     def _():
+        for number in range(slabs if sets > 1 else 0):
+            for choice in range(sets):
+
+                @pl.when(place_ref[2] == choice)
+                def _(number=number, choice=choice):
+                    held_ref[number] = source_refs[choice * slabs + number][...]
+
         first = pl.multiple_of(place_ref[0] * npoints, npoints)
         wanted = points_ref[:, pl.ds(first, npoints)]
         spot = lax.broadcasted_iota(jnp.int32, (slab_size, npoints), 0)
@@ -66,12 +80,13 @@
                 out_ref[:, 0, part] = pieces.astype(jnp.bfloat16)
 
 
-def make_fields(slabs, points, groups, place):
-    slab_size, channels = slabs[0].shape
+def make_fields(sources, points, groups, place):
+    slab_size, channels = sources[0][0].shape
+    slabs = [slab for source in sources for slab in source]
     npoints = points.shape[1] // 2
     length = npoints // groups
     return pl.pallas_call(
-        functools.partial(field_kernel, len(slabs)),
+        functools.partial(field_kernel, len(sources)),
         grid_spec=pltpu.PrefetchScalarGridSpec(
             num_scalar_prefetch=1,
             grid=(SPLIT,),
@@ -81,7 +96,10 @@
                 (groups, 1, 2, length, slab_size),
                 lambda step, place: (0, place[1] % SPLIT ^ step, 0, 0, 0),
             ),
-            scratch_shapes=[pltpu.VMEM((2, npoints, channels), jnp.bfloat16)],
+            scratch_shapes=[
+                pltpu.VMEM((2, npoints, channels), jnp.bfloat16),
+                pltpu.VMEM((len(sources[0]), slab_size, channels), jnp.bfloat16),
+            ],
         ),
         out_shape=jax.ShapeDtypeStruct((groups, SPLIT, 2, length, slab_size), jnp.bfloat16),
         compiler_params=pltpu.CompilerParams(vmem_limit_bytes=VMEM_LIMIT),
@@ -140,41 +158,49 @@
 
 def on_device(orbitals, minus_table, points):
     kdevice, slab_size, channels = orbitals.shape
-    half = lax.axis_index("half")
-    groups = lax.axis_size("inner")
+    half, quarter = lax.axis_index("half"), lax.axis_index("quarter")
+    hi, lo = lax.axis_index("hi"), lax.axis_index("lo")
+    groups = lax.axis_size("quarter") * lax.axis_size("inner")
+    slabs = lax.axis_size("hi") * lax.axis_size("lo")
     total_k = 2 * groups * kdevice
 
-    lo = lax.axis_index("lo")
-    slabs = lax.axis_size("hi") * SPLIT
     mine = lax.dynamic_index_in_dim(orbitals, lo, 0, keepdims=False)
     other = lax.dynamic_index_in_dim(orbitals, 1 - lo, 0, keepdims=False)
-    near = [mine] + [swap(other if x & 1 else mine, 0, x) for x in range(1, slabs)]
-    far = [swap(other if x & 1 else mine, 1, x) for x in range(slabs)]
+    near = [mine] + [swap(other if x & 1 else mine, x) for x in range(1, slabs)]
+    outer = [swap(other if x & 1 else mine, x, OUTER) for x in range(slabs)]
+    later = lax.optimization_barrier(near)
+    middle = [swap(slab, 0, MIDDLE) for slab in later]
 
     points = points.reshape(1, -1)
-    place = jnp.stack([half, lax.axis_index("hi") * SPLIT + lo])
+    place = jnp.stack([half, hi * SPLIT + lo, (half == quarter).astype(jnp.int32)])
 
     def flat(fields):
         return fields.reshape((groups * SPLIT,) + fields.shape[2:])
 
     def share(fields):
-        return lax.all_to_all(fields, ("inner", "lo"), split_axis=0, concat_axis=0, tiled=True)
-
-    near_fields = flat(make_fields(near, points, groups, place))
+        around = ("quarter", "inner", "lo")
+        return lax.all_to_all(fields, around, split_axis=0, concat_axis=0, tiled=True)
+
+    near_fields = flat(make_fields([near], points, groups, place))
     near_fields, points = lax.optimization_barrier((near_fields, points))
-    far_fields = flat(make_fields(far, points, groups, place))
+    far_fields = flat(make_fields([middle, outer], points, groups, place))
     near_fields = lax.cond(half >= 0, share, lambda fields: fields, near_fields)
     near_fields, far_fields = lax.optimization_barrier((near_fields, far_fields))
     far_fields = share(far_fields)
 
+    def mirrored(kpoints):
+        return total_k // 2 + (kpoints + total_k // 4) % (total_k // 2)
+
     turn = half * (total_k // 2)
     table = (jnp.roll(minus_table, -turn, axis=1) - turn) % total_k
-    return make_pairs(near_fields, far_fields, table)
+    table = jnp.where(table < total_k // 2, table, mirrored(table))
+    first, third, fourth = jnp.split(table, (total_k // 2, 3 * total_k // 4), axis=1)
+    return make_pairs(near_fields, far_fields, jnp.concatenate([first, fourth, third], axis=1))
 
 
 def solution(mesh):
     kplaces, slabs = mesh.shape["ka"], mesh.shape["ga"]
-    devices = mesh.devices.reshape(2, kplaces // 2, slabs // SPLIT, SPLIT)
+    devices = mesh.devices.reshape(2, 2, kplaces // 4, slabs // SPLIT, SPLIT)
     finer = Mesh(devices, KA + GA)
     return jax.shard_map(
         on_device,

time: 67.8 us -> 65.8 us (0.971)
  starting transfers between devices: 8.32 us -> 14.4 us
  waiting for transfers between devices: 20.5 us -> 15.6 us
  blocking collectives: 29 us -> 25 us
    ppermute x3 -> x5, starting transfers between devices: 4.45 us -> 10.6 us  [swap(): return lax.ppermute(block, KA + GA, route)]
    ppermute x3 -> x5, waiting for transfers between devices: 4.76 us -> 0.01 us  [swap(): return lax.ppermute(block, KA + GA, route)]
    all_to_all x1, blocking collectives: 29 us -> 25 us  [share(): lax.all_to_all(fields, around, split_axis=0, concat_axis=0, tiled=True)]
  transfers between devices with their start and end apart: 4 -> 6, of which waited for: 2 -> 1; matrix products, arithmetic and copies ran while one was open for 0% -> 1% of each run, Pallas kernels for 3% -> 3%
where the time goes in v9:
time: 65.8 us; the launch traced here: 65.4 us
  blocking collectives  25 us (38%)
  waiting for transfers between devices  15.6 us (24%)
  starting transfers between devices  14.4 us (22%)
  Pallas kernels  7.46 us (11%)
  local copies, waits for them, and re-layouts  2.51 us (4%)
    all_to_all x1, blocking collectives, share(): lax.all_to_all(fields, around, split_axis=0, concat_axis=0, tiled=True)  25 us
    all_to_all x1, waiting for transfers between devices, share(): lax.all_to_all(fields, around, split_axis=0, concat_axis=0, tiled=True)  15.6 us
    ppermute x5, starting transfers between devices, swap(): return lax.ppermute(block, KA + GA, route)  10.6 us
    pallas_call x2, Pallas kernels, make_fields(): pl.pallas_call(functools.partial(field_kernel, len(sources)), grid_spec=p...  4.34 us
    all_to_all x1, starting transfers between devices, share(): lax.all_to_all(fields, around, split_axis=0, concat_axis=0, tiled=True)  3.79 us
    pallas_call x1, Pallas kernels, make_pairs(): pl.pallas_call(functools.partial(pair_kernel, 1.0 / math.sqrt(2 * half_k)...  3.12 us
  transfers between devices with their start and end apart: 6, of which 1 were waited for; matrix products, arithmetic and copies ran while one was open for 1% of the time, Pallas kernels for 3%

profile of v9, /device:TPU:1, one launch (start us, length us, event | category | flops | bytes accessed | tf_op | source)
XLA Modules:
  0.0 65.4 jit_solution(650866203429131609)
XLA Ops:
  0.0 1.1 %dynamic-slice_bitcast_fusion = (bf16[512,256]{1,0:T(8,128)(2,1)S(1)}, bf16[512,256]{1,0:T(8,128)(2,1)S(1)}) fusion(bf16[2,512,256]{2,1,0:T(8,128)(2,1)} %param.5, s32[]{:T(128)S(6)} %select_n.40, s32[]{:T(128)S(6)} %select_n.39), kind=kLoop, calls=%fused_computation | loop fusion | bytes 1048584 | tf_op jit(solution)/shard_map/jit(dynamic_index_in_dim)/squeeze | solution.py:168
  1.1 2.1 %collective-permute-start = (bf16[512,256]{1,0:T(8,128)(2,1)S(1)}, bf16[512,256]{1,0:T(8,128)(2,1)S(1)}, u32[]{:S(2)}, u32[]{:S(2)}) collective-permute-start(bf16[512,256]{1,0:T(8,128)(2,1)S(1)} %get-tuple-element.22), channel_id=1, source_target_pairs={{0,1},{1,0},{2,3},{3,2},{4,5},{5,4},{6,7},{7,6},{8,9},{9,8},{10,11... | collective-permute-start | bytes 786440 | tf_op jit(solution)/shard_map/ppermute | solution.py:29
  3.2 5.2 %collective-permute-start.4 = (bf16[512,256]{1,0:T(8,128)(2,1)S(1)}, bf16[512,256]{1,0:T(8,128)(2,1)S(1)}, u32[]{:S(2)}, u32[]{:S(2)}) collective-permute-start(bf16[512,256]{1,0:T(8,128)(2,1)S(1)} %get-tuple-element.22), channel_id=1, source_target_pairs={{0,25},{1,24},{2,27},{3,26},{4,29},{5,28},{6,31},{7,30},{24,1},{25... | collective-permute-start | bytes 786440 | tf_op jit(solution)/shard_map/ppermute | solution.py:29
  8.4 2.0 %collective-permute-start.3 = (bf16[512,256]{1,0:T(8,128)(2,1)S(1)}, bf16[512,256]{1,0:T(8,128)(2,1)S(1)}, u32[]{:S(2)}, u32[]{:S(2)}) collective-permute-start(bf16[512,256]{1,0:T(8,128)(2,1)S(1)} %get-tuple-element.18.refs_0_), channel_id=1, source_target_pairs={{0,24},{1,25},{2,26},{3,27},{4,28},{5,29},{6,30},{7,31},{24,0},{25... | collective-permute-start | bytes 786440 | tf_op jit(solution)/shard_map/ppermute | solution.py:29
  10.4 0.0 collective-permute-done.refs_1_
  10.4 0.7 %collective-permute-start.1 = (bf16[512,256]{1,0:T(8,128)(2,1)S(1)}, bf16[512,256]{1,0:T(8,128)(2,1)S(1)}, u32[]{:S(2)}, u32[]{:S(2)}) collective-permute-start(bf16[512,256]{1,0:T(8,128)(2,1)S(1)} %get-tuple-element.18.refs_0_), channel_id=1, source_target_pairs={{8,16},{9,17},{10,18},{11,19},{12,20},{13,21},{14,22},{15,23},{16,... | collective-permute-start | bytes 786440 | tf_op jit(solution)/shard_map/ppermute | solution.py:29
  11.1 0.7 %collective-permute-start.2 = (bf16[512,256]{1,0:T(8,128)(2,1)S(1)}, bf16[512,256]{1,0:T(8,128)(2,1)S(1)}, u32[]{:S(2)}, u32[]{:S(2)}) collective-permute-start(bf16[512,256]{1,0:T(8,128)(2,1)S(1)} %collective-permute-done.refs_1_), channel_id=1, source_target_pairs={{8,16},{9,17},{10,18},{11,19},{12,20},{13,21},{14,22},{15,23},{16,... | collective-permute-start | bytes 786440 | tf_op jit(solution)/shard_map/ppermute | solution.py:29
  11.7 0.0 copy-start
  11.8 0.1 pad_add_fusion.2.place_ref
  11.8 0.6 copy-done
  12.4 1.8 %fields.2 = bf16[8,2,2,32,512]{4,3,2,1,0:T(8,128)(2,1)S(1)} custom-call(s32[3]{0:T(128)S(1)} %pad_add_fusion.2.place_ref, s32[1,512]{1,0:T(1,128)S(1)} %bitcast.11, bf16[512,256]{1,0:T(8,128)(2,1)S(1)} %get-tuple-element.18.refs_0_, bf16[512,256]{1,0:T(8,128)(2,1)S(1)} %collective-permute-done.refs_1_), custom_call_target="tpu_custom_call" | custom-call | tf_op jit(solution)/shard_map/fields/pallas_call | solution.py:88
  14.2 25.2 %conditional.1 = (bf16[16,2,32,512]{3,2,1,0:T(8,128)(2,1)S(1)}) conditional(s32[]{:T(128)} %convert_element_type.4, bf16[16,2,32,512]{3,2,1,0:T(8,128)(2,1)S(1)} %bitcast.13, bf16[16,2,32,512]{3,2,1,0:T(8,128)(2,1)S(1)} %bitcast.14), branch_computations={%region_0.1_spmd, %region_1.2_spmd} | conditional | bytes 4194312 | solution.py:187
  14.2 0.1 copy.6
  14.3 25.0 %all_to_all.9 = bf16[16,2,32,512]{3,2,1,0:T(8,128)(2,1)S(1)} all-to-all(bf16[16,2,32,512]{3,2,1,0:T(8,128)(2,1)S(1)} %copy.6), channel_id=1, replica_groups=mesh['half'=2,'quarter'=2,'inner'=4,'hi'=1,'lo'=2] {'quarter','inner','lo'}, dimensions={0} | all-to-all | bytes 2097152 | tf_op jit(solution)/shard_map/cond/branch_1_fun/all_to_all | solution.py:182
  39.4 0.0 collective-permute-done.3.refs_2_
  39.4 0.0 collective-permute-done.4.refs_3_
  39.4 0.0 collective-permute-done.1.refs_0_
  39.4 0.0 collective-permute-done.2.refs_1_
  39.4 2.6 %fields.3 = bf16[8,2,2,32,512]{4,3,2,1,0:T(8,128)(2,1)} custom-call(s32[3]{0:T(128)S(1)} %pad_add_fusion.2.place_ref, s32[1,512]{1,0:T(1,128)S(1)} %bitcast.12, bf16[512,256]{1,0:T(8,128)(2,1)S(1)} %collective-permute-done.1.refs_0_, bf16[512,256]{1,0:T(8,128)(2,1)S(1)} %collective-permute-done.2.refs_1_, ...), custom_call_target="tpu_custom_call" | custom-call | tf_op jit(solution)/shard_map/fields/pallas_call | solution.py:88
  42.0 3.8 %all-to-all-start.1 = ((bf16[16,2,32,512]{3,2,1,0:T(8,128)(2,1)}), bf16[16,2,32,512]{3,2,1,0:T(8,128)(2,1)S(1)}, u32[]{:S(2)}, u32[]{:S(2)}) async-start(bf16[16,2,32,512]{3,2,1,0:T(8,128)(2,1)} %bitcast.7), calls=%async_computation.1 | async-start | bytes 2097152 | tf_op jit(solution)/shard_map/all_to_all | solution.py:182
  45.7 0.0 copy-start.1
  45.8 0.7 %copy-done.1 = s32[2,32]{1,0:T(2,128)S(1)} copy-done((s32[2,32]{1,0:T(2,128)S(1)}, s32[2,32]{1,0:T(2,128)}, u32[]{:S(2)}) %copy-start.1) | copy-done | bytes 280
  46.4 0.1 pad_add_fusion
  46.5 0.1 compare_select_fusion
  46.6 0.1 fusion.3
  46.7 0.1 pad_add_fusion.1.table_ref
  46.7 15.6 %all-to-all-done.1.far_ref = bf16[16,2,32,512]{3,2,1,0:T(8,128)(2,1)S(1)} async-done(((bf16[16,2,32,512]{3,2,1,0:T(8,128)(2,1)}), bf16[16,2,32,512]{3,2,1,0:T(8,128)(2,1)S(1)}, u32[]{:S(2)}, u32[]{:S(2)}) %all-to-all-start.1) | async-done | bytes 1048608 | tf_op jit(solution)/shard_map/all_to_all | solution.py:182
  62.3 3.1 %pairs.1 = f32[32,2,2,512]{3,2,1,0:T(2,128)} custom-call(s32[2,32]{1,0:T(2,128)S(1)} %pad_add_fusion.1.table_ref, bf16[16,2,32,512]{3,2,1,0:T(8,128)(2,1)S(1)} %get-tuple-element.26.near_ref, bf16[16,2,32,512]{3,2,1,0:T(8,128)(2,1)S(1)} %all-to-all-done.1.far_ref), custom_call_target="tpu_custom_call" | custom-call | tf_op jit(solution)/shard_map/pairs/pallas_call | solution.py:144
Async XLA Ops:
  1.1 9.3 %collective-permute-start = (bf16[512,256]{1,0:T(8,128)(2,1)S(1)}, bf16[512,256]{1,0:T(8,128)(2,1)S(1)}, u32[]{:S(2)}, u32[]{:S(2)}) collective-permute-start(bf16[512,256]{1,0:T(8,128)(2,1)S(1)} %get-tuple-element.22), channel_id=1, source_target_pairs={{0,1},{1,0},{2,3},{3,2},{4,5},{5,4},{6,7},{7,6},{8,9},{9,8},{10,11... | collective-permute-start | bytes 786440 | tf_op jit(solution)/shard_map/ppermute | solution.py:29
  3.2 36.2 %collective-permute-start.4 = (bf16[512,256]{1,0:T(8,128)(2,1)S(1)}, bf16[512,256]{1,0:T(8,128)(2,1)S(1)}, u32[]{:S(2)}, u32[]{:S(2)}) collective-permute-start(bf16[512,256]{1,0:T(8,128)(2,1)S(1)} %get-tuple-element.22), channel_id=1, source_target_pairs={{0,25},{1,24},{2,27},{3,26},{4,29},{5,28},{6,31},{7,30},{24,1},{25... | collective-permute-start | bytes 786440 | tf_op jit(solution)/shard_map/ppermute | solution.py:29
  8.4 31.0 %collective-permute-start.3 = (bf16[512,256]{1,0:T(8,128)(2,1)S(1)}, bf16[512,256]{1,0:T(8,128)(2,1)S(1)}, u32[]{:S(2)}, u32[]{:S(2)}) collective-permute-start(bf16[512,256]{1,0:T(8,128)(2,1)S(1)} %get-tuple-element.18.refs_0_), channel_id=1, source_target_pairs={{0,24},{1,25},{2,26},{3,27},{4,28},{5,29},{6,30},{7,31},{24,0},{25... | collective-permute-start | bytes 786440 | tf_op jit(solution)/shard_map/ppermute | solution.py:29
  10.4 29.0 %collective-permute-start.1 = (bf16[512,256]{1,0:T(8,128)(2,1)S(1)}, bf16[512,256]{1,0:T(8,128)(2,1)S(1)}, u32[]{:S(2)}, u32[]{:S(2)}) collective-permute-start(bf16[512,256]{1,0:T(8,128)(2,1)S(1)} %get-tuple-element.18.refs_0_), channel_id=1, source_target_pairs={{8,16},{9,17},{10,18},{11,19},{12,20},{13,21},{14,22},{15,23},{16,... | collective-permute-start | bytes 786440 | tf_op jit(solution)/shard_map/ppermute | solution.py:29
  11.1 28.3 %collective-permute-start.2 = (bf16[512,256]{1,0:T(8,128)(2,1)S(1)}, bf16[512,256]{1,0:T(8,128)(2,1)S(1)}, u32[]{:S(2)}, u32[]{:S(2)}) collective-permute-start(bf16[512,256]{1,0:T(8,128)(2,1)S(1)} %collective-permute-done.refs_1_), channel_id=1, source_target_pairs={{8,16},{9,17},{10,18},{11,19},{12,20},{13,21},{14,22},{15,23},{16,... | collective-permute-start | bytes 786440 | tf_op jit(solution)/shard_map/ppermute | solution.py:29
  11.7 0.7 %copy-start = (s32[512]{0:T(512)S(1)}, s32[512]{0:T(512)}, u32[]{:S(2)}) copy-start(s32[512]{0:T(512)} %param.7) | copy-start | bytes 6148
  42.0 20.4 %all-to-all-start.1 = ((bf16[16,2,32,512]{3,2,1,0:T(8,128)(2,1)}), bf16[16,2,32,512]{3,2,1,0:T(8,128)(2,1)S(1)}, u32[]{:S(2)}, u32[]{:S(2)}) async-start(bf16[16,2,32,512]{3,2,1,0:T(8,128)(2,1)} %bitcast.7), calls=%async_computation.1 | async-start | bytes 2097152 | tf_op jit(solution)/shard_map/all_to_all | solution.py:182
  45.7 0.7 %copy-start.1 = (s32[2,32]{1,0:T(2,128)S(1)}, s32[2,32]{1,0:T(2,128)}, u32[]{:S(2)}) copy-start(s32[2,32]{1,0:T(2,128)} %param.6) | copy-start | bytes 772

commit v10 on v8

--- a/solution.py
+++ b/solution.py
@@ -149,7 +149,7 @@
     mine = lax.dynamic_index_in_dim(orbitals, lo, 0, keepdims=False)
     other = lax.dynamic_index_in_dim(orbitals, 1 - lo, 0, keepdims=False)
     near = [mine] + [swap(other if x & 1 else mine, 0, x) for x in range(1, slabs)]
-    far = [swap(other if x & 1 else mine, 1, x) for x in range(slabs)]
+    far = [swap(mine, 1, 0)]
 
     points = points.reshape(1, -1)
     place = jnp.stack([half, lax.axis_index("hi") * SPLIT + lo])
@@ -160,12 +160,14 @@
     def share(fields):
         return lax.all_to_all(fields, ("inner", "lo"), split_axis=0, concat_axis=0, tiled=True)
 
+    def cross(fields, slabs):
+        return share(fields), [swap(slab, 1, 0) for slab in slabs]
+
     near_fields = flat(make_fields(near, points, groups, place))
-    near_fields, points = lax.optimization_barrier((near_fields, points))
-    far_fields = flat(make_fields(far, points, groups, place))
-    near_fields = lax.cond(half >= 0, share, lambda fields: fields, near_fields)
-    near_fields, far_fields = lax.optimization_barrier((near_fields, far_fields))
-    far_fields = share(far_fields)
+    near_fields, crossed = lax.cond(
+        half >= 0, cross, lambda fields, slabs: (fields, slabs), near_fields, near[1:]
+    )
+    far_fields = share(flat(make_fields(far + crossed, points, groups, place)))
 
     turn = half * (total_k // 2)
     table = (jnp.roll(minus_table, -turn, axis=1) - turn) % total_k

time: 67.8 us -> 68.5 us (1.010)
  blocking collectives: 29 us -> 0 us
  waiting for transfers between devices: 20.5 us -> 36.6 us
  starting transfers between devices: 8.32 us -> 19.6 us
  Pallas kernels: 7.46 us -> 8.99 us
  local copies, waits for them, and re-layouts: 1.84 us -> 2.73 us
    all_to_all x1 -> x0, blocking collectives: 29 us -> none  [share(): lax.all_to_all(fields, ('inner', 'lo'), split_axis=0, concat_axis=0, tile...]
    ppermute x3, waiting for transfers between devices: 4.76 us -> 20.1 us  [swap(): return lax.ppermute(block, KA + GA, route)]
    all_to_all x1 -> x2, starting transfers between devices: 3.88 us -> 12.9 us  [share(): lax.all_to_all(fields, ('inner', 'lo'), split_axis=0, concat_axis=0, tile...]
    ppermute x3, starting transfers between devices: 4.45 us -> 6.75 us  [swap(): return lax.ppermute(block, KA + GA, route)]
    cond x1 -> x2, local copies, waits for them, and re-layouts: 0.1 us -> 0.99 us
    pallas_call x1, Pallas kernels: 3.12 us -> 3.99 us  [make_pairs(): pl.pallas_call(functools.partial(pair_kernel, 1.0 / math.sqrt(2 * half_k)...]
    all_to_all x1 -> x2, waiting for transfers between devices: 15.7 us -> 16.5 us  [share(): lax.all_to_all(fields, ('inner', 'lo'), split_axis=0, concat_axis=0, tile...]
  transfers between devices with their start and end apart: 4 -> 5, of which waited for: 2 -> 4; matrix products, arithmetic and copies ran while one was open for 0% -> 2% of each run, Pallas kernels for 3% -> 4%
where the time goes in v10:
time: 68.5 us; the launch traced here: 68.2 us
  waiting for transfers between devices  36.6 us (53%)
  starting transfers between devices  19.6 us (29%)
  Pallas kernels  8.99 us (13%)
  local copies, waits for them, and re-layouts  2.73 us (4%)
    ppermute x3, waiting for transfers between devices, swap(): return lax.ppermute(block, KA + GA, route)  20.1 us
    all_to_all x2, waiting for transfers between devices, share(): lax.all_to_all(fields, ('inner', 'lo'), split_axis=0, concat_axis=0, tile...  16.5 us
    all_to_all x2, starting transfers between devices, share(): lax.all_to_all(fields, ('inner', 'lo'), split_axis=0, concat_axis=0, tile...  12.9 us
    ppermute x3, starting transfers between devices, swap(): return lax.ppermute(block, KA + GA, route)  6.75 us
    pallas_call x2, Pallas kernels, make_fields(): pl.pallas_call(functools.partial(field_kernel, len(slabs)), grid_spec=plt...  4.99 us
    pallas_call x1, Pallas kernels, make_pairs(): pl.pallas_call(functools.partial(pair_kernel, 1.0 / math.sqrt(2 * half_k)...  3.99 us
  transfers between devices with their start and end apart: 5, of which 4 were waited for; matrix products, arithmetic and copies ran while one was open for 2% of the time, Pallas kernels for 4%

profile of v10, /device:TPU:1, one launch (start us, length us, event | category | flops | bytes accessed | tf_op | source)
XLA Modules:
  0.0 68.2 jit_solution(18305982873939977590)
XLA Ops:
  0.0 1.1 %dynamic-slice_bitcast_fusion = (bf16[512,256]{1,0:T(8,128)(2,1)S(1)}, bf16[512,256]{1,0:T(8,128)(2,1)S(1)}) fusion(bf16[2,512,256]{2,1,0:T(8,128)(2,1)} %param.5, s32[]{:T(128)S(6)} %select_n.30, s32[]{:T(128)S(6)} %select_n.29), kind=kLoop, calls=%fused_computation | loop fusion | bytes 1048584 | tf_op jit(solution)/shard_map/jit(dynamic_index_in_dim)/squeeze | solution.py:150
  1.1 2.1 %collective-permute-start.1 = (bf16[512,256]{1,0:T(8,128)(2,1)S(1)}, bf16[512,256]{1,0:T(8,128)(2,1)S(1)}, u32[]{:S(2)}, u32[]{:S(2)}) collective-permute-start(bf16[512,256]{1,0:T(8,128)(2,1)S(1)} %get-tuple-element.19), channel_id=1, source_target_pairs={{0,1},{1,0},{2,3},{3,2},{4,5},{5,4},{6,7},{7,6},{8,9},{9,8},{10,11... | collective-permute-start | bytes 786440 | tf_op jit(solution)/shard_map/ppermute | solution.py:25
  3.2 2.3 %collective-permute-start.2 = (bf16[512,256]{1,0:T(8,128)(2,1)S(1)}, bf16[512,256]{1,0:T(8,128)(2,1)S(1)}, u32[]{:S(2)}, u32[]{:S(2)}) collective-permute-start(bf16[512,256]{1,0:T(8,128)(2,1)S(1)} %get-tuple-element.20.refs_0_), channel_id=1, source_target_pairs={{0,16},{1,17},{2,18},{3,19},{4,20},{5,21},{6,22},{7,23},{8,24},{9,... | collective-permute-start | bytes 786440 | tf_op jit(solution)/shard_map/ppermute | solution.py:25
  5.5 0.0 copy-start
  5.5 0.1 pad_add_fusion.1.place_ref
  5.6 3.6 %collective-permute-done.1.refs_1_ = bf16[512,256]{1,0:T(8,128)(2,1)S(1)} collective-permute-done((bf16[512,256]{1,0:T(8,128)(2,1)S(1)}, bf16[512,256]{1,0:T(8,128)(2,1)S(1)}, u32[]{:S(2)}, u32[]{:S(2)}) %collective-permute-start.1) | collective-permute-done | bytes 262176 | tf_op jit(solution)/shard_map/ppermute | solution.py:25
  9.2 0.0 copy-done
  9.2 2.5 %fields.2 = bf16[8,2,2,32,512]{4,3,2,1,0:T(8,128)(2,1)} custom-call(s32[2]{0:T(128)S(1)} %pad_add_fusion.1.place_ref, s32[1,512]{1,0:T(1,128)S(1)} %bitcast.9, bf16[512,256]{1,0:T(8,128)(2,1)S(1)} %get-tuple-element.20.refs_0_, bf16[512,256]{1,0:T(8,128)(2,1)S(1)} %collective-permute-done.1.refs_1_), custom_call_target="tpu_custom_call" | custom-call | tf_op jit(solution)/shard_map/fields/pallas_call | solution.py:73
  11.7 26.8 %conditional.1 = ((bf16[16,2,32,512]{3,2,1,0:T(8,128)(2,1)}, bf16[512,256]{1,0:T(8,128)(2,1)S(1)})) conditional(s32[]{:T(128)} %convert_element_type.3, (bf16[16,2,32,512]{3,2,1,0:T(8,128)(2,1)}, bf16[512,256]{1,0:T(8,128)(2,1)S(1)}) %tuple.12, (bf16[16,2,32,512]{3,2,1,0:T(8,128)(2,1)}, bf16[512,256]{1,0:T(8,128)(2,1)S(1)}) %tuple.12), branch_computations={%region_0.1_spmd, %region_1.2_spmd} | conditional | bytes 6815840 | solution.py:167
  11.7 6.2 %all-to-all-start = ((bf16[16,2,32,512]{3,2,1,0:T(8,128)(2,1)}), bf16[16,2,32,512]{3,2,1,0:T(8,128)(2,1)S(1)}, u32[]{:S(2)}, u32[]{:S(2)}) async-start(bf16[16,2,32,512]{3,2,1,0:T(8,128)(2,1)} %get-tuple-element.13), calls=%async_computation | async-start | bytes 2097152 | tf_op jit(solution)/shard_map/cond/branch_1_fun/all_to_all | solution.py:161
  18.0 2.3 %collective-permute-start = (bf16[512,256]{1,0:T(8,128)(2,1)S(1)}, bf16[512,256]{1,0:T(8,128)(2,1)S(1)}, u32[]{:S(2)}, u32[]{:S(2)}) collective-permute-start(bf16[512,256]{1,0:T(8,128)(2,1)S(1)} %get-tuple-element.14), channel_id=1, source_target_pairs={{0,16},{1,17},{2,18},{3,19},{4,20},{5,21},{6,22},{7,23},{8,24},{9,... | collective-permute-start | bytes 786440 | tf_op jit(solution)/shard_map/cond/branch_1_fun/ppermute | solution.py:25
  20.3 16.4 %collective-permute-done = bf16[512,256]{1,0:T(8,128)(2,1)S(1)} collective-permute-done((bf16[512,256]{1,0:T(8,128)(2,1)S(1)}, bf16[512,256]{1,0:T(8,128)(2,1)S(1)}, u32[]{:S(2)}, u32[]{:S(2)}) %collective-permute-start) | collective-permute-done | bytes 262176 | tf_op jit(solution)/shard_map/cond/branch_1_fun/ppermute | solution.py:25
  36.7 0.8 %all-to-all-done = bf16[16,2,32,512]{3,2,1,0:T(8,128)(2,1)S(1)} async-done(((bf16[16,2,32,512]{3,2,1,0:T(8,128)(2,1)}), bf16[16,2,32,512]{3,2,1,0:T(8,128)(2,1)S(1)}, u32[]{:S(2)}, u32[]{:S(2)}) %all-to-all-start) | async-done | bytes 1048608 | tf_op jit(solution)/shard_map/cond/branch_1_fun/all_to_all | solution.py:161
  37.5 1.0 %copy.6 = bf16[16,2,32,512]{3,2,1,0:T(8,128)(2,1)} copy(bf16[16,2,32,512]{3,2,1,0:T(8,128)(2,1)S(1)} %all-to-all-done) | data formatting | bytes 2097152 | tf_op jit(solution)/shard_map/cond
  38.5 0.0 collective-permute-done.2.refs_0_
  38.5 2.5 %fields.3 = bf16[8,2,2,32,512]{4,3,2,1,0:T(8,128)(2,1)} custom-call(s32[2]{0:T(128)S(1)} %pad_add_fusion.1.place_ref, s32[1,512]{1,0:T(1,128)S(1)} %bitcast.10, bf16[512,256]{1,0:T(8,128)(2,1)S(1)} %collective-permute-done.2.refs_0_, bf16[512,256]{1,0:T(8,128)(2,1)S(1)} %get-tuple-element.18.refs_1_), custom_call_target="tpu_custom_call" | custom-call | tf_op jit(solution)/shard_map/fields/pallas_call | solution.py:73
  41.0 6.6 %all-to-all-start.1 = ((bf16[16,2,32,512]{3,2,1,0:T(8,128)(2,1)}), bf16[16,2,32,512]{3,2,1,0:T(8,128)(2,1)S(1)}, u32[]{:S(2)}, u32[]{:S(2)}) async-start(bf16[16,2,32,512]{3,2,1,0:T(8,128)(2,1)} %bitcast.6), calls=%async_computation.1 | async-start | bytes 2097152 | tf_op jit(solution)/shard_map/all_to_all | solution.py:161
  47.6 0.0 copy-start.1
  47.7 0.7 copy-done.1
  48.3 0.1 pad_add_fusion
  48.4 0.1 and_select_fusion.table_ref
  48.5 15.7 %all-to-all-done.1.far_ref = bf16[16,2,32,512]{3,2,1,0:T(8,128)(2,1)S(1)} async-done(((bf16[16,2,32,512]{3,2,1,0:T(8,128)(2,1)}), bf16[16,2,32,512]{3,2,1,0:T(8,128)(2,1)S(1)}, u32[]{:S(2)}, u32[]{:S(2)}) %all-to-all-start.1) | async-done | bytes 1048608 | tf_op jit(solution)/shard_map/all_to_all | solution.py:161
  64.2 4.0 %pairs.1 = f32[32,2,2,512]{3,2,1,0:T(2,128)} custom-call(s32[2,32]{1,0:T(2,128)S(1)} %and_select_fusion.table_ref, bf16[16,2,32,512]{3,2,1,0:T(8,128)(2,1)} %get-tuple-element.17.near_ref, bf16[16,2,32,512]{3,2,1,0:T(8,128)(2,1)S(1)} %all-to-all-done.1.far_ref), custom_call_target="tpu_custom_call" | custom-call | tf_op jit(solution)/shard_map/pairs/pallas_call | solution.py:126
  (1 shorter events, 0.0 us)
Async XLA Ops:
  1.1 8.2 %collective-permute-start.1 = (bf16[512,256]{1,0:T(8,128)(2,1)S(1)}, bf16[512,256]{1,0:T(8,128)(2,1)S(1)}, u32[]{:S(2)}, u32[]{:S(2)}) collective-permute-start(bf16[512,256]{1,0:T(8,128)(2,1)S(1)} %get-tuple-element.19), channel_id=1, source_target_pairs={{0,1},{1,0},{2,3},{3,2},{4,5},{5,4},{6,7},{7,6},{8,9},{9,8},{10,11... | collective-permute-start | bytes 786440 | tf_op jit(solution)/shard_map/ppermute | solution.py:25
  3.2 35.3 %collective-permute-start.2 = (bf16[512,256]{1,0:T(8,128)(2,1)S(1)}, bf16[512,256]{1,0:T(8,128)(2,1)S(1)}, u32[]{:S(2)}, u32[]{:S(2)}) collective-permute-start(bf16[512,256]{1,0:T(8,128)(2,1)S(1)} %get-tuple-element.20.refs_0_), channel_id=1, source_target_pairs={{0,16},{1,17},{2,18},{3,19},{4,20},{5,21},{6,22},{7,23},{8,24},{9,... | collective-permute-start | bytes 786440 | tf_op jit(solution)/shard_map/ppermute | solution.py:25
  5.5 3.7 %copy-start = (s32[512]{0:T(512)S(1)}, s32[512]{0:T(512)}, u32[]{:S(2)}) copy-start(s32[512]{0:T(512)} %param.7) | copy-start | bytes 6148
  11.7 25.8 %all-to-all-start = ((bf16[16,2,32,512]{3,2,1,0:T(8,128)(2,1)}), bf16[16,2,32,512]{3,2,1,0:T(8,128)(2,1)S(1)}, u32[]{:S(2)}, u32[]{:S(2)}) async-start(bf16[16,2,32,512]{3,2,1,0:T(8,128)(2,1)} %get-tuple-element.13), calls=%async_computation | async-start | bytes 2097152 | tf_op jit(solution)/shard_map/cond/branch_1_fun/all_to_all | solution.py:161
  18.0 18.7 %collective-permute-start = (bf16[512,256]{1,0:T(8,128)(2,1)S(1)}, bf16[512,256]{1,0:T(8,128)(2,1)S(1)}, u32[]{:S(2)}, u32[]{:S(2)}) collective-permute-start(bf16[512,256]{1,0:T(8,128)(2,1)S(1)} %get-tuple-element.14), channel_id=1, source_target_pairs={{0,16},{1,17},{2,18},{3,19},{4,20},{5,21},{6,22},{7,23},{8,24},{9,... | collective-permute-start | bytes 786440 | tf_op jit(solution)/shard_map/cond/branch_1_fun/ppermute | solution.py:25
  41.0 23.2 %all-to-all-start.1 = ((bf16[16,2,32,512]{3,2,1,0:T(8,128)(2,1)}), bf16[16,2,32,512]{3,2,1,0:T(8,128)(2,1)S(1)}, u32[]{:S(2)}, u32[]{:S(2)}) async-start(bf16[16,2,32,512]{3,2,1,0:T(8,128)(2,1)} %bitcast.6), calls=%async_computation.1 | async-start | bytes 2097152 | tf_op jit(solution)/shard_map/all_to_all | solution.py:161
  47.6 0.7 copy-start.1

commit v11 on v8

v11 whole, which is shorter than its diff:
```python
import functools
import math

import jax
import jax.numpy as jnp
from jax import lax
from jax.experimental import pallas as pl
from jax.experimental.pallas import tpu as pltpu
from jax.sharding import Mesh
from jax.sharding import PartitionSpec as P

VMEM_LIMIT = 40 * 1024 * 1024
SPLIT = 2
KA, GA = ("half", "inner"), ("hi", "lo")


def swap(block, cut, other):
    half, inner, hi, lo = (lax.axis_size(name) for name in KA + GA)
    slabs = hi * lo
    route = []
    for place in range(half * inner * slabs):
        kplace, slab = divmod(place, slabs)
        kplace = (kplace + cut * inner) % (half * inner)
        route.append((place, kplace * slabs + (slab ^ other)))
    return lax.ppermute(block, KA + GA, route)


def field_kernel(plan, place_ref, points_ref, *refs):
    *slab_refs, out_ref, picked_ref = refs
    slabs = len(slab_refs) // len(plan)
    slab_size, channels = slab_refs[0].shape
    npoints = points_ref.shape[1] // 2
    middle = channels // 2
    groups, _, _, length, _ = out_ref.shape
    step = pl.program_id(0)

    @pl.when(step == 0)
    def _():
        first = pl.multiple_of(place_ref[0] * npoints, npoints)
        wanted = points_ref[:, pl.ds(first, npoints)]
        spot = lax.broadcasted_iota(jnp.int32, (slab_size, npoints), 0)
        for source in range(len(plan)):
            picked = jnp.zeros((npoints, channels), jnp.float32)
            for number in range(slabs):
                chosen = spot == wanted - (place_ref[1] ^ number) * slab_size
                picked += lax.dot_general(
                    chosen.astype(jnp.float32).astype(jnp.bfloat16),
                    slab_refs[source * slabs + number][...],
                    (((0,), (0,)), ((), ())),
                    preferred_element_type=jnp.float32,
                )
            rotated = jnp.concatenate([-picked[:, middle:], picked[:, :middle]], axis=1)
            picked_ref[source, 0] = picked.astype(jnp.bfloat16)
            picked_ref[source, 1] = rotated.astype(jnp.bfloat16)

    for number in range(SPLIT):

        @pl.when(step == number)
        def _(number=number):
            wanted = [(source, part) for source, parts in enumerate(plan) for part in parts]
            for place, (source, part) in enumerate(wanted):
                product = lax.dot_general(
                    picked_ref[source, part],
                    slab_refs[source * slabs + number][...],
                    (((1,), (1,)), ((), ())),
                    preferred_element_type=jnp.float32,
                )
                pieces = product.reshape(groups, length, slab_size)
                out_ref[:, 0, place] = pieces.astype(jnp.bfloat16)


def make_fields(sources, plan, points, groups, place):
    slab_size, channels = sources[0][0].shape
    slabs = [slab for source in sources for slab in source]
    npoints = points.shape[1] // 2
    length = npoints // groups
    parts = sum(len(parts) for parts in plan)
    out = pl.pallas_call(
        functools.partial(field_kernel, plan),
        grid_spec=pltpu.PrefetchScalarGridSpec(
            num_scalar_prefetch=1,
            grid=(SPLIT,),
            in_specs=[pl.BlockSpec(points.shape, lambda step, place: (0, 0))]
            + [pl.BlockSpec((slab_size, channels), lambda step, place: (0, 0)) for _ in slabs],
            out_specs=pl.BlockSpec(
                (groups, 1, parts, length, slab_size),
                lambda step, place: (0, place[1] % SPLIT ^ step, 0, 0, 0),
            ),
            scratch_shapes=[pltpu.VMEM((len(sources), 2, npoints, channels), jnp.bfloat16)],
        ),
        out_shape=jax.ShapeDtypeStruct((groups, SPLIT, parts, length, slab_size), jnp.bfloat16),
        compiler_params=pltpu.CompilerParams(vmem_limit_bytes=VMEM_LIMIT),
        name="fields",
    )(place, points, *slabs)
    return out.reshape((groups * SPLIT,) + out.shape[2:])


def pair_kernel(scale, table_ref, first_ref, second_ref, out_ref, held_ref):
    total_k, _, length, width = held_ref.shape
    transfers = table_ref.shape[0]
    near, far = pl.ds(0, total_k // 2), pl.ds(total_k // 2, total_k // 2)
    held_ref[near, 0] = first_ref[:, 0].astype(jnp.float32)
    held_ref[near, 1] = second_ref[:, 0].astype(jnp.float32)
    held_ref[far] = second_ref[:, 1:].astype(jnp.float32)

    def load(k, part, start, count):
        return held_ref[k, part, pl.ds(start, count), :]

    count = min(16, length)
    for start in range(0, length, count):

        def step(k, sums):
            real, imag = load(k, 0, start, count), load(k, 1, start, count)
            after = []
            for transfer in range(transfers):
                other = table_ref[transfer, k]
                other_real = load(other, 0, start, count)
                other_imag = load(other, 1, start, count)
                after.append(sums[2 * transfer] + (real * other_real + imag * other_imag))
                after.append(sums[2 * transfer + 1] + (imag * other_real - real * other_imag))
            return tuple(after)

        zero = jnp.zeros((count, width), jnp.float32)
        sums = lax.fori_loop(0, total_k, step, (zero,) * (2 * transfers), unroll=4)
        for place, value in enumerate(sums):
            out_ref[pl.ds(start, count), place // 2, place % 2, :] = value * scale


def make_pairs(first, second, table):
    half_k, _, length, slab_size = first.shape
    transfers = table.shape[0]
    width = 256
    fields = [
        pl.BlockSpec((half_k, array.shape[1], length, width), lambda r, table: (0, 0, 0, r))
        for array in (first, second)
    ]
    return pl.pallas_call(
        functools.partial(pair_kernel, 1.0 / math.sqrt(2 * half_k)),
        grid_spec=pltpu.PrefetchScalarGridSpec(
            num_scalar_prefetch=1,
            grid=(slab_size // width,),
            in_specs=fields,
            out_specs=pl.BlockSpec((length, transfers, 2, width), lambda r, table: (0, 0, 0, r)),
            scratch_shapes=[pltpu.VMEM((2 * half_k, 2, length, width), jnp.float32)],
        ),
        out_shape=jax.ShapeDtypeStruct((length, transfers, 2, slab_size), jnp.float32),
        compiler_params=pltpu.CompilerParams(vmem_limit_bytes=VMEM_LIMIT),
        name="pairs",
    )(table, first, second)


def on_device(orbitals, minus_table, points):
    kdevice, slab_size, channels = orbitals.shape
    half = lax.axis_index("half")
    groups = lax.axis_size("inner")
    total_k = 2 * groups * kdevice

    lo = lax.axis_index("lo")
    slabs = lax.axis_size("hi") * SPLIT
    mine = lax.dynamic_index_in_dim(orbitals, lo, 0, keepdims=False)
    other = lax.dynamic_index_in_dim(orbitals, 1 - lo, 0, keepdims=False)
    near = [mine] + [swap(other if x & 1 else mine, 0, x) for x in range(1, slabs)]
    far = [swap(other if x & 1 else mine, 1, x) for x in range(slabs)]

    points = points.reshape(1, -1)
    place = jnp.stack([half, lax.axis_index("hi") * SPLIT + lo])

    def share(fields):
        return lax.all_to_all(fields, ("inner", "lo"), split_axis=0, concat_axis=0, tiled=True)

    first = make_fields([near], ((0,),), points, groups, place)
    first, points = lax.optimization_barrier((first, points))
    second = make_fields([near, far], ((1,), (0, 1)), points, groups, place)
    first = lax.cond(half >= 0, share, lambda fields: fields, first)
    first, second = lax.optimization_barrier((first, second))
    second = share(second)

    turn = half * (total_k // 2)
    table = (jnp.roll(minus_table, -turn, axis=1) - turn) % total_k
    return make_pairs(first, second, table)


def solution(mesh):
    kplaces, slabs = mesh.shape["ka"], mesh.shape["ga"]
    devices = mesh.devices.reshape(2, kplaces // 2, slabs // SPLIT, SPLIT)
    finer = Mesh(devices, KA + GA)
    return jax.shard_map(
        on_device,
        mesh=finer,
        in_specs=(P(KA, GA, None), P(), P()),
        out_specs=P(KA, None, None, GA),
        check_vma=False,
    )
```

time: 67.8 us -> 69.8 us (1.029)
  waiting for transfers between devices: 20.5 us -> 26.7 us
  blocking collectives: 29 us -> 23 us
  starting transfers between devices: 8.32 us -> 9.76 us
    all_to_all x1, waiting for transfers between devices: 15.7 us -> 23.1 us  [share(): lax.all_to_all(fields, ('inner', 'lo'), split_axis=0, concat_axis=0, tile...]
    all_to_all x1, blocking collectives: 29 us -> 23 us  [share(): lax.all_to_all(fields, ('inner', 'lo'), split_axis=0, concat_axis=0, tile...]
    all_to_all x1, starting transfers between devices: 3.88 us -> 5.31 us  [share(): lax.all_to_all(fields, ('inner', 'lo'), split_axis=0, concat_axis=0, tile...]
    ppermute x3, waiting for transfers between devices: 4.76 us -> 3.65 us  [swap(): return lax.ppermute(block, KA + GA, route)]
  transfers between devices with their start and end apart: 4 -> 4, of which waited for: 2 -> 2; matrix products, arithmetic and copies ran while one was open for 0% -> 0% of each run, Pallas kernels for 3% -> 2%
where the time goes in v11:
time: 69.8 us; the launch traced here: 68.9 us
  waiting for transfers between devices  26.7 us (38%)
  blocking collectives  23 us (33%)
  starting transfers between devices  9.76 us (14%)
  Pallas kernels  7.25 us (10%)
  local copies, waits for them, and re-layouts  1.79 us (3%)
    all_to_all x1, waiting for transfers between devices, share(): lax.all_to_all(fields, ('inner', 'lo'), split_axis=0, concat_axis=0, tile...  23.1 us
    all_to_all x1, blocking collectives, share(): lax.all_to_all(fields, ('inner', 'lo'), split_axis=0, concat_axis=0, tile...  23 us
    all_to_all x1, starting transfers between devices, share(): lax.all_to_all(fields, ('inner', 'lo'), split_axis=0, concat_axis=0, tile...  5.31 us
    ppermute x3, starting transfers between devices, swap(): return lax.ppermute(block, KA + GA, route)  4.45 us
    pallas_call x2, Pallas kernels, make_fields(): pl.pallas_call(functools.partial(field_kernel, plan), grid_spec=pltpu.Pre...  4.14 us
    ppermute x3, waiting for transfers between devices, swap(): return lax.ppermute(block, KA + GA, route)  3.65 us
    pallas_call x1, Pallas kernels, make_pairs(): pl.pallas_call(functools.partial(pair_kernel, 1.0 / math.sqrt(2 * half_k)...  3.12 us
  transfers between devices with their start and end apart: 4, of which 2 were waited for; matrix products, arithmetic and copies ran while one was open for 0% of the time, Pallas kernels for 2%

profile of v11, /device:TPU:1, one launch (start us, length us, event | category | flops | bytes accessed | tf_op | source)
XLA Modules:
  0.0 68.9 jit_solution(3381773993440717118)
XLA Ops:
  0.0 1.1 %dynamic-slice_bitcast_fusion = (bf16[512,256]{1,0:T(8,128)(2,1)S(1)}, bf16[512,256]{1,0:T(8,128)(2,1)S(1)}) fusion(bf16[2,512,256]{2,1,0:T(8,128)(2,1)} %param.5, s32[]{:T(128)S(6)} %select_n.30, s32[]{:T(128)S(6)} %select_n.29), kind=kLoop, calls=%fused_computation | loop fusion | bytes 1048584 | tf_op jit(solution)/shard_map/jit(dynamic_index_in_dim)/squeeze | solution.py:161
  1.1 2.1 %collective-permute-start = (bf16[512,256]{1,0:T(8,128)(2,1)S(1)}, bf16[512,256]{1,0:T(8,128)(2,1)S(1)}, u32[]{:S(2)}, u32[]{:S(2)}) collective-permute-start(bf16[512,256]{1,0:T(8,128)(2,1)S(1)} %get-tuple-element.18), channel_id=1, source_target_pairs={{0,1},{1,0},{2,3},{3,2},{4,5},{5,4},{6,7},{7,6},{8,9},{9,8},{10,11... | collective-permute-start | bytes 786440 | tf_op jit(solution)/shard_map/ppermute | solution.py:25
  3.2 2.3 %collective-permute-start.1 = (bf16[512,256]{1,0:T(8,128)(2,1)S(1)}, bf16[512,256]{1,0:T(8,128)(2,1)S(1)}, u32[]{:S(2)}, u32[]{:S(2)}) collective-permute-start(bf16[512,256]{1,0:T(8,128)(2,1)S(1)} %get-tuple-element.19.refs_0_), channel_id=1, source_target_pairs={{0,16},{1,17},{2,18},{3,19},{4,20},{5,21},{6,22},{7,23},{8,24},{9,... | collective-permute-start | bytes 786440 | tf_op jit(solution)/shard_map/ppermute | solution.py:25
  5.5 0.0 collective-permute-start.2
  5.5 0.1 pad_add_fusion.1.place_ref
  5.6 3.6 %collective-permute-done.refs_1_ = bf16[512,256]{1,0:T(8,128)(2,1)S(1)} collective-permute-done((bf16[512,256]{1,0:T(8,128)(2,1)S(1)}, bf16[512,256]{1,0:T(8,128)(2,1)S(1)}, u32[]{:S(2)}, u32[]{:S(2)}) %collective-permute-start) | collective-permute-done | bytes 262176 | tf_op jit(solution)/shard_map/ppermute | solution.py:25
  9.2 0.0 copy-start
  9.2 0.7 copy-done
  9.9 0.0 copy-start.1
  9.9 1.5 %fields.2 = bf16[8,2,1,32,512]{4,3,2,1,0:T(8,128)(2,1)S(1)} custom-call(s32[2]{0:T(128)S(1)} %pad_add_fusion.1.place_ref, s32[1,512]{1,0:T(1,128)S(1)} %bitcast.11, bf16[512,256]{1,0:T(8,128)(2,1)S(1)} %get-tuple-element.19.refs_0_, bf16[512,256]{1,0:T(8,128)(2,1)S(1)} %collective-permute-done.refs_1_), custom_call_target="tpu_custom_call" | custom-call | tf_op jit(solution)/shard_map/fields/pallas_call | solution.py:78
  11.4 23.1 %conditional.1 = (bf16[16,1,32,512]{3,2,1,0:T(8,128)(2,1)S(1)}) conditional(s32[]{:T(128)} %convert_element_type.3, bf16[16,1,32,512]{3,2,0,1:T(8,128)(2,1)S(1)} %bitcast.13, bf16[16,1,32,512]{3,2,0,1:T(8,128)(2,1)S(1)} %bitcast.14), branch_computations={%region_0.1_spmd, %region_1.2_spmd} | conditional | bytes 2097160 | solution.py:174
  11.5 23.0 %all_to_all.9 = bf16[16,1,32,512]{3,2,1,0:T(8,128)(2,1)S(1)} all-to-all(bf16[16,1,32,512]{3,2,1,0:T(8,128)(2,1)S(1)} %copy.9), channel_id=1, replica_groups=mesh['half'=2,'inner'=8,'hi'=1,'lo'=2] {'inner','lo'}, dimensions={0} | all-to-all | bytes 1048576 | tf_op jit(solution)/shard_map/cond/branch_1_fun/all_to_all | solution.py:169
  34.5 0.0 collective-permute-done.1.refs_2_
  34.5 0.0 collective-permute-done.2.refs_3_
  34.5 0.0 copy-done.1
  34.5 2.7 %fields.3 = bf16[8,2,3,32,512]{4,3,2,1,0:T(8,128)(2,1)} custom-call(s32[2]{0:T(128)S(1)} %pad_add_fusion.1.place_ref, s32[1,512]{1,0:T(1,128)S(1)} %bitcast.12, bf16[512,256]{1,0:T(8,128)(2,1)S(1)} %get-tuple-element.19.refs_0_, bf16[512,256]{1,0:T(8,128)(2,1)S(1)} %collective-permute-done.refs_1_, bf16[512,256]{1,0:T(8,128)(2,1)S(1)} %collective-permute-done.1.refs_2_, ...), custom_call_target="tpu_custom_call" | custom-call | tf_op jit(solution)/shard_map/fields/pallas_call | solution.py:78
  37.2 0.0 copy-start.2
  37.2 5.3 %all-to-all-start.1 = ((bf16[16,3,32,512]{3,2,1,0:T(8,128)(2,1)}), bf16[16,3,32,512]{3,2,1,0:T(8,128)(2,1)S(1)}, u32[]{:S(2)}, u32[]{:S(2)}) async-start(bf16[16,3,32,512]{3,2,1,0:T(8,128)(2,1)} %bitcast.8), calls=%async_computation.1 | async-start | bytes 3145728 | tf_op jit(solution)/shard_map/all_to_all | solution.py:169
  42.5 0.0 copy-done.2
  42.5 0.1 pad_add_fusion
  42.6 0.1 and_select_fusion.table_ref
  42.6 23.1 %all-to-all-done.1.second_ref = bf16[16,3,32,512]{3,2,1,0:T(8,128)(2,1)S(1)} async-done(((bf16[16,3,32,512]{3,2,1,0:T(8,128)(2,1)}), bf16[16,3,32,512]{3,2,1,0:T(8,128)(2,1)S(1)}, u32[]{:S(2)}, u32[]{:S(2)}) %all-to-all-start.1) | async-done | bytes 1572896 | tf_op jit(solution)/shard_map/all_to_all | solution.py:169
  65.7 3.1 %pairs.1 = f32[32,2,2,512]{3,2,1,0:T(2,128)} custom-call(s32[2,32]{1,0:T(2,128)S(1)} %and_select_fusion.table_ref, bf16[16,1,32,512]{3,2,1,0:T(8,128)(2,1)S(1)} %get-tuple-element.20.first_ref, bf16[16,3,32,512]{3,2,1,0:T(8,128)(2,1)S(1)} %all-to-all-done.1.second_ref), custom_call_target="tpu_custom_call" | custom-call | tf_op jit(solution)/shard_map/pairs/pallas_call | solution.py:137
  (1 shorter events, 0.0 us)
Async XLA Ops:
  1.1 8.2 %collective-permute-start = (bf16[512,256]{1,0:T(8,128)(2,1)S(1)}, bf16[512,256]{1,0:T(8,128)(2,1)S(1)}, u32[]{:S(2)}, u32[]{:S(2)}) collective-permute-start(bf16[512,256]{1,0:T(8,128)(2,1)S(1)} %get-tuple-element.18), channel_id=1, source_target_pairs={{0,1},{1,0},{2,3},{3,2},{4,5},{5,4},{6,7},{7,6},{8,9},{9,8},{10,11... | collective-permute-start | bytes 786440 | tf_op jit(solution)/shard_map/ppermute | solution.py:25
  3.2 31.3 %collective-permute-start.1 = (bf16[512,256]{1,0:T(8,128)(2,1)S(1)}, bf16[512,256]{1,0:T(8,128)(2,1)S(1)}, u32[]{:S(2)}, u32[]{:S(2)}) collective-permute-start(bf16[512,256]{1,0:T(8,128)(2,1)S(1)} %get-tuple-element.19.refs_0_), channel_id=1, source_target_pairs={{0,16},{1,17},{2,18},{3,19},{4,20},{5,21},{6,22},{7,23},{8,24},{9,... | collective-permute-start | bytes 786440 | tf_op jit(solution)/shard_map/ppermute | solution.py:25
  5.5 29.0 %collective-permute-start.2 = (bf16[512,256]{1,0:T(8,128)(2,1)S(1)}, bf16[512,256]{1,0:T(8,128)(2,1)S(1)}, u32[]{:S(2)}, u32[]{:S(2)}) collective-permute-start(bf16[512,256]{1,0:T(8,128)(2,1)S(1)} %get-tuple-element.18), channel_id=1, source_target_pairs={{0,17},{1,16},{2,19},{3,18},{4,21},{5,20},{6,23},{7,22},{8,25},{9,... | collective-permute-start | bytes 786440 | tf_op jit(solution)/shard_map/ppermute | solution.py:25
  9.2 0.7 copy-start
  9.9 24.6 %copy-start.1 = (s32[512]{0:T(512)S(1)}, s32[512]{0:T(512)}, u32[]{:S(2)}) copy-start(s32[512]{0:T(512)} %param.7) | copy-start | bytes 6148
  37.2 5.3 %copy-start.2 = (s32[2,32]{1,0:T(2,128)S(1)}, s32[2,32]{1,0:T(2,128)}, u32[]{:S(2)}) copy-start(s32[2,32]{1,0:T(2,128)} %param.6) | copy-start | bytes 772
  37.2 28.6 %all-to-all-start.1 = ((bf16[16,3,32,512]{3,2,1,0:T(8,128)(2,1)}), bf16[16,3,32,512]{3,2,1,0:T(8,128)(2,1)S(1)}, u32[]{:S(2)}, u32[]{:S(2)}) async-start(bf16[16,3,32,512]{3,2,1,0:T(8,128)(2,1)} %bitcast.8), calls=%async_computation.1 | async-start | bytes 3145728 | tf_op jit(solution)/shard_map/all_to_all | solution.py:169

commit v12 on v9

--- a/solution.py
+++ b/solution.py
@@ -167,9 +167,7 @@
     mine = lax.dynamic_index_in_dim(orbitals, lo, 0, keepdims=False)
     other = lax.dynamic_index_in_dim(orbitals, 1 - lo, 0, keepdims=False)
     near = [mine] + [swap(other if x & 1 else mine, x) for x in range(1, slabs)]
-    outer = [swap(other if x & 1 else mine, x, OUTER) for x in range(slabs)]
-    later = lax.optimization_barrier(near)
-    middle = [swap(slab, 0, MIDDLE) for slab in later]
+    outer = [swap(slab, 0, OUTER) for slab in near]
 
     points = points.reshape(1, -1)
     place = jnp.stack([half, hi * SPLIT + lo, (half == quarter).astype(jnp.int32)])
@@ -181,12 +179,14 @@
         around = ("quarter", "inner", "lo")
         return lax.all_to_all(fields, around, split_axis=0, concat_axis=0, tiled=True)
 
+    def cross(fields, slabs):
+        return share(fields), [swap(slab, 0, MIDDLE) for slab in slabs]
+
     near_fields = flat(make_fields([near], points, groups, place))
-    near_fields, points = lax.optimization_barrier((near_fields, points))
-    far_fields = flat(make_fields([middle, outer], points, groups, place))
-    near_fields = lax.cond(half >= 0, share, lambda fields: fields, near_fields)
-    near_fields, far_fields = lax.optimization_barrier((near_fields, far_fields))
-    far_fields = share(far_fields)
+    near_fields, middle = lax.cond(
+        half >= 0, cross, lambda fields, slabs: (fields, slabs), near_fields, near
+    )
+    far_fields = share(flat(make_fields([middle, outer], points, groups, place)))
 
     def mirrored(kpoints):
         return total_k // 2 + (kpoints + total_k // 4) % (total_k // 2)

time: 65.8 us -> 70.8 us (1.076)
  blocking collectives: 25 us -> 0 us
  waiting for transfers between devices: 15.6 us -> 30.3 us
  starting transfers between devices: 14.4 us -> 24.4 us
  Pallas kernels: 7.46 us -> 11.2 us
  local copies, waits for them, and re-layouts: 2.51 us -> 4.09 us
    all_to_all x1 -> x0, blocking collectives: 25 us -> none  [share(): lax.all_to_all(fields, around, split_axis=0, concat_axis=0, tiled=True)]
    all_to_all x1 -> x2, waiting for transfers between devices: 15.6 us -> 29.4 us  [share(): lax.all_to_all(fields, around, split_axis=0, concat_axis=0, tiled=True)]
    all_to_all x1 -> x2, starting transfers between devices: 3.79 us -> 9.23 us  [share(): lax.all_to_all(fields, around, split_axis=0, concat_axis=0, tiled=True)]
    ppermute x5, starting transfers between devices: 10.6 us -> 15.1 us  [swap(): return lax.ppermute(block, KA + GA, route)]
    pallas_call x2, Pallas kernels: 4.34 us -> 7.2 us  [make_fields(): pl.pallas_call(functools.partial(field_kernel, len(sources)), grid_spec=p...]
    ppermute x5, waiting for transfers between devices: 0.01 us -> 0.92 us  [swap(): return lax.ppermute(block, KA + GA, route)]
    cond x1, local copies, waits for them, and re-layouts: 0.1 us -> 0.98 us
    pallas_call x1, Pallas kernels: 3.12 us -> 3.99 us  [make_pairs(): pl.pallas_call(functools.partial(pair_kernel, 1.0 / math.sqrt(2 * half_k)...]
  transfers between devices with their start and end apart: 6 -> 7, of which waited for: 1 -> 3; matrix products, arithmetic and copies ran while one was open for 1% -> 2% of each run, Pallas kernels for 3% -> 5%
where the time goes in v12:
time: 70.8 us; the launch traced here: 70.3 us
  waiting for transfers between devices  30.3 us (43%)
  starting transfers between devices  24.4 us (34%)
  Pallas kernels  11.2 us (16%)
  local copies, waits for them, and re-layouts  4.09 us (6%)
    all_to_all x2, waiting for transfers between devices, share(): lax.all_to_all(fields, around, split_axis=0, concat_axis=0, tiled=True)  29.4 us
    ppermute x5, starting transfers between devices, swap(): return lax.ppermute(block, KA + GA, route)  15.1 us
    all_to_all x2, starting transfers between devices, share(): lax.all_to_all(fields, around, split_axis=0, concat_axis=0, tiled=True)  9.23 us
    pallas_call x2, Pallas kernels, make_fields(): pl.pallas_call(functools.partial(field_kernel, len(sources)), grid_spec=p...  7.2 us
    pallas_call x1, Pallas kernels, make_pairs(): pl.pallas_call(functools.partial(pair_kernel, 1.0 / math.sqrt(2 * half_k)...  3.99 us
    squeeze x1, local copies, waits for them, and re-layouts, on_device(): other = lax.dynamic_index_in_dim(orbitals, 1 - lo, 0, keepdims=False)  1.76 us
  transfers between devices with their start and end apart: 7, of which 3 were waited for; matrix products, arithmetic and copies ran while one was open for 2% of the time, Pallas kernels for 5%

profile of v12, /device:TPU:1, one launch (start us, length us, event | category | flops | bytes accessed | tf_op | source)
XLA Modules:
  0.0 70.3 jit_solution(7358214343721322096)
XLA Ops:
  0.0 1.8 %dynamic-slice_bitcast_fusion = (bf16[512,256]{1,0:T(8,128)(2,1)S(1)}, bf16[512,256]{1,0:T(8,128)(2,1)}) fusion(bf16[2,512,256]{2,1,0:T(8,128)(2,1)} %param.5, s32[]{:T(128)S(6)} %select_n.40, s32[]{:T(128)S(6)} %select_n.39), kind=kLoop, calls=%fused_computation | loop fusion | bytes 1048584 | tf_op jit(solution)/shard_map/jit(dynamic_index_in_dim)/squeeze | solution.py:168
  1.8 2.1 %collective-permute-start.2 = (bf16[512,256]{1,0:T(8,128)(2,1)S(1)}, bf16[512,256]{1,0:T(8,128)(2,1)}, u32[]{:S(2)}, u32[]{:S(2)}) collective-permute-start(bf16[512,256]{1,0:T(8,128)(2,1)S(1)} %get-tuple-element.26), channel_id=1, source_target_pairs={{0,1},{1,0},{2,3},{3,2},{4,5},{5,4},{6,7},{7,6},{8,9},{9,8},{10,11... | collective-permute-start | bytes 786440 | tf_op jit(solution)/shard_map/ppermute | solution.py:29
  3.8 5.2 %collective-permute-start.3 = (bf16[512,256]{1,0:T(8,128)(2,1)}, bf16[512,256]{1,0:T(8,128)(2,1)S(1)}, u32[]{:S(2)}, u32[]{:S(2)}) collective-permute-start(bf16[512,256]{1,0:T(8,128)(2,1)} %get-tuple-element.27.refs_0_), channel_id=1, source_target_pairs={{0,24},{1,25},{2,26},{3,27},{4,28},{5,29},{6,30},{7,31},{24,0},{25... | collective-permute-start | bytes 786440 | tf_op jit(solution)/shard_map/ppermute | solution.py:29
  9.1 0.9 %collective-permute-done.2.refs_1_ = bf16[512,256]{1,0:T(8,128)(2,1)} collective-permute-done((bf16[512,256]{1,0:T(8,128)(2,1)S(1)}, bf16[512,256]{1,0:T(8,128)(2,1)}, u32[]{:S(2)}, u32[]{:S(2)}) %collective-permute-start.2) | collective-permute-done | bytes 262176 | tf_op jit(solution)/shard_map/ppermute | solution.py:29
  10.0 5.1 %collective-permute-start.4 = (bf16[512,256]{1,0:T(8,128)(2,1)}, bf16[512,256]{1,0:T(8,128)(2,1)S(1)}, u32[]{:S(2)}, u32[]{:S(2)}) collective-permute-start(bf16[512,256]{1,0:T(8,128)(2,1)} %collective-permute-done.2.refs_1_), channel_id=1, source_target_pairs={{0,24},{1,25},{2,26},{3,27},{4,28},{5,29},{6,30},{7,31},{24,0},{25... | collective-permute-start | bytes 786440 | tf_op jit(solution)/shard_map/ppermute | solution.py:29
  15.1 0.0 copy-start
  15.1 0.1 pad_add_fusion.2.place_ref
  15.2 0.6 copy-done
  15.8 3.6 %fields.2 = bf16[8,2,2,32,512]{4,3,2,1,0:T(8,128)(2,1)} custom-call(s32[3]{0:T(128)S(1)} %pad_add_fusion.2.place_ref, s32[1,512]{1,0:T(1,128)S(1)} %bitcast.11, bf16[512,256]{1,0:T(8,128)(2,1)} %get-tuple-element.27.refs_0_, bf16[512,256]{1,0:T(8,128)(2,1)} %collective-permute-done.2.refs_1_), custom_call_target="tpu_custom_call" | custom-call | tf_op jit(solution)/shard_map/fields/pallas_call | solution.py:88
  19.4 23.1 %conditional.1 = (bf16[16,2,32,512]{3,2,1,0:T(8,128)(2,1)}, bf16[512,256]{1,0:T(8,128)(2,1)}, bf16[512,256]{1,0:T(8,128)(2,1)}) conditional(s32[]{:T(128)} %convert_element_type.4, (bf16[16,2,32,512]{3,2,1,0:T(8,128)(2,1)}, bf16[512,256]{1,0:T(8,128)(2,1)}, bf16[512,256]{1,0:T(8,128)(2,1)}) %tuple.12, (bf16[16,2,32,512]{3,2,1,0:T(8,128)(2,1)}, ...), branch_computations={%region_0.1_spmd, %region_1.2_spmd} | conditional | bytes 7340168 | solution.py:186
  19.4 5.5 %all-to-all-start = ((bf16[16,2,32,512]{3,2,1,0:T(8,128)(2,1)}), bf16[16,2,32,512]{3,2,1,0:T(8,128)(2,1)S(1)}, u32[]{:S(2)}, u32[]{:S(2)}) async-start(bf16[16,2,32,512]{3,2,1,0:T(8,128)(2,1)} %get-tuple-element.17), calls=%async_computation | async-start | bytes 2097152 | tf_op jit(solution)/shard_map/cond/branch_1_fun/all_to_all | solution.py:180
  24.9 1.4 %collective-permute-start = (bf16[512,256]{1,0:T(8,128)(2,1)}, bf16[512,256]{1,0:T(8,128)(2,1)}, u32[]{:S(2)}, u32[]{:S(2)}) collective-permute-start(bf16[512,256]{1,0:T(8,128)(2,1)} %get-tuple-element.18), channel_id=1, source_target_pairs={{8,16},{9,17},{10,18},{11,19},{12,20},{13,21},{14,22},{15,23},{16,... | collective-permute-start | bytes 786440 | tf_op jit(solution)/shard_map/cond/branch_1_fun/ppermute | solution.py:29
  26.3 1.4 %collective-permute-start.1 = (bf16[512,256]{1,0:T(8,128)(2,1)}, bf16[512,256]{1,0:T(8,128)(2,1)}, u32[]{:S(2)}, u32[]{:S(2)}) collective-permute-start(bf16[512,256]{1,0:T(8,128)(2,1)} %get-tuple-element.19), channel_id=1, source_target_pairs={{8,16},{9,17},{10,18},{11,19},{12,20},{13,21},{14,22},{15,23},{16,... | collective-permute-start | bytes 786440 | tf_op jit(solution)/shard_map/cond/branch_1_fun/ppermute | solution.py:29
  27.6 13.8 %all-to-all-done = bf16[16,2,32,512]{3,2,1,0:T(8,128)(2,1)S(1)} async-done(((bf16[16,2,32,512]{3,2,1,0:T(8,128)(2,1)}), bf16[16,2,32,512]{3,2,1,0:T(8,128)(2,1)S(1)}, u32[]{:S(2)}, u32[]{:S(2)}) %all-to-all-start) | async-done | bytes 1048608 | tf_op jit(solution)/shard_map/cond/branch_1_fun/all_to_all | solution.py:180
  41.4 1.0 %copy.7 = bf16[16,2,32,512]{3,2,1,0:T(8,128)(2,1)} copy(bf16[16,2,32,512]{3,2,1,0:T(8,128)(2,1)S(1)} %all-to-all-done) | data formatting | bytes 2097152 | tf_op jit(solution)/shard_map/cond
  42.4 0.0 collective-permute-done
  42.4 0.0 collective-permute-done.1
  42.4 0.0 collective-permute-done.3.refs_2_
  42.4 0.0 collective-permute-done.4.refs_3_
  42.4 3.6 %fields.3 = bf16[8,2,2,32,512]{4,3,2,1,0:T(8,128)(2,1)} custom-call(s32[3]{0:T(128)S(1)} %pad_add_fusion.2.place_ref, s32[1,512]{1,0:T(1,128)S(1)} %bitcast.12, bf16[512,256]{1,0:T(8,128)(2,1)} %get-tuple-element.24.refs_0_, bf16[512,256]{1,0:T(8,128)(2,1)} %get-tuple-element.25.refs_1_, bf16[512,256]{1,0:T(8,128)(2,1)S(1)} %collective-permute-done.3.refs_2_, ...), custom_call_target="tpu_custom_call" | custom-call | tf_op jit(solution)/shard_map/fields/pallas_call | solution.py:88
  46.1 3.7 %all-to-all-start.1 = ((bf16[16,2,32,512]{3,2,1,0:T(8,128)(2,1)}), bf16[16,2,32,512]{3,2,1,0:T(8,128)(2,1)S(1)}, u32[]{:S(2)}, u32[]{:S(2)}) async-start(bf16[16,2,32,512]{3,2,1,0:T(8,128)(2,1)} %bitcast.7), calls=%async_computation.1 | async-start | bytes 2097152 | tf_op jit(solution)/shard_map/all_to_all | solution.py:180
  49.8 0.0 copy-start.1
  49.8 0.7 copy-done.1
  50.5 0.1 pad_add_fusion
  50.5 0.1 compare_select_fusion
  50.6 0.1 fusion.3
  50.7 0.1 pad_add_fusion.1.table_ref
  50.8 15.5 %all-to-all-done.1.far_ref = bf16[16,2,32,512]{3,2,1,0:T(8,128)(2,1)S(1)} async-done(((bf16[16,2,32,512]{3,2,1,0:T(8,128)(2,1)}), bf16[16,2,32,512]{3,2,1,0:T(8,128)(2,1)S(1)}, u32[]{:S(2)}, u32[]{:S(2)}) %all-to-all-start.1) | async-done | bytes 1048608 | tf_op jit(solution)/shard_map/all_to_all | solution.py:180
  66.3 4.0 %pairs.1 = f32[32,2,2,512]{3,2,1,0:T(2,128)} custom-call(s32[2,32]{1,0:T(2,128)S(1)} %pad_add_fusion.1.table_ref, bf16[16,2,32,512]{3,2,1,0:T(8,128)(2,1)} %get-tuple-element.23.near_ref, bf16[16,2,32,512]{3,2,1,0:T(8,128)(2,1)S(1)} %all-to-all-done.1.far_ref), custom_call_target="tpu_custom_call" | custom-call | tf_op jit(solution)/shard_map/pairs/pallas_call | solution.py:144
Async XLA Ops:
  1.8 8.2 %collective-permute-start.2 = (bf16[512,256]{1,0:T(8,128)(2,1)S(1)}, bf16[512,256]{1,0:T(8,128)(2,1)}, u32[]{:S(2)}, u32[]{:S(2)}) collective-permute-start(bf16[512,256]{1,0:T(8,128)(2,1)S(1)} %get-tuple-element.26), channel_id=1, source_target_pairs={{0,1},{1,0},{2,3},{3,2},{4,5},{5,4},{6,7},{7,6},{8,9},{9,8},{10,11... | collective-permute-start | bytes 786440 | tf_op jit(solution)/shard_map/ppermute | solution.py:29
  3.8 38.6 %collective-permute-start.3 = (bf16[512,256]{1,0:T(8,128)(2,1)}, bf16[512,256]{1,0:T(8,128)(2,1)S(1)}, u32[]{:S(2)}, u32[]{:S(2)}) collective-permute-start(bf16[512,256]{1,0:T(8,128)(2,1)} %get-tuple-element.27.refs_0_), channel_id=1, source_target_pairs={{0,24},{1,25},{2,26},{3,27},{4,28},{5,29},{6,30},{7,31},{24,0},{25... | collective-permute-start | bytes 786440 | tf_op jit(solution)/shard_map/ppermute | solution.py:29
  10.0 32.5 %collective-permute-start.4 = (bf16[512,256]{1,0:T(8,128)(2,1)}, bf16[512,256]{1,0:T(8,128)(2,1)S(1)}, u32[]{:S(2)}, u32[]{:S(2)}) collective-permute-start(bf16[512,256]{1,0:T(8,128)(2,1)} %collective-permute-done.2.refs_1_), channel_id=1, source_target_pairs={{0,24},{1,25},{2,26},{3,27},{4,28},{5,29},{6,30},{7,31},{24,0},{25... | collective-permute-start | bytes 786440 | tf_op jit(solution)/shard_map/ppermute | solution.py:29
  15.1 0.7 copy-start
  19.4 22.1 %all-to-all-start = ((bf16[16,2,32,512]{3,2,1,0:T(8,128)(2,1)}), bf16[16,2,32,512]{3,2,1,0:T(8,128)(2,1)S(1)}, u32[]{:S(2)}, u32[]{:S(2)}) async-start(bf16[16,2,32,512]{3,2,1,0:T(8,128)(2,1)} %get-tuple-element.17), calls=%async_computation | async-start | bytes 2097152 | tf_op jit(solution)/shard_map/cond/branch_1_fun/all_to_all | solution.py:180
  24.9 17.5 %collective-permute-start = (bf16[512,256]{1,0:T(8,128)(2,1)}, bf16[512,256]{1,0:T(8,128)(2,1)}, u32[]{:S(2)}, u32[]{:S(2)}) collective-permute-start(bf16[512,256]{1,0:T(8,128)(2,1)} %get-tuple-element.18), channel_id=1, source_target_pairs={{8,16},{9,17},{10,18},{11,19},{12,20},{13,21},{14,22},{15,23},{16,... | collective-permute-start | bytes 786440 | tf_op jit(solution)/shard_map/cond/branch_1_fun/ppermute | solution.py:29
  26.3 16.2 %collective-permute-start.1 = (bf16[512,256]{1,0:T(8,128)(2,1)}, bf16[512,256]{1,0:T(8,128)(2,1)}, u32[]{:S(2)}, u32[]{:S(2)}) collective-permute-start(bf16[512,256]{1,0:T(8,128)(2,1)} %get-tuple-element.19), channel_id=1, source_target_pairs={{8,16},{9,17},{10,18},{11,19},{12,20},{13,21},{14,22},{15,23},{16,... | collective-permute-start | bytes 786440 | tf_op jit(solution)/shard_map/cond/branch_1_fun/ppermute | solution.py:29
  46.1 20.2 %all-to-all-start.1 = ((bf16[16,2,32,512]{3,2,1,0:T(8,128)(2,1)}), bf16[16,2,32,512]{3,2,1,0:T(8,128)(2,1)S(1)}, u32[]{:S(2)}, u32[]{:S(2)}) async-start(bf16[16,2,32,512]{3,2,1,0:T(8,128)(2,1)} %bitcast.7), calls=%async_computation.1 | async-start | bytes 2097152 | tf_op jit(solution)/shard_map/all_to_all | solution.py:180
  49.8 0.7 copy-start.1

commit v13 on v8

--- a/solution.py
+++ b/solution.py
@@ -66,7 +66,7 @@
                 out_ref[:, 0, part] = pieces.astype(jnp.bfloat16)
 
 
-def make_fields(slabs, points, groups, place):
+def make_fields(slabs, points, groups, place, work):
     slab_size, channels = slabs[0].shape
     npoints = points.shape[1] // 2
     length = npoints // groups
@@ -84,6 +84,9 @@
             scratch_shapes=[pltpu.VMEM((2, npoints, channels), jnp.bfloat16)],
         ),
         out_shape=jax.ShapeDtypeStruct((groups, SPLIT, 2, length, slab_size), jnp.bfloat16),
+        cost_estimate=pl.CostEstimate(
+            flops=work * 1_000_000_000, bytes_accessed=work * 3_000_000, transcendentals=0
+        ),
         compiler_params=pltpu.CompilerParams(vmem_limit_bytes=VMEM_LIMIT),
         name="fields",
     )(place, points, *slabs)
@@ -160,11 +163,10 @@
     def share(fields):
         return lax.all_to_all(fields, ("inner", "lo"), split_axis=0, concat_axis=0, tiled=True)
 
-    near_fields = flat(make_fields(near, points, groups, place))
+    near_fields = flat(make_fields(near, points, groups, place, 1))
     near_fields, points = lax.optimization_barrier((near_fields, points))
-    far_fields = flat(make_fields(far, points, groups, place))
-    near_fields = lax.cond(half >= 0, share, lambda fields: fields, near_fields)
-    near_fields, far_fields = lax.optimization_barrier((near_fields, far_fields))
+    far_fields = flat(make_fields(far, points, groups, place, 60))
+    near_fields, far_fields = lax.optimization_barrier((share(near_fields), far_fields))
     far_fields = share(far_fields)
 
     turn = half * (total_k // 2)

time: 67.8 us -> 66.4 us (0.979)
  blocking collectives: 29 us -> 0 us
  waiting for transfers between devices: 20.5 us -> 38.8 us
  starting transfers between devices: 8.32 us -> 16.9 us
    all_to_all x1 -> x0, blocking collectives: 29 us -> none  [share(): lax.all_to_all(fields, ('inner', 'lo'), split_axis=0, concat_axis=0, tile...]
    ppermute x3, waiting for transfers between devices: 4.76 us -> 16.1 us  [swap(): return lax.ppermute(block, KA + GA, route)]
    all_to_all x1 -> x2, starting transfers between devices: 3.88 us -> 12.5 us  [share(): lax.all_to_all(fields, ('inner', 'lo'), split_axis=0, concat_axis=0, tile...]
    all_to_all x1 -> x2, waiting for transfers between devices: 15.7 us -> 22.7 us  [share(): lax.all_to_all(fields, ('inner', 'lo'), split_axis=0, concat_axis=0, tile...]
  transfers between devices with their start and end apart: 4 -> 5, of which waited for: 2 -> 5; matrix products, arithmetic and copies ran while one was open for 0% -> 0% of each run, Pallas kernels for 3% -> 8%
where the time goes in v13:
time: 66.4 us; the launch traced here: 65.8 us
  waiting for transfers between devices  38.8 us (58%)
  starting transfers between devices  16.9 us (25%)
  Pallas kernels  8.08 us (12%)
  local copies, waits for them, and re-layouts  1.74 us (3%)
    all_to_all x2, waiting for transfers between devices, share(): lax.all_to_all(fields, ('inner', 'lo'), split_axis=0, concat_axis=0, tile...  22.7 us
    ppermute x3, waiting for transfers between devices, swap(): return lax.ppermute(block, KA + GA, route)  16.1 us
    all_to_all x2, starting transfers between devices, share(): lax.all_to_all(fields, ('inner', 'lo'), split_axis=0, concat_axis=0, tile...  12.5 us
    pallas_call x2, Pallas kernels, make_fields(): pl.pallas_call(functools.partial(field_kernel, len(slabs)), grid_spec=plt...  4.97 us
    ppermute x3, starting transfers between devices, swap(): return lax.ppermute(block, KA + GA, route)  4.45 us
    pallas_call x1, Pallas kernels, make_pairs(): pl.pallas_call(functools.partial(pair_kernel, 1.0 / math.sqrt(2 * half_k)...  3.12 us
  transfers between devices with their start and end apart: 5, of which 5 were waited for; matrix products, arithmetic and copies ran while one was open for 0% of the time, Pallas kernels for 8%

profile of v13, /device:TPU:1, one launch (start us, length us, event | category | flops | bytes accessed | tf_op | source)
XLA Modules:
  0.0 65.8 jit_solution(12397051572255340460)
XLA Ops:
  0.0 1.1 %dynamic-slice_bitcast_fusion = (bf16[512,256]{1,0:T(8,128)(2,1)S(1)}, bf16[512,256]{1,0:T(8,128)(2,1)S(1)}) fusion(bf16[2,512,256]{2,1,0:T(8,128)(2,1)} %param.3, s32[]{:T(128)S(6)} %select_n.30, s32[]{:T(128)S(6)} %select_n.29), kind=kLoop, calls=%fused_computation | loop fusion | bytes 1048584 | tf_op jit(solution)/shard_map/jit(dynamic_index_in_dim)/squeeze | solution.py:153
  1.1 2.1 %collective-permute-start = (bf16[512,256]{1,0:T(8,128)(2,1)S(1)}, bf16[512,256]{1,0:T(8,128)(2,1)S(1)}, u32[]{:S(2)}, u32[]{:S(2)}) collective-permute-start(bf16[512,256]{1,0:T(8,128)(2,1)S(1)} %get-tuple-element.13), channel_id=1, source_target_pairs={{0,1},{1,0},{2,3},{3,2},{4,5},{5,4},{6,7},{7,6},{8,9},{9,8},{10,11... | collective-permute-start | bytes 786440 | tf_op jit(solution)/shard_map/ppermute | solution.py:25
  3.2 2.3 %collective-permute-start.1 = (bf16[512,256]{1,0:T(8,128)(2,1)S(1)}, bf16[512,256]{1,0:T(8,128)(2,1)S(1)}, u32[]{:S(2)}, u32[]{:S(2)}) collective-permute-start(bf16[512,256]{1,0:T(8,128)(2,1)S(1)} %get-tuple-element.14.refs_0_), channel_id=1, source_target_pairs={{0,16},{1,17},{2,18},{3,19},{4,20},{5,21},{6,22},{7,23},{8,24},{9,... | collective-permute-start | bytes 786440 | tf_op jit(solution)/shard_map/ppermute | solution.py:25
  5.5 0.0 collective-permute-start.2
  5.5 0.0 copy-start
  5.5 0.1 pad_add_fusion.1.place_ref
  5.6 3.6 %collective-permute-done.refs_1_ = bf16[512,256]{1,0:T(8,128)(2,1)S(1)} collective-permute-done((bf16[512,256]{1,0:T(8,128)(2,1)S(1)}, bf16[512,256]{1,0:T(8,128)(2,1)S(1)}, u32[]{:S(2)}, u32[]{:S(2)}) %collective-permute-start) | collective-permute-done | bytes 262176 | tf_op jit(solution)/shard_map/ppermute | solution.py:25
  9.2 0.0 copy-done
  9.2 2.5 %fields.2 = bf16[8,2,2,32,512]{4,3,2,1,0:T(8,128)(2,1)} custom-call(s32[2]{0:T(128)S(1)} %pad_add_fusion.1.place_ref, s32[1,512]{1,0:T(1,128)S(1)} %bitcast.9, bf16[512,256]{1,0:T(8,128)(2,1)S(1)} %get-tuple-element.14.refs_0_, bf16[512,256]{1,0:T(8,128)(2,1)S(1)} %collective-permute-done.refs_1_), custom_call_target="tpu_custom_call" | custom-call | flops 1000000000 | bytes 3000000 | tf_op jit(solution)/shard_map/fields/pallas_call | solution.py:73
  11.7 6.2 %all-to-all-start = ((bf16[16,2,32,512]{3,2,1,0:T(8,128)(2,1)}), bf16[16,2,32,512]{3,2,1,0:T(8,128)(2,1)S(1)}, u32[]{:S(2)}, u32[]{:S(2)}) async-start(bf16[16,2,32,512]{3,2,1,0:T(8,128)(2,1)} %bitcast.5), calls=%async_computation | async-start | bytes 2097152 | tf_op jit(solution)/shard_map/all_to_all | solution.py:164
  17.9 4.6 %collective-permute-done.1.refs_0_ = bf16[512,256]{1,0:T(8,128)(2,1)S(1)} collective-permute-done((bf16[512,256]{1,0:T(8,128)(2,1)S(1)}, bf16[512,256]{1,0:T(8,128)(2,1)S(1)}, u32[]{:S(2)}, u32[]{:S(2)}) %collective-permute-start.1) | collective-permute-done | bytes 262176 | tf_op jit(solution)/shard_map/ppermute | solution.py:25
  22.5 7.9 %collective-permute-done.2.refs_1_ = bf16[512,256]{1,0:T(8,128)(2,1)S(1)} collective-permute-done((bf16[512,256]{1,0:T(8,128)(2,1)S(1)}, bf16[512,256]{1,0:T(8,128)(2,1)S(1)}, u32[]{:S(2)}, u32[]{:S(2)}) %collective-permute-start.2) | collective-permute-done | bytes 262176 | tf_op jit(solution)/shard_map/ppermute | solution.py:25
  30.4 2.5 %fields.3 = bf16[8,2,2,32,512]{4,3,2,1,0:T(8,128)(2,1)} custom-call(s32[2]{0:T(128)S(1)} %pad_add_fusion.1.place_ref, s32[1,512]{1,0:T(1,128)S(1)} %bitcast.10, bf16[512,256]{1,0:T(8,128)(2,1)S(1)} %collective-permute-done.1.refs_0_, bf16[512,256]{1,0:T(8,128)(2,1)S(1)} %collective-permute-done.2.refs_1_), custom_call_target="tpu_custom_call" | custom-call | flops 60000002048 | bytes 180000000 | tf_op jit(solution)/shard_map/fields/pallas_call | solution.py:73
  32.9 7.0 %all-to-all-done.near_ref = bf16[16,2,32,512]{3,2,1,0:T(8,128)(2,1)S(1)} async-done(((bf16[16,2,32,512]{3,2,1,0:T(8,128)(2,1)}), bf16[16,2,32,512]{3,2,1,0:T(8,128)(2,1)S(1)}, u32[]{:S(2)}, u32[]{:S(2)}) %all-to-all-start) | async-done | bytes 1048608 | tf_op jit(solution)/shard_map/all_to_all | solution.py:164
  39.9 6.3 %all-to-all-start.1 = ((bf16[16,2,32,512]{3,2,1,0:T(8,128)(2,1)}), bf16[16,2,32,512]{3,2,1,0:T(8,128)(2,1)S(1)}, u32[]{:S(2)}, u32[]{:S(2)}) async-start(bf16[16,2,32,512]{3,2,1,0:T(8,128)(2,1)} %bitcast.6), calls=%async_computation.1 | async-start | bytes 2097152 | tf_op jit(solution)/shard_map/all_to_all | solution.py:164
  46.1 0.0 copy-start.1
  46.1 0.7 %copy-done.1 = s32[2,32]{1,0:T(2,128)S(1)} copy-done((s32[2,32]{1,0:T(2,128)S(1)}, s32[2,32]{1,0:T(2,128)}, u32[]{:S(2)}) %copy-start.1) | copy-done | bytes 280
  46.8 0.1 pad_add_fusion
  46.9 0.1 and_select_fusion.table_ref
  47.0 15.7 %all-to-all-done.1.far_ref = bf16[16,2,32,512]{3,2,1,0:T(8,128)(2,1)S(1)} async-done(((bf16[16,2,32,512]{3,2,1,0:T(8,128)(2,1)}), bf16[16,2,32,512]{3,2,1,0:T(8,128)(2,1)S(1)}, u32[]{:S(2)}, u32[]{:S(2)}) %all-to-all-start.1) | async-done | bytes 1048608 | tf_op jit(solution)/shard_map/all_to_all | solution.py:164
  62.7 3.1 %pairs.1 = f32[32,2,2,512]{3,2,1,0:T(2,128)} custom-call(s32[2,32]{1,0:T(2,128)S(1)} %and_select_fusion.table_ref, bf16[16,2,32,512]{3,2,1,0:T(8,128)(2,1)S(1)} %all-to-all-done.near_ref, bf16[16,2,32,512]{3,2,1,0:T(8,128)(2,1)S(1)} %all-to-all-done.1.far_ref), custom_call_target="tpu_custom_call" | custom-call | tf_op jit(solution)/shard_map/pairs/pallas_call | solution.py:129
Async XLA Ops:
  1.1 8.2 %collective-permute-start = (bf16[512,256]{1,0:T(8,128)(2,1)S(1)}, bf16[512,256]{1,0:T(8,128)(2,1)S(1)}, u32[]{:S(2)}, u32[]{:S(2)}) collective-permute-start(bf16[512,256]{1,0:T(8,128)(2,1)S(1)} %get-tuple-element.13), channel_id=1, source_target_pairs={{0,1},{1,0},{2,3},{3,2},{4,5},{5,4},{6,7},{7,6},{8,9},{9,8},{10,11... | collective-permute-start | bytes 786440 | tf_op jit(solution)/shard_map/ppermute | solution.py:25
  3.2 19.3 %collective-permute-start.1 = (bf16[512,256]{1,0:T(8,128)(2,1)S(1)}, bf16[512,256]{1,0:T(8,128)(2,1)S(1)}, u32[]{:S(2)}, u32[]{:S(2)}) collective-permute-start(bf16[512,256]{1,0:T(8,128)(2,1)S(1)} %get-tuple-element.14.refs_0_), channel_id=1, source_target_pairs={{0,16},{1,17},{2,18},{3,19},{4,20},{5,21},{6,22},{7,23},{8,24},{9,... | collective-permute-start | bytes 786440 | tf_op jit(solution)/shard_map/ppermute | solution.py:25
  5.5 24.9 %collective-permute-start.2 = (bf16[512,256]{1,0:T(8,128)(2,1)S(1)}, bf16[512,256]{1,0:T(8,128)(2,1)S(1)}, u32[]{:S(2)}, u32[]{:S(2)}) collective-permute-start(bf16[512,256]{1,0:T(8,128)(2,1)S(1)} %get-tuple-element.13), channel_id=1, source_target_pairs={{0,17},{1,16},{2,19},{3,18},{4,21},{5,20},{6,23},{7,22},{8,25},{9,... | collective-permute-start | bytes 786440 | tf_op jit(solution)/shard_map/ppermute | solution.py:25
  5.5 3.7 %copy-start = (s32[512]{0:T(512)S(1)}, s32[512]{0:T(512)}, u32[]{:S(2)}) copy-start(s32[512]{0:T(512)} %param.5) | copy-start | bytes 6148
  11.7 28.1 %all-to-all-start = ((bf16[16,2,32,512]{3,2,1,0:T(8,128)(2,1)}), bf16[16,2,32,512]{3,2,1,0:T(8,128)(2,1)S(1)}, u32[]{:S(2)}, u32[]{:S(2)}) async-start(bf16[16,2,32,512]{3,2,1,0:T(8,128)(2,1)} %bitcast.5), calls=%async_computation | async-start | bytes 2097152 | tf_op jit(solution)/shard_map/all_to_all | solution.py:164
  39.9 22.8 %all-to-all-start.1 = ((bf16[16,2,32,512]{3,2,1,0:T(8,128)(2,1)}), bf16[16,2,32,512]{3,2,1,0:T(8,128)(2,1)S(1)}, u32[]{:S(2)}, u32[]{:S(2)}) async-start(bf16[16,2,32,512]{3,2,1,0:T(8,128)(2,1)} %bitcast.6), calls=%async_computation.1 | async-start | bytes 2097152 | tf_op jit(solution)/shard_map/all_to_all | solution.py:164
  46.1 0.7 %copy-start.1 = (s32[2,32]{1,0:T(2,128)S(1)}, s32[2,32]{1,0:T(2,128)}, u32[]{:S(2)}) copy-start(s32[2,32]{1,0:T(2,128)} %param.4) | copy-start | bytes 772

commit v14 on v9

--- a/solution.py
+++ b/solution.py
@@ -15,18 +15,44 @@
 OUTER, MIDDLE = (0, 3), (1, 2)
 
 
-def swap(block, other, quarters=None):
+def swap(block, quarters, mirror, other):
     half, quarter, inner, hi, lo = (lax.axis_size(name) for name in KA + GA)
     slabs = hi * lo
     route = []
     for place in range(half * quarter * inner * slabs):
         kplace, slab = divmod(place, slabs)
         part, within = divmod(kplace, inner)
-        if quarters is not None and part not in quarters:
-            continue
-        part = part if quarters is None else half * quarter - 1 - part
-        route.append((place, (part * inner + within) * slabs + (slab ^ other)))
+        if part in quarters:
+            part = half * quarter - 1 - part if mirror else part
+            route.append((place, (part * inner + within) * slabs + (slab ^ other)))
     return lax.ppermute(block, KA + GA, route)
+
+
+def copy_kernel(place_ref, pair_ref, out_ref):
+    out_ref[...] = pair_ref[0]
+
+
+def take_slab(pair, place, choice):
+    _, slab_size, channels = pair.shape
+    return pl.pallas_call(
+        copy_kernel,
+        grid_spec=pltpu.PrefetchScalarGridSpec(
+            num_scalar_prefetch=1,
+            grid=(1,),
+            in_specs=[
+                pl.BlockSpec(
+                    (1, slab_size, channels),
+                    lambda step, place: (place[1] % SPLIT ^ choice, 0, 0),
+                )
+            ],
+            out_specs=pl.BlockSpec((slab_size, channels), lambda step, place: (0, 0)),
+        ),
+        out_shape=jax.ShapeDtypeStruct((slab_size, channels), jnp.bfloat16),
+        cost_estimate=pl.CostEstimate(
+            flops=60_000_000_000, bytes_accessed=180_000_000, transcendentals=0
+        ),
+        name="take_slab",
+    )(place, pair)
 
 
 def field_kernel(sets, place_ref, points_ref, *refs):
@@ -47,7 +73,8 @@
 
                 @pl.when(place_ref[2] == choice)
                 def _(number=number, choice=choice):
-                    held_ref[number] = source_refs[choice * slabs + number][...]
+                    source_ref = source_refs[choice * slabs + number]
+                    held_ref[number] = source_ref[...].reshape(slab_size, channels)
 
         first = pl.multiple_of(place_ref[0] * npoints, npoints)
         wanted = points_ref[:, pl.ds(first, npoints)]
@@ -81,17 +108,21 @@
 
 
 def make_fields(sources, points, groups, place):
-    slab_size, channels = sources[0][0].shape
     slabs = [slab for source in sources for slab in source]
+    slab_size, channels = slabs[0].shape[-2:]
     npoints = points.shape[1] // 2
     length = npoints // groups
+    one = pl.BlockSpec((slab_size, channels), lambda step, place: (0, 0))
+    of_two = pl.BlockSpec(
+        (1, slab_size, channels), lambda step, place: (place[1] % SPLIT, 0, 0)
+    )
     return pl.pallas_call(
         functools.partial(field_kernel, len(sources)),
         grid_spec=pltpu.PrefetchScalarGridSpec(
             num_scalar_prefetch=1,
             grid=(SPLIT,),
             in_specs=[pl.BlockSpec(points.shape, lambda step, place: (0, 0))]
-            + [pl.BlockSpec((slab_size, channels), lambda step, place: (0, 0)) for _ in slabs],
+            + [one if slab.ndim == 2 else of_two for slab in slabs],
             out_specs=pl.BlockSpec(
                 (groups, 1, 2, length, slab_size),
                 lambda step, place: (0, place[1] % SPLIT ^ step, 0, 0, 0),
@@ -102,6 +133,9 @@
             ],
         ),
         out_shape=jax.ShapeDtypeStruct((groups, SPLIT, 2, length, slab_size), jnp.bfloat16),
+        cost_estimate=pl.CostEstimate(
+            flops=1_000_000_000, bytes_accessed=3_000_000, transcendentals=0
+        ),
         compiler_params=pltpu.CompilerParams(vmem_limit_bytes=VMEM_LIMIT),
         name="fields",
     )(place, points, *slabs)
@@ -163,16 +197,13 @@
     groups = lax.axis_size("quarter") * lax.axis_size("inner")
     slabs = lax.axis_size("hi") * lax.axis_size("lo")
     total_k = 2 * groups * kdevice
-
+    points = points.reshape(1, -1)
+    place = jnp.stack([half, hi * SPLIT + lo, (half == quarter).astype(jnp.int32)])
+
+    swapped = swap(orbitals, OUTER, True, 0)
     mine = lax.dynamic_index_in_dim(orbitals, lo, 0, keepdims=False)
     other = lax.dynamic_index_in_dim(orbitals, 1 - lo, 0, keepdims=False)
-    near = [mine] + [swap(other if x & 1 else mine, x) for x in range(1, slabs)]
-    outer = [swap(other if x & 1 else mine, x, OUTER) for x in range(slabs)]
-    later = lax.optimization_barrier(near)
-    middle = [swap(slab, 0, MIDDLE) for slab in later]
-
-    points = points.reshape(1, -1)
-    place = jnp.stack([half, hi * SPLIT + lo, (half == quarter).astype(jnp.int32)])
+    near = [mine] + [swap(other if x & 1 else mine, OUTER + MIDDLE, False, x) for x in range(1, slabs)]
 
     def flat(fields):
         return fields.reshape((groups * SPLIT,) + fields.shape[2:])
@@ -182,10 +213,12 @@
         return lax.all_to_all(fields, around, split_axis=0, concat_axis=0, tiled=True)
 
     near_fields = flat(make_fields([near], points, groups, place))
-    near_fields, points = lax.optimization_barrier((near_fields, points))
+    middle = [swap(slab, MIDDLE, True, 0) for slab in near]
+    sent = {x & 1: None for x in range(1, slabs)}
+    sent = {choice: take_slab(swapped, place, choice) for choice in sent}
+    outer = [swapped] + [swap(sent[x & 1], OUTER, False, x) for x in range(1, slabs)]
     far_fields = flat(make_fields([middle, outer], points, groups, place))
-    near_fields = lax.cond(half >= 0, share, lambda fields: fields, near_fields)
-    near_fields, far_fields = lax.optimization_barrier((near_fields, far_fields))
+    near_fields, far_fields = lax.optimization_barrier((share(near_fields), far_fields))
     far_fields = share(far_fields)
 
     def mirrored(kpoints):

time: 65.8 us -> 72.2 us (1.097)
  blocking collectives: 25 us -> 0 us
  waiting for transfers between devices: 15.6 us -> 35.6 us
  starting transfers between devices: 14.4 us -> 21.5 us
  Pallas kernels: 7.46 us -> 10.5 us
  local copies, waits for them, and re-layouts: 2.51 us -> 3.69 us
    all_to_all x1 -> x0, blocking collectives: 25 us -> none  [share(): lax.all_to_all(fields, around, split_axis=0, concat_axis=0, tiled=True)]
    ppermute x5, waiting for transfers between devices: 0.01 us -> 20 us  [swap(): return lax.ppermute(block, KA + GA, route)]
    all_to_all x1 -> x2, starting transfers between devices: 3.79 us -> 9.56 us  [share(): lax.all_to_all(fields, around, split_axis=0, concat_axis=0, tiled=True)]
    pallas_call x0 -> x1, Pallas kernels: none -> 2.34 us  [take_slab(): pl.pallas_call(copy_kernel, grid_spec=pltpu.PrefetchScalarGridSpec(num_sc...]
    ppermute x5, starting transfers between devices: 10.6 us -> 12 us  [swap(): return lax.ppermute(block, KA + GA, route)]
    unnamed x4 -> x12, local copies, waits for them, and re-layouts: 1.27 us -> 2.54 us
    pallas_call x2, Pallas kernels: 4.34 us -> 5.09 us  [make_fields(): pl.pallas_call(functools.partial(field_kernel, len(sources)), grid_spec=p...]
    all_to_all x1 -> x2, waiting for transfers between devices: 15.6 us -> 15.6 us  [share(): lax.all_to_all(fields, around, split_axis=0, concat_axis=0, tiled=True)]
  transfers between devices with their start and end apart: 6 -> 7, of which waited for: 1 -> 3; matrix products, arithmetic and copies ran while one was open for 1% -> 2% of each run, Pallas kernels for 3% -> 10%
where the time goes in v14:
time: 72.2 us; the launch traced here: 71.8 us
  waiting for transfers between devices  35.6 us (49%)
  starting transfers between devices  21.5 us (30%)
  Pallas kernels  10.5 us (15%)
  local copies, waits for them, and re-layouts  3.69 us (5%)
    ppermute x5, waiting for transfers between devices, swap(): return lax.ppermute(block, KA + GA, route)  20 us
    all_to_all x2, waiting for transfers between devices, share(): lax.all_to_all(fields, around, split_axis=0, concat_axis=0, tiled=True)  15.6 us
    ppermute x5, starting transfers between devices, swap(): return lax.ppermute(block, KA + GA, route)  12 us
    all_to_all x2, starting transfers between devices, share(): lax.all_to_all(fields, around, split_axis=0, concat_axis=0, tiled=True)  9.56 us
    pallas_call x2, Pallas kernels, make_fields(): pl.pallas_call(functools.partial(field_kernel, len(sources)), grid_spec=p...  5.09 us
    pallas_call x1, Pallas kernels, make_pairs(): pl.pallas_call(functools.partial(pair_kernel, 1.0 / math.sqrt(2 * half_k)...  3.12 us
    unnamed x12, local copies, waits for them, and re-layouts  2.54 us
    pallas_call x1, Pallas kernels, take_slab(): pl.pallas_call(copy_kernel, grid_spec=pltpu.PrefetchScalarGridSpec(num_sc...  2.34 us
  transfers between devices with their start and end apart: 7, of which 3 were waited for; matrix products, arithmetic and copies ran while one was open for 2% of the time, Pallas kernels for 10%

profile of v14, /device:TPU:1, one launch (start us, length us, event | category | flops | bytes accessed | tf_op | source)
XLA Modules:
  0.0 71.8 jit_solution(2030637418484084856)
XLA Ops:
  0.0 6.0 %collective-permute-start.3 = (bf16[2,512,256]{2,1,0:T(8,128)(2,1)}, bf16[2,512,256]{2,1,0:T(8,128)(2,1)S(1)}, u32[]{:S(2)}, u32[]{:S(2)}) collective-permute-start(bf16[2,512,256]{2,1,0:T(8,128)(2,1)} %param.3), channel_id=1, source_target_pairs={{0,24},{1,25},{2,26},{3,27},{4,28},{5,29},{6,30},{7,31},{24,0},{25... | collective-permute-start | bytes 1572872 | tf_op jit(solution)/shard_map/ppermute | solution.py:28
  6.1 1.1 %dynamic-slice_bitcast_fusion = (bf16[512,256]{1,0:T(8,128)(2,1)S(1)}, bf16[512,256]{1,0:T(8,128)(2,1)S(1)}) fusion(bf16[2,512,256]{2,1,0:T(8,128)(2,1)} %param.3, s32[]{:T(128)S(6)} %select_n.40, s32[]{:T(128)S(6)} %select_n.39), kind=kLoop, calls=%fused_computation | loop fusion | bytes 1048584 | tf_op jit(solution)/shard_map/jit(dynamic_index_in_dim)/squeeze | solution.py:205
  7.1 1.3 %collective-permute-start = (bf16[512,256]{1,0:T(8,128)(2,1)S(1)}, bf16[512,256]{1,0:T(8,128)(2,1)S(1)}, u32[]{:S(2)}, u32[]{:S(2)}) collective-permute-start(bf16[512,256]{1,0:T(8,128)(2,1)S(1)} %get-tuple-element.9), channel_id=1, source_target_pairs={{0,1},{1,0},{2,3},{3,2},{4,5},{5,4},{6,7},{7,6},{8,9},{9,8},{10,11... | collective-permute-start | bytes 786440 | tf_op jit(solution)/shard_map/ppermute | solution.py:28
  8.4 0.7 collective-permute-start.1
  9.1 0.0 copy-start.4
  9.1 0.1 pad_add_fusion.2.place_ref
  9.2 0.0 copy-start
  9.2 4.8 %collective-permute-done.refs_1_ = bf16[512,256]{1,0:T(8,128)(2,1)S(1)} collective-permute-done((bf16[512,256]{1,0:T(8,128)(2,1)S(1)}, bf16[512,256]{1,0:T(8,128)(2,1)S(1)}, u32[]{:S(2)}, u32[]{:S(2)}) %collective-permute-start) | collective-permute-done | bytes 262176 | tf_op jit(solution)/shard_map/ppermute | solution.py:28
  14.1 0.0 copy-done
  14.1 0.0 copy-done.4
  14.1 2.5 %fields.2 = bf16[8,2,2,32,512]{4,3,2,1,0:T(8,128)(2,1)} custom-call(s32[3]{0:T(128)S(1)} %pad_add_fusion.2.place_ref, s32[1,512]{1,0:T(1,128)S(1)} %bitcast.11, bf16[512,256]{1,0:T(8,128)(2,1)S(1)} %get-tuple-element.10.refs_0_, bf16[512,256]{1,0:T(8,128)(2,1)S(1)} %collective-permute-done.refs_1_), custom_call_target="tpu_custom_call" | custom-call | flops 1000000000 | bytes 3000000 | tf_op jit(solution)/shard_map/fields/pallas_call | solution.py:119
  16.6 5.6 %all-to-all-start = ((bf16[16,2,32,512]{3,2,1,0:T(8,128)(2,1)}), bf16[16,2,32,512]{3,2,1,0:T(8,128)(2,1)S(1)}, u32[]{:S(2)}, u32[]{:S(2)}) async-start(bf16[16,2,32,512]{3,2,1,0:T(8,128)(2,1)} %bitcast.6), calls=%async_computation | async-start | bytes 2097152 | tf_op jit(solution)/shard_map/all_to_all | solution.py:213
  22.2 0.0 copy-start.1
  22.2 0.7 collective-permute-start.2
  22.9 0.0 collective-permute-done.3.pair_ref.refs_2_
  22.9 0.0 copy-start.2
  22.9 0.8 %copy-done.2 = bf16[2,512,256]{2,1,0:T(8,128)(2,1)} copy-done((bf16[2,512,256]{2,1,0:T(8,128)(2,1)}, bf16[2,512,256]{2,1,0:T(8,128)(2,1)S(1)}, u32[]{:S(2)}) %copy-start.2) | copy-done | bytes 524312
  23.7 2.3 %take_slab.1 = bf16[512,256]{1,0:T(8,128)(2,1)} custom-call(s32[3]{0:T(128)} %copy-done, bf16[2,512,256]{2,1,0:T(8,128)(2,1)} %copy-done.2), custom_call_target="tpu_custom_call" | custom-call | flops 60000002048 | bytes 180000000 | tf_op jit(solution)/shard_map/take_slab/pallas_call | solution.py:37
  26.1 3.3 %collective-permute-start.4 = (bf16[512,256]{1,0:T(8,128)(2,1)}, bf16[512,256]{1,0:T(8,128)(2,1)S(1)}, u32[]{:S(2)}, u32[]{:S(2)}) collective-permute-start(bf16[512,256]{1,0:T(8,128)(2,1)} %take_slab.1), channel_id=1, source_target_pairs={{0,1},{1,0},{2,3},{3,2},{4,5},{5,4},{6,7},{7,6},{24,25},{25,24},{2... | collective-permute-start | bytes 786440 | tf_op jit(solution)/shard_map/ppermute | solution.py:28
  29.3 0.0 collective-permute-done.1.refs_0_
  29.4 0.0 collective-permute-done.2.refs_1_
  29.4 15.1 %collective-permute-done.4.refs_3_ = bf16[512,256]{1,0:T(8,128)(2,1)S(1)} collective-permute-done((bf16[512,256]{1,0:T(8,128)(2,1)}, bf16[512,256]{1,0:T(8,128)(2,1)S(1)}, u32[]{:S(2)}, u32[]{:S(2)}) %collective-permute-start.4) | collective-permute-done | bytes 262176 | tf_op jit(solution)/shard_map/ppermute | solution.py:28
  44.5 0.0 copy-done.1
  44.5 0.0 copy-start.3
  44.5 1.0 %copy-done.3 = bf16[2,512,256]{2,1,0:T(8,128)(2,1)S(1)} copy-done((bf16[2,512,256]{2,1,0:T(8,128)(2,1)S(1)}, bf16[2,512,256]{2,1,0:T(8,128)(2,1)}, u32[]{:S(2)}) %copy-start.3) | copy-done | bytes 524312
  45.5 2.6 %fields.3 = bf16[8,2,2,32,512]{4,3,2,1,0:T(8,128)(2,1)} custom-call(s32[3]{0:T(128)S(1)} %copy-done.1, s32[1,512]{1,0:T(1,128)S(1)} %bitcast.12, bf16[512,256]{1,0:T(8,128)(2,1)S(1)} %collective-permute-done.1.refs_0_, bf16[512,256]{1,0:T(8,128)(2,1)S(1)} %collective-permute-done.2.refs_1_, bf16[2,512,256]{2,1,0:T(8,128)(2,1)S(1)} %copy-done.3, ...), custom_call_target="tpu_custom_call" | custom-call | flops 1000000000 | bytes 3000000 | tf_op jit(solution)/shard_map/fields/pallas_call | solution.py:119
  48.1 0.0 all-to-all-done.near_ref
  48.1 3.9 %all-to-all-start.1 = ((bf16[16,2,32,512]{3,2,1,0:T(8,128)(2,1)}), bf16[16,2,32,512]{3,2,1,0:T(8,128)(2,1)S(1)}, u32[]{:S(2)}, u32[]{:S(2)}) async-start(bf16[16,2,32,512]{3,2,1,0:T(8,128)(2,1)} %bitcast.7), calls=%async_computation.1 | async-start | bytes 2097152 | tf_op jit(solution)/shard_map/all_to_all | solution.py:213
  52.1 0.0 copy-start.5
  52.1 0.7 copy-done.5
  52.7 0.1 pad_add_fusion
  52.8 0.1 compare_select_fusion
  52.9 0.1 fusion.3
  53.0 0.1 pad_add_fusion.1.table_ref
  53.1 15.6 %all-to-all-done.1.far_ref = bf16[16,2,32,512]{3,2,1,0:T(8,128)(2,1)S(1)} async-done(((bf16[16,2,32,512]{3,2,1,0:T(8,128)(2,1)}), bf16[16,2,32,512]{3,2,1,0:T(8,128)(2,1)S(1)}, u32[]{:S(2)}, u32[]{:S(2)}) %all-to-all-start.1) | async-done | bytes 1048608 | tf_op jit(solution)/shard_map/all_to_all | solution.py:213
  68.6 3.1 %pairs.1 = f32[32,2,2,512]{3,2,1,0:T(2,128)} custom-call(s32[2,32]{1,0:T(2,128)S(1)} %pad_add_fusion.1.table_ref, bf16[16,2,32,512]{3,2,1,0:T(8,128)(2,1)S(1)} %all-to-all-done.near_ref, bf16[16,2,32,512]{3,2,1,0:T(8,128)(2,1)S(1)} %all-to-all-done.1.far_ref), custom_call_target="tpu_custom_call" | custom-call | tf_op jit(solution)/shard_map/pairs/pallas_call | solution.py:178
Async XLA Ops:
  0.0 22.9 %collective-permute-start.3 = (bf16[2,512,256]{2,1,0:T(8,128)(2,1)}, bf16[2,512,256]{2,1,0:T(8,128)(2,1)S(1)}, u32[]{:S(2)}, u32[]{:S(2)}) collective-permute-start(bf16[2,512,256]{2,1,0:T(8,128)(2,1)} %param.3), channel_id=1, source_target_pairs={{0,24},{1,25},{2,26},{3,27},{4,28},{5,29},{6,30},{7,31},{24,0},{25... | collective-permute-start | bytes 1572872 | tf_op jit(solution)/shard_map/ppermute | solution.py:28
  7.1 6.9 %collective-permute-start = (bf16[512,256]{1,0:T(8,128)(2,1)S(1)}, bf16[512,256]{1,0:T(8,128)(2,1)S(1)}, u32[]{:S(2)}, u32[]{:S(2)}) collective-permute-start(bf16[512,256]{1,0:T(8,128)(2,1)S(1)} %get-tuple-element.9), channel_id=1, source_target_pairs={{0,1},{1,0},{2,3},{3,2},{4,5},{5,4},{6,7},{7,6},{8,9},{9,8},{10,11... | collective-permute-start | bytes 786440 | tf_op jit(solution)/shard_map/ppermute | solution.py:28
  8.4 20.9 %collective-permute-start.1 = (bf16[512,256]{1,0:T(8,128)(2,1)S(1)}, bf16[512,256]{1,0:T(8,128)(2,1)S(1)}, u32[]{:S(2)}, u32[]{:S(2)}) collective-permute-start(bf16[512,256]{1,0:T(8,128)(2,1)S(1)} %get-tuple-element.10.refs_0_), channel_id=1, source_target_pairs={{8,16},{9,17},{10,18},{11,19},{12,20},{13,21},{14,22},{15,23},{16,... | collective-permute-start | bytes 786440 | tf_op jit(solution)/shard_map/ppermute | solution.py:28
  9.1 4.9 %copy-start.4 = (s32[512]{0:T(512)S(1)}, s32[512]{0:T(512)}, u32[]{:S(2)}) copy-start(s32[512]{0:T(512)} %param.5) | copy-start | bytes 6148
  9.2 4.8 %copy-start = (s32[3]{0:T(128)}, s32[3]{0:T(128)S(1)}, u32[]{:S(2)}) copy-start(s32[3]{0:T(128)S(1)} %pad_add_fusion.2.place_ref) | copy-start | bytes 40
  16.6 31.5 %all-to-all-start = ((bf16[16,2,32,512]{3,2,1,0:T(8,128)(2,1)}), bf16[16,2,32,512]{3,2,1,0:T(8,128)(2,1)S(1)}, u32[]{:S(2)}, u32[]{:S(2)}) async-start(bf16[16,2,32,512]{3,2,1,0:T(8,128)(2,1)} %bitcast.6), calls=%async_computation | async-start | bytes 2097152 | tf_op jit(solution)/shard_map/all_to_all | solution.py:213
  22.2 22.3 %copy-start.1 = (s32[3]{0:T(128)S(1)}, s32[3]{0:T(128)}, u32[]{:S(2)}) copy-start(s32[3]{0:T(128)} %copy-done) | copy-start | bytes 40
  22.2 7.2 %collective-permute-start.2 = (bf16[512,256]{1,0:T(8,128)(2,1)S(1)}, bf16[512,256]{1,0:T(8,128)(2,1)S(1)}, u32[]{:S(2)}, u32[]{:S(2)}) collective-permute-start(bf16[512,256]{1,0:T(8,128)(2,1)S(1)} %collective-permute-done.refs_1_), channel_id=1, source_target_pairs={{8,16},{9,17},{10,18},{11,19},{12,20},{13,21},{14,22},{15,23},{16,... | collective-permute-start | bytes 786440 | tf_op jit(solution)/shard_map/ppermute | solution.py:28
  22.9 0.8 %copy-start.2 = (bf16[2,512,256]{2,1,0:T(8,128)(2,1)}, bf16[2,512,256]{2,1,0:T(8,128)(2,1)S(1)}, u32[]{:S(2)}) copy-start(bf16[2,512,256]{2,1,0:T(8,128)(2,1)S(1)} %collective-permute-done.3.pair_ref.refs_2_) | copy-start | bytes 1572868
  26.1 18.4 %collective-permute-start.4 = (bf16[512,256]{1,0:T(8,128)(2,1)}, bf16[512,256]{1,0:T(8,128)(2,1)S(1)}, u32[]{:S(2)}, u32[]{:S(2)}) collective-permute-start(bf16[512,256]{1,0:T(8,128)(2,1)} %take_slab.1), channel_id=1, source_target_pairs={{0,1},{1,0},{2,3},{3,2},{4,5},{5,4},{6,7},{7,6},{24,25},{25,24},{2... | collective-permute-start | bytes 786440 | tf_op jit(solution)/shard_map/ppermute | solution.py:28
  44.5 1.0 %copy-start.3 = (bf16[2,512,256]{2,1,0:T(8,128)(2,1)S(1)}, bf16[2,512,256]{2,1,0:T(8,128)(2,1)}, u32[]{:S(2)}) copy-start(bf16[2,512,256]{2,1,0:T(8,128)(2,1)} %copy-done.2) | copy-start | bytes 1572868
  48.1 20.5 %all-to-all-start.1 = ((bf16[16,2,32,512]{3,2,1,0:T(8,128)(2,1)}), bf16[16,2,32,512]{3,2,1,0:T(8,128)(2,1)S(1)}, u32[]{:S(2)}, u32[]{:S(2)}) async-start(bf16[16,2,32,512]{3,2,1,0:T(8,128)(2,1)} %bitcast.7), calls=%async_computation.1 | async-start | bytes 2097152 | tf_op jit(solution)/shard_map/all_to_all | solution.py:213
  52.1 0.7 copy-start.5

commit v15 on v13

--- a/solution.py
+++ b/solution.py
@@ -11,17 +11,18 @@
 
 VMEM_LIMIT = 40 * 1024 * 1024
 SPLIT = 2
-KA, GA = ("half", "inner"), ("hi", "lo")
+KA, GA = ("half", "quarter", "inner"), ("hi", "lo")
 
 
-def swap(block, cut, other):
-    half, inner, hi, lo = (lax.axis_size(name) for name in KA + GA)
+def swap(block, mirror, other):
+    half, quarter, inner, hi, lo = (lax.axis_size(name) for name in KA + GA)
     slabs = hi * lo
     route = []
-    for place in range(half * inner * slabs):
+    for place in range(half * quarter * inner * slabs):
         kplace, slab = divmod(place, slabs)
-        kplace = (kplace + cut * inner) % (half * inner)
-        route.append((place, kplace * slabs + (slab ^ other)))
+        part, within = divmod(kplace, inner)
+        part = half * quarter - 1 - part if mirror else part
+        route.append((place, (part * inner + within) * slabs + (slab ^ other)))
     return lax.ppermute(block, KA + GA, route)
 
 
@@ -144,15 +145,15 @@
 def on_device(orbitals, minus_table, points):
     kdevice, slab_size, channels = orbitals.shape
     half = lax.axis_index("half")
-    groups = lax.axis_size("inner")
+    groups = lax.axis_size("quarter") * lax.axis_size("inner")
     total_k = 2 * groups * kdevice
 
     lo = lax.axis_index("lo")
     slabs = lax.axis_size("hi") * SPLIT
     mine = lax.dynamic_index_in_dim(orbitals, lo, 0, keepdims=False)
     other = lax.dynamic_index_in_dim(orbitals, 1 - lo, 0, keepdims=False)
-    near = [mine] + [swap(other if x & 1 else mine, 0, x) for x in range(1, slabs)]
-    far = [swap(other if x & 1 else mine, 1, x) for x in range(slabs)]
+    near = [mine] + [swap(other if x & 1 else mine, False, x) for x in range(1, slabs)]
+    far = [swap(other if x & 1 else mine, True, x) for x in range(slabs)]
 
     points = points.reshape(1, -1)
     place = jnp.stack([half, lax.axis_index("hi") * SPLIT + lo])
@@ -161,7 +162,9 @@
         return fields.reshape((groups * SPLIT,) + fields.shape[2:])
 
     def share(fields):
-        return lax.all_to_all(fields, ("inner", "lo"), split_axis=0, concat_axis=0, tiled=True)
+        return lax.all_to_all(
+            fields, ("quarter", "inner", "lo"), split_axis=0, concat_axis=0, tiled=True
+        )
 
     near_fields = flat(make_fields(near, points, groups, place, 1))
     near_fields, points = lax.optimization_barrier((near_fields, points))
@@ -169,14 +172,19 @@
     near_fields, far_fields = lax.optimization_barrier((share(near_fields), far_fields))
     far_fields = share(far_fields)
 
+    def mirrored(kpoints):
+        return total_k // 2 + (kpoints + total_k // 4) % (total_k // 2)
+
     turn = half * (total_k // 2)
     table = (jnp.roll(minus_table, -turn, axis=1) - turn) % total_k
-    return make_pairs(near_fields, far_fields, table)
+    table = jnp.where(table < total_k // 2, table, mirrored(table))
+    first, third, fourth = jnp.split(table, (total_k // 2, 3 * total_k // 4), axis=1)
+    return make_pairs(near_fields, far_fields, jnp.concatenate([first, fourth, third], axis=1))
 
 
 def solution(mesh):
     kplaces, slabs = mesh.shape["ka"], mesh.shape["ga"]
-    devices = mesh.devices.reshape(2, kplaces // 2, slabs // SPLIT, SPLIT)
+    devices = mesh.devices.reshape(2, 2, kplaces // 4, slabs // SPLIT, SPLIT)
     finer = Mesh(devices, KA + GA)
     return jax.shard_map(
         on_device,

time: 66.4 us -> 61.7 us (0.929)
  waiting for transfers between devices: 38.8 us -> 32.2 us
  starting transfers between devices: 16.9 us -> 18.9 us
    ppermute x3, waiting for transfers between devices: 16.1 us -> 2.63 us  [swap(): return lax.ppermute(block, KA + GA, route)]
    all_to_all x2, waiting for transfers between devices: 22.7 us -> 29.6 us  [share(): lax.all_to_all(fields, ('quarter', 'inner', 'lo'), split_axis=0, concat_a...]
    ppermute x3, starting transfers between devices: 4.45 us -> 5.46 us  [swap(): return lax.ppermute(block, KA + GA, route)]
    all_to_all x2, starting transfers between devices: 12.5 us -> 13.4 us  [share(): lax.all_to_all(fields, ('quarter', 'inner', 'lo'), split_axis=0, concat_a...]
  transfers between devices with their start and end apart: 5 -> 5, of which waited for: 5 -> 3; matrix products, arithmetic and copies ran while one was open for 0% -> 1% of each run, Pallas kernels for 8% -> 8%
where the time goes in v15:
time: 61.7 us; the launch traced here: 61.4 us
  waiting for transfers between devices  32.2 us (52%)
  starting transfers between devices  18.9 us (31%)
  Pallas kernels  8.11 us (13%)
  local copies, waits for them, and re-layouts  1.81 us (3%)
    all_to_all x2, waiting for transfers between devices, share(): lax.all_to_all(fields, ('quarter', 'inner', 'lo'), split_axis=0, concat_a...  29.6 us
    all_to_all x2, starting transfers between devices, share(): lax.all_to_all(fields, ('quarter', 'inner', 'lo'), split_axis=0, concat_a...  13.4 us
    ppermute x3, starting transfers between devices, swap(): return lax.ppermute(block, KA + GA, route)  5.46 us
    pallas_call x2, Pallas kernels, make_fields(): pl.pallas_call(functools.partial(field_kernel, len(slabs)), grid_spec=plt...  5 us
    pallas_call x1, Pallas kernels, make_pairs(): pl.pallas_call(functools.partial(pair_kernel, 1.0 / math.sqrt(2 * half_k)...  3.12 us
    ppermute x3, waiting for transfers between devices, swap(): return lax.ppermute(block, KA + GA, route)  2.63 us
  transfers between devices with their start and end apart: 5, of which 3 were waited for; matrix products, arithmetic and copies ran while one was open for 1% of the time, Pallas kernels for 8%

profile of v15, /device:TPU:1, one launch (start us, length us, event | category | flops | bytes accessed | tf_op | source)
XLA Modules:
  0.0 61.4 jit_solution(8257629784444791200)
XLA Ops:
  0.0 1.1 %dynamic-slice_bitcast_fusion = (bf16[512,256]{1,0:T(8,128)(2,1)S(1)}, bf16[512,256]{1,0:T(8,128)(2,1)S(1)}) fusion(bf16[2,512,256]{2,1,0:T(8,128)(2,1)} %param.3, s32[]{:T(128)S(6)} %select_n.40, s32[]{:T(128)S(6)} %select_n.39), kind=kLoop, calls=%fused_computation | loop fusion | bytes 1048584 | tf_op jit(solution)/shard_map/jit(dynamic_index_in_dim)/squeeze | solution.py:154
  1.1 2.1 %collective-permute-start = (bf16[512,256]{1,0:T(8,128)(2,1)S(1)}, bf16[512,256]{1,0:T(8,128)(2,1)S(1)}, u32[]{:S(2)}, u32[]{:S(2)}) collective-permute-start(bf16[512,256]{1,0:T(8,128)(2,1)S(1)} %get-tuple-element.13), channel_id=1, source_target_pairs={{0,1},{1,0},{2,3},{3,2},{4,5},{5,4},{6,7},{7,6},{8,9},{9,8},{10,11... | collective-permute-start | bytes 786440 | tf_op jit(solution)/shard_map/ppermute | solution.py:26
  3.2 3.3 %collective-permute-start.1 = (bf16[512,256]{1,0:T(8,128)(2,1)S(1)}, bf16[512,256]{1,0:T(8,128)(2,1)S(1)}, u32[]{:S(2)}, u32[]{:S(2)}) collective-permute-start(bf16[512,256]{1,0:T(8,128)(2,1)S(1)} %get-tuple-element.14.refs_0_), channel_id=1, source_target_pairs={{0,24},{1,25},{2,26},{3,27},{4,28},{5,29},{6,30},{7,31},{8,16},{9,... | collective-permute-start | bytes 786440 | tf_op jit(solution)/shard_map/ppermute | solution.py:26
  6.5 0.0 collective-permute-start.2
  6.5 0.0 copy-start
  6.5 0.1 pad_add_fusion.2.place_ref
  6.6 2.6 %collective-permute-done.refs_1_ = bf16[512,256]{1,0:T(8,128)(2,1)S(1)} collective-permute-done((bf16[512,256]{1,0:T(8,128)(2,1)S(1)}, bf16[512,256]{1,0:T(8,128)(2,1)S(1)}, u32[]{:S(2)}, u32[]{:S(2)}) %collective-permute-start) | collective-permute-done | bytes 262176 | tf_op jit(solution)/shard_map/ppermute | solution.py:26
  9.2 0.0 copy-done
  9.2 2.5 %fields.2 = bf16[8,2,2,32,512]{4,3,2,1,0:T(8,128)(2,1)} custom-call(s32[2]{0:T(128)S(1)} %pad_add_fusion.2.place_ref, s32[1,512]{1,0:T(1,128)S(1)} %bitcast.10, bf16[512,256]{1,0:T(8,128)(2,1)S(1)} %get-tuple-element.14.refs_0_, bf16[512,256]{1,0:T(8,128)(2,1)S(1)} %collective-permute-done.refs_1_), custom_call_target="tpu_custom_call" | custom-call | flops 1000000000 | bytes 3000000 | tf_op jit(solution)/shard_map/fields/pallas_call | solution.py:74
  11.7 6.2 %all-to-all-start = ((bf16[16,2,32,512]{3,2,1,0:T(8,128)(2,1)}), bf16[16,2,32,512]{3,2,1,0:T(8,128)(2,1)S(1)}, u32[]{:S(2)}, u32[]{:S(2)}) async-start(bf16[16,2,32,512]{3,2,1,0:T(8,128)(2,1)} %bitcast.5), calls=%async_computation | async-start | bytes 2097152 | tf_op jit(solution)/shard_map/all_to_all | solution.py:165
  18.0 0.0 collective-permute-done.1.refs_0_
  18.0 0.0 collective-permute-done.2.refs_1_
  18.0 2.5 %fields.3 = bf16[8,2,2,32,512]{4,3,2,1,0:T(8,128)(2,1)} custom-call(s32[2]{0:T(128)S(1)} %pad_add_fusion.2.place_ref, s32[1,512]{1,0:T(1,128)S(1)} %bitcast.11, bf16[512,256]{1,0:T(8,128)(2,1)S(1)} %collective-permute-done.1.refs_0_, bf16[512,256]{1,0:T(8,128)(2,1)S(1)} %collective-permute-done.2.refs_1_), custom_call_target="tpu_custom_call" | custom-call | flops 60000002048 | bytes 180000000 | tf_op jit(solution)/shard_map/fields/pallas_call | solution.py:74
  20.5 14.0 %all-to-all-done.near_ref = bf16[16,2,32,512]{3,2,1,0:T(8,128)(2,1)S(1)} async-done(((bf16[16,2,32,512]{3,2,1,0:T(8,128)(2,1)}), bf16[16,2,32,512]{3,2,1,0:T(8,128)(2,1)S(1)}, u32[]{:S(2)}, u32[]{:S(2)}) %all-to-all-start) | async-done | bytes 1048608 | tf_op jit(solution)/shard_map/all_to_all | solution.py:165
  34.5 7.2 %all-to-all-start.1 = ((bf16[16,2,32,512]{3,2,1,0:T(8,128)(2,1)}), bf16[16,2,32,512]{3,2,1,0:T(8,128)(2,1)S(1)}, u32[]{:S(2)}, u32[]{:S(2)}) async-start(bf16[16,2,32,512]{3,2,1,0:T(8,128)(2,1)} %bitcast.6), calls=%async_computation.1 | async-start | bytes 2097152 | tf_op jit(solution)/shard_map/all_to_all | solution.py:165
  41.7 0.0 copy-start.1
  41.7 0.7 %copy-done.1 = s32[2,32]{1,0:T(2,128)S(1)} copy-done((s32[2,32]{1,0:T(2,128)S(1)}, s32[2,32]{1,0:T(2,128)}, u32[]{:S(2)}) %copy-start.1) | copy-done | bytes 280
  42.4 0.1 pad_add_fusion
  42.4 0.1 compare_select_fusion
  42.5 0.1 fusion.3
  42.6 0.1 pad_add_fusion.1.table_ref
  42.7 15.5 %all-to-all-done.1.far_ref = bf16[16,2,32,512]{3,2,1,0:T(8,128)(2,1)S(1)} async-done(((bf16[16,2,32,512]{3,2,1,0:T(8,128)(2,1)}), bf16[16,2,32,512]{3,2,1,0:T(8,128)(2,1)S(1)}, u32[]{:S(2)}, u32[]{:S(2)}) %all-to-all-start.1) | async-done | bytes 1048608 | tf_op jit(solution)/shard_map/all_to_all | solution.py:165
  58.2 3.1 %pairs.1 = f32[32,2,2,512]{3,2,1,0:T(2,128)} custom-call(s32[2,32]{1,0:T(2,128)S(1)} %pad_add_fusion.1.table_ref, bf16[16,2,32,512]{3,2,1,0:T(8,128)(2,1)S(1)} %all-to-all-done.near_ref, bf16[16,2,32,512]{3,2,1,0:T(8,128)(2,1)S(1)} %all-to-all-done.1.far_ref), custom_call_target="tpu_custom_call" | custom-call | tf_op jit(solution)/shard_map/pairs/pallas_call | solution.py:130
Async XLA Ops:
  1.1 8.2 %collective-permute-start = (bf16[512,256]{1,0:T(8,128)(2,1)S(1)}, bf16[512,256]{1,0:T(8,128)(2,1)S(1)}, u32[]{:S(2)}, u32[]{:S(2)}) collective-permute-start(bf16[512,256]{1,0:T(8,128)(2,1)S(1)} %get-tuple-element.13), channel_id=1, source_target_pairs={{0,1},{1,0},{2,3},{3,2},{4,5},{5,4},{6,7},{7,6},{8,9},{9,8},{10,11... | collective-permute-start | bytes 786440 | tf_op jit(solution)/shard_map/ppermute | solution.py:26
  3.2 14.8 %collective-permute-start.1 = (bf16[512,256]{1,0:T(8,128)(2,1)S(1)}, bf16[512,256]{1,0:T(8,128)(2,1)S(1)}, u32[]{:S(2)}, u32[]{:S(2)}) collective-permute-start(bf16[512,256]{1,0:T(8,128)(2,1)S(1)} %get-tuple-element.14.refs_0_), channel_id=1, source_target_pairs={{0,24},{1,25},{2,26},{3,27},{4,28},{5,29},{6,30},{7,31},{8,16},{9,... | collective-permute-start | bytes 786440 | tf_op jit(solution)/shard_map/ppermute | solution.py:26
  6.5 11.4 %collective-permute-start.2 = (bf16[512,256]{1,0:T(8,128)(2,1)S(1)}, bf16[512,256]{1,0:T(8,128)(2,1)S(1)}, u32[]{:S(2)}, u32[]{:S(2)}) collective-permute-start(bf16[512,256]{1,0:T(8,128)(2,1)S(1)} %get-tuple-element.13), channel_id=1, source_target_pairs={{0,25},{1,24},{2,27},{3,26},{4,29},{5,28},{6,31},{7,30},{8,17},{9,... | collective-permute-start | bytes 786440 | tf_op jit(solution)/shard_map/ppermute | solution.py:26
  6.5 2.7 %copy-start = (s32[512]{0:T(512)S(1)}, s32[512]{0:T(512)}, u32[]{:S(2)}) copy-start(s32[512]{0:T(512)} %param.5) | copy-start | bytes 6148
  11.7 22.8 %all-to-all-start = ((bf16[16,2,32,512]{3,2,1,0:T(8,128)(2,1)}), bf16[16,2,32,512]{3,2,1,0:T(8,128)(2,1)S(1)}, u32[]{:S(2)}, u32[]{:S(2)}) async-start(bf16[16,2,32,512]{3,2,1,0:T(8,128)(2,1)} %bitcast.5), calls=%async_computation | async-start | bytes 2097152 | tf_op jit(solution)/shard_map/all_to_all | solution.py:165
  34.5 23.7 %all-to-all-start.1 = ((bf16[16,2,32,512]{3,2,1,0:T(8,128)(2,1)}), bf16[16,2,32,512]{3,2,1,0:T(8,128)(2,1)S(1)}, u32[]{:S(2)}, u32[]{:S(2)}) async-start(bf16[16,2,32,512]{3,2,1,0:T(8,128)(2,1)} %bitcast.6), calls=%async_computation.1 | async-start | bytes 2097152 | tf_op jit(solution)/shard_map/all_to_all | solution.py:165
  41.7 0.7 %copy-start.1 = (s32[2,32]{1,0:T(2,128)S(1)}, s32[2,32]{1,0:T(2,128)}, u32[]{:S(2)}) copy-start(s32[2,32]{1,0:T(2,128)} %param.4) | copy-start | bytes 772

commit v16 on v15

--- a/solution.py
+++ b/solution.py
@@ -26,53 +26,117 @@
     return lax.ppermute(block, KA + GA, route)
 
 
-def field_kernel(count, place_ref, points_ref, *refs):
-    slab_refs, (out_ref, picked_ref) = refs[:count], refs[count:]
+def one_hot(points_ref, half, slab, slab_size, npoints):
+    first = pl.multiple_of(half * npoints, npoints)
+    wanted = points_ref[:, pl.ds(first, npoints)] - slab * slab_size
+    spot = lax.broadcasted_iota(jnp.int32, (slab_size, npoints), 0)
+    return (spot == wanted).astype(jnp.float32).astype(jnp.bfloat16)
+
+
+def pick(chosen, slab):
+    return lax.dot_general(
+        chosen, slab, (((0,), (0,)), ((), ())), preferred_element_type=jnp.float32
+    )
+
+
+def rotate(picked):
+    middle = picked.shape[1] // 2
+    return jnp.concatenate([-picked[:, middle:], picked[:, :middle]], axis=1)
+
+
+def product(rows, slab, groups):
+    out = lax.dot_general(
+        rows, slab, (((1,), (1,)), ((), ())), preferred_element_type=jnp.float32
+    )
+    return out.reshape(groups, -1, out.shape[1]).astype(jnp.bfloat16)
+
+
+def front_kernel(place_ref, points_ref, orbitals_ref, mine_ref, other_ref, picked_ref):
+    kdevice, slab_size, _ = orbitals_ref.shape
+    mine = place_ref[1] % SPLIT
+    mine_ref[...] = orbitals_ref[mine]
+    other_ref[...] = orbitals_ref[1 - mine]
+    chosen = one_hot(points_ref, place_ref[0], place_ref[1], slab_size, picked_ref.shape[1])
+    for k in range(kdevice):
+        picked_ref[k] = pick(chosen, orbitals_ref[k]).astype(jnp.bfloat16)
+
+
+def make_front(orbitals, points, place):
+    kdevice, slab_size, channels = orbitals.shape
+    vmem = pl.BlockSpec(memory_space=pltpu.VMEM)
+    slab = jax.ShapeDtypeStruct((slab_size, channels), jnp.bfloat16)
+    return pl.pallas_call(
+        front_kernel,
+        in_specs=[pl.BlockSpec(memory_space=pltpu.SMEM), vmem, vmem],
+        out_specs=[vmem] * 3,
+        out_shape=[
+            slab,
+            slab,
+            jax.ShapeDtypeStruct((kdevice, points.shape[1] // 2, channels), jnp.bfloat16),
+        ],
+        compiler_params=pltpu.CompilerParams(vmem_limit_bytes=VMEM_LIMIT),
+        name="front",
+    )(place, points, orbitals)
+
+
+def near_kernel(orbitals_ref, *refs):
+    *picked_refs, out_ref = refs
+    groups = out_ref.shape[0]
+    rows = sum(picked_ref[0].astype(jnp.float32) for picked_ref in picked_refs)
+    for part, turned in enumerate((rows, rotate(rows))):
+        out_ref[:, 0, part] = product(turned.astype(jnp.bfloat16), orbitals_ref[0], groups)
+
+
+def make_near(orbitals, shares, groups):
+    kdevice, slab_size, channels = orbitals.shape
+    npoints = shares[0].shape[1]
+    length = npoints // groups
+    return pl.pallas_call(
+        near_kernel,
+        grid=(kdevice,),
+        in_specs=[pl.BlockSpec((1, slab_size, channels), lambda k: (k, 0, 0))]
+        + [pl.BlockSpec((1, npoints, channels), lambda k: (k, 0, 0)) for _ in shares],
+        out_specs=pl.BlockSpec((groups, 1, 2, length, slab_size), lambda k: (0, k, 0, 0, 0)),
+        out_shape=jax.ShapeDtypeStruct((groups, kdevice, 2, length, slab_size), jnp.bfloat16),
+        cost_estimate=pl.CostEstimate(
+            flops=1_000_000_000, bytes_accessed=3_000_000, transcendentals=0
+        ),
+        compiler_params=pltpu.CompilerParams(vmem_limit_bytes=VMEM_LIMIT),
+        name="near",
+    )(orbitals, *shares)
+
+
+def far_kernel(place_ref, points_ref, *refs):
+    *slab_refs, out_ref, picked_ref = refs
     slab_size, channels = slab_refs[0].shape
     npoints = points_ref.shape[1] // 2
-    middle = channels // 2
-    groups, _, _, length, _ = out_ref.shape
+    groups = out_ref.shape[0]
     step = pl.program_id(0)
 
     @pl.when(step == 0)
     def _():
-        first = pl.multiple_of(place_ref[0] * npoints, npoints)
-        wanted = points_ref[:, pl.ds(first, npoints)]
-        spot = lax.broadcasted_iota(jnp.int32, (slab_size, npoints), 0)
         picked = jnp.zeros((npoints, channels), jnp.float32)
         for number, slab_ref in enumerate(slab_refs):
-            chosen = spot == wanted - (place_ref[1] ^ number) * slab_size
-            picked += lax.dot_general(
-                chosen.astype(jnp.float32).astype(jnp.bfloat16),
-                slab_ref[...],
-                (((0,), (0,)), ((), ())),
-                preferred_element_type=jnp.float32,
-            )
-        rotated = jnp.concatenate([-picked[:, middle:], picked[:, :middle]], axis=1)
+            slab = place_ref[1] ^ number
+            chosen = one_hot(points_ref, place_ref[0], slab, slab_size, npoints)
+            picked += pick(chosen, slab_ref[...])
         picked_ref[0] = picked.astype(jnp.bfloat16)
-        picked_ref[1] = rotated.astype(jnp.bfloat16)
+        picked_ref[1] = rotate(picked).astype(jnp.bfloat16)
 
     for number in range(SPLIT):
 
         @pl.when(step == number)
         def _(number=number):
             for part in range(2):
-                product = lax.dot_general(
-                    picked_ref[part],
-                    slab_refs[number][...],
-                    (((1,), (1,)), ((), ())),
-                    preferred_element_type=jnp.float32,
-                )
-                pieces = product.reshape(groups, length, slab_size)
-                out_ref[:, 0, part] = pieces.astype(jnp.bfloat16)
-
-
-def make_fields(slabs, points, groups, place, work):
+                out_ref[:, 0, part] = product(picked_ref[part], slab_refs[number][...], groups)
+
+
+def make_far(slabs, points, groups, place):
     slab_size, channels = slabs[0].shape
     npoints = points.shape[1] // 2
     length = npoints // groups
     return pl.pallas_call(
-        functools.partial(field_kernel, len(slabs)),
+        far_kernel,
         grid_spec=pltpu.PrefetchScalarGridSpec(
             num_scalar_prefetch=1,
             grid=(SPLIT,),
@@ -86,10 +150,10 @@
         ),
         out_shape=jax.ShapeDtypeStruct((groups, SPLIT, 2, length, slab_size), jnp.bfloat16),
         cost_estimate=pl.CostEstimate(
-            flops=work * 1_000_000_000, bytes_accessed=work * 3_000_000, transcendentals=0
-        ),
-        compiler_params=pltpu.CompilerParams(vmem_limit_bytes=VMEM_LIMIT),
-        name="fields",
+            flops=60_000_000_000, bytes_accessed=180_000_000, transcendentals=0
+        ),
+        compiler_params=pltpu.CompilerParams(vmem_limit_bytes=VMEM_LIMIT),
+        name="far",
     )(place, points, *slabs)
 
 
@@ -146,31 +210,25 @@
     kdevice, slab_size, channels = orbitals.shape
     half = lax.axis_index("half")
     groups = lax.axis_size("quarter") * lax.axis_size("inner")
+    slabs = lax.axis_size("hi") * lax.axis_size("lo")
     total_k = 2 * groups * kdevice
-
-    lo = lax.axis_index("lo")
-    slabs = lax.axis_size("hi") * SPLIT
-    mine = lax.dynamic_index_in_dim(orbitals, lo, 0, keepdims=False)
-    other = lax.dynamic_index_in_dim(orbitals, 1 - lo, 0, keepdims=False)
-    near = [mine] + [swap(other if x & 1 else mine, False, x) for x in range(1, slabs)]
+    points = points.reshape(1, -1)
+    place = jnp.stack([half, lax.axis_index("hi") * SPLIT + lax.axis_index("lo")])
+
+    mine, other, share = make_front(orbitals, points, place)
+    shares = [share] + [swap(share, False, x) for x in range(1, slabs)]
     far = [swap(other if x & 1 else mine, True, x) for x in range(slabs)]
 
-    points = points.reshape(1, -1)
-    place = jnp.stack([half, lax.axis_index("hi") * SPLIT + lo])
-
-    def flat(fields):
-        return fields.reshape((groups * SPLIT,) + fields.shape[2:])
-
-    def share(fields):
-        return lax.all_to_all(
-            fields, ("quarter", "inner", "lo"), split_axis=0, concat_axis=0, tiled=True
-        )
-
-    near_fields = flat(make_fields(near, points, groups, place, 1))
+    def send(fields, around):
+        fields = fields.reshape((-1,) + fields.shape[-3:])
+        return lax.all_to_all(fields, around, split_axis=0, concat_axis=0, tiled=True)
+
+    near_fields = make_near(orbitals, shares, groups)
     near_fields, points = lax.optimization_barrier((near_fields, points))
-    far_fields = flat(make_fields(far, points, groups, place, 60))
-    near_fields, far_fields = lax.optimization_barrier((share(near_fields), far_fields))
-    far_fields = share(far_fields)
+    far_fields = make_far(far, points, groups, place)
+    near_fields = send(near_fields, ("quarter", "inner"))
+    near_fields, far_fields = lax.optimization_barrier((near_fields, far_fields))
+    far_fields = send(far_fields, ("quarter", "inner", "lo"))
 
     def mirrored(kpoints):
         return total_k // 2 + (kpoints + total_k // 4) % (total_k // 2)

time: 61.7 us -> 57.5 us (0.932)
  starting transfers between devices: 18.9 us -> 16.5 us
  waiting for transfers between devices: 32.2 us -> 29.9 us
    all_to_all x2, waiting for transfers between devices: 29.6 us -> 25.3 us  [send(): lax.all_to_all(fields, around, split_axis=0, concat_axis=0, tiled=True)]
    all_to_all x2, starting transfers between devices: 13.4 us -> 11.1 us  [send(): lax.all_to_all(fields, around, split_axis=0, concat_axis=0, tiled=True)]
    ppermute x3, waiting for transfers between devices: 2.63 us -> 4.6 us  [swap(): return lax.ppermute(block, KA + GA, route)]
    unnamed x4 -> x8, local copies, waits for them, and re-layouts: 0.67 us -> 2.32 us
    squeeze x1 -> x0, local copies, waits for them, and re-layouts: 1.06 us -> none  [on_device(): other = lax.dynamic_index_in_dim(orbitals, 1 - lo, 0, keepdims=False)]
    pallas_call x2 -> x3, Pallas kernels: 5 us -> 4.9 us  [the longest x1 2.49 us: make_far(): pl.pallas_call(far_kernel, grid_spec=pltpu.PrefetchScalarGridSpec(num_sca...]
  transfers between devices with their start and end apart: 5 -> 5, of which waited for: 3 -> 4; matrix products, arithmetic and copies ran while one was open for 1% -> 1% of each run, Pallas kernels for 8% -> 7%
where the time goes in v16:
time: 57.5 us; the launch traced here: 57.2 us
  waiting for transfers between devices  29.9 us (52%)
  starting transfers between devices  16.5 us (29%)
  Pallas kernels  8.01 us (14%)
  local copies, waits for them, and re-layouts  2.4 us (4%)
    all_to_all x2, waiting for transfers between devices, send(): lax.all_to_all(fields, around, split_axis=0, concat_axis=0, tiled=True)  25.3 us
    all_to_all x2, starting transfers between devices, send(): lax.all_to_all(fields, around, split_axis=0, concat_axis=0, tiled=True)  11.1 us
    ppermute x3, starting transfers between devices, swap(): return lax.ppermute(block, KA + GA, route)  5.46 us
    ppermute x3, waiting for transfers between devices, swap(): return lax.ppermute(block, KA + GA, route)  4.6 us
    pallas_call x1, Pallas kernels, make_pairs(): pl.pallas_call(functools.partial(pair_kernel, 1.0 / math.sqrt(2 * half_k)...  3.12 us
    pallas_call x1, Pallas kernels, make_far(): pl.pallas_call(far_kernel, grid_spec=pltpu.PrefetchScalarGridSpec(num_sca...  2.49 us
    unnamed x8, local copies, waits for them, and re-layouts  2.32 us
    pallas_call x1, Pallas kernels, make_near(): pl.pallas_call(near_kernel, grid=(kdevice,), in_specs=[pl.BlockSpec((1, s...  1.53 us
  transfers between devices with their start and end apart: 5, of which 4 were waited for; matrix products, arithmetic and copies ran while one was open for 1% of the time, Pallas kernels for 7%

profile of v16, /device:TPU:1, one launch (start us, length us, event | category | flops | bytes accessed | tf_op | source)
XLA Modules:
  0.0 57.2 jit_solution(12463903654073518459)
XLA Ops:
  0.0 0.0 copy-start.2
  0.0 0.1 pad_add_fusion.2.place_ref
  0.1 0.6 %copy-done.2 = s32[512]{0:T(512)S(1)} copy-done((s32[512]{0:T(512)S(1)}, s32[512]{0:T(512)}, u32[]{:S(2)}) %copy-start.2) | copy-done | bytes 2072
  0.7 0.0 copy-start
  0.7 1.0 %copy-done = bf16[2,512,256]{2,1,0:T(8,128)(2,1)S(1)} copy-done((bf16[2,512,256]{2,1,0:T(8,128)(2,1)S(1)}, bf16[2,512,256]{2,1,0:T(8,128)(2,1)}, u32[]{:S(2)}) %copy-start) | copy-done | bytes 524312
  1.7 0.0 copy-start.1
  1.7 0.9 %front.1 = (bf16[512,256]{1,0:T(8,128)(2,1)S(1)}, bf16[512,256]{1,0:T(8,128)(2,1)S(1)}, bf16[2,256,256]{2,1,0:T(8,128)(2,1)S(1)}) custom-call(s32[2]{0:T(128)S(1)} %pad_add_fusion.2.place_ref, s32[1,512]{1,0:T(1,128)S(1)} %bitcast.6, bf16[2,512,256]{2,1,0:T(8,128)(2,1)S(1)} %copy-done), custom_call_target="tpu_custom_call" | custom-call | tf_op jit(solution)/shard_map/front/pallas_call | solution.py:68
  2.6 2.1 %collective-permute-start = (bf16[2,256,256]{2,1,0:T(8,128)(2,1)S(1)}, bf16[2,256,256]{2,1,0:T(8,128)(2,1)S(1)}, u32[]{:S(2)}, u32[]{:S(2)}) collective-permute-start(bf16[2,256,256]{2,1,0:T(8,128)(2,1)S(1)} %get-tuple-element.12.refs_0_), channel_id=1, source_target_pairs={{0,1},{1,0},{2,3},{3,2},{4,5},{5,4},{6,7},{7,6},{8,9},{9,8},{10,11... | collective-permute-start | bytes 786440 | tf_op jit(solution)/shard_map/ppermute | solution.py:26
  4.7 3.3 %collective-permute-start.1 = (bf16[512,256]{1,0:T(8,128)(2,1)S(1)}, bf16[512,256]{1,0:T(8,128)(2,1)S(1)}, u32[]{:S(2)}, u32[]{:S(2)}) collective-permute-start(bf16[512,256]{1,0:T(8,128)(2,1)S(1)} %get-tuple-element.15), channel_id=1, source_target_pairs={{0,24},{1,25},{2,26},{3,27},{4,28},{5,29},{6,30},{7,31},{8,16},{9,... | collective-permute-start | bytes 786440 | tf_op jit(solution)/shard_map/ppermute | solution.py:26
  8.1 0.0 collective-permute-start.2
  8.1 2.7 %collective-permute-done.refs_1_ = bf16[2,256,256]{2,1,0:T(8,128)(2,1)S(1)} collective-permute-done((bf16[2,256,256]{2,1,0:T(8,128)(2,1)S(1)}, bf16[2,256,256]{2,1,0:T(8,128)(2,1)S(1)}, u32[]{:S(2)}, u32[]{:S(2)}) %collective-permute-start) | collective-permute-done | bytes 262176 | tf_op jit(solution)/shard_map/ppermute | solution.py:26
  10.8 0.0 copy-done.1
  10.8 1.5 %near.1 = bf16[8,2,2,32,512]{4,3,2,1,0:T(8,128)(2,1)} custom-call(bf16[2,512,256]{2,1,0:T(8,128)(2,1)S(1)} %copy-done.1, bf16[2,256,256]{2,1,0:T(8,128)(2,1)S(1)} %get-tuple-element.12.refs_0_, bf16[2,256,256]{2,1,0:T(8,128)(2,1)S(1)} %collective-permute-done.refs_1_), custom_call_target="tpu_custom_call" | custom-call | flops 1000000000 | bytes 3000000 | tf_op jit(solution)/shard_map/near/pallas_call | solution.py:94
  12.3 5.2 %all-to-all-start = ((bf16[16,2,32,512]{3,2,1,0:T(8,128)(2,1)}), bf16[16,2,32,512]{3,2,1,0:T(8,128)(2,1)S(1)}, u32[]{:S(2)}, u32[]{:S(2)}) async-start(bf16[16,2,32,512]{3,2,1,0:T(8,128)(2,1)} %bitcast.3), calls=%async_computation | async-start | bytes 2097152 | tf_op jit(solution)/shard_map/all_to_all | solution.py:224
  17.5 0.0 collective-permute-done.1.refs_0_
  17.5 1.9 %collective-permute-done.2.refs_1_ = bf16[512,256]{1,0:T(8,128)(2,1)S(1)} collective-permute-done((bf16[512,256]{1,0:T(8,128)(2,1)S(1)}, bf16[512,256]{1,0:T(8,128)(2,1)S(1)}, u32[]{:S(2)}, u32[]{:S(2)}) %collective-permute-start.2) | collective-permute-done | bytes 262176 | tf_op jit(solution)/shard_map/ppermute | solution.py:26
  19.4 2.5 %far.1 = bf16[8,2,2,32,512]{4,3,2,1,0:T(8,128)(2,1)} custom-call(s32[2]{0:T(128)S(1)} %pad_add_fusion.2.place_ref, s32[1,512]{1,0:T(1,128)S(1)} %bitcast.7, bf16[512,256]{1,0:T(8,128)(2,1)S(1)} %collective-permute-done.1.refs_0_, bf16[512,256]{1,0:T(8,128)(2,1)S(1)} %collective-permute-done.2.refs_1_), custom_call_target="tpu_custom_call" | custom-call | flops 60000002048 | bytes 180000000 | tf_op jit(solution)/shard_map/far/pallas_call | solution.py:138
  21.9 9.7 %all-to-all-done.near_ref = bf16[16,2,32,512]{3,2,1,0:T(8,128)(2,1)S(1)} async-done(((bf16[16,2,32,512]{3,2,1,0:T(8,128)(2,1)}), bf16[16,2,32,512]{3,2,1,0:T(8,128)(2,1)S(1)}, u32[]{:S(2)}, u32[]{:S(2)}) %all-to-all-start) | async-done | bytes 1048608 | tf_op jit(solution)/shard_map/all_to_all | solution.py:224
  31.7 5.9 %all-to-all-start.1 = ((bf16[16,2,32,512]{3,2,1,0:T(8,128)(2,1)}), bf16[16,2,32,512]{3,2,1,0:T(8,128)(2,1)S(1)}, u32[]{:S(2)}, u32[]{:S(2)}) async-start(bf16[16,2,32,512]{3,2,1,0:T(8,128)(2,1)} %bitcast.4), calls=%async_computation.1 | async-start | bytes 2097152 | tf_op jit(solution)/shard_map/all_to_all | solution.py:224
  37.5 0.0 copy-start.3
  37.5 0.7 %copy-done.3 = s32[2,32]{1,0:T(2,128)S(1)} copy-done((s32[2,32]{1,0:T(2,128)S(1)}, s32[2,32]{1,0:T(2,128)}, u32[]{:S(2)}) %copy-start.3) | copy-done | bytes 280
  38.2 0.1 pad_add_fusion
  38.3 0.1 compare_select_fusion
  38.4 0.1 fusion.3
  38.4 0.1 pad_add_fusion.1.table_ref
  38.5 15.5 %all-to-all-done.1.far_ref = bf16[16,2,32,512]{3,2,1,0:T(8,128)(2,1)S(1)} async-done(((bf16[16,2,32,512]{3,2,1,0:T(8,128)(2,1)}), bf16[16,2,32,512]{3,2,1,0:T(8,128)(2,1)S(1)}, u32[]{:S(2)}, u32[]{:S(2)}) %all-to-all-start.1) | async-done | bytes 1048608 | tf_op jit(solution)/shard_map/all_to_all | solution.py:224
  54.1 3.1 %pairs.1 = f32[32,2,2,512]{3,2,1,0:T(2,128)} custom-call(s32[2,32]{1,0:T(2,128)S(1)} %pad_add_fusion.1.table_ref, bf16[16,2,32,512]{3,2,1,0:T(8,128)(2,1)S(1)} %all-to-all-done.near_ref, bf16[16,2,32,512]{3,2,1,0:T(8,128)(2,1)S(1)} %all-to-all-done.1.far_ref), custom_call_target="tpu_custom_call" | custom-call | tf_op jit(solution)/shard_map/pairs/pallas_call | solution.py:194
Async XLA Ops:
  0.0 0.7 %copy-start.2 = (s32[512]{0:T(512)S(1)}, s32[512]{0:T(512)}, u32[]{:S(2)}) copy-start(s32[512]{0:T(512)} %param.5) | copy-start | bytes 6148
  0.7 1.0 %copy-start = (bf16[2,512,256]{2,1,0:T(8,128)(2,1)S(1)}, bf16[2,512,256]{2,1,0:T(8,128)(2,1)}, u32[]{:S(2)}) copy-start(bf16[2,512,256]{2,1,0:T(8,128)(2,1)} %orbitals_ref.3) | copy-start | bytes 1572868
  1.7 9.1 %copy-start.1 = (bf16[2,512,256]{2,1,0:T(8,128)(2,1)S(1)}, bf16[2,512,256]{2,1,0:T(8,128)(2,1)}, u32[]{:S(2)}) copy-start(bf16[2,512,256]{2,1,0:T(8,128)(2,1)} %orbitals_ref.3) | copy-start | bytes 1572868
  2.6 8.2 %collective-permute-start = (bf16[2,256,256]{2,1,0:T(8,128)(2,1)S(1)}, bf16[2,256,256]{2,1,0:T(8,128)(2,1)S(1)}, u32[]{:S(2)}, u32[]{:S(2)}) collective-permute-start(bf16[2,256,256]{2,1,0:T(8,128)(2,1)S(1)} %get-tuple-element.12.refs_0_), channel_id=1, source_target_pairs={{0,1},{1,0},{2,3},{3,2},{4,5},{5,4},{6,7},{7,6},{8,9},{9,8},{10,11... | collective-permute-start | bytes 786440 | tf_op jit(solution)/shard_map/ppermute | solution.py:26
  4.7 12.8 %collective-permute-start.1 = (bf16[512,256]{1,0:T(8,128)(2,1)S(1)}, bf16[512,256]{1,0:T(8,128)(2,1)S(1)}, u32[]{:S(2)}, u32[]{:S(2)}) collective-permute-start(bf16[512,256]{1,0:T(8,128)(2,1)S(1)} %get-tuple-element.15), channel_id=1, source_target_pairs={{0,24},{1,25},{2,26},{3,27},{4,28},{5,29},{6,30},{7,31},{8,16},{9,... | collective-permute-start | bytes 786440 | tf_op jit(solution)/shard_map/ppermute | solution.py:26
  8.1 11.4 %collective-permute-start.2 = (bf16[512,256]{1,0:T(8,128)(2,1)S(1)}, bf16[512,256]{1,0:T(8,128)(2,1)S(1)}, u32[]{:S(2)}, u32[]{:S(2)}) collective-permute-start(bf16[512,256]{1,0:T(8,128)(2,1)S(1)} %get-tuple-element.16), channel_id=1, source_target_pairs={{0,25},{1,24},{2,27},{3,26},{4,29},{5,28},{6,31},{7,30},{8,17},{9,... | collective-permute-start | bytes 786440 | tf_op jit(solution)/shard_map/ppermute | solution.py:26
  12.3 19.4 %all-to-all-start = ((bf16[16,2,32,512]{3,2,1,0:T(8,128)(2,1)}), bf16[16,2,32,512]{3,2,1,0:T(8,128)(2,1)S(1)}, u32[]{:S(2)}, u32[]{:S(2)}) async-start(bf16[16,2,32,512]{3,2,1,0:T(8,128)(2,1)} %bitcast.3), calls=%async_computation | async-start | bytes 2097152 | tf_op jit(solution)/shard_map/all_to_all | solution.py:224
  31.7 22.4 %all-to-all-start.1 = ((bf16[16,2,32,512]{3,2,1,0:T(8,128)(2,1)}), bf16[16,2,32,512]{3,2,1,0:T(8,128)(2,1)S(1)}, u32[]{:S(2)}, u32[]{:S(2)}) async-start(bf16[16,2,32,512]{3,2,1,0:T(8,128)(2,1)} %bitcast.4), calls=%async_computation.1 | async-start | bytes 2097152 | tf_op jit(solution)/shard_map/all_to_all | solution.py:224
  37.5 0.7 %copy-start.3 = (s32[2,32]{1,0:T(2,128)S(1)}, s32[2,32]{1,0:T(2,128)}, u32[]{:S(2)}) copy-start(s32[2,32]{1,0:T(2,128)} %param.4) | copy-start | bytes 772

commit v17 on v16

--- a/solution.py
+++ b/solution.py
@@ -157,50 +157,57 @@
     )(place, points, *slabs)
 
 
-def pair_kernel(scale, table_ref, near_ref, far_ref, out_ref, held_ref):
+def pair_kernel(scale, table_ref, near_ref, far_ref, out_ref, held_ref, sums_ref, sems):
     total_k, _, length, width = held_ref.shape
     transfers = table_ref.shape[0]
     held_ref[: total_k // 2] = near_ref[...].astype(jnp.float32)
     held_ref[total_k // 2 :] = far_ref[...].astype(jnp.float32)
 
-    def load(k, part, start, count):
-        return held_ref[k, part, pl.ds(start, count), :]
-
-    count = min(16, length)
+    count, columns = min(16, length), min(256, width)
+    copies = []
     for start in range(0, length, count):
-
-        def step(k, sums):
-            real, imag = load(k, 0, start, count), load(k, 1, start, count)
-            after = []
-            for transfer in range(transfers):
-                other = table_ref[transfer, k]
-                other_real = load(other, 0, start, count)
-                other_imag = load(other, 1, start, count)
-                after.append(sums[2 * transfer] + (real * other_real + imag * other_imag))
-                after.append(sums[2 * transfer + 1] + (imag * other_real - real * other_imag))
-            return tuple(after)
-
-        zero = jnp.zeros((count, width), jnp.float32)
-        sums = lax.fori_loop(0, total_k, step, (zero,) * (2 * transfers), unroll=4)
-        for place, value in enumerate(sums):
-            out_ref[pl.ds(start, count), place // 2, place % 2, :] = value * scale
+        rows = pl.ds(start, count)
+        for column in range(0, width, columns):
+            lanes = pl.ds(column, columns)
+
+            def step(k, sums):
+                real, imag = held_ref[k, 0, rows, lanes], held_ref[k, 1, rows, lanes]
+                after = []
+                for transfer in range(transfers):
+                    other = table_ref[transfer, k]
+                    other_real = held_ref[other, 0, rows, lanes]
+                    other_imag = held_ref[other, 1, rows, lanes]
+                    after.append(sums[2 * transfer] + (real * other_real + imag * other_imag))
+                    after.append(sums[2 * transfer + 1] + (imag * other_real - real * other_imag))
+                return tuple(after)
+
+            zero = jnp.zeros((count, columns), jnp.float32)
+            sums = lax.fori_loop(0, total_k, step, (zero,) * (2 * transfers), unroll=4)
+            for place, value in enumerate(sums):
+                sums_ref[rows, place // 2, place % 2, lanes] = value * scale
+        copies.append(
+            pltpu.make_async_copy(sums_ref.at[rows], out_ref.at[rows], sems.at[start // count])
+        )
+        copies[-1].start()
+    for copy in copies:
+        copy.wait()
 
 
 def make_pairs(near, far, table):
     half_k, _, length, slab_size = near.shape
     transfers = table.shape[0]
-    width = 256
-    fields = pl.BlockSpec((half_k, 2, length, width), lambda r, table: (0, 0, 0, r))
+    out = jax.ShapeDtypeStruct((length, transfers, 2, slab_size), jnp.float32)
+    vmem = pl.BlockSpec(memory_space=pltpu.VMEM)
     return pl.pallas_call(
         functools.partial(pair_kernel, 1.0 / math.sqrt(2 * half_k)),
-        grid_spec=pltpu.PrefetchScalarGridSpec(
-            num_scalar_prefetch=1,
-            grid=(slab_size // width,),
-            in_specs=[fields, fields],
-            out_specs=pl.BlockSpec((length, transfers, 2, width), lambda r, table: (0, 0, 0, r)),
-            scratch_shapes=[pltpu.VMEM((2 * half_k, 2, length, width), jnp.float32)],
-        ),
-        out_shape=jax.ShapeDtypeStruct((length, transfers, 2, slab_size), jnp.float32),
+        in_specs=[pl.BlockSpec(memory_space=pltpu.SMEM), vmem, vmem],
+        out_specs=pl.BlockSpec(memory_space=pl.ANY),
+        out_shape=out,
+        scratch_shapes=[
+            pltpu.VMEM((2 * half_k, 2, length, slab_size), jnp.float32),
+            pltpu.VMEM(out.shape, jnp.float32),
+            pltpu.SemaphoreType.DMA((length // min(16, length),)),
+        ],
         compiler_params=pltpu.CompilerParams(vmem_limit_bytes=VMEM_LIMIT),
         name="pairs",
     )(table, near, far)

time: 57.5 us -> 57.4 us (level)
  no operation moved by 1% of the time
where the time goes in v17:
time: 57.4 us; the launch traced here: 57 us
  waiting for transfers between devices  29.9 us (52%)
  starting transfers between devices  16.5 us (29%)
  Pallas kernels  7.86 us (14%)
  local copies, waits for them, and re-layouts  2.4 us (4%)
    all_to_all x2, waiting for transfers between devices, send(): lax.all_to_all(fields, around, split_axis=0, concat_axis=0, tiled=True)  25.3 us
    all_to_all x2, starting transfers between devices, send(): lax.all_to_all(fields, around, split_axis=0, concat_axis=0, tiled=True)  11.1 us
    ppermute x3, starting transfers between devices, swap(): return lax.ppermute(block, KA + GA, route)  5.46 us
    ppermute x3, waiting for transfers between devices, swap(): return lax.ppermute(block, KA + GA, route)  4.6 us
    pallas_call x1, Pallas kernels, make_pairs(): pl.pallas_call(functools.partial(pair_kernel, 1.0 / math.sqrt(2 * half_k)...  2.96 us
    pallas_call x1, Pallas kernels, make_far(): pl.pallas_call(far_kernel, grid_spec=pltpu.PrefetchScalarGridSpec(num_sca...  2.49 us
    unnamed x8, local copies, waits for them, and re-layouts  2.32 us
    pallas_call x1, Pallas kernels, make_near(): pl.pallas_call(near_kernel, grid=(kdevice,), in_specs=[pl.BlockSpec((1, s...  1.53 us
  transfers between devices with their start and end apart: 5, of which 4 were waited for; matrix products, arithmetic and copies ran while one was open for 1% of the time, Pallas kernels for 7%

profile of v17, /device:TPU:1, one launch (start us, length us, event | category | flops | bytes accessed | tf_op | source)
XLA Modules:
  0.0 57.0 jit_solution(89871052669089570)
XLA Ops:
  0.0 0.0 copy-start.2
  0.0 0.1 pad_add_fusion.2.place_ref
  0.1 0.6 %copy-done.2 = s32[512]{0:T(512)S(1)} copy-done((s32[512]{0:T(512)S(1)}, s32[512]{0:T(512)}, u32[]{:S(2)}) %copy-start.2) | copy-done | bytes 2072
  0.7 0.0 copy-start
  0.7 1.0 %copy-done = bf16[2,512,256]{2,1,0:T(8,128)(2,1)S(1)} copy-done((bf16[2,512,256]{2,1,0:T(8,128)(2,1)S(1)}, bf16[2,512,256]{2,1,0:T(8,128)(2,1)}, u32[]{:S(2)}) %copy-start) | copy-done | bytes 524312
  1.7 0.0 copy-start.1
  1.7 0.9 %front.1 = (bf16[512,256]{1,0:T(8,128)(2,1)S(1)}, bf16[512,256]{1,0:T(8,128)(2,1)S(1)}, bf16[2,256,256]{2,1,0:T(8,128)(2,1)S(1)}) custom-call(s32[2]{0:T(128)S(1)} %pad_add_fusion.2.place_ref, s32[1,512]{1,0:T(1,128)S(1)} %bitcast.6, bf16[2,512,256]{2,1,0:T(8,128)(2,1)S(1)} %copy-done), custom_call_target="tpu_custom_call" | custom-call | tf_op jit(solution)/shard_map/front/pallas_call | solution.py:68
  2.6 2.1 %collective-permute-start = (bf16[2,256,256]{2,1,0:T(8,128)(2,1)S(1)}, bf16[2,256,256]{2,1,0:T(8,128)(2,1)S(1)}, u32[]{:S(2)}, u32[]{:S(2)}) collective-permute-start(bf16[2,256,256]{2,1,0:T(8,128)(2,1)S(1)} %get-tuple-element.12.refs_0_), channel_id=1, source_target_pairs={{0,1},{1,0},{2,3},{3,2},{4,5},{5,4},{6,7},{7,6},{8,9},{9,8},{10,11... | collective-permute-start | bytes 786440 | tf_op jit(solution)/shard_map/ppermute | solution.py:26
  4.7 3.3 %collective-permute-start.1 = (bf16[512,256]{1,0:T(8,128)(2,1)S(1)}, bf16[512,256]{1,0:T(8,128)(2,1)S(1)}, u32[]{:S(2)}, u32[]{:S(2)}) collective-permute-start(bf16[512,256]{1,0:T(8,128)(2,1)S(1)} %get-tuple-element.15), channel_id=1, source_target_pairs={{0,24},{1,25},{2,26},{3,27},{4,28},{5,29},{6,30},{7,31},{8,16},{9,... | collective-permute-start | bytes 786440 | tf_op jit(solution)/shard_map/ppermute | solution.py:26
  8.1 0.0 collective-permute-start.2
  8.1 2.7 %collective-permute-done.refs_1_ = bf16[2,256,256]{2,1,0:T(8,128)(2,1)S(1)} collective-permute-done((bf16[2,256,256]{2,1,0:T(8,128)(2,1)S(1)}, bf16[2,256,256]{2,1,0:T(8,128)(2,1)S(1)}, u32[]{:S(2)}, u32[]{:S(2)}) %collective-permute-start) | collective-permute-done | bytes 262176 | tf_op jit(solution)/shard_map/ppermute | solution.py:26
  10.8 0.0 copy-done.1
  10.8 1.5 %near.1 = bf16[8,2,2,32,512]{4,3,2,1,0:T(8,128)(2,1)} custom-call(bf16[2,512,256]{2,1,0:T(8,128)(2,1)S(1)} %copy-done.1, bf16[2,256,256]{2,1,0:T(8,128)(2,1)S(1)} %get-tuple-element.12.refs_0_, bf16[2,256,256]{2,1,0:T(8,128)(2,1)S(1)} %collective-permute-done.refs_1_), custom_call_target="tpu_custom_call" | custom-call | flops 1000000000 | bytes 3000000 | tf_op jit(solution)/shard_map/near/pallas_call | solution.py:94
  12.3 5.2 %all-to-all-start = ((bf16[16,2,32,512]{3,2,1,0:T(8,128)(2,1)}), bf16[16,2,32,512]{3,2,1,0:T(8,128)(2,1)S(1)}, u32[]{:S(2)}, u32[]{:S(2)}) async-start(bf16[16,2,32,512]{3,2,1,0:T(8,128)(2,1)} %bitcast.3), calls=%async_computation | async-start | bytes 2097152 | tf_op jit(solution)/shard_map/all_to_all | solution.py:231
  17.5 0.0 collective-permute-done.1.refs_0_
  17.5 1.9 %collective-permute-done.2.refs_1_ = bf16[512,256]{1,0:T(8,128)(2,1)S(1)} collective-permute-done((bf16[512,256]{1,0:T(8,128)(2,1)S(1)}, bf16[512,256]{1,0:T(8,128)(2,1)S(1)}, u32[]{:S(2)}, u32[]{:S(2)}) %collective-permute-start.2) | collective-permute-done | bytes 262176 | tf_op jit(solution)/shard_map/ppermute | solution.py:26
  19.4 2.5 %far.1 = bf16[8,2,2,32,512]{4,3,2,1,0:T(8,128)(2,1)} custom-call(s32[2]{0:T(128)S(1)} %pad_add_fusion.2.place_ref, s32[1,512]{1,0:T(1,128)S(1)} %bitcast.7, bf16[512,256]{1,0:T(8,128)(2,1)S(1)} %collective-permute-done.1.refs_0_, bf16[512,256]{1,0:T(8,128)(2,1)S(1)} %collective-permute-done.2.refs_1_), custom_call_target="tpu_custom_call" | custom-call | flops 60000002048 | bytes 180000000 | tf_op jit(solution)/shard_map/far/pallas_call | solution.py:138
  21.9 9.7 %all-to-all-done.near_ref = bf16[16,2,32,512]{3,2,1,0:T(8,128)(2,1)S(1)} async-done(((bf16[16,2,32,512]{3,2,1,0:T(8,128)(2,1)}), bf16[16,2,32,512]{3,2,1,0:T(8,128)(2,1)S(1)}, u32[]{:S(2)}, u32[]{:S(2)}) %all-to-all-start) | async-done | bytes 1048608 | tf_op jit(solution)/shard_map/all_to_all | solution.py:231
  31.7 5.9 %all-to-all-start.1 = ((bf16[16,2,32,512]{3,2,1,0:T(8,128)(2,1)}), bf16[16,2,32,512]{3,2,1,0:T(8,128)(2,1)S(1)}, u32[]{:S(2)}, u32[]{:S(2)}) async-start(bf16[16,2,32,512]{3,2,1,0:T(8,128)(2,1)} %bitcast.4), calls=%async_computation.1 | async-start | bytes 2097152 | tf_op jit(solution)/shard_map/all_to_all | solution.py:231
  37.5 0.0 copy-start.3
  37.5 0.7 %copy-done.3 = s32[2,32]{1,0:T(2,128)S(1)} copy-done((s32[2,32]{1,0:T(2,128)S(1)}, s32[2,32]{1,0:T(2,128)}, u32[]{:S(2)}) %copy-start.3) | copy-done | bytes 280
  38.2 0.1 pad_add_fusion
  38.3 0.1 compare_select_fusion
  38.4 0.1 fusion.3
  38.4 0.1 pad_add_fusion.1.table_ref
  38.5 15.5 %all-to-all-done.1.far_ref = bf16[16,2,32,512]{3,2,1,0:T(8,128)(2,1)S(1)} async-done(((bf16[16,2,32,512]{3,2,1,0:T(8,128)(2,1)}), bf16[16,2,32,512]{3,2,1,0:T(8,128)(2,1)S(1)}, u32[]{:S(2)}, u32[]{:S(2)}) %all-to-all-start.1) | async-done | bytes 1048608 | tf_op jit(solution)/shard_map/all_to_all | solution.py:231
  54.1 3.0 %pairs.1 = f32[32,2,2,512]{3,2,1,0:T(2,128)} custom-call(s32[2,32]{1,0:T(2,128)S(1)} %pad_add_fusion.1.table_ref, bf16[16,2,32,512]{3,2,1,0:T(8,128)(2,1)S(1)} %all-to-all-done.near_ref, bf16[16,2,32,512]{3,2,1,0:T(8,128)(2,1)S(1)} %all-to-all-done.1.far_ref), custom_call_target="tpu_custom_call" | custom-call | tf_op jit(solution)/shard_map/pairs/pallas_call | solution.py:201
Async XLA Ops:
  0.0 0.7 %copy-start.2 = (s32[512]{0:T(512)S(1)}, s32[512]{0:T(512)}, u32[]{:S(2)}) copy-start(s32[512]{0:T(512)} %param.5) | copy-start | bytes 6148
  0.7 1.0 %copy-start = (bf16[2,512,256]{2,1,0:T(8,128)(2,1)S(1)}, bf16[2,512,256]{2,1,0:T(8,128)(2,1)}, u32[]{:S(2)}) copy-start(bf16[2,512,256]{2,1,0:T(8,128)(2,1)} %orbitals_ref.3) | copy-start | bytes 1572868
  1.7 9.1 %copy-start.1 = (bf16[2,512,256]{2,1,0:T(8,128)(2,1)S(1)}, bf16[2,512,256]{2,1,0:T(8,128)(2,1)}, u32[]{:S(2)}) copy-start(bf16[2,512,256]{2,1,0:T(8,128)(2,1)} %orbitals_ref.3) | copy-start | bytes 1572868
  2.6 8.2 %collective-permute-start = (bf16[2,256,256]{2,1,0:T(8,128)(2,1)S(1)}, bf16[2,256,256]{2,1,0:T(8,128)(2,1)S(1)}, u32[]{:S(2)}, u32[]{:S(2)}) collective-permute-start(bf16[2,256,256]{2,1,0:T(8,128)(2,1)S(1)} %get-tuple-element.12.refs_0_), channel_id=1, source_target_pairs={{0,1},{1,0},{2,3},{3,2},{4,5},{5,4},{6,7},{7,6},{8,9},{9,8},{10,11... | collective-permute-start | bytes 786440 | tf_op jit(solution)/shard_map/ppermute | solution.py:26
  4.7 12.8 %collective-permute-start.1 = (bf16[512,256]{1,0:T(8,128)(2,1)S(1)}, bf16[512,256]{1,0:T(8,128)(2,1)S(1)}, u32[]{:S(2)}, u32[]{:S(2)}) collective-permute-start(bf16[512,256]{1,0:T(8,128)(2,1)S(1)} %get-tuple-element.15), channel_id=1, source_target_pairs={{0,24},{1,25},{2,26},{3,27},{4,28},{5,29},{6,30},{7,31},{8,16},{9,... | collective-permute-start | bytes 786440 | tf_op jit(solution)/shard_map/ppermute | solution.py:26
  8.1 11.4 %collective-permute-start.2 = (bf16[512,256]{1,0:T(8,128)(2,1)S(1)}, bf16[512,256]{1,0:T(8,128)(2,1)S(1)}, u32[]{:S(2)}, u32[]{:S(2)}) collective-permute-start(bf16[512,256]{1,0:T(8,128)(2,1)S(1)} %get-tuple-element.16), channel_id=1, source_target_pairs={{0,25},{1,24},{2,27},{3,26},{4,29},{5,28},{6,31},{7,30},{8,17},{9,... | collective-permute-start | bytes 786440 | tf_op jit(solution)/shard_map/ppermute | solution.py:26
  12.3 19.4 %all-to-all-start = ((bf16[16,2,32,512]{3,2,1,0:T(8,128)(2,1)}), bf16[16,2,32,512]{3,2,1,0:T(8,128)(2,1)S(1)}, u32[]{:S(2)}, u32[]{:S(2)}) async-start(bf16[16,2,32,512]{3,2,1,0:T(8,128)(2,1)} %bitcast.3), calls=%async_computation | async-start | bytes 2097152 | tf_op jit(solution)/shard_map/all_to_all | solution.py:231
  31.7 22.4 %all-to-all-start.1 = ((bf16[16,2,32,512]{3,2,1,0:T(8,128)(2,1)}), bf16[16,2,32,512]{3,2,1,0:T(8,128)(2,1)S(1)}, u32[]{:S(2)}, u32[]{:S(2)}) async-start(bf16[16,2,32,512]{3,2,1,0:T(8,128)(2,1)} %bitcast.4), calls=%async_computation.1 | async-start | bytes 2097152 | tf_op jit(solution)/shard_map/all_to_all | solution.py:231
  37.5 0.7 %copy-start.3 = (s32[2,32]{1,0:T(2,128)S(1)}, s32[2,32]{1,0:T(2,128)}, u32[]{:S(2)}) copy-start(s32[2,32]{1,0:T(2,128)} %param.4) | copy-start | bytes 772

commit v18 on v17

--- a/solution.py
+++ b/solution.py
@@ -14,13 +14,13 @@
 KA, GA = ("half", "quarter", "inner"), ("hi", "lo")
 
 
-def swap(block, mirror, other):
+def swap(block, mirror=False, other=0, around=0):
     half, quarter, inner, hi, lo = (lax.axis_size(name) for name in KA + GA)
     slabs = hi * lo
     route = []
     for place in range(half * quarter * inner * slabs):
         kplace, slab = divmod(place, slabs)
-        part, within = divmod(kplace, inner)
+        part, within = divmod(kplace ^ around, inner)
         part = half * quarter - 1 - part if mirror else part
         route.append((place, (part * inner + within) * slabs + (slab ^ other)))
     return lax.ppermute(block, KA + GA, route)
@@ -79,31 +79,38 @@
     )(place, points, orbitals)
 
 
-def near_kernel(orbitals_ref, *refs):
-    *picked_refs, out_ref = refs
-    groups = out_ref.shape[0]
+def near_kernel(place_ref, orbitals_ref, *refs):
+    *refs, held_ref = refs
+    groups = held_ref.shape[0]
+    picked_refs, out_refs = refs[:-groups], refs[-groups:]
     rows = sum(picked_ref[0].astype(jnp.float32) for picked_ref in picked_refs)
     for part, turned in enumerate((rows, rotate(rows))):
-        out_ref[:, 0, part] = product(turned.astype(jnp.bfloat16), orbitals_ref[0], groups)
-
-
-def make_near(orbitals, shares, groups):
+        held_ref[...] = product(turned.astype(jnp.bfloat16), orbitals_ref[0], groups)
+        for x, out_ref in enumerate(out_refs):
+            out_ref[0, part] = held_ref[place_ref[2] ^ x]
+
+
+def make_near(orbitals, shares, groups, place):
     kdevice, slab_size, channels = orbitals.shape
     npoints = shares[0].shape[1]
     length = npoints // groups
     return pl.pallas_call(
         near_kernel,
-        grid=(kdevice,),
-        in_specs=[pl.BlockSpec((1, slab_size, channels), lambda k: (k, 0, 0))]
-        + [pl.BlockSpec((1, npoints, channels), lambda k: (k, 0, 0)) for _ in shares],
-        out_specs=pl.BlockSpec((groups, 1, 2, length, slab_size), lambda k: (0, k, 0, 0, 0)),
-        out_shape=jax.ShapeDtypeStruct((groups, kdevice, 2, length, slab_size), jnp.bfloat16),
+        grid_spec=pltpu.PrefetchScalarGridSpec(
+            num_scalar_prefetch=1,
+            grid=(kdevice,),
+            in_specs=[pl.BlockSpec((1, slab_size, channels), lambda k, place: (k, 0, 0))]
+            + [pl.BlockSpec((1, npoints, channels), lambda k, place: (k, 0, 0)) for _ in shares],
+            out_specs=[pl.BlockSpec((1, 2, length, slab_size), lambda k, place: (k, 0, 0, 0))] * groups,
+            scratch_shapes=[pltpu.VMEM((groups, length, slab_size), jnp.bfloat16)],
+        ),
+        out_shape=[jax.ShapeDtypeStruct((kdevice, 2, length, slab_size), jnp.bfloat16)] * groups,
         cost_estimate=pl.CostEstimate(
             flops=1_000_000_000, bytes_accessed=3_000_000, transcendentals=0
         ),
         compiler_params=pltpu.CompilerParams(vmem_limit_bytes=VMEM_LIMIT),
         name="near",
-    )(orbitals, *shares)
+    )(place, orbitals, *shares)
 
 
 def far_kernel(place_ref, points_ref, *refs):
@@ -157,10 +164,14 @@
     )(place, points, *slabs)
 
 
-def pair_kernel(scale, table_ref, near_ref, far_ref, out_ref, held_ref, sums_ref, sems):
+def pair_kernel(scale, table_ref, place_ref, *refs):
+    *near_refs, far_ref, out_ref, held_ref, sums_ref, sems = refs
     total_k, _, length, width = held_ref.shape
     transfers = table_ref.shape[0]
-    held_ref[: total_k // 2] = near_ref[...].astype(jnp.float32)
+    for x, near_ref in enumerate(near_refs):
+        kdevice = near_ref.shape[0]
+        source = place_ref[2] ^ x
+        held_ref[pl.ds(source * kdevice, kdevice)] = near_ref[...].astype(jnp.float32)
     held_ref[total_k // 2 :] = far_ref[...].astype(jnp.float32)
 
     count, columns = min(16, length), min(256, width)
@@ -193,14 +204,14 @@
         copy.wait()
 
 
-def make_pairs(near, far, table):
-    half_k, _, length, slab_size = near.shape
+def make_pairs(near, far, table, place):
+    half_k, _, length, slab_size = far.shape
     transfers = table.shape[0]
     out = jax.ShapeDtypeStruct((length, transfers, 2, slab_size), jnp.float32)
     vmem = pl.BlockSpec(memory_space=pltpu.VMEM)
     return pl.pallas_call(
         functools.partial(pair_kernel, 1.0 / math.sqrt(2 * half_k)),
-        in_specs=[pl.BlockSpec(memory_space=pltpu.SMEM), vmem, vmem],
+        in_specs=[pl.BlockSpec(memory_space=pltpu.SMEM)] * 2 + [vmem] * (len(near) + 1),
         out_specs=pl.BlockSpec(memory_space=pl.ANY),
         out_shape=out,
         scratch_shapes=[
@@ -210,7 +221,7 @@
         ],
         compiler_params=pltpu.CompilerParams(vmem_limit_bytes=VMEM_LIMIT),
         name="pairs",
-    )(table, near, far)
+    )(table, place, *near, far)
 
 
 def on_device(orbitals, minus_table, points):
@@ -220,22 +231,20 @@
     slabs = lax.axis_size("hi") * lax.axis_size("lo")
     total_k = 2 * groups * kdevice
     points = points.reshape(1, -1)
-    place = jnp.stack([half, lax.axis_index("hi") * SPLIT + lax.axis_index("lo")])
+    member = lax.axis_index("quarter") * lax.axis_size("inner") + lax.axis_index("inner")
+    place = jnp.stack([half, lax.axis_index("hi") * SPLIT + lax.axis_index("lo"), member])
 
     mine, other, share = make_front(orbitals, points, place)
-    shares = [share] + [swap(share, False, x) for x in range(1, slabs)]
-    far = [swap(other if x & 1 else mine, True, x) for x in range(slabs)]
-
-    def send(fields, around):
-        fields = fields.reshape((-1,) + fields.shape[-3:])
-        return lax.all_to_all(fields, around, split_axis=0, concat_axis=0, tiled=True)
-
-    near_fields = make_near(orbitals, shares, groups)
+    shares = [share] + [swap(share, other=x) for x in range(1, slabs)]
+    far = [swap(other if x & 1 else mine, mirror=True, other=x) for x in range(slabs)]
+
+    near_fields = make_near(orbitals, shares, groups, place)
     near_fields, points = lax.optimization_barrier((near_fields, points))
-    far_fields = make_far(far, points, groups, place)
-    near_fields = send(near_fields, ("quarter", "inner"))
+    far_fields = make_far(far, points, groups, place).reshape((groups * SPLIT, 2, -1, slab_size))
+    near_fields = [near_fields[0]] + [swap(near_fields[x], around=x) for x in range(1, groups)]
     near_fields, far_fields = lax.optimization_barrier((near_fields, far_fields))
-    far_fields = send(far_fields, ("quarter", "inner", "lo"))
+    around = ("quarter", "inner", "lo")
+    far_fields = lax.all_to_all(far_fields, around, split_axis=0, concat_axis=0, tiled=True)
 
     def mirrored(kpoints):
         return total_k // 2 + (kpoints + total_k // 4) % (total_k // 2)
@@ -244,7 +253,7 @@
     table = (jnp.roll(minus_table, -turn, axis=1) - turn) % total_k
     table = jnp.where(table < total_k // 2, table, mirrored(table))
     first, third, fourth = jnp.split(table, (total_k // 2, 3 * total_k // 4), axis=1)
-    return make_pairs(near_fields, far_fields, jnp.concatenate([first, fourth, third], axis=1))
+    return make_pairs(near_fields, far_fields, jnp.concatenate([first, fourth, third], axis=1), place)
 
 
 def solution(mesh):

time: 57.4 us -> 65.5 us (1.14)
  starting transfers between devices: 16.5 us -> 31.5 us
  waiting for transfers between devices: 29.9 us -> 23.4 us
    ppermute x3 -> x10, starting transfers between devices: 5.46 us -> 26.4 us  [swap(): return lax.ppermute(block, KA + GA, route)]
    all_to_all x2 -> x1, waiting for transfers between devices: 25.3 us -> 15.5 us  [on_device(): lax.all_to_all(far_fields, around, split_axis=0, concat_axis=0, tiled=True)]
    all_to_all x2 -> x1, starting transfers between devices: 11.1 us -> 5.04 us  [on_device(): lax.all_to_all(far_fields, around, split_axis=0, concat_axis=0, tiled=True)]
    ppermute x3 -> x10, waiting for transfers between devices: 4.6 us -> 7.81 us  [swap(): return lax.ppermute(block, KA + GA, route)]
  transfers between devices with their start and end apart: 5 -> 11, of which waited for: 4 -> 4; matrix products, arithmetic and copies ran while one was open for 1% -> 0% of each run, Pallas kernels for 7% -> 6%
where the time goes in v18:
time: 65.5 us; the launch traced here: 65.2 us
  starting transfers between devices  31.5 us (48%)
  waiting for transfers between devices  23.4 us (36%)
  Pallas kernels  7.64 us (12%)
  local copies, waits for them, and re-layouts  2.4 us (4%)
    ppermute x10, starting transfers between devices, swap(): return lax.ppermute(block, KA + GA, route)  26.4 us
    all_to_all x1, waiting for transfers between devices, on_device(): lax.all_to_all(far_fields, around, split_axis=0, concat_axis=0, tiled=True)  15.5 us
    ppermute x10, waiting for transfers between devices, swap(): return lax.ppermute(block, KA + GA, route)  7.81 us
    all_to_all x1, starting transfers between devices, on_device(): lax.all_to_all(far_fields, around, split_axis=0, concat_axis=0, tiled=True)  5.04 us
    pallas_call x1, Pallas kernels, make_pairs(): pl.pallas_call(functools.partial(pair_kernel, 1.0 / math.sqrt(2 * half_k)...  2.97 us
    pallas_call x1, Pallas kernels, make_far(): pl.pallas_call(far_kernel, grid_spec=pltpu.PrefetchScalarGridSpec(num_sca...  2.5 us
    unnamed x8, local copies, waits for them, and re-layouts  2.32 us
  transfers between devices with their start and end apart: 11, of which 4 were waited for; matrix products, arithmetic and copies ran while one was open for 0% of the time, Pallas kernels for 6%

profile of v18, /device:TPU:1, one launch (start us, length us, event | category | flops | bytes accessed | tf_op | source)
XLA Modules:
  0.0 65.2 jit_solution(14997477397228269221)
XLA Ops:
  0.0 0.0 copy-start.2
  0.0 0.1 pad_add_fusion.2.place_ref
  0.1 0.6 copy-done.2
  0.7 0.0 copy-start
  0.7 1.0 %copy-done = bf16[2,512,256]{2,1,0:T(8,128)(2,1)S(1)} copy-done((bf16[2,512,256]{2,1,0:T(8,128)(2,1)S(1)}, bf16[2,512,256]{2,1,0:T(8,128)(2,1)}, u32[]{:S(2)}) %copy-start) | copy-done | bytes 524312
  1.7 0.0 copy-start.1
  1.7 0.9 %front.1 = (bf16[512,256]{1,0:T(8,128)(2,1)S(1)}, bf16[512,256]{1,0:T(8,128)(2,1)S(1)}, bf16[2,256,256]{2,1,0:T(8,128)(2,1)S(1)}) custom-call(s32[3]{0:T(128)S(1)} %pad_add_fusion.2.place_ref, s32[1,512]{1,0:T(1,128)S(1)} %bitcast.6, bf16[2,512,256]{2,1,0:T(8,128)(2,1)S(1)} %copy-done), custom_call_target="tpu_custom_call" | custom-call | tf_op jit(solution)/shard_map/front/pallas_call | solution.py:68
  2.6 2.1 %collective-permute-start = (bf16[2,256,256]{2,1,0:T(8,128)(2,1)S(1)}, bf16[2,256,256]{2,1,0:T(8,128)(2,1)S(1)}, u32[]{:S(2)}, u32[]{:S(2)}) collective-permute-start(bf16[2,256,256]{2,1,0:T(8,128)(2,1)S(1)} %get-tuple-element.34.refs_0_), channel_id=1, source_target_pairs={{0,1},{1,0},{2,3},{3,2},{4,5},{5,4},{6,7},{7,6},{8,9},{9,8},{10,11... | collective-permute-start | bytes 786440 | tf_op jit(solution)/shard_map/ppermute | solution.py:26
  4.7 3.3 %collective-permute-start.8 = (bf16[512,256]{1,0:T(8,128)(2,1)S(1)}, bf16[512,256]{1,0:T(8,128)(2,1)S(1)}, u32[]{:S(2)}, u32[]{:S(2)}) collective-permute-start(bf16[512,256]{1,0:T(8,128)(2,1)S(1)} %get-tuple-element.52), channel_id=1, source_target_pairs={{0,24},{1,25},{2,26},{3,27},{4,28},{5,29},{6,30},{7,31},{8,16},{9,... | collective-permute-start | bytes 786440 | tf_op jit(solution)/shard_map/ppermute | solution.py:26
  8.1 0.0 collective-permute-start.9
  8.1 2.7 %collective-permute-done.refs_1_ = bf16[2,256,256]{2,1,0:T(8,128)(2,1)S(1)} collective-permute-done((bf16[2,256,256]{2,1,0:T(8,128)(2,1)S(1)}, bf16[2,256,256]{2,1,0:T(8,128)(2,1)S(1)}, u32[]{:S(2)}, u32[]{:S(2)}) %collective-permute-start) | collective-permute-done | bytes 262176 | tf_op jit(solution)/shard_map/ppermute | solution.py:26
  10.8 0.0 copy-done.1
  10.8 1.3 %near.1 = (bf16[2,2,32,512]{3,2,1,0:T(8,128)(2,1)S(1)}, bf16[2,2,32,512]{3,2,1,0:T(8,128)(2,1)S(1)}, bf16[2,2,32,512]{3,2,1,0:T(8,128)(2,1)S(1)}, bf16[2,2,32,51...) custom-call(s32[3]{0:T(128)S(1)} %pad_add_fusion.2.place_ref, ...), custom_call_target="tpu_custom_call" | custom-call | flops 1000000000 | bytes 3000000 | tf_op jit(solution)/shard_map/near/pallas_call | solution.py:97
  12.1 1.3 %collective-permute-start.1 = (bf16[2,2,32,512]{3,2,1,0:T(8,128)(2,1)S(1)}, bf16[2,2,32,512]{3,2,1,0:T(8,128)(2,1)S(1)}, u32[]{:S(2)}, u32[]{:S(2)}) collective-permute-start(bf16[2,2,32,512]{3,2,1,0:T(8,128)(2,1)S(1)} %get-tuple-element.44), channel_id=1, source_target_pairs={{0,2},{1,3},{2,0},{3,1},{4,6},{5,7},{6,4},{7,5},{8,10},{9,11},{10,... | collective-permute-start | bytes 393224 | tf_op jit(solution)/shard_map/ppermute | solution.py:26
  13.4 1.4 %collective-permute-start.2 = (bf16[2,2,32,512]{3,2,1,0:T(8,128)(2,1)S(1)}, bf16[2,2,32,512]{3,2,1,0:T(8,128)(2,1)S(1)}, u32[]{:S(2)}, u32[]{:S(2)}) collective-permute-start(bf16[2,2,32,512]{3,2,1,0:T(8,128)(2,1)S(1)} %get-tuple-element.45), channel_id=1, source_target_pairs={{0,4},{1,5},{2,6},{3,7},{4,0},{5,1},{6,2},{7,3},{8,12},{9,13},{10,... | collective-permute-start | bytes 393224 | tf_op jit(solution)/shard_map/ppermute | solution.py:26
  14.8 0.3 collective-permute-start.3
  15.1 0.0 collective-permute-done.8.refs_0_
  15.1 9.5 %collective-permute-start.4 = (bf16[2,2,32,512]{3,2,1,0:T(8,128)(2,1)S(1)}, bf16[2,2,32,512]{3,2,1,0:T(8,128)(2,1)S(1)}, u32[]{:S(2)}, u32[]{:S(2)}) collective-permute-start(bf16[2,2,32,512]{3,2,1,0:T(8,128)(2,1)S(1)} %get-tuple-element.47), channel_id=1, source_target_pairs={{0,8},{1,9},{2,10},{3,11},{4,12},{5,13},{6,14},{7,15},{8,0},{9,1},... | collective-permute-start | bytes 393224 | tf_op jit(solution)/shard_map/ppermute | solution.py:26
  24.6 0.0 collective-permute-done.9.refs_1_
  24.6 6.8 %collective-permute-start.5 = (bf16[2,2,32,512]{3,2,1,0:T(8,128)(2,1)S(1)}, bf16[2,2,32,512]{3,2,1,0:T(8,128)(2,1)S(1)}, u32[]{:S(2)}, u32[]{:S(2)}) collective-permute-start(bf16[2,2,32,512]{3,2,1,0:T(8,128)(2,1)S(1)} %get-tuple-element.48), channel_id=1, source_target_pairs={{0,10},{1,11},{2,8},{3,9},{4,14},{5,15},{6,12},{7,13},{8,2},{9,3},... | collective-permute-start | bytes 393224 | tf_op jit(solution)/shard_map/ppermute | solution.py:26
  31.4 0.0 collective-permute-done.1.refs_1_
  31.4 0.0 collective-permute-start.6
  31.4 0.0 collective-permute-done.2.refs_2_
  31.5 1.6 %collective-permute-start.7 = (bf16[2,2,32,512]{3,2,1,0:T(8,128)(2,1)S(1)}, bf16[2,2,32,512]{3,2,1,0:T(8,128)(2,1)S(1)}, u32[]{:S(2)}, u32[]{:S(2)}) collective-permute-start(bf16[2,2,32,512]{3,2,1,0:T(8,128)(2,1)S(1)} %get-tuple-element.50), channel_id=1, source_target_pairs={{0,14},{1,15},{2,12},{3,13},{4,10},{5,11},{6,8},{7,9},{8,6},{9,7},... | collective-permute-start | bytes 393224 | tf_op jit(solution)/shard_map/ppermute | solution.py:26
  33.1 2.5 %far.1 = bf16[8,2,2,32,512]{4,3,2,1,0:T(8,128)(2,1)} custom-call(s32[3]{0:T(128)S(1)} %pad_add_fusion.2.place_ref, s32[1,512]{1,0:T(1,128)S(1)} %bitcast.7, bf16[512,256]{1,0:T(8,128)(2,1)S(1)} %collective-permute-done.8.refs_0_, bf16[512,256]{1,0:T(8,128)(2,1)S(1)} %collective-permute-done.9.refs_1_), custom_call_target="tpu_custom_call" | custom-call | flops 60000002048 | bytes 180000000 | tf_op jit(solution)/shard_map/far/pallas_call | solution.py:145
  35.6 0.0 collective-permute-done.3.refs_3_
  35.6 0.0 collective-permute-done.4.refs_4_
  35.6 0.0 collective-permute-done.5.refs_5_
  35.6 2.3 %collective-permute-done.6.refs_6_ = bf16[2,2,32,512]{3,2,1,0:T(8,128)(2,1)S(1)} collective-permute-done((bf16[2,2,32,512]{3,2,1,0:T(8,128)(2,1)S(1)}, bf16[2,2,32,512]{3,2,1,0:T(8,128)(2,1)S(1)}, u32[]{:S(2)}, u32[]{:S(2)}) %collective-permute-start.6) | collective-permute-done | bytes 131104 | tf_op jit(solution)/shard_map/ppermute | solution.py:26
  37.9 2.8 %collective-permute-done.7.refs_7_ = bf16[2,2,32,512]{3,2,1,0:T(8,128)(2,1)S(1)} collective-permute-done((bf16[2,2,32,512]{3,2,1,0:T(8,128)(2,1)S(1)}, bf16[2,2,32,512]{3,2,1,0:T(8,128)(2,1)S(1)}, u32[]{:S(2)}, u32[]{:S(2)}) %collective-permute-start.7) | collective-permute-done | bytes 131104 | tf_op jit(solution)/shard_map/ppermute | solution.py:26
  40.7 5.0 %all-to-all-start = ((bf16[16,2,32,512]{3,2,1,0:T(8,128)(2,1)}), bf16[16,2,32,512]{3,2,1,0:T(8,128)(2,1)S(1)}, u32[]{:S(2)}, u32[]{:S(2)}) async-start(bf16[16,2,32,512]{3,2,1,0:T(8,128)(2,1)} %bitcast.4), calls=%async_computation | async-start | bytes 2097152 | tf_op jit(solution)/shard_map/all_to_all | solution.py:247
  45.7 0.0 copy-start.3
  45.7 0.7 %copy-done.3 = s32[2,32]{1,0:T(2,128)S(1)} copy-done((s32[2,32]{1,0:T(2,128)S(1)}, s32[2,32]{1,0:T(2,128)}, u32[]{:S(2)}) %copy-start.3) | copy-done | bytes 280
  46.4 0.1 pad_add_fusion
  46.5 0.1 compare_select_fusion
  46.6 0.1 fusion.3
  46.6 0.1 pad_add_fusion.1.table_ref
  46.7 15.5 %all-to-all-done.refs_8_ = bf16[16,2,32,512]{3,2,1,0:T(8,128)(2,1)S(1)} async-done(((bf16[16,2,32,512]{3,2,1,0:T(8,128)(2,1)}), bf16[16,2,32,512]{3,2,1,0:T(8,128)(2,1)S(1)}, u32[]{:S(2)}, u32[]{:S(2)}) %all-to-all-start) | async-done | bytes 1048608 | tf_op jit(solution)/shard_map/all_to_all | solution.py:247
  62.3 3.0 %pairs.1 = f32[32,2,2,512]{3,2,1,0:T(2,128)} custom-call(s32[2,32]{1,0:T(2,128)S(1)} %pad_add_fusion.1.table_ref, s32[3]{0:T(128)S(1)} %pad_add_fusion.2.place_ref, bf16[2,2,32,512]{3,2,1,0:T(8,128)(2,1)S(1)} %get-tuple-element.54.refs_0_, bf16[2,2,32,512]{3,2,1,0:T(8,128)(2,1)S(1)} %collective-permute-done.1.refs_1_, ...), custom_call_target="tpu_custom_call" | custom-call | tf_op jit(solution)/shard_map/pairs/pallas_call | solution.py:212
Async XLA Ops:
  0.0 0.7 %copy-start.2 = (s32[512]{0:T(512)S(1)}, s32[512]{0:T(512)}, u32[]{:S(2)}) copy-start(s32[512]{0:T(512)} %param.5) | copy-start | bytes 6148
  0.7 1.0 %copy-start = (bf16[2,512,256]{2,1,0:T(8,128)(2,1)S(1)}, bf16[2,512,256]{2,1,0:T(8,128)(2,1)}, u32[]{:S(2)}) copy-start(bf16[2,512,256]{2,1,0:T(8,128)(2,1)} %orbitals_ref.3) | copy-start | bytes 1572868
  1.7 9.1 %copy-start.1 = (bf16[2,512,256]{2,1,0:T(8,128)(2,1)S(1)}, bf16[2,512,256]{2,1,0:T(8,128)(2,1)}, u32[]{:S(2)}) copy-start(bf16[2,512,256]{2,1,0:T(8,128)(2,1)} %orbitals_ref.3) | copy-start | bytes 1572868
  2.6 8.2 %collective-permute-start = (bf16[2,256,256]{2,1,0:T(8,128)(2,1)S(1)}, bf16[2,256,256]{2,1,0:T(8,128)(2,1)S(1)}, u32[]{:S(2)}, u32[]{:S(2)}) collective-permute-start(bf16[2,256,256]{2,1,0:T(8,128)(2,1)S(1)} %get-tuple-element.34.refs_0_), channel_id=1, source_target_pairs={{0,1},{1,0},{2,3},{3,2},{4,5},{5,4},{6,7},{7,6},{8,9},{9,8},{10,11... | collective-permute-start | bytes 786440 | tf_op jit(solution)/shard_map/ppermute | solution.py:26
  4.7 10.4 %collective-permute-start.8 = (bf16[512,256]{1,0:T(8,128)(2,1)S(1)}, bf16[512,256]{1,0:T(8,128)(2,1)S(1)}, u32[]{:S(2)}, u32[]{:S(2)}) collective-permute-start(bf16[512,256]{1,0:T(8,128)(2,1)S(1)} %get-tuple-element.52), channel_id=1, source_target_pairs={{0,24},{1,25},{2,26},{3,27},{4,28},{5,29},{6,30},{7,31},{8,16},{9,... | collective-permute-start | bytes 786440 | tf_op jit(solution)/shard_map/ppermute | solution.py:26
  8.1 16.5 %collective-permute-start.9 = (bf16[512,256]{1,0:T(8,128)(2,1)S(1)}, bf16[512,256]{1,0:T(8,128)(2,1)S(1)}, u32[]{:S(2)}, u32[]{:S(2)}) collective-permute-start(bf16[512,256]{1,0:T(8,128)(2,1)S(1)} %get-tuple-element.53), channel_id=1, source_target_pairs={{0,25},{1,24},{2,27},{3,26},{4,29},{5,28},{6,31},{7,30},{8,17},{9,... | collective-permute-start | bytes 786440 | tf_op jit(solution)/shard_map/ppermute | solution.py:26
  12.1 19.4 %collective-permute-start.1 = (bf16[2,2,32,512]{3,2,1,0:T(8,128)(2,1)S(1)}, bf16[2,2,32,512]{3,2,1,0:T(8,128)(2,1)S(1)}, u32[]{:S(2)}, u32[]{:S(2)}) collective-permute-start(bf16[2,2,32,512]{3,2,1,0:T(8,128)(2,1)S(1)} %get-tuple-element.44), channel_id=1, source_target_pairs={{0,2},{1,3},{2,0},{3,1},{4,6},{5,7},{6,4},{7,5},{8,10},{9,11},{10,... | collective-permute-start | bytes 393224 | tf_op jit(solution)/shard_map/ppermute | solution.py:26
  13.4 18.1 %collective-permute-start.2 = (bf16[2,2,32,512]{3,2,1,0:T(8,128)(2,1)S(1)}, bf16[2,2,32,512]{3,2,1,0:T(8,128)(2,1)S(1)}, u32[]{:S(2)}, u32[]{:S(2)}) collective-permute-start(bf16[2,2,32,512]{3,2,1,0:T(8,128)(2,1)S(1)} %get-tuple-element.45), channel_id=1, source_target_pairs={{0,4},{1,5},{2,6},{3,7},{4,0},{5,1},{6,2},{7,3},{8,12},{9,13},{10,... | collective-permute-start | bytes 393224 | tf_op jit(solution)/shard_map/ppermute | solution.py:26
  14.8 20.8 %collective-permute-start.3 = (bf16[2,2,32,512]{3,2,1,0:T(8,128)(2,1)S(1)}, bf16[2,2,32,512]{3,2,1,0:T(8,128)(2,1)S(1)}, u32[]{:S(2)}, u32[]{:S(2)}) collective-permute-start(bf16[2,2,32,512]{3,2,1,0:T(8,128)(2,1)S(1)} %get-tuple-element.46), channel_id=1, source_target_pairs={{0,6},{1,7},{2,4},{3,5},{4,2},{5,3},{6,0},{7,1},{8,14},{9,15},{10,... | collective-permute-start | bytes 393224 | tf_op jit(solution)/shard_map/ppermute | solution.py:26
  15.1 20.5 %collective-permute-start.4 = (bf16[2,2,32,512]{3,2,1,0:T(8,128)(2,1)S(1)}, bf16[2,2,32,512]{3,2,1,0:T(8,128)(2,1)S(1)}, u32[]{:S(2)}, u32[]{:S(2)}) collective-permute-start(bf16[2,2,32,512]{3,2,1,0:T(8,128)(2,1)S(1)} %get-tuple-element.47), channel_id=1, source_target_pairs={{0,8},{1,9},{2,10},{3,11},{4,12},{5,13},{6,14},{7,15},{8,0},{9,1},... | collective-permute-start | bytes 393224 | tf_op jit(solution)/shard_map/ppermute | solution.py:26
  24.6 11.0 %collective-permute-start.5 = (bf16[2,2,32,512]{3,2,1,0:T(8,128)(2,1)S(1)}, bf16[2,2,32,512]{3,2,1,0:T(8,128)(2,1)S(1)}, u32[]{:S(2)}, u32[]{:S(2)}) collective-permute-start(bf16[2,2,32,512]{3,2,1,0:T(8,128)(2,1)S(1)} %get-tuple-element.48), channel_id=1, source_target_pairs={{0,10},{1,11},{2,8},{3,9},{4,14},{5,15},{6,12},{7,13},{8,2},{9,3},... | collective-permute-start | bytes 393224 | tf_op jit(solution)/shard_map/ppermute | solution.py:26
  31.4 6.4 %collective-permute-start.6 = (bf16[2,2,32,512]{3,2,1,0:T(8,128)(2,1)S(1)}, bf16[2,2,32,512]{3,2,1,0:T(8,128)(2,1)S(1)}, u32[]{:S(2)}, u32[]{:S(2)}) collective-permute-start(bf16[2,2,32,512]{3,2,1,0:T(8,128)(2,1)S(1)} %get-tuple-element.49), channel_id=1, source_target_pairs={{0,12},{1,13},{2,14},{3,15},{4,8},{5,9},{6,10},{7,11},{8,4},{9,5},... | collective-permute-start | bytes 393224 | tf_op jit(solution)/shard_map/ppermute | solution.py:26
  31.5 9.2 %collective-permute-start.7 = (bf16[2,2,32,512]{3,2,1,0:T(8,128)(2,1)S(1)}, bf16[2,2,32,512]{3,2,1,0:T(8,128)(2,1)S(1)}, u32[]{:S(2)}, u32[]{:S(2)}) collective-permute-start(bf16[2,2,32,512]{3,2,1,0:T(8,128)(2,1)S(1)} %get-tuple-element.50), channel_id=1, source_target_pairs={{0,14},{1,15},{2,12},{3,13},{4,10},{5,11},{6,8},{7,9},{8,6},{9,7},... | collective-permute-start | bytes 393224 | tf_op jit(solution)/shard_map/ppermute | solution.py:26
  40.7 21.6 %all-to-all-start = ((bf16[16,2,32,512]{3,2,1,0:T(8,128)(2,1)}), bf16[16,2,32,512]{3,2,1,0:T(8,128)(2,1)S(1)}, u32[]{:S(2)}, u32[]{:S(2)}) async-start(bf16[16,2,32,512]{3,2,1,0:T(8,128)(2,1)} %bitcast.4), calls=%async_computation | async-start | bytes 2097152 | tf_op jit(solution)/shard_map/all_to_all | solution.py:247
  45.7 0.7 %copy-start.3 = (s32[2,32]{1,0:T(2,128)S(1)}, s32[2,32]{1,0:T(2,128)}, u32[]{:S(2)}) copy-start(s32[2,32]{1,0:T(2,128)} %param.4) | copy-start | bytes 772

commit v19 on v17

v19 whole, which is shorter than its diff:
```python
import functools
import math

import jax
import jax.numpy as jnp
from jax import lax
from jax.experimental import pallas as pl
from jax.experimental.pallas import tpu as pltpu
from jax.sharding import Mesh
from jax.sharding import PartitionSpec as P

VMEM_LIMIT = 40 * 1024 * 1024
SPLIT = 2
KA, GA = ("half", "quarter", "inner"), ("hi", "lo")


def swap(block, mirror, other):
    half, quarter, inner, hi, lo = (lax.axis_size(name) for name in KA + GA)
    slabs = hi * lo
    route = []
    for place in range(half * quarter * inner * slabs):
        kplace, slab = divmod(place, slabs)
        part, within = divmod(kplace, inner)
        part = half * quarter - 1 - part if mirror else part
        route.append((place, (part * inner + within) * slabs + (slab ^ other)))
    return lax.ppermute(block, KA + GA, route)


def rotate(picked):
    middle = picked.shape[1] // 2
    return jnp.concatenate([-picked[:, middle:], picked[:, :middle]], axis=1)


def front_kernel(
    place_ref, points_ref, orbitals_ref, mine_ref, other_ref, picked_ref, wanted_ref, sems
):
    slab_size, channels = mine_ref.shape
    npoints = wanted_ref.shape[1]
    first = pl.multiple_of(place_ref[0] * npoints, npoints)
    mine = place_ref[1] % SPLIT
    points_copy = pltpu.make_async_copy(
        points_ref.at[:, pl.ds(first, npoints)], wanted_ref, sems.at[0]
    )
    points_copy.start()
    parts = slab_size // 2
    copies = []
    for number, (k, slab_ref) in enumerate(((mine, mine_ref), (1 - mine, other_ref))):
        for part in range(2):
            rows = pl.ds(part * parts, parts)
            copies.append(
                pltpu.make_async_copy(
                    orbitals_ref.at[k, rows], slab_ref.at[rows], sems.at[1 + 2 * number + part]
                )
            )
            copies[-1].start()
    points_copy.wait()
    wanted = wanted_ref[...] - place_ref[1] * slab_size
    spot = lax.broadcasted_iota(jnp.int32, (slab_size, npoints), 0)
    chosen = (spot == wanted).astype(jnp.float32).astype(jnp.bfloat16)
    for number, (k, slab_ref) in enumerate(((mine, mine_ref), (1 - mine, other_ref))):
        copies[2 * number].wait()
        copies[2 * number + 1].wait()
        picked = lax.dot_general(
            chosen, slab_ref[...], (((0,), (0,)), ((), ())), preferred_element_type=jnp.float32
        )
        picked_ref[k] = picked.astype(jnp.bfloat16)


def make_front(orbitals, points, place):
    kdevice, slab_size, channels = orbitals.shape
    npoints = points.shape[1] // 2
    vmem = pl.BlockSpec(memory_space=pltpu.VMEM)
    hbm = pl.BlockSpec(memory_space=pl.ANY)
    slab = jax.ShapeDtypeStruct((slab_size, channels), jnp.bfloat16)
    return pl.pallas_call(
        front_kernel,
        in_specs=[pl.BlockSpec(memory_space=pltpu.SMEM), hbm, hbm],
        out_specs=[vmem] * 3,
        out_shape=[slab, slab, jax.ShapeDtypeStruct((kdevice, npoints, channels), jnp.bfloat16)],
        scratch_shapes=[pltpu.VMEM((1, npoints), jnp.int32), pltpu.SemaphoreType.DMA((5,))],
        compiler_params=pltpu.CompilerParams(vmem_limit_bytes=VMEM_LIMIT),
        name="front",
    )(place, points, orbitals)


def send_products(picked, slab_refs, places, out_ref, parts_ref, sems):
    groups, _, _, length, slab_size = out_ref.shape
    copies = []
    for slab_ref, rows, place in zip(slab_refs, picked, places, strict=True):
        for part, turned in enumerate((rows, rotate(rows))):
            product = lax.dot_general(
                turned.astype(jnp.bfloat16),
                slab_ref[...],
                (((1,), (1,)), ((), ())),
                preferred_element_type=jnp.float32,
            )
            number = len(copies)
            pieces = product.reshape(groups, length, slab_size)
            parts_ref[number] = pieces.astype(jnp.bfloat16)
            copies.append(
                pltpu.make_async_copy(
                    parts_ref.at[number], out_ref.at[:, place, part], sems.at[number]
                )
            )
            copies[-1].start()
    for copy in copies:
        copy.wait()


def near_kernel(place_ref, mine_ref, other_ref, *refs):
    *picked_refs, out_ref, parts_ref, sems = refs
    mine = place_ref[1] % SPLIT
    places = (mine, 1 - mine)
    picked = [
        sum(picked_ref[place].astype(jnp.float32) for picked_ref in picked_refs)
        for place in places
    ]
    send_products(picked, (mine_ref, other_ref), places, out_ref, parts_ref, sems)


def far_kernel(place_ref, rows_ref, *refs):
    *slab_refs, out_ref, parts_ref, sems = refs
    slab_size, _ = slab_refs[0].shape
    npoints = rows_ref.shape[0]
    mine = place_ref[1] % SPLIT
    spot = lax.broadcasted_iota(jnp.int32, (npoints, slab_size), 1)
    picked = 0.0
    for number, slab_ref in enumerate(slab_refs):
        chosen = (rows_ref[:, number : number + 1] == spot).astype(jnp.float32)
        picked += jnp.dot(
            chosen.astype(jnp.bfloat16), slab_ref[...], preferred_element_type=jnp.float32
        )
    send_products(
        (picked,) * SPLIT, slab_refs[:SPLIT], (mine, 1 - mine), out_ref, parts_ref, sems
    )


def make_fields(kernel, inputs, place, groups, length, slab_size, work):
    vmem = pl.BlockSpec(memory_space=pltpu.VMEM)
    return pl.pallas_call(
        kernel,
        in_specs=[pl.BlockSpec(memory_space=pltpu.SMEM)] + [vmem] * len(inputs),
        out_specs=pl.BlockSpec(memory_space=pl.ANY),
        out_shape=jax.ShapeDtypeStruct((groups, SPLIT, 2, length, slab_size), jnp.bfloat16),
        scratch_shapes=[
            pltpu.VMEM((2 * SPLIT, groups, length, slab_size), jnp.bfloat16),
            pltpu.SemaphoreType.DMA((2 * SPLIT,)),
        ],
        cost_estimate=pl.CostEstimate(
            flops=work * 1_000_000_000, bytes_accessed=work * 3_000_000, transcendentals=0
        ),
        compiler_params=pltpu.CompilerParams(vmem_limit_bytes=VMEM_LIMIT),
        name="fields",
    )(place, *inputs)


def pair_kernel(scale, table_ref, near_ref, far_ref, out_ref, held_ref, sums_ref, sems):
    total_k, _, length, width = held_ref.shape
    transfers = table_ref.shape[0]
    held_ref[: total_k // 2] = near_ref[...].astype(jnp.float32)
    held_ref[total_k // 2 :] = far_ref[...].astype(jnp.float32)

    count, columns = min(16, length), min(256, width)
    copies = []
    for start in range(0, length, count):
        rows = pl.ds(start, count)
        for column in range(0, width, columns):
            lanes = pl.ds(column, columns)

            def step(k, sums):
                real, imag = held_ref[k, 0, rows, lanes], held_ref[k, 1, rows, lanes]
                after = []
                for transfer in range(transfers):
                    other = table_ref[transfer, k]
                    other_real = held_ref[other, 0, rows, lanes]
                    other_imag = held_ref[other, 1, rows, lanes]
                    after.append(sums[2 * transfer] + (real * other_real + imag * other_imag))
                    after.append(sums[2 * transfer + 1] + (imag * other_real - real * other_imag))
                return tuple(after)

            zero = jnp.zeros((count, columns), jnp.float32)
            sums = lax.fori_loop(0, total_k, step, (zero,) * (2 * transfers), unroll=4)
            for place, value in enumerate(sums):
                sums_ref[rows, place // 2, place % 2, lanes] = value * scale
        copies.append(
            pltpu.make_async_copy(sums_ref.at[rows], out_ref.at[rows], sems.at[start // count])
        )
        copies[-1].start()
    for copy in copies:
        copy.wait()


def make_pairs(near, far, table):
    half_k, _, length, slab_size = near.shape
    transfers = table.shape[0]
    out = jax.ShapeDtypeStruct((length, transfers, 2, slab_size), jnp.float32)
    vmem = pl.BlockSpec(memory_space=pltpu.VMEM)
    return pl.pallas_call(
        functools.partial(pair_kernel, 1.0 / math.sqrt(2 * half_k)),
        in_specs=[pl.BlockSpec(memory_space=pltpu.SMEM), vmem, vmem],
        out_specs=pl.BlockSpec(memory_space=pl.ANY),
        out_shape=out,
        scratch_shapes=[
            pltpu.VMEM((2 * half_k, 2, length, slab_size), jnp.float32),
            pltpu.VMEM(out.shape, jnp.float32),
            pltpu.SemaphoreType.DMA((length // min(16, length),)),
        ],
        compiler_params=pltpu.CompilerParams(vmem_limit_bytes=VMEM_LIMIT),
        name="pairs",
    )(table, near, far)


def on_device(orbitals, minus_table, points):
    kdevice, slab_size, channels = orbitals.shape
    half = lax.axis_index("half")
    groups = lax.axis_size("quarter") * lax.axis_size("inner")
    slabs = lax.axis_size("hi") * lax.axis_size("lo")
    total_k = 2 * groups * kdevice
    npoints = points.shape[0] // 2
    sizes = (groups, npoints // groups, slab_size)
    here = lax.axis_index("hi") * SPLIT + lax.axis_index("lo")
    place = jnp.stack([half, here])

    mine, other, share = make_front(orbitals, points.reshape(1, -1), place)
    shares = [share] + [swap(share, False, x) for x in range(1, slabs)]
    far = [swap(other if x & 1 else mine, True, x) for x in range(slabs)]

    def send(fields, around):
        fields = fields.reshape((-1,) + fields.shape[-3:])
        return lax.all_to_all(fields, around, split_axis=0, concat_axis=0, tiled=True)

    near_fields = make_fields(near_kernel, [mine, other] + shares, place, *sizes, 1)
    wanted = lax.dynamic_slice_in_dim(points, half * npoints, npoints)
    starts = jnp.stack([(here ^ x) * slab_size for x in range(slabs)])
    rows = wanted[:, None] - starts[None, :]
    near_fields, rows = lax.optimization_barrier((near_fields, rows))
    far_fields = make_fields(far_kernel, [rows] + far, place, *sizes, 60)
    near_fields = send(near_fields, ("quarter", "inner"))
    near_fields, far_fields = lax.optimization_barrier((near_fields, far_fields))
    far_fields = send(far_fields, ("quarter", "inner", "lo"))

    def mirrored(kpoints):
        return total_k // 2 + (kpoints + total_k // 4) % (total_k // 2)

    turn = half * (total_k // 2)
    table = (jnp.roll(minus_table, -turn, axis=1) - turn) % total_k
    table = jnp.where(table < total_k // 2, table, mirrored(table))
    first, third, fourth = jnp.split(table, (total_k // 2, 3 * total_k // 4), axis=1)
    return make_pairs(near_fields, far_fields, jnp.concatenate([first, fourth, third], axis=1))


def solution(mesh):
    kplaces, slabs = mesh.shape["ka"], mesh.shape["ga"]
    devices = mesh.devices.reshape(2, 2, kplaces // 4, slabs // SPLIT, SPLIT)
    finer = Mesh(devices, KA + GA)
    return jax.shard_map(
        on_device,
        mesh=finer,
        in_specs=(P(KA, GA, None), P(), P()),
        out_specs=P(KA, None, None, GA),
        check_vma=False,
    )
```

time: 57.4 us -> 58.3 us (1.016)
  Pallas kernels: 7.86 us -> 9.01 us
  waiting for transfers between devices: 29.9 us -> 29.3 us
    pallas_call x1, Pallas kernels: 0.87 us -> 1.97 us  [make_front(): pl.pallas_call(front_kernel, in_specs=[pl.BlockSpec(memory_space=pltpu.SM...]
    unnamed x8 -> x6, local copies, waits for them, and re-layouts: 2.32 us -> 2.32 us
where the time goes in v19:
time: 58.3 us; the launch traced here: 58 us
  waiting for transfers between devices  29.3 us (50%)
  starting transfers between devices  16.6 us (28%)
  Pallas kernels  9.01 us (15%)
  local copies, waits for them, and re-layouts  2.47 us (4%)
    all_to_all x2, waiting for transfers between devices, send(): lax.all_to_all(fields, around, split_axis=0, concat_axis=0, tiled=True)  25.3 us
    all_to_all x2, starting transfers between devices, send(): lax.all_to_all(fields, around, split_axis=0, concat_axis=0, tiled=True)  11.2 us
    ppermute x3, starting transfers between devices, swap(): return lax.ppermute(block, KA + GA, route)  5.46 us
    pallas_call x2, Pallas kernels, make_fields(): pl.pallas_call(kernel, in_specs=[pl.BlockSpec(memory_space=pltpu.SMEM)] +...  4.08 us
    ppermute x3, waiting for transfers between devices, swap(): return lax.ppermute(block, KA + GA, route)  4.05 us
    pallas_call x1, Pallas kernels, make_pairs(): pl.pallas_call(functools.partial(pair_kernel, 1.0 / math.sqrt(2 * half_k)...  2.96 us
    unnamed x6, local copies, waits for them, and re-layouts  2.32 us
    pallas_call x1, Pallas kernels, make_front(): pl.pallas_call(front_kernel, in_specs=[pl.BlockSpec(memory_space=pltpu.SM...  1.97 us
  transfers between devices with their start and end apart: 5, of which 4 were waited for; matrix products, arithmetic and copies ran while one was open for 1% of the time, Pallas kernels for 7%

profile of v19, /device:TPU:1, one launch (start us, length us, event | category | flops | bytes accessed | tf_op | source)
XLA Modules:
  0.0 58.0 jit_solution(10340200804119833451)
XLA Ops:
  0.0 0.0 copy-start.1
  0.0 0.1 pad_add_fusion.2.place_ref
  0.1 0.6 %copy-done.1 = s32[512]{0:T(512)S(1)} copy-done((s32[512]{0:T(512)S(1)}, s32[512]{0:T(512)}, u32[]{:S(2)}) %copy-start.1) | copy-done | bytes 2072
  0.7 0.0 copy-start
  0.7 1.0 %copy-done = bf16[2,512,256]{2,1,0:T(8,128)(2,1)S(1)} copy-done((bf16[2,512,256]{2,1,0:T(8,128)(2,1)S(1)}, bf16[2,512,256]{2,1,0:T(8,128)(2,1)}, u32[]{:S(2)}) %copy-start) | copy-done | bytes 524312
  1.7 2.0 %front.1 = (bf16[512,256]{1,0:T(8,128)(2,1)S(1)}, bf16[512,256]{1,0:T(8,128)(2,1)S(1)}, bf16[2,256,256]{2,1,0:T(8,128)(2,1)S(1)}) custom-call(s32[2]{0:T(128)S(1)} %pad_add_fusion.2.place_ref, s32[1,512]{1,0:T(1,128)S(1)} %bitcast.8, bf16[2,512,256]{2,1,0:T(8,128)(2,1)S(1)} %copy-done), custom_call_target="tpu_custom_call" | custom-call | tf_op jit(solution)/shard_map/front/pallas_call | solution.py:75
  3.7 2.1 %collective-permute-start = (bf16[2,256,256]{2,1,0:T(8,128)(2,1)S(1)}, bf16[2,256,256]{2,1,0:T(8,128)(2,1)S(1)}, u32[]{:S(2)}, u32[]{:S(2)}) collective-permute-start(bf16[2,256,256]{2,1,0:T(8,128)(2,1)S(1)} %get-tuple-element.14.refs_0_), channel_id=1, source_target_pairs={{0,1},{1,0},{2,3},{3,2},{4,5},{5,4},{6,7},{7,6},{8,9},{9,8},{10,11... | collective-permute-start | bytes 786440 | tf_op jit(solution)/shard_map/ppermute | solution.py:26
  5.8 3.3 %collective-permute-start.1 = (bf16[512,256]{1,0:T(8,128)(2,1)S(1)}, bf16[512,256]{1,0:T(8,128)(2,1)S(1)}, u32[]{:S(2)}, u32[]{:S(2)}) collective-permute-start(bf16[512,256]{1,0:T(8,128)(2,1)S(1)} %get-tuple-element.12.mine_ref), channel_id=1, source_target_pairs={{0,24},{1,25},{2,26},{3,27},{4,28},{5,29},{6,30},{7,31},{8,16},{9,... | collective-permute-start | bytes 786440 | tf_op jit(solution)/shard_map/ppermute | solution.py:26
  9.2 0.0 collective-permute-start.2
  9.2 0.1 pad_add_fusion.3
  9.2 0.1 dynamic_slice.8
  9.3 0.1 broadcast_subtract_fusion.rows_ref
  9.4 2.5 %collective-permute-done.refs_1_ = bf16[2,256,256]{2,1,0:T(8,128)(2,1)S(1)} collective-permute-done((bf16[2,256,256]{2,1,0:T(8,128)(2,1)S(1)}, bf16[2,256,256]{2,1,0:T(8,128)(2,1)S(1)}, u32[]{:S(2)}, u32[]{:S(2)}) %collective-permute-start) | collective-permute-done | bytes 262176 | tf_op jit(solution)/shard_map/ppermute | solution.py:26
  11.9 1.8 %fields.2 = bf16[8,2,2,32,512]{4,3,2,1,0:T(8,128)(2,1)} custom-call(s32[2]{0:T(128)S(1)} %pad_add_fusion.2.place_ref, bf16[512,256]{1,0:T(8,128)(2,1)S(1)} %get-tuple-element.12.mine_ref, bf16[512,256]{1,0:T(8,128)(2,1)S(1)} %get-tuple-element.13.other_ref, bf16[2,256,256]{2,1,0:T(8,128)(2,1)S(1)} %get-tuple-element.14.refs_0_, ...), custom_call_target="tpu_custom_call" | custom-call | flops 1000000000 | bytes 3000000 | tf_op jit(solution)/shard_map/fields/pallas_call | solution.py:140
  13.7 5.2 %all-to-all-start = ((bf16[16,2,32,512]{3,2,1,0:T(8,128)(2,1)}), bf16[16,2,32,512]{3,2,1,0:T(8,128)(2,1)S(1)}, u32[]{:S(2)}, u32[]{:S(2)}) async-start(bf16[16,2,32,512]{3,2,1,0:T(8,128)(2,1)} %bitcast.5), calls=%async_computation | async-start | bytes 2097152 | tf_op jit(solution)/shard_map/all_to_all | solution.py:230
  18.9 0.0 collective-permute-done.1.refs_0_
  18.9 1.6 %collective-permute-done.2.refs_1_ = bf16[512,256]{1,0:T(8,128)(2,1)S(1)} collective-permute-done((bf16[512,256]{1,0:T(8,128)(2,1)S(1)}, bf16[512,256]{1,0:T(8,128)(2,1)S(1)}, u32[]{:S(2)}, u32[]{:S(2)}) %collective-permute-start.2) | collective-permute-done | bytes 262176 | tf_op jit(solution)/shard_map/ppermute | solution.py:26
  20.5 2.3 %fields.3 = bf16[8,2,2,32,512]{4,3,2,1,0:T(8,128)(2,1)} custom-call(s32[2]{0:T(128)S(1)} %pad_add_fusion.2.place_ref, s32[256,2]{1,0:T(8,128)S(1)} %broadcast_subtract_fusion.rows_ref, bf16[512,256]{1,0:T(8,128)(2,1)S(1)} %collective-permute-done.1.refs_0_, bf16[512,256]{1,0:T(8,128)(2,1)S(1)} %collective-permute-done.2.refs_1_), custom_call_target="tpu_custom_call" | custom-call | flops 60000002048 | bytes 180000000 | tf_op jit(solution)/shard_map/fields/pallas_call | solution.py:140
  22.8 9.7 %all-to-all-done.near_ref = bf16[16,2,32,512]{3,2,1,0:T(8,128)(2,1)S(1)} async-done(((bf16[16,2,32,512]{3,2,1,0:T(8,128)(2,1)}), bf16[16,2,32,512]{3,2,1,0:T(8,128)(2,1)S(1)}, u32[]{:S(2)}, u32[]{:S(2)}) %all-to-all-start) | async-done | bytes 1048608 | tf_op jit(solution)/shard_map/all_to_all | solution.py:230
  32.5 6.0 %all-to-all-start.1 = ((bf16[16,2,32,512]{3,2,1,0:T(8,128)(2,1)}), bf16[16,2,32,512]{3,2,1,0:T(8,128)(2,1)S(1)}, u32[]{:S(2)}, u32[]{:S(2)}) async-start(bf16[16,2,32,512]{3,2,1,0:T(8,128)(2,1)} %bitcast.6), calls=%async_computation.1 | async-start | bytes 2097152 | tf_op jit(solution)/shard_map/all_to_all | solution.py:230
  38.5 0.0 copy-start.2
  38.5 0.7 %copy-done.2 = s32[2,32]{1,0:T(2,128)S(1)} copy-done((s32[2,32]{1,0:T(2,128)S(1)}, s32[2,32]{1,0:T(2,128)}, u32[]{:S(2)}) %copy-start.2) | copy-done | bytes 280
  39.2 0.1 pad_add_fusion
  39.2 0.1 compare_select_fusion
  39.3 0.1 fusion.3
  39.4 0.1 pad_add_fusion.1.table_ref
  39.5 15.5 %all-to-all-done.1.far_ref = bf16[16,2,32,512]{3,2,1,0:T(8,128)(2,1)S(1)} async-done(((bf16[16,2,32,512]{3,2,1,0:T(8,128)(2,1)}), bf16[16,2,32,512]{3,2,1,0:T(8,128)(2,1)S(1)}, u32[]{:S(2)}, u32[]{:S(2)}) %all-to-all-start.1) | async-done | bytes 1048608 | tf_op jit(solution)/shard_map/all_to_all | solution.py:230
  55.0 3.0 %pairs.1 = f32[32,2,2,512]{3,2,1,0:T(2,128)} custom-call(s32[2,32]{1,0:T(2,128)S(1)} %pad_add_fusion.1.table_ref, bf16[16,2,32,512]{3,2,1,0:T(8,128)(2,1)S(1)} %all-to-all-done.near_ref, bf16[16,2,32,512]{3,2,1,0:T(8,128)(2,1)S(1)} %all-to-all-done.1.far_ref), custom_call_target="tpu_custom_call" | custom-call | tf_op jit(solution)/shard_map/pairs/pallas_call | solution.py:198
Async XLA Ops:
  0.0 0.7 %copy-start.1 = (s32[512]{0:T(512)S(1)}, s32[512]{0:T(512)}, u32[]{:S(2)}) copy-start(s32[512]{0:T(512)} %param.5) | copy-start | bytes 6148
  0.7 1.0 %copy-start = (bf16[2,512,256]{2,1,0:T(8,128)(2,1)S(1)}, bf16[2,512,256]{2,1,0:T(8,128)(2,1)}, u32[]{:S(2)}) copy-start(bf16[2,512,256]{2,1,0:T(8,128)(2,1)} %orbitals_ref.1) | copy-start | bytes 1572868
  3.7 8.2 %collective-permute-start = (bf16[2,256,256]{2,1,0:T(8,128)(2,1)S(1)}, bf16[2,256,256]{2,1,0:T(8,128)(2,1)S(1)}, u32[]{:S(2)}, u32[]{:S(2)}) collective-permute-start(bf16[2,256,256]{2,1,0:T(8,128)(2,1)S(1)} %get-tuple-element.14.refs_0_), channel_id=1, source_target_pairs={{0,1},{1,0},{2,3},{3,2},{4,5},{5,4},{6,7},{7,6},{8,9},{9,8},{10,11... | collective-permute-start | bytes 786440 | tf_op jit(solution)/shard_map/ppermute | solution.py:26
  5.8 13.1 %collective-permute-start.1 = (bf16[512,256]{1,0:T(8,128)(2,1)S(1)}, bf16[512,256]{1,0:T(8,128)(2,1)S(1)}, u32[]{:S(2)}, u32[]{:S(2)}) collective-permute-start(bf16[512,256]{1,0:T(8,128)(2,1)S(1)} %get-tuple-element.12.mine_ref), channel_id=1, source_target_pairs={{0,24},{1,25},{2,26},{3,27},{4,28},{5,29},{6,30},{7,31},{8,16},{9,... | collective-permute-start | bytes 786440 | tf_op jit(solution)/shard_map/ppermute | solution.py:26
  9.2 11.4 %collective-permute-start.2 = (bf16[512,256]{1,0:T(8,128)(2,1)S(1)}, bf16[512,256]{1,0:T(8,128)(2,1)S(1)}, u32[]{:S(2)}, u32[]{:S(2)}) collective-permute-start(bf16[512,256]{1,0:T(8,128)(2,1)S(1)} %get-tuple-element.13.other_ref), channel_id=1, source_target_pairs={{0,25},{1,24},{2,27},{3,26},{4,29},{5,28},{6,31},{7,30},{8,17},{9,... | collective-permute-start | bytes 786440 | tf_op jit(solution)/shard_map/ppermute | solution.py:26
  13.7 18.8 %all-to-all-start = ((bf16[16,2,32,512]{3,2,1,0:T(8,128)(2,1)}), bf16[16,2,32,512]{3,2,1,0:T(8,128)(2,1)S(1)}, u32[]{:S(2)}, u32[]{:S(2)}) async-start(bf16[16,2,32,512]{3,2,1,0:T(8,128)(2,1)} %bitcast.5), calls=%async_computation | async-start | bytes 2097152 | tf_op jit(solution)/shard_map/all_to_all | solution.py:230
  32.5 22.5 %all-to-all-start.1 = ((bf16[16,2,32,512]{3,2,1,0:T(8,128)(2,1)}), bf16[16,2,32,512]{3,2,1,0:T(8,128)(2,1)S(1)}, u32[]{:S(2)}, u32[]{:S(2)}) async-start(bf16[16,2,32,512]{3,2,1,0:T(8,128)(2,1)} %bitcast.6), calls=%async_computation.1 | async-start | bytes 2097152 | tf_op jit(solution)/shard_map/all_to_all | solution.py:230
  38.5 0.7 %copy-start.2 = (s32[2,32]{1,0:T(2,128)S(1)}, s32[2,32]{1,0:T(2,128)}, u32[]{:S(2)}) copy-start(s32[2,32]{1,0:T(2,128)} %param.4) | copy-start | bytes 772

commit v20 on v19

--- a/solution.py
+++ b/solution.py
@@ -10,6 +10,7 @@
 from jax.sharding import PartitionSpec as P
 
 VMEM_LIMIT = 40 * 1024 * 1024
+FRONT_LIMIT = 60 * 1024 * 1024
 SPLIT = 2
 KA, GA = ("half", "quarter", "inner"), ("hi", "lo")
 
@@ -32,114 +33,129 @@
 
 
 def front_kernel(
-    place_ref, points_ref, orbitals_ref, mine_ref, other_ref, picked_ref, wanted_ref, sems
+    place_ref, points_ref, orbitals_ref, mine_ref, other_ref, picked_ref, *scratch
 ):
-    slab_size, channels = mine_ref.shape
+    wanted_ref, slab_ref, rows_ref, sems = scratch
+    kdevice, slab_size, _ = orbitals_ref.shape
     npoints = wanted_ref.shape[1]
     first = pl.multiple_of(place_ref[0] * npoints, npoints)
     mine = place_ref[1] % SPLIT
-    points_copy = pltpu.make_async_copy(
-        points_ref.at[:, pl.ds(first, npoints)], wanted_ref, sems.at[0]
-    )
-    points_copy.start()
-    parts = slab_size // 2
-    copies = []
-    for number, (k, slab_ref) in enumerate(((mine, mine_ref), (1 - mine, other_ref))):
-        for part in range(2):
-            rows = pl.ds(part * parts, parts)
-            copies.append(
-                pltpu.make_async_copy(
-                    orbitals_ref.at[k, rows], slab_ref.at[rows], sems.at[1 + 2 * number + part]
-                )
-            )
-            copies[-1].start()
-    points_copy.wait()
+    pairs = [(points_ref.at[:, pl.ds(first, npoints)], wanted_ref)]
+    pairs += [(orbitals_ref.at[k], slab_ref.at[k]) for k in range(kdevice)]
+    pairs += [(orbitals_ref.at[mine], mine_ref), (orbitals_ref.at[1 - mine], other_ref)]
+    pairs += [(rows_ref.at[k], picked_ref.at[k]) for k in range(kdevice)]
+    copies = [
+        pltpu.make_async_copy(source, target, sems.at[number])
+        for number, (source, target) in enumerate(pairs)
+    ]
+    for copy in copies[:-kdevice]:
+        copy.start()
+    copies[0].wait()
     wanted = wanted_ref[...] - place_ref[1] * slab_size
     spot = lax.broadcasted_iota(jnp.int32, (slab_size, npoints), 0)
     chosen = (spot == wanted).astype(jnp.float32).astype(jnp.bfloat16)
-    for number, (k, slab_ref) in enumerate(((mine, mine_ref), (1 - mine, other_ref))):
-        copies[2 * number].wait()
-        copies[2 * number + 1].wait()
+    for k in range(kdevice):
+        copies[1 + k].wait()
         picked = lax.dot_general(
-            chosen, slab_ref[...], (((0,), (0,)), ((), ())), preferred_element_type=jnp.float32
-        )
-        picked_ref[k] = picked.astype(jnp.bfloat16)
+            chosen, slab_ref[k], (((0,), (0,)), ((), ())), preferred_element_type=jnp.float32
+        )
+        rows_ref[k] = picked.astype(jnp.bfloat16)
+        copies[k - kdevice].start()
+    for copy in copies[1 + kdevice :]:
+        copy.wait()
 
 
 def make_front(orbitals, points, place):
     kdevice, slab_size, channels = orbitals.shape
     npoints = points.shape[1] // 2
-    vmem = pl.BlockSpec(memory_space=pltpu.VMEM)
     hbm = pl.BlockSpec(memory_space=pl.ANY)
     slab = jax.ShapeDtypeStruct((slab_size, channels), jnp.bfloat16)
+    picked = jax.ShapeDtypeStruct((kdevice, npoints, channels), jnp.bfloat16)
     return pl.pallas_call(
         front_kernel,
         in_specs=[pl.BlockSpec(memory_space=pltpu.SMEM), hbm, hbm],
-        out_specs=[vmem] * 3,
-        out_shape=[slab, slab, jax.ShapeDtypeStruct((kdevice, npoints, channels), jnp.bfloat16)],
-        scratch_shapes=[pltpu.VMEM((1, npoints), jnp.int32), pltpu.SemaphoreType.DMA((5,))],
-        compiler_params=pltpu.CompilerParams(vmem_limit_bytes=VMEM_LIMIT),
+        out_specs=[hbm] * 3,
+        out_shape=[slab, slab, picked],
+        scratch_shapes=[
+            pltpu.VMEM((1, npoints), jnp.int32),
+            pltpu.VMEM(orbitals.shape, jnp.bfloat16),
+            pltpu.VMEM(picked.shape, jnp.bfloat16),
+            pltpu.SemaphoreType.DMA((3 + 2 * kdevice,)),
+        ],
+        compiler_params=pltpu.CompilerParams(vmem_limit_bytes=FRONT_LIMIT),
         name="front",
     )(place, points, orbitals)
 
 
-def send_products(picked, slab_refs, places, out_ref, parts_ref, sems):
+def near_kernel(orbitals_ref, *refs):
+    *picked_refs, out_ref = refs
     groups, _, _, length, slab_size = out_ref.shape
-    copies = []
-    for slab_ref, rows, place in zip(slab_refs, picked, places, strict=True):
-        for part, turned in enumerate((rows, rotate(rows))):
-            product = lax.dot_general(
-                turned.astype(jnp.bfloat16),
-                slab_ref[...],
-                (((1,), (1,)), ((), ())),
-                preferred_element_type=jnp.float32,
-            )
-            number = len(copies)
-            pieces = product.reshape(groups, length, slab_size)
-            parts_ref[number] = pieces.astype(jnp.bfloat16)
-            copies.append(
-                pltpu.make_async_copy(
-                    parts_ref.at[number], out_ref.at[:, place, part], sems.at[number]
-                )
-            )
-            copies[-1].start()
-    for copy in copies:
-        copy.wait()
-
-
-def near_kernel(place_ref, mine_ref, other_ref, *refs):
-    *picked_refs, out_ref, parts_ref, sems = refs
-    mine = place_ref[1] % SPLIT
-    places = (mine, 1 - mine)
-    picked = [
-        sum(picked_ref[place].astype(jnp.float32) for picked_ref in picked_refs)
-        for place in places
-    ]
-    send_products(picked, (mine_ref, other_ref), places, out_ref, parts_ref, sems)
+    rows = sum(picked_ref[0].astype(jnp.float32) for picked_ref in picked_refs)
+    for part, turned in enumerate((rows, rotate(rows))):
+        product = lax.dot_general(
+            turned.astype(jnp.bfloat16),
+            orbitals_ref[0],
+            (((1,), (1,)), ((), ())),
+            preferred_element_type=jnp.float32,
+        )
+        out_ref[:, 0, part] = product.reshape(groups, length, slab_size).astype(jnp.bfloat16)
+
+
+def make_near(orbitals, shares, groups):
+    kdevice, slab_size, channels = orbitals.shape
+    npoints = shares[0].shape[1]
+    length = npoints // groups
+    return pl.pallas_call(
+        near_kernel,
+        grid=(kdevice,),
+        in_specs=[pl.BlockSpec((1, slab_size, channels), lambda k: (k, 0, 0))]
+        + [pl.BlockSpec((1, npoints, channels), lambda k: (k, 0, 0)) for _ in shares],
+        out_specs=pl.BlockSpec((groups, 1, 2, length, slab_size), lambda k: (0, k, 0, 0, 0)),
+        out_shape=jax.ShapeDtypeStruct((groups, kdevice, 2, length, slab_size), jnp.bfloat16),
+        cost_estimate=pl.CostEstimate(
+            flops=1_000_000_000, bytes_accessed=3_000_000, transcendentals=0
+        ),
+        compiler_params=pltpu.CompilerParams(vmem_limit_bytes=VMEM_LIMIT),
+        name="near",
+    )(orbitals, *shares)
 
 
 def far_kernel(place_ref, rows_ref, *refs):
     *slab_refs, out_ref, parts_ref, sems = refs
-    slab_size, _ = slab_refs[0].shape
-    npoints = rows_ref.shape[0]
-    mine = place_ref[1] % SPLIT
-    spot = lax.broadcasted_iota(jnp.int32, (npoints, slab_size), 1)
+    groups, _, _, length, slab_size = out_ref.shape
+    spot = lax.broadcasted_iota(jnp.int32, (rows_ref.shape[0], slab_size), 1)
     picked = 0.0
     for number, slab_ref in enumerate(slab_refs):
         chosen = (rows_ref[:, number : number + 1] == spot).astype(jnp.float32)
         picked += jnp.dot(
             chosen.astype(jnp.bfloat16), slab_ref[...], preferred_element_type=jnp.float32
         )
-    send_products(
-        (picked,) * SPLIT, slab_refs[:SPLIT], (mine, 1 - mine), out_ref, parts_ref, sems
-    )
-
-
-def make_fields(kernel, inputs, place, groups, length, slab_size, work):
+    turned = [rows.astype(jnp.bfloat16) for rows in (picked, rotate(picked))]
+    copies = []
+    for number in range(SPLIT):
+        for part in range(2):
+            product = lax.dot_general(
+                turned[part],
+                slab_refs[number][...],
+                (((1,), (1,)), ((), ())),
+                preferred_element_type=jnp.float32,
+            )
+            place = len(copies)
+            parts_ref[place] = product.reshape(groups, length, slab_size).astype(jnp.bfloat16)
+            target = out_ref.at[:, place_ref[1] % SPLIT ^ number, part]
+            copies.append(pltpu.make_async_copy(parts_ref.at[place], target, sems.at[place]))
+            copies[-1].start()
+    for copy in copies:
+        copy.wait()
+
+
+def make_far(rows, slabs, place, groups):
+    slab_size, _ = slabs[0].shape
+    length = rows.shape[0] // groups
     vmem = pl.BlockSpec(memory_space=pltpu.VMEM)
     return pl.pallas_call(
-        kernel,
-        in_specs=[pl.BlockSpec(memory_space=pltpu.SMEM)] + [vmem] * len(inputs),
+        far_kernel,
+        in_specs=[pl.BlockSpec(memory_space=pltpu.SMEM), vmem] + [vmem] * len(slabs),
         out_specs=pl.BlockSpec(memory_space=pl.ANY),
         out_shape=jax.ShapeDtypeStruct((groups, SPLIT, 2, length, slab_size), jnp.bfloat16),
         scratch_shapes=[
@@ -147,11 +163,11 @@
             pltpu.SemaphoreType.DMA((2 * SPLIT,)),
         ],
         cost_estimate=pl.CostEstimate(
-            flops=work * 1_000_000_000, bytes_accessed=work * 3_000_000, transcendentals=0
+            flops=60_000_000_000, bytes_accessed=180_000_000, transcendentals=0
         ),
         compiler_params=pltpu.CompilerParams(vmem_limit_bytes=VMEM_LIMIT),
-        name="fields",
-    )(place, *inputs)
+        name="far",
+    )(place, rows, *slabs)
 
 
 def pair_kernel(scale, table_ref, near_ref, far_ref, out_ref, held_ref, sums_ref, sems):
@@ -217,7 +233,6 @@
     slabs = lax.axis_size("hi") * lax.axis_size("lo")
     total_k = 2 * groups * kdevice
     npoints = points.shape[0] // 2
-    sizes = (groups, npoints // groups, slab_size)
     here = lax.axis_index("hi") * SPLIT + lax.axis_index("lo")
     place = jnp.stack([half, here])
 
@@ -229,12 +244,12 @@
         fields = fields.reshape((-1,) + fields.shape[-3:])
         return lax.all_to_all(fields, around, split_axis=0, concat_axis=0, tiled=True)
 
-    near_fields = make_fields(near_kernel, [mine, other] + shares, place, *sizes, 1)
+    near_fields = make_near(orbitals, shares, groups)
     wanted = lax.dynamic_slice_in_dim(points, half * npoints, npoints)
     starts = jnp.stack([(here ^ x) * slab_size for x in range(slabs)])
     rows = wanted[:, None] - starts[None, :]
     near_fields, rows = lax.optimization_barrier((near_fields, rows))
-    far_fields = make_fields(far_kernel, [rows] + far, place, *sizes, 60)
+    far_fields = make_far(rows, far, place, groups)
     near_fields = send(near_fields, ("quarter", "inner"))
     near_fields, far_fields = lax.optimization_barrier((near_fields, far_fields))
     far_fields = send(far_fields, ("quarter", "inner", "lo"))

time: 58.3 us -> 73.1 us (1.25)
  Pallas kernels: 9.01 us -> 24.5 us
    pallas_call x1, Pallas kernels: 1.97 us -> 17.7 us  [make_front(): pl.pallas_call(front_kernel, in_specs=[pl.BlockSpec(memory_space=pltpu.SM...]
    ppermute x3, waiting for transfers between devices: 4.05 us -> 2.8 us  [swap(): return lax.ppermute(block, KA + GA, route)]
    all_to_all x2, waiting for transfers between devices: 25.3 us -> 26 us  [send(): lax.all_to_all(fields, around, split_axis=0, concat_axis=0, tiled=True)]
    unnamed x6 -> x10, local copies, waits for them, and re-layouts: 2.32 us -> 2.31 us
  transfers between devices with their start and end apart: 5 -> 5, of which waited for: 4 -> 4; matrix products, arithmetic and copies ran while one was open for 1% -> 1% of each run, Pallas kernels for 7% -> 5%
where the time goes in v20:
time: 73.1 us; the launch traced here: 72.8 us
  waiting for transfers between devices  28.8 us (39%)
  Pallas kernels  24.5 us (34%)
  starting transfers between devices  16 us (22%)
  local copies, waits for them, and re-layouts  2.46 us (3%)
  other arithmetic  1 us (1%)
    all_to_all x2, waiting for transfers between devices, send(): lax.all_to_all(fields, around, split_axis=0, concat_axis=0, tiled=True)  26 us
    pallas_call x1, Pallas kernels, make_front(): pl.pallas_call(front_kernel, in_specs=[pl.BlockSpec(memory_space=pltpu.SM...  17.7 us
    all_to_all x2, starting transfers between devices, send(): lax.all_to_all(fields, around, split_axis=0, concat_axis=0, tiled=True)  10.5 us
    ppermute x3, starting transfers between devices, swap(): return lax.ppermute(block, KA + GA, route)  5.46 us
    pallas_call x1, Pallas kernels, make_pairs(): pl.pallas_call(functools.partial(pair_kernel, 1.0 / math.sqrt(2 * half_k)...  2.96 us
    ppermute x3, waiting for transfers between devices, swap(): return lax.ppermute(block, KA + GA, route)  2.8 us
    unnamed x10, local copies, waits for them, and re-layouts  2.31 us
    pallas_call x1, Pallas kernels, make_far(): pl.pallas_call(far_kernel, in_specs=[pl.BlockSpec(memory_space=pltpu.SMEM...  2.28 us
  transfers between devices with their start and end apart: 5, of which 4 were waited for; matrix products, arithmetic and copies ran while one was open for 1% of the time, Pallas kernels for 5%

profile of v20, /device:TPU:1, one launch (start us, length us, event | category | flops | bytes accessed | tf_op | source)
XLA Modules:
  0.0 72.8 jit_solution(8893089656661556005)
XLA Ops:
  0.0 0.0 copy-start
  0.0 0.6 pad_add_fusion.2.place_ref
  0.6 17.7 %front.1 = (bf16[512,256]{1,0:T(8,128)(2,1)}, bf16[512,256]{1,0:T(8,128)(2,1)}, bf16[2,256,256]{2,1,0:T(8,128)(2,1)}) custom-call(s32[2]{0:T(128)} %pad_add_fusion.2.place_ref, s32[1,512]{1,0:T(1,128)} %bitcast.9, bf16[2,512,256]{2,1,0:T(8,128)(2,1)} %orbitals_ref.3), custom_call_target="tpu_custom_call" | custom-call | tf_op jit(solution)/shard_map/front/pallas_call | solution.py:74
  18.3 2.1 %collective-permute-start = (bf16[2,256,256]{2,1,0:T(8,128)(2,1)}, bf16[2,256,256]{2,1,0:T(8,128)(2,1)S(1)}, u32[]{:S(2)}, u32[]{:S(2)}) collective-permute-start(bf16[2,256,256]{2,1,0:T(8,128)(2,1)} %get-tuple-element.12.refs_0_), channel_id=1, source_target_pairs={{0,1},{1,0},{2,3},{3,2},{4,5},{5,4},{6,7},{7,6},{8,9},{9,8},{10,11... | collective-permute-start | bytes 786440 | tf_op jit(solution)/shard_map/ppermute | solution.py:27
  20.4 3.3 %collective-permute-start.1 = (bf16[512,256]{1,0:T(8,128)(2,1)}, bf16[512,256]{1,0:T(8,128)(2,1)S(1)}, u32[]{:S(2)}, u32[]{:S(2)}) collective-permute-start(bf16[512,256]{1,0:T(8,128)(2,1)} %get-tuple-element.15), channel_id=1, source_target_pairs={{0,24},{1,25},{2,26},{3,27},{4,28},{5,29},{6,30},{7,31},{8,16},{9,... | collective-permute-start | bytes 786440 | tf_op jit(solution)/shard_map/ppermute | solution.py:27
  23.8 0.0 collective-permute-start.2
  23.8 0.1 pad_add_fusion.3
  23.9 0.0 copy-start.3
  23.9 0.7 copy-done.3
  24.5 0.1 dynamic_slice.8
  24.6 0.1 broadcast_subtract_fusion.rows_ref
  24.7 2.0 %collective-permute-done.refs_1_ = bf16[2,256,256]{2,1,0:T(8,128)(2,1)S(1)} collective-permute-done((bf16[2,256,256]{2,1,0:T(8,128)(2,1)}, bf16[2,256,256]{2,1,0:T(8,128)(2,1)S(1)}, u32[]{:S(2)}, u32[]{:S(2)}) %collective-permute-start) | collective-permute-done | bytes 262176 | tf_op jit(solution)/shard_map/ppermute | solution.py:27
  26.7 0.0 copy-done
  26.7 0.0 copy-start.2
  26.7 0.9 %copy-done.2 = bf16[2,256,256]{2,1,0:T(8,128)(2,1)S(1)} copy-done((bf16[2,256,256]{2,1,0:T(8,128)(2,1)S(1)}, bf16[2,256,256]{2,1,0:T(8,128)(2,1)}, u32[]{:S(2)}) %copy-start.2) | copy-done | bytes 262168
  27.6 1.5 %near.1 = bf16[8,2,2,32,512]{4,3,2,1,0:T(8,128)(2,1)} custom-call(bf16[2,512,256]{2,1,0:T(8,128)(2,1)S(1)} %copy-done, bf16[2,256,256]{2,1,0:T(8,128)(2,1)S(1)} %copy-done.2, bf16[2,256,256]{2,1,0:T(8,128)(2,1)S(1)} %collective-permute-done.refs_1_), custom_call_target="tpu_custom_call" | custom-call | flops 1000000000 | bytes 3000000 | tf_op jit(solution)/shard_map/near/pallas_call | solution.py:108
  29.2 0.0 copy-start.1
  29.2 5.4 %all-to-all-start = ((bf16[16,2,32,512]{3,2,1,0:T(8,128)(2,1)}), bf16[16,2,32,512]{3,2,1,0:T(8,128)(2,1)S(1)}, u32[]{:S(2)}, u32[]{:S(2)}) async-start(bf16[16,2,32,512]{3,2,1,0:T(8,128)(2,1)} %bitcast.5), calls=%async_computation | async-start | bytes 2097152 | tf_op jit(solution)/shard_map/all_to_all | solution.py:245
  34.5 0.0 collective-permute-done.1.refs_0_
  34.5 0.8 %collective-permute-done.2.refs_1_ = bf16[512,256]{1,0:T(8,128)(2,1)S(1)} collective-permute-done((bf16[512,256]{1,0:T(8,128)(2,1)}, bf16[512,256]{1,0:T(8,128)(2,1)S(1)}, u32[]{:S(2)}, u32[]{:S(2)}) %collective-permute-start.2) | collective-permute-done | bytes 262176 | tf_op jit(solution)/shard_map/ppermute | solution.py:27
  35.3 0.0 copy-done.1
  35.3 2.3 %far.1 = bf16[8,2,2,32,512]{4,3,2,1,0:T(8,128)(2,1)} custom-call(s32[2]{0:T(128)S(1)} %copy-done.1, s32[256,2]{1,0:T(8,128)S(1)} %broadcast_subtract_fusion.rows_ref, bf16[512,256]{1,0:T(8,128)(2,1)S(1)} %collective-permute-done.1.refs_0_, bf16[512,256]{1,0:T(8,128)(2,1)S(1)} %collective-permute-done.2.refs_1_), custom_call_target="tpu_custom_call" | custom-call | flops 60000002048 | bytes 180000000 | tf_op jit(solution)/shard_map/far/pallas_call | solution.py:156
  37.6 10.5 %all-to-all-done.near_ref = bf16[16,2,32,512]{3,2,1,0:T(8,128)(2,1)S(1)} async-done(((bf16[16,2,32,512]{3,2,1,0:T(8,128)(2,1)}), bf16[16,2,32,512]{3,2,1,0:T(8,128)(2,1)S(1)}, u32[]{:S(2)}, u32[]{:S(2)}) %all-to-all-start) | async-done | bytes 1048608 | tf_op jit(solution)/shard_map/all_to_all | solution.py:245
  48.1 5.1 %all-to-all-start.1 = ((bf16[16,2,32,512]{3,2,1,0:T(8,128)(2,1)}), bf16[16,2,32,512]{3,2,1,0:T(8,128)(2,1)S(1)}, u32[]{:S(2)}, u32[]{:S(2)}) async-start(bf16[16,2,32,512]{3,2,1,0:T(8,128)(2,1)} %bitcast.6), calls=%async_computation.1 | async-start | bytes 2097152 | tf_op jit(solution)/shard_map/all_to_all | solution.py:245
  53.3 0.0 copy-start.4
  53.3 0.7 copy-done.4
  53.9 0.1 pad_add_fusion
  54.0 0.1 compare_select_fusion
  54.1 0.1 fusion.3
  54.2 0.1 pad_add_fusion.1.table_ref
  54.3 15.5 %all-to-all-done.1.far_ref = bf16[16,2,32,512]{3,2,1,0:T(8,128)(2,1)S(1)} async-done(((bf16[16,2,32,512]{3,2,1,0:T(8,128)(2,1)}), bf16[16,2,32,512]{3,2,1,0:T(8,128)(2,1)S(1)}, u32[]{:S(2)}, u32[]{:S(2)}) %all-to-all-start.1) | async-done | bytes 1048608 | tf_op jit(solution)/shard_map/all_to_all | solution.py:245
  69.8 3.0 %pairs.1 = f32[32,2,2,512]{3,2,1,0:T(2,128)} custom-call(s32[2,32]{1,0:T(2,128)S(1)} %pad_add_fusion.1.table_ref, bf16[16,2,32,512]{3,2,1,0:T(8,128)(2,1)S(1)} %all-to-all-done.near_ref, bf16[16,2,32,512]{3,2,1,0:T(8,128)(2,1)S(1)} %all-to-all-done.1.far_ref), custom_call_target="tpu_custom_call" | custom-call | tf_op jit(solution)/shard_map/pairs/pallas_call | solution.py:214
Async XLA Ops:
  0.0 26.7 %copy-start = (bf16[2,512,256]{2,1,0:T(8,128)(2,1)S(1)}, bf16[2,512,256]{2,1,0:T(8,128)(2,1)}, u32[]{:S(2)}) copy-start(bf16[2,512,256]{2,1,0:T(8,128)(2,1)} %orbitals_ref.3) | copy-start | bytes 1572868
  18.3 8.4 %collective-permute-start = (bf16[2,256,256]{2,1,0:T(8,128)(2,1)}, bf16[2,256,256]{2,1,0:T(8,128)(2,1)S(1)}, u32[]{:S(2)}, u32[]{:S(2)}) collective-permute-start(bf16[2,256,256]{2,1,0:T(8,128)(2,1)} %get-tuple-element.12.refs_0_), channel_id=1, source_target_pairs={{0,1},{1,0},{2,3},{3,2},{4,5},{5,4},{6,7},{7,6},{8,9},{9,8},{10,11... | collective-permute-start | bytes 786440 | tf_op jit(solution)/shard_map/ppermute | solution.py:27
  20.4 14.1 %collective-permute-start.1 = (bf16[512,256]{1,0:T(8,128)(2,1)}, bf16[512,256]{1,0:T(8,128)(2,1)S(1)}, u32[]{:S(2)}, u32[]{:S(2)}) collective-permute-start(bf16[512,256]{1,0:T(8,128)(2,1)} %get-tuple-element.15), channel_id=1, source_target_pairs={{0,24},{1,25},{2,26},{3,27},{4,28},{5,29},{6,30},{7,31},{8,16},{9,... | collective-permute-start | bytes 786440 | tf_op jit(solution)/shard_map/ppermute | solution.py:27
  23.8 11.6 %collective-permute-start.2 = (bf16[512,256]{1,0:T(8,128)(2,1)}, bf16[512,256]{1,0:T(8,128)(2,1)S(1)}, u32[]{:S(2)}, u32[]{:S(2)}) collective-permute-start(bf16[512,256]{1,0:T(8,128)(2,1)} %get-tuple-element.16), channel_id=1, source_target_pairs={{0,25},{1,24},{2,27},{3,26},{4,29},{5,28},{6,31},{7,30},{8,17},{9,... | collective-permute-start | bytes 786440 | tf_op jit(solution)/shard_map/ppermute | solution.py:27
  23.9 0.7 copy-start.3
  26.7 1.0 %copy-start.2 = (bf16[2,256,256]{2,1,0:T(8,128)(2,1)S(1)}, bf16[2,256,256]{2,1,0:T(8,128)(2,1)}, u32[]{:S(2)}) copy-start(bf16[2,256,256]{2,1,0:T(8,128)(2,1)} %get-tuple-element.12.refs_0_) | copy-start | bytes 786436
  29.2 6.2 %copy-start.1 = (s32[2]{0:T(128)S(1)}, s32[2]{0:T(128)}, u32[]{:S(2)}) copy-start(s32[2]{0:T(128)} %pad_add_fusion.2.place_ref) | copy-start | bytes 28
  29.2 19.0 %all-to-all-start = ((bf16[16,2,32,512]{3,2,1,0:T(8,128)(2,1)}), bf16[16,2,32,512]{3,2,1,0:T(8,128)(2,1)S(1)}, u32[]{:S(2)}, u32[]{:S(2)}) async-start(bf16[16,2,32,512]{3,2,1,0:T(8,128)(2,1)} %bitcast.5), calls=%async_computation | async-start | bytes 2097152 | tf_op jit(solution)/shard_map/all_to_all | solution.py:245
  48.1 21.7 %all-to-all-start.1 = ((bf16[16,2,32,512]{3,2,1,0:T(8,128)(2,1)}), bf16[16,2,32,512]{3,2,1,0:T(8,128)(2,1)S(1)}, u32[]{:S(2)}, u32[]{:S(2)}) async-start(bf16[16,2,32,512]{3,2,1,0:T(8,128)(2,1)} %bitcast.6), calls=%async_computation.1 | async-start | bytes 2097152 | tf_op jit(solution)/shard_map/all_to_all | solution.py:245
  53.3 0.7 copy-start.4

commit v21 on v20

--- a/solution.py
+++ b/solution.py
@@ -42,20 +42,23 @@
     mine = place_ref[1] % SPLIT
     pairs = [(points_ref.at[:, pl.ds(first, npoints)], wanted_ref)]
     pairs += [(orbitals_ref.at[k], slab_ref.at[k]) for k in range(kdevice)]
-    pairs += [(orbitals_ref.at[mine], mine_ref), (orbitals_ref.at[1 - mine], other_ref)]
+    pairs += [(slab_ref.at[mine], mine_ref), (slab_ref.at[1 - mine], other_ref)]
     pairs += [(rows_ref.at[k], picked_ref.at[k]) for k in range(kdevice)]
     copies = [
         pltpu.make_async_copy(source, target, sems.at[number])
         for number, (source, target) in enumerate(pairs)
     ]
-    for copy in copies[:-kdevice]:
+    for copy in copies[: 1 + kdevice]:
         copy.start()
     copies[0].wait()
     wanted = wanted_ref[...] - place_ref[1] * slab_size
     spot = lax.broadcasted_iota(jnp.int32, (slab_size, npoints), 0)
     chosen = (spot == wanted).astype(jnp.float32).astype(jnp.bfloat16)
+    for copy in copies[1 : 1 + kdevice]:
+        copy.wait()
+    for copy in copies[1 + kdevice : -kdevice]:
+        copy.start()
     for k in range(kdevice):
-        copies[1 + k].wait()
         picked = lax.dot_general(
             chosen, slab_ref[k], (((0,), (0,)), ((), ())), preferred_element_type=jnp.float32
         )

time: 73.1 us -> 58.2 us (0.80)
  Pallas kernels: 24.5 us -> 9.55 us
    pallas_call x1, Pallas kernels: 17.7 us -> 2.78 us  [make_front(): pl.pallas_call(front_kernel, in_specs=[pl.BlockSpec(memory_space=pltpu.SM...]
  transfers between devices with their start and end apart: 5 -> 5, of which waited for: 4 -> 4; matrix products, arithmetic and copies ran while one was open for 1% -> 1% of each run, Pallas kernels for 5% -> 7%
where the time goes in v21:
time: 58.2 us; the launch traced here: 57.8 us
  waiting for transfers between devices  28.8 us (49%)
  starting transfers between devices  16 us (27%)
  Pallas kernels  9.55 us (16%)
  local copies, waits for them, and re-layouts  2.46 us (4%)
  other arithmetic  1 us (2%)
    all_to_all x2, waiting for transfers between devices, send(): lax.all_to_all(fields, around, split_axis=0, concat_axis=0, tiled=True)  26 us
    all_to_all x2, starting transfers between devices, send(): lax.all_to_all(fields, around, split_axis=0, concat_axis=0, tiled=True)  10.5 us
    ppermute x3, starting transfers between devices, swap(): return lax.ppermute(block, KA + GA, route)  5.46 us
    pallas_call x1, Pallas kernels, make_pairs(): pl.pallas_call(functools.partial(pair_kernel, 1.0 / math.sqrt(2 * half_k)...  2.96 us
    ppermute x3, waiting for transfers between devices, swap(): return lax.ppermute(block, KA + GA, route)  2.8 us
    pallas_call x1, Pallas kernels, make_front(): pl.pallas_call(front_kernel, in_specs=[pl.BlockSpec(memory_space=pltpu.SM...  2.78 us
    unnamed x10, local copies, waits for them, and re-layouts  2.31 us
    pallas_call x1, Pallas kernels, make_far(): pl.pallas_call(far_kernel, in_specs=[pl.BlockSpec(memory_space=pltpu.SMEM...  2.28 us
  transfers between devices with their start and end apart: 5, of which 4 were waited for; matrix products, arithmetic and copies ran while one was open for 1% of the time, Pallas kernels for 7%

profile of v21, /device:TPU:1, one launch (start us, length us, event | category | flops | bytes accessed | tf_op | source)
XLA Modules:
  0.0 57.8 jit_solution(3884672614153150325)
XLA Ops:
  0.0 0.0 copy-start
  0.0 0.6 %pad_add_fusion.2.place_ref = s32[2]{0:T(128)} fusion(s32[1]{0:T(128)} %bitcast.1, s32[1]{0:T(128)} %bitcast), kind=kLoop, calls=%fused_computation.13 | loop fusion | flops 2 | bytes 16 | tf_op jit(solution)/shard_map/stack | solution.py:240
  0.6 2.8 %front.1 = (bf16[512,256]{1,0:T(8,128)(2,1)}, bf16[512,256]{1,0:T(8,128)(2,1)}, bf16[2,256,256]{2,1,0:T(8,128)(2,1)}) custom-call(s32[2]{0:T(128)} %pad_add_fusion.2.place_ref, s32[1,512]{1,0:T(1,128)} %bitcast.9, bf16[2,512,256]{2,1,0:T(8,128)(2,1)} %orbitals_ref.3), custom_call_target="tpu_custom_call" | custom-call | tf_op jit(solution)/shard_map/front/pallas_call | solution.py:77
  3.4 2.1 %collective-permute-start = (bf16[2,256,256]{2,1,0:T(8,128)(2,1)}, bf16[2,256,256]{2,1,0:T(8,128)(2,1)S(1)}, u32[]{:S(2)}, u32[]{:S(2)}) collective-permute-start(bf16[2,256,256]{2,1,0:T(8,128)(2,1)} %get-tuple-element.12.refs_0_), channel_id=1, source_target_pairs={{0,1},{1,0},{2,3},{3,2},{4,5},{5,4},{6,7},{7,6},{8,9},{9,8},{10,11... | collective-permute-start | bytes 786440 | tf_op jit(solution)/shard_map/ppermute | solution.py:27
  5.5 3.3 %collective-permute-start.1 = (bf16[512,256]{1,0:T(8,128)(2,1)}, bf16[512,256]{1,0:T(8,128)(2,1)S(1)}, u32[]{:S(2)}, u32[]{:S(2)}) collective-permute-start(bf16[512,256]{1,0:T(8,128)(2,1)} %get-tuple-element.15), channel_id=1, source_target_pairs={{0,24},{1,25},{2,26},{3,27},{4,28},{5,29},{6,30},{7,31},{8,16},{9,... | collective-permute-start | bytes 786440 | tf_op jit(solution)/shard_map/ppermute | solution.py:27
  8.8 0.0 collective-permute-start.2
  8.8 0.1 pad_add_fusion.3
  8.9 0.0 copy-start.3
  8.9 0.7 %copy-done.3 = s32[512]{0:T(512)S(1)} copy-done((s32[512]{0:T(512)S(1)}, s32[512]{0:T(512)}, u32[]{:S(2)}) %copy-start.3) | copy-done | bytes 2072
  9.6 0.1 dynamic_slice.8
  9.7 0.1 broadcast_subtract_fusion.rows_ref
  9.8 2.0 %collective-permute-done.refs_1_ = bf16[2,256,256]{2,1,0:T(8,128)(2,1)S(1)} collective-permute-done((bf16[2,256,256]{2,1,0:T(8,128)(2,1)}, bf16[2,256,256]{2,1,0:T(8,128)(2,1)S(1)}, u32[]{:S(2)}, u32[]{:S(2)}) %collective-permute-start) | collective-permute-done | bytes 262176 | tf_op jit(solution)/shard_map/ppermute | solution.py:27
  11.8 0.0 copy-done
  11.8 0.0 copy-start.2
  11.8 0.9 %copy-done.2 = bf16[2,256,256]{2,1,0:T(8,128)(2,1)S(1)} copy-done((bf16[2,256,256]{2,1,0:T(8,128)(2,1)S(1)}, bf16[2,256,256]{2,1,0:T(8,128)(2,1)}, u32[]{:S(2)}) %copy-start.2) | copy-done | bytes 262168
  12.7 1.5 %near.1 = bf16[8,2,2,32,512]{4,3,2,1,0:T(8,128)(2,1)} custom-call(bf16[2,512,256]{2,1,0:T(8,128)(2,1)S(1)} %copy-done, bf16[2,256,256]{2,1,0:T(8,128)(2,1)S(1)} %copy-done.2, bf16[2,256,256]{2,1,0:T(8,128)(2,1)S(1)} %collective-permute-done.refs_1_), custom_call_target="tpu_custom_call" | custom-call | flops 1000000000 | bytes 3000000 | tf_op jit(solution)/shard_map/near/pallas_call | solution.py:111
  14.2 0.0 copy-start.1
  14.2 5.4 %all-to-all-start = ((bf16[16,2,32,512]{3,2,1,0:T(8,128)(2,1)}), bf16[16,2,32,512]{3,2,1,0:T(8,128)(2,1)S(1)}, u32[]{:S(2)}, u32[]{:S(2)}) async-start(bf16[16,2,32,512]{3,2,1,0:T(8,128)(2,1)} %bitcast.5), calls=%async_computation | async-start | bytes 2097152 | tf_op jit(solution)/shard_map/all_to_all | solution.py:248
  19.6 0.0 collective-permute-done.1.refs_0_
  19.6 0.8 %collective-permute-done.2.refs_1_ = bf16[512,256]{1,0:T(8,128)(2,1)S(1)} collective-permute-done((bf16[512,256]{1,0:T(8,128)(2,1)}, bf16[512,256]{1,0:T(8,128)(2,1)S(1)}, u32[]{:S(2)}, u32[]{:S(2)}) %collective-permute-start.2) | collective-permute-done | bytes 262176 | tf_op jit(solution)/shard_map/ppermute | solution.py:27
  20.4 0.0 copy-done.1
  20.4 2.3 %far.1 = bf16[8,2,2,32,512]{4,3,2,1,0:T(8,128)(2,1)} custom-call(s32[2]{0:T(128)S(1)} %copy-done.1, s32[256,2]{1,0:T(8,128)S(1)} %broadcast_subtract_fusion.rows_ref, bf16[512,256]{1,0:T(8,128)(2,1)S(1)} %collective-permute-done.1.refs_0_, bf16[512,256]{1,0:T(8,128)(2,1)S(1)} %collective-permute-done.2.refs_1_), custom_call_target="tpu_custom_call" | custom-call | flops 60000002048 | bytes 180000000 | tf_op jit(solution)/shard_map/far/pallas_call | solution.py:159
  22.7 10.5 %all-to-all-done.near_ref = bf16[16,2,32,512]{3,2,1,0:T(8,128)(2,1)S(1)} async-done(((bf16[16,2,32,512]{3,2,1,0:T(8,128)(2,1)}), bf16[16,2,32,512]{3,2,1,0:T(8,128)(2,1)S(1)}, u32[]{:S(2)}, u32[]{:S(2)}) %all-to-all-start) | async-done | bytes 1048608 | tf_op jit(solution)/shard_map/all_to_all | solution.py:248
  33.2 5.2 %all-to-all-start.1 = ((bf16[16,2,32,512]{3,2,1,0:T(8,128)(2,1)}), bf16[16,2,32,512]{3,2,1,0:T(8,128)(2,1)S(1)}, u32[]{:S(2)}, u32[]{:S(2)}) async-start(bf16[16,2,32,512]{3,2,1,0:T(8,128)(2,1)} %bitcast.6), calls=%async_computation.1 | async-start | bytes 2097152 | tf_op jit(solution)/shard_map/all_to_all | solution.py:248
  38.3 0.0 copy-start.4
  38.3 0.7 %copy-done.4 = s32[2,32]{1,0:T(2,128)S(1)} copy-done((s32[2,32]{1,0:T(2,128)S(1)}, s32[2,32]{1,0:T(2,128)}, u32[]{:S(2)}) %copy-start.4) | copy-done | bytes 280
  39.0 0.1 pad_add_fusion
  39.1 0.1 compare_select_fusion
  39.2 0.1 fusion.3
  39.2 0.1 pad_add_fusion.1.table_ref
  39.3 15.5 %all-to-all-done.1.far_ref = bf16[16,2,32,512]{3,2,1,0:T(8,128)(2,1)S(1)} async-done(((bf16[16,2,32,512]{3,2,1,0:T(8,128)(2,1)}), bf16[16,2,32,512]{3,2,1,0:T(8,128)(2,1)S(1)}, u32[]{:S(2)}, u32[]{:S(2)}) %all-to-all-start.1) | async-done | bytes 1048608 | tf_op jit(solution)/shard_map/all_to_all | solution.py:248
  54.9 3.0 %pairs.1 = f32[32,2,2,512]{3,2,1,0:T(2,128)} custom-call(s32[2,32]{1,0:T(2,128)S(1)} %pad_add_fusion.1.table_ref, bf16[16,2,32,512]{3,2,1,0:T(8,128)(2,1)S(1)} %all-to-all-done.near_ref, bf16[16,2,32,512]{3,2,1,0:T(8,128)(2,1)S(1)} %all-to-all-done.1.far_ref), custom_call_target="tpu_custom_call" | custom-call | tf_op jit(solution)/shard_map/pairs/pallas_call | solution.py:217
Async XLA Ops:
  0.0 11.8 %copy-start = (bf16[2,512,256]{2,1,0:T(8,128)(2,1)S(1)}, bf16[2,512,256]{2,1,0:T(8,128)(2,1)}, u32[]{:S(2)}) copy-start(bf16[2,512,256]{2,1,0:T(8,128)(2,1)} %orbitals_ref.3) | copy-start | bytes 1572868
  3.4 8.4 %collective-permute-start = (bf16[2,256,256]{2,1,0:T(8,128)(2,1)}, bf16[2,256,256]{2,1,0:T(8,128)(2,1)S(1)}, u32[]{:S(2)}, u32[]{:S(2)}) collective-permute-start(bf16[2,256,256]{2,1,0:T(8,128)(2,1)} %get-tuple-element.12.refs_0_), channel_id=1, source_target_pairs={{0,1},{1,0},{2,3},{3,2},{4,5},{5,4},{6,7},{7,6},{8,9},{9,8},{10,11... | collective-permute-start | bytes 786440 | tf_op jit(solution)/shard_map/ppermute | solution.py:27
  5.5 14.1 %collective-permute-start.1 = (bf16[512,256]{1,0:T(8,128)(2,1)}, bf16[512,256]{1,0:T(8,128)(2,1)S(1)}, u32[]{:S(2)}, u32[]{:S(2)}) collective-permute-start(bf16[512,256]{1,0:T(8,128)(2,1)} %get-tuple-element.15), channel_id=1, source_target_pairs={{0,24},{1,25},{2,26},{3,27},{4,28},{5,29},{6,30},{7,31},{8,16},{9,... | collective-permute-start | bytes 786440 | tf_op jit(solution)/shard_map/ppermute | solution.py:27
  8.8 11.6 %collective-permute-start.2 = (bf16[512,256]{1,0:T(8,128)(2,1)}, bf16[512,256]{1,0:T(8,128)(2,1)S(1)}, u32[]{:S(2)}, u32[]{:S(2)}) collective-permute-start(bf16[512,256]{1,0:T(8,128)(2,1)} %get-tuple-element.16), channel_id=1, source_target_pairs={{0,25},{1,24},{2,27},{3,26},{4,29},{5,28},{6,31},{7,30},{8,17},{9,... | collective-permute-start | bytes 786440 | tf_op jit(solution)/shard_map/ppermute | solution.py:27
  8.9 0.7 %copy-start.3 = (s32[512]{0:T(512)S(1)}, s32[512]{0:T(512)}, u32[]{:S(2)}) copy-start(s32[512]{0:T(512)} %param.5) | copy-start | bytes 6148
  11.8 1.0 %copy-start.2 = (bf16[2,256,256]{2,1,0:T(8,128)(2,1)S(1)}, bf16[2,256,256]{2,1,0:T(8,128)(2,1)}, u32[]{:S(2)}) copy-start(bf16[2,256,256]{2,1,0:T(8,128)(2,1)} %get-tuple-element.12.refs_0_) | copy-start | bytes 786436
  14.2 6.2 %copy-start.1 = (s32[2]{0:T(128)S(1)}, s32[2]{0:T(128)}, u32[]{:S(2)}) copy-start(s32[2]{0:T(128)} %pad_add_fusion.2.place_ref) | copy-start | bytes 28
  14.2 19.0 %all-to-all-start = ((bf16[16,2,32,512]{3,2,1,0:T(8,128)(2,1)}), bf16[16,2,32,512]{3,2,1,0:T(8,128)(2,1)S(1)}, u32[]{:S(2)}, u32[]{:S(2)}) async-start(bf16[16,2,32,512]{3,2,1,0:T(8,128)(2,1)} %bitcast.5), calls=%async_computation | async-start | bytes 2097152 | tf_op jit(solution)/shard_map/all_to_all | solution.py:248
  33.2 21.7 %all-to-all-start.1 = ((bf16[16,2,32,512]{3,2,1,0:T(8,128)(2,1)}), bf16[16,2,32,512]{3,2,1,0:T(8,128)(2,1)S(1)}, u32[]{:S(2)}, u32[]{:S(2)}) async-start(bf16[16,2,32,512]{3,2,1,0:T(8,128)(2,1)} %bitcast.6), calls=%async_computation.1 | async-start | bytes 2097152 | tf_op jit(solution)/shard_map/all_to_all | solution.py:248
  38.3 0.7 %copy-start.4 = (s32[2,32]{1,0:T(2,128)S(1)}, s32[2,32]{1,0:T(2,128)}, u32[]{:S(2)}) copy-start(s32[2,32]{1,0:T(2,128)} %param.4) | copy-start | bytes 772

commit v22 on v17

--- a/solution.py
+++ b/solution.py
@@ -106,111 +106,152 @@
     )(orbitals, *shares)
 
 
-def far_kernel(place_ref, points_ref, *refs):
-    *slab_refs, out_ref, picked_ref = refs
-    slab_size, channels = slab_refs[0].shape
-    npoints = points_ref.shape[1] // 2
-    groups = out_ref.shape[0]
-    step = pl.program_id(0)
-
-    @pl.when(step == 0)
-    def _():
-        picked = jnp.zeros((npoints, channels), jnp.float32)
-        for number, slab_ref in enumerate(slab_refs):
-            slab = place_ref[1] ^ number
-            chosen = one_hot(points_ref, place_ref[0], slab, slab_size, npoints)
-            picked += pick(chosen, slab_ref[...])
-        picked_ref[0] = picked.astype(jnp.bfloat16)
-        picked_ref[1] = rotate(picked).astype(jnp.bfloat16)
-
+def far_kernel(place_ref, rows_ref, *refs):
+    *slab_refs, out_ref, parts_ref, sems = refs
+    groups, _, _, length, slab_size = out_ref.shape
+    spot = lax.broadcasted_iota(jnp.int32, (rows_ref.shape[0], slab_size), 1)
+    picked = 0.0
+    for number, slab_ref in enumerate(slab_refs):
+        chosen = (rows_ref[:, number : number + 1] == spot).astype(jnp.float32)
+        picked += jnp.dot(
+            chosen.astype(jnp.bfloat16), slab_ref[...], preferred_element_type=jnp.float32
+        )
+    turned = [rows.astype(jnp.bfloat16) for rows in (picked, rotate(picked))]
+    copies = []
     for number in range(SPLIT):
-
-        @pl.when(step == number)
-        def _(number=number):
-            for part in range(2):
-                out_ref[:, 0, part] = product(picked_ref[part], slab_refs[number][...], groups)
-
-
-def make_far(slabs, points, groups, place):
-    slab_size, channels = slabs[0].shape
-    npoints = points.shape[1] // 2
-    length = npoints // groups
+        for part in range(2):
+            product = lax.dot_general(
+                turned[part],
+                slab_refs[number][...],
+                (((1,), (1,)), ((), ())),
+                preferred_element_type=jnp.float32,
+            )
+            place = len(copies)
+            parts_ref[place] = product.reshape(groups, length, slab_size).astype(jnp.bfloat16)
+            target = out_ref.at[:, place_ref[1] % SPLIT ^ number, part]
+            copies.append(pltpu.make_async_copy(parts_ref.at[place], target, sems.at[place]))
+            copies[-1].start()
+    for copy in copies:
+        copy.wait()
+
+
+def make_far(rows, slabs, place, groups):
+    slab_size, _ = slabs[0].shape
+    length = rows.shape[0] // groups
+    vmem = pl.BlockSpec(memory_space=pltpu.VMEM)
     return pl.pallas_call(
         far_kernel,
-        grid_spec=pltpu.PrefetchScalarGridSpec(
-            num_scalar_prefetch=1,
-            grid=(SPLIT,),
-            in_specs=[pl.BlockSpec(points.shape, lambda step, place: (0, 0))]
-            + [pl.BlockSpec((slab_size, channels), lambda step, place: (0, 0)) for _ in slabs],
-            out_specs=pl.BlockSpec(
-                (groups, 1, 2, length, slab_size),
-                lambda step, place: (0, place[1] % SPLIT ^ step, 0, 0, 0),
-            ),
-            scratch_shapes=[pltpu.VMEM((2, npoints, channels), jnp.bfloat16)],
-        ),
+        in_specs=[pl.BlockSpec(memory_space=pltpu.SMEM), vmem] + [vmem] * len(slabs),
+        out_specs=pl.BlockSpec(memory_space=pl.ANY),
         out_shape=jax.ShapeDtypeStruct((groups, SPLIT, 2, length, slab_size), jnp.bfloat16),
+        scratch_shapes=[
+            pltpu.VMEM((2 * SPLIT, groups, length, slab_size), jnp.bfloat16),
+            pltpu.SemaphoreType.DMA((2 * SPLIT,)),
+        ],
         cost_estimate=pl.CostEstimate(
             flops=60_000_000_000, bytes_accessed=180_000_000, transcendentals=0
         ),
         compiler_params=pltpu.CompilerParams(vmem_limit_bytes=VMEM_LIMIT),
         name="far",
-    )(place, points, *slabs)
-
-
-def pair_kernel(scale, table_ref, near_ref, far_ref, out_ref, held_ref, sums_ref, sems):
-    total_k, _, length, width = held_ref.shape
+    )(place, rows, *slabs)
+
+
+def add_products(table_ref, held_ref, sums_ref, own_half, write):
+    total_k = table_ref.shape[1]
+    half_k = total_k // 2
+    _, _, length, _ = held_ref.shape
     transfers = table_ref.shape[0]
-    held_ref[: total_k // 2] = near_ref[...].astype(jnp.float32)
-    held_ref[total_k // 2 :] = far_ref[...].astype(jnp.float32)
-
-    count, columns = min(16, length), min(256, width)
-    copies = []
+    count = min(16, length)
     for start in range(0, length, count):
         rows = pl.ds(start, count)
-        for column in range(0, width, columns):
-            lanes = pl.ds(column, columns)
-
-            def step(k, sums):
-                real, imag = held_ref[k, 0, rows, lanes], held_ref[k, 1, rows, lanes]
-                after = []
-                for transfer in range(transfers):
-                    other = table_ref[transfer, k]
-                    other_real = held_ref[other, 0, rows, lanes]
-                    other_imag = held_ref[other, 1, rows, lanes]
-                    after.append(sums[2 * transfer] + (real * other_real + imag * other_imag))
-                    after.append(sums[2 * transfer + 1] + (imag * other_real - real * other_imag))
-                return tuple(after)
-
-            zero = jnp.zeros((count, columns), jnp.float32)
-            sums = lax.fori_loop(0, total_k, step, (zero,) * (2 * transfers), unroll=4)
-            for place, value in enumerate(sums):
-                sums_ref[rows, place // 2, place % 2, lanes] = value * scale
+        for transfer in range(transfers):
+            shift = lax.rem(total_k - table_ref[transfer, 0], total_k)
+            past = jnp.where(shift < half_k, half_k, shift - half_k)
+            if own_half:
+                begin = jnp.where(shift < half_k, shift, 0)
+                steps = past - begin
+            else:
+                begin = past
+                steps = jnp.where(shift < half_k, half_k + shift, total_k + half_k - shift)
+
+            def step(i, sums, begin=begin, shift=shift, rows=rows):
+                real_sum, imag_sum = sums
+                for place in range(2):
+                    k = lax.rem(begin + 2 * i + place, total_k)
+                    other = lax.rem(k + total_k - shift, total_k)
+                    real, imag = held_ref[k, 0, rows], held_ref[k, 1, rows]
+                    other_real, other_imag = held_ref[other, 0, rows], held_ref[other, 1, rows]
+                    real_sum += real * other_real + imag * other_imag
+                    imag_sum += imag * other_real - real * other_imag
+                return real_sum, imag_sum
+
+            if own_half:
+                sums = (jnp.zeros((count, held_ref.shape[3]), jnp.float32),) * 2
+            else:
+                sums = sums_ref[rows, transfer, 0], sums_ref[rows, transfer, 1]
+            sums = lax.fori_loop(0, lax.div(steps, 2), step, sums)
+            for part, value in enumerate(sums):
+                sums_ref[rows, transfer, part] = value
+        if write is not None:
+            write(start // count, rows)
+
+
+def early_kernel(table_ref, near_ref, sums_ref, held_ref):
+    held_ref[...] = near_ref[...].astype(jnp.float32)
+    add_products(table_ref, held_ref, sums_ref, True, None)
+
+
+def pair_kernel(scale, table_ref, near_ref, far_ref, early_ref, out_ref, *scratch):
+    held_ref, sums_ref, sems = scratch
+    half_k = near_ref.shape[0]
+    quarter_k = half_k // 2
+    held_ref[:half_k] = near_ref[...].astype(jnp.float32)
+    held_ref[half_k : half_k + quarter_k] = far_ref[quarter_k:].astype(jnp.float32)
+    held_ref[half_k + quarter_k :] = far_ref[:quarter_k].astype(jnp.float32)
+    sums_ref[...] = early_ref[...]
+    copies = []
+
+    def write(number, rows):
+        sums_ref[rows] = sums_ref[rows] * scale
         copies.append(
-            pltpu.make_async_copy(sums_ref.at[rows], out_ref.at[rows], sems.at[start // count])
+            pltpu.make_async_copy(sums_ref.at[rows], out_ref.at[rows], sems.at[number])
         )
         copies[-1].start()
+
+    add_products(table_ref, held_ref, sums_ref, False, write)
     for copy in copies:
         copy.wait()
 
 
 def make_pairs(near, far, table):
     half_k, _, length, slab_size = near.shape
-    transfers = table.shape[0]
-    out = jax.ShapeDtypeStruct((length, transfers, 2, slab_size), jnp.float32)
-    vmem = pl.BlockSpec(memory_space=pltpu.VMEM)
+    out = jax.ShapeDtypeStruct((length, table.shape[0], 2, slab_size), jnp.float32)
+    smem, vmem = pl.BlockSpec(memory_space=pltpu.SMEM), pl.BlockSpec(memory_space=pltpu.VMEM)
+    early = pl.pallas_call(
+        early_kernel,
+        in_specs=[smem, vmem],
+        out_specs=vmem,
+        out_shape=out,
+        scratch_shapes=[pltpu.VMEM(near.shape, jnp.float32)],
+        cost_estimate=pl.CostEstimate(
+            flops=60_000_000_000, bytes_accessed=180_000_000, transcendentals=0
+        ),
+        compiler_params=pltpu.CompilerParams(vmem_limit_bytes=VMEM_LIMIT),
+        name="early",
+    )(table, near)
     return pl.pallas_call(
         functools.partial(pair_kernel, 1.0 / math.sqrt(2 * half_k)),
-        in_specs=[pl.BlockSpec(memory_space=pltpu.SMEM), vmem, vmem],
+        in_specs=[smem, vmem, vmem, vmem],
         out_specs=pl.BlockSpec(memory_space=pl.ANY),
         out_shape=out,
         scratch_shapes=[
-            pltpu.VMEM((2 * half_k, 2, length, slab_size), jnp.float32),
+            pltpu.VMEM((2 * half_k,) + near.shape[1:], jnp.float32),
             pltpu.VMEM(out.shape, jnp.float32),
             pltpu.SemaphoreType.DMA((length // min(16, length),)),
         ],
         compiler_params=pltpu.CompilerParams(vmem_limit_bytes=VMEM_LIMIT),
         name="pairs",
-    )(table, near, far)
+    )(table, near, far, early)
 
 
 def on_device(orbitals, minus_table, points):
@@ -218,7 +259,6 @@
     half = lax.axis_index("half")
     groups = lax.axis_size("quarter") * lax.axis_size("inner")
     slabs = lax.axis_size("hi") * lax.axis_size("lo")
-    total_k = 2 * groups * kdevice
     points = points.reshape(1, -1)
     place = jnp.stack([half, lax.axis_index("hi") * SPLIT + lax.axis_index("lo")])
 
@@ -231,20 +271,15 @@
         return lax.all_to_all(fields, around, split_axis=0, concat_axis=0, tiled=True)
 
     near_fields = make_near(orbitals, shares, groups)
-    near_fields, points = lax.optimization_barrier((near_fields, points))
-    far_fields = make_far(far, points, groups, place)
+    npoints = points.shape[1] // 2
+    wanted = lax.dynamic_slice_in_dim(points[0], half * npoints, npoints)
+    starts = jnp.stack([(place[1] ^ x) * slab_size for x in range(slabs)])
+    rows = wanted[:, None] - starts[None, :]
+    near_fields, rows = lax.optimization_barrier((near_fields, rows))
+    far_fields = make_far(rows, far, place, groups)
     near_fields = send(near_fields, ("quarter", "inner"))
-    near_fields, far_fields = lax.optimization_barrier((near_fields, far_fields))
     far_fields = send(far_fields, ("quarter", "inner", "lo"))
-
-    def mirrored(kpoints):
-        return total_k // 2 + (kpoints + total_k // 4) % (total_k // 2)
-
-    turn = half * (total_k // 2)
-    table = (jnp.roll(minus_table, -turn, axis=1) - turn) % total_k
-    table = jnp.where(table < total_k // 2, table, mirrored(table))
-    first, third, fourth = jnp.split(table, (total_k // 2, 3 * total_k // 4), axis=1)
-    return make_pairs(near_fields, far_fields, jnp.concatenate([first, fourth, third], axis=1))
+    return make_pairs(near_fields, far_fields, minus_table)
 
 
 def solution(mesh):

time: 57.4 us -> 57.2 us (level)
  Pallas kernels: 7.86 us -> 8.94 us
  local copies, waits for them, and re-layouts: 2.4 us -> 1.73 us
    pallas_call x1 -> x2, Pallas kernels: 2.49 us -> 3.63 us  [the longest x1 2.27 us: make_far(): pl.pallas_call(far_kernel, in_specs=[pl.BlockSpec(memory_space=pltpu.SMEM...]
    unnamed x8, local copies, waits for them, and re-layouts: 2.32 us -> 1.65 us
  transfers between devices with their start and end apart: 5 -> 5, of which waited for: 4 -> 4; matrix products, arithmetic and copies ran while one was open for 1% -> 0% of each run, Pallas kernels for 7% -> 9%
where the time goes in v22:
time: 57.2 us; the launch traced here: 56.9 us
  waiting for transfers between devices  29.5 us (52%)
  starting transfers between devices  16.4 us (29%)
  Pallas kernels  8.94 us (16%)
  local copies, waits for them, and re-layouts  1.73 us (3%)
    all_to_all x2, waiting for transfers between devices, send(): lax.all_to_all(fields, around, split_axis=0, concat_axis=0, tiled=True)  25.2 us
    all_to_all x2, starting transfers between devices, send(): lax.all_to_all(fields, around, split_axis=0, concat_axis=0, tiled=True)  10.9 us
    ppermute x3, starting transfers between devices, swap(): return lax.ppermute(block, KA + GA, route)  5.46 us
    ppermute x3, waiting for transfers between devices, swap(): return lax.ppermute(block, KA + GA, route)  4.38 us
    pallas_call x1, Pallas kernels, make_pairs(): pl.pallas_call(functools.partial(pair_kernel, 1.0 / math.sqrt(2 * half_k)...  2.94 us
    pallas_call x1, Pallas kernels, make_far(): pl.pallas_call(far_kernel, in_specs=[pl.BlockSpec(memory_space=pltpu.SMEM...  2.27 us
    unnamed x8, local copies, waits for them, and re-layouts  1.65 us
    pallas_call x1, Pallas kernels, make_near(): pl.pallas_call(near_kernel, grid=(kdevice,), in_specs=[pl.BlockSpec((1, s...  1.5 us
  transfers between devices with their start and end apart: 5, of which 4 were waited for; matrix products, arithmetic and copies ran while one was open for 0% of the time, Pallas kernels for 9%

profile of v22, /device:TPU:1, one launch (start us, length us, event | category | flops | bytes accessed | tf_op | source)
XLA Modules:
  0.0 56.9 jit_solution(14837364779360882662)
XLA Ops:
  0.0 0.0 copy-start.2
  0.0 0.1 pad_add_fusion.place_ref
  0.1 0.6 %copy-done.2 = s32[512]{0:T(512)S(1)} copy-done((s32[512]{0:T(512)S(1)}, s32[512]{0:T(512)}, u32[]{:S(2)}) %copy-start.2) | copy-done | bytes 2072
  0.7 0.0 copy-start
  0.7 1.0 %copy-done = bf16[2,512,256]{2,1,0:T(8,128)(2,1)S(1)} copy-done((bf16[2,512,256]{2,1,0:T(8,128)(2,1)S(1)}, bf16[2,512,256]{2,1,0:T(8,128)(2,1)}, u32[]{:S(2)}) %copy-start) | copy-done | bytes 524312
  1.7 0.0 copy-start.1
  1.7 0.9 %front.1 = (bf16[512,256]{1,0:T(8,128)(2,1)S(1)}, bf16[512,256]{1,0:T(8,128)(2,1)S(1)}, bf16[2,256,256]{2,1,0:T(8,128)(2,1)S(1)}) custom-call(s32[2]{0:T(128)S(1)} %pad_add_fusion.place_ref, s32[1,512]{1,0:T(1,128)S(1)} %bitcast.7, bf16[2,512,256]{2,1,0:T(8,128)(2,1)S(1)} %copy-done), custom_call_target="tpu_custom_call" | custom-call | tf_op jit(solution)/shard_map/front/pallas_call | solution.py:68
  2.6 2.1 %collective-permute-start = (bf16[2,256,256]{2,1,0:T(8,128)(2,1)S(1)}, bf16[2,256,256]{2,1,0:T(8,128)(2,1)S(1)}, u32[]{:S(2)}, u32[]{:S(2)}) collective-permute-start(bf16[2,256,256]{2,1,0:T(8,128)(2,1)S(1)} %get-tuple-element.10.refs_0_), channel_id=1, source_target_pairs={{0,1},{1,0},{2,3},{3,2},{4,5},{5,4},{6,7},{7,6},{8,9},{9,8},{10,11... | collective-permute-start | bytes 786440 | tf_op jit(solution)/shard_map/ppermute | solution.py:26
  4.7 3.3 %collective-permute-start.1 = (bf16[512,256]{1,0:T(8,128)(2,1)S(1)}, bf16[512,256]{1,0:T(8,128)(2,1)S(1)}, u32[]{:S(2)}, u32[]{:S(2)}) collective-permute-start(bf16[512,256]{1,0:T(8,128)(2,1)S(1)} %get-tuple-element.13), channel_id=1, source_target_pairs={{0,24},{1,25},{2,26},{3,27},{4,28},{5,29},{6,30},{7,31},{8,16},{9,... | collective-permute-start | bytes 786440 | tf_op jit(solution)/shard_map/ppermute | solution.py:26
  8.1 0.0 collective-permute-start.2
  8.1 0.1 pad_add_fusion.1
  8.1 0.1 dynamic_slice.3
  8.2 0.1 broadcast_subtract_fusion.rows_ref
  8.3 2.5 %collective-permute-done.refs_1_ = bf16[2,256,256]{2,1,0:T(8,128)(2,1)S(1)} collective-permute-done((bf16[2,256,256]{2,1,0:T(8,128)(2,1)S(1)}, bf16[2,256,256]{2,1,0:T(8,128)(2,1)S(1)}, u32[]{:S(2)}, u32[]{:S(2)}) %collective-permute-start) | collective-permute-done | bytes 262176 | tf_op jit(solution)/shard_map/ppermute | solution.py:26
  10.8 0.0 copy-done.1
  10.8 1.5 %near.1 = bf16[8,2,2,32,512]{4,3,2,1,0:T(8,128)(2,1)} custom-call(bf16[2,512,256]{2,1,0:T(8,128)(2,1)S(1)} %copy-done.1, bf16[2,256,256]{2,1,0:T(8,128)(2,1)S(1)} %get-tuple-element.10.refs_0_, bf16[2,256,256]{2,1,0:T(8,128)(2,1)S(1)} %collective-permute-done.refs_1_), custom_call_target="tpu_custom_call" | custom-call | flops 1000000000 | bytes 3000000 | tf_op jit(solution)/shard_map/near/pallas_call | solution.py:94
  12.3 5.2 %all-to-all-start = ((bf16[16,2,32,512]{3,2,1,0:T(8,128)(2,1)}), bf16[16,2,32,512]{3,2,1,0:T(8,128)(2,1)S(1)}, u32[]{:S(2)}, u32[]{:S(2)}) async-start(bf16[16,2,32,512]{3,2,1,0:T(8,128)(2,1)} %bitcast.5), calls=%async_computation | async-start | bytes 2097152 | tf_op jit(solution)/shard_map/all_to_all | solution.py:271
  17.5 0.0 collective-permute-done.1.refs_0_
  17.5 1.9 %collective-permute-done.2.refs_1_ = bf16[512,256]{1,0:T(8,128)(2,1)S(1)} collective-permute-done((bf16[512,256]{1,0:T(8,128)(2,1)S(1)}, bf16[512,256]{1,0:T(8,128)(2,1)S(1)}, u32[]{:S(2)}, u32[]{:S(2)}) %collective-permute-start.2) | collective-permute-done | bytes 262176 | tf_op jit(solution)/shard_map/ppermute | solution.py:26
  19.4 2.3 %far.1 = bf16[8,2,2,32,512]{4,3,2,1,0:T(8,128)(2,1)} custom-call(s32[2]{0:T(128)S(1)} %pad_add_fusion.place_ref, s32[256,2]{1,0:T(8,128)S(1)} %broadcast_subtract_fusion.rows_ref, bf16[512,256]{1,0:T(8,128)(2,1)S(1)} %collective-permute-done.1.refs_0_, bf16[512,256]{1,0:T(8,128)(2,1)S(1)} %collective-permute-done.2.refs_1_), custom_call_target="tpu_custom_call" | custom-call | flops 60000002048 | bytes 180000000 | tf_op jit(solution)/shard_map/far/pallas_call | solution.py:142
  21.7 10.0 %all-to-all-done.near_ref = bf16[16,2,32,512]{3,2,1,0:T(8,128)(2,1)S(1)} async-done(((bf16[16,2,32,512]{3,2,1,0:T(8,128)(2,1)}), bf16[16,2,32,512]{3,2,1,0:T(8,128)(2,1)S(1)}, u32[]{:S(2)}, u32[]{:S(2)}) %all-to-all-start) | async-done | bytes 1048608 | tf_op jit(solution)/shard_map/all_to_all | solution.py:271
  31.7 0.0 copy-start.3
  31.7 5.7 %all-to-all-start.1 = ((bf16[16,2,32,512]{3,2,1,0:T(8,128)(2,1)}), bf16[16,2,32,512]{3,2,1,0:T(8,128)(2,1)S(1)}, u32[]{:S(2)}, u32[]{:S(2)}) async-start(bf16[16,2,32,512]{3,2,1,0:T(8,128)(2,1)} %bitcast.6), calls=%async_computation.1 | async-start | bytes 2097152 | tf_op jit(solution)/shard_map/all_to_all | solution.py:271
  37.4 0.0 copy-done.3
  37.4 1.4 %early.1.early_ref = f32[32,2,2,512]{3,2,1,0:T(2,128)S(1)} custom-call(s32[2,32]{1,0:T(2,128)S(1)} %copy-done.3, bf16[16,2,32,512]{3,2,1,0:T(8,128)(2,1)S(1)} %all-to-all-done.near_ref), custom_call_target="tpu_custom_call" | custom-call | flops 60000002048 | bytes 180000000 | tf_op jit(solution)/shard_map/early/pallas_call | solution.py:230
  38.8 15.2 %all-to-all-done.1.far_ref = bf16[16,2,32,512]{3,2,1,0:T(8,128)(2,1)S(1)} async-done(((bf16[16,2,32,512]{3,2,1,0:T(8,128)(2,1)}), bf16[16,2,32,512]{3,2,1,0:T(8,128)(2,1)S(1)}, u32[]{:S(2)}, u32[]{:S(2)}) %all-to-all-start.1) | async-done | bytes 1048608 | tf_op jit(solution)/shard_map/all_to_all | solution.py:271
  53.9 2.9 %pairs.1 = f32[32,2,2,512]{3,2,1,0:T(2,128)} custom-call(s32[2,32]{1,0:T(2,128)S(1)} %copy-done.3, bf16[16,2,32,512]{3,2,1,0:T(8,128)(2,1)S(1)} %all-to-all-done.near_ref, bf16[16,2,32,512]{3,2,1,0:T(8,128)(2,1)S(1)} %all-to-all-done.1.far_ref, f32[32,2,2,512]{3,2,1,0:T(2,128)S(1)} %early.1.early_ref), custom_call_target="tpu_custom_call" | custom-call | tf_op jit(solution)/shard_map/pairs/pallas_call | solution.py:242
Async XLA Ops:
  0.0 0.7 %copy-start.2 = (s32[512]{0:T(512)S(1)}, s32[512]{0:T(512)}, u32[]{:S(2)}) copy-start(s32[512]{0:T(512)} %param.5) | copy-start | bytes 6148
  0.7 1.0 %copy-start = (bf16[2,512,256]{2,1,0:T(8,128)(2,1)S(1)}, bf16[2,512,256]{2,1,0:T(8,128)(2,1)}, u32[]{:S(2)}) copy-start(bf16[2,512,256]{2,1,0:T(8,128)(2,1)} %orbitals_ref.3) | copy-start | bytes 1572868
  1.7 9.1 %copy-start.1 = (bf16[2,512,256]{2,1,0:T(8,128)(2,1)S(1)}, bf16[2,512,256]{2,1,0:T(8,128)(2,1)}, u32[]{:S(2)}) copy-start(bf16[2,512,256]{2,1,0:T(8,128)(2,1)} %orbitals_ref.3) | copy-start | bytes 1572868
  2.6 8.2 %collective-permute-start = (bf16[2,256,256]{2,1,0:T(8,128)(2,1)S(1)}, bf16[2,256,256]{2,1,0:T(8,128)(2,1)S(1)}, u32[]{:S(2)}, u32[]{:S(2)}) collective-permute-start(bf16[2,256,256]{2,1,0:T(8,128)(2,1)S(1)} %get-tuple-element.10.refs_0_), channel_id=1, source_target_pairs={{0,1},{1,0},{2,3},{3,2},{4,5},{5,4},{6,7},{7,6},{8,9},{9,8},{10,11... | collective-permute-start | bytes 786440 | tf_op jit(solution)/shard_map/ppermute | solution.py:26
  4.7 12.8 %collective-permute-start.1 = (bf16[512,256]{1,0:T(8,128)(2,1)S(1)}, bf16[512,256]{1,0:T(8,128)(2,1)S(1)}, u32[]{:S(2)}, u32[]{:S(2)}) collective-permute-start(bf16[512,256]{1,0:T(8,128)(2,1)S(1)} %get-tuple-element.13), channel_id=1, source_target_pairs={{0,24},{1,25},{2,26},{3,27},{4,28},{5,29},{6,30},{7,31},{8,16},{9,... | collective-permute-start | bytes 786440 | tf_op jit(solution)/shard_map/ppermute | solution.py:26
  8.1 11.4 %collective-permute-start.2 = (bf16[512,256]{1,0:T(8,128)(2,1)S(1)}, bf16[512,256]{1,0:T(8,128)(2,1)S(1)}, u32[]{:S(2)}, u32[]{:S(2)}) collective-permute-start(bf16[512,256]{1,0:T(8,128)(2,1)S(1)} %get-tuple-element.14), channel_id=1, source_target_pairs={{0,25},{1,24},{2,27},{3,26},{4,29},{5,28},{6,31},{7,30},{8,17},{9,... | collective-permute-start | bytes 786440 | tf_op jit(solution)/shard_map/ppermute | solution.py:26
  12.3 19.4 %all-to-all-start = ((bf16[16,2,32,512]{3,2,1,0:T(8,128)(2,1)}), bf16[16,2,32,512]{3,2,1,0:T(8,128)(2,1)S(1)}, u32[]{:S(2)}, u32[]{:S(2)}) async-start(bf16[16,2,32,512]{3,2,1,0:T(8,128)(2,1)} %bitcast.5), calls=%async_computation | async-start | bytes 2097152 | tf_op jit(solution)/shard_map/all_to_all | solution.py:271
  31.7 5.7 %copy-start.3 = (s32[2,32]{1,0:T(2,128)S(1)}, s32[2,32]{1,0:T(2,128)}, u32[]{:S(2)}) copy-start(s32[2,32]{1,0:T(2,128)} %table_ref.3) | copy-start | bytes 772
  31.7 22.2 %all-to-all-start.1 = ((bf16[16,2,32,512]{3,2,1,0:T(8,128)(2,1)}), bf16[16,2,32,512]{3,2,1,0:T(8,128)(2,1)S(1)}, u32[]{:S(2)}, u32[]{:S(2)}) async-start(bf16[16,2,32,512]{3,2,1,0:T(8,128)(2,1)} %bitcast.6), calls=%async_computation.1 | async-start | bytes 2097152 | tf_op jit(solution)/shard_map/all_to_all | solution.py:271

commit v23 on v20

--- a/solution.py
+++ b/solution.py
@@ -10,7 +10,6 @@
 from jax.sharding import PartitionSpec as P
 
 VMEM_LIMIT = 40 * 1024 * 1024
-FRONT_LIMIT = 60 * 1024 * 1024
 SPLIT = 2
 KA, GA = ("half", "quarter", "inner"), ("hi", "lo")
 
@@ -27,78 +26,60 @@
     return lax.ppermute(block, KA + GA, route)
 
 
+def one_hot(points_ref, half, slab, slab_size, npoints):
+    first = pl.multiple_of(half * npoints, npoints)
+    wanted = points_ref[:, pl.ds(first, npoints)] - slab * slab_size
+    spot = lax.broadcasted_iota(jnp.int32, (slab_size, npoints), 0)
+    return (spot == wanted).astype(jnp.float32).astype(jnp.bfloat16)
+
+
+def pick(chosen, slab):
+    return lax.dot_general(
+        chosen, slab, (((0,), (0,)), ((), ())), preferred_element_type=jnp.float32
+    )
+
+
 def rotate(picked):
     middle = picked.shape[1] // 2
     return jnp.concatenate([-picked[:, middle:], picked[:, :middle]], axis=1)
 
 
-def front_kernel(
-    place_ref, points_ref, orbitals_ref, mine_ref, other_ref, picked_ref, *scratch
-):
-    wanted_ref, slab_ref, rows_ref, sems = scratch
-    kdevice, slab_size, _ = orbitals_ref.shape
-    npoints = wanted_ref.shape[1]
-    first = pl.multiple_of(place_ref[0] * npoints, npoints)
+def product(rows, slab, groups):
+    out = lax.dot_general(
+        rows, slab, (((1,), (1,)), ((), ())), preferred_element_type=jnp.float32
+    )
+    return out.reshape(groups, -1, out.shape[1]).astype(jnp.bfloat16)
+
+
+def front_kernel(place_ref, points_ref, mine_ref, other_ref, picked_ref):
+    slab_size, _ = mine_ref.shape
+    _, npoints, _ = picked_ref.shape
     mine = place_ref[1] % SPLIT
-    pairs = [(points_ref.at[:, pl.ds(first, npoints)], wanted_ref)]
-    pairs += [(orbitals_ref.at[k], slab_ref.at[k]) for k in range(kdevice)]
-    pairs += [(orbitals_ref.at[mine], mine_ref), (orbitals_ref.at[1 - mine], other_ref)]
-    pairs += [(rows_ref.at[k], picked_ref.at[k]) for k in range(kdevice)]
-    copies = [
-        pltpu.make_async_copy(source, target, sems.at[number])
-        for number, (source, target) in enumerate(pairs)
-    ]
-    for copy in copies[:-kdevice]:
-        copy.start()
-    copies[0].wait()
-    wanted = wanted_ref[...] - place_ref[1] * slab_size
-    spot = lax.broadcasted_iota(jnp.int32, (slab_size, npoints), 0)
-    chosen = (spot == wanted).astype(jnp.float32).astype(jnp.bfloat16)
-    for k in range(kdevice):
-        copies[1 + k].wait()
-        picked = lax.dot_general(
-            chosen, slab_ref[k], (((0,), (0,)), ((), ())), preferred_element_type=jnp.float32
-        )
-        rows_ref[k] = picked.astype(jnp.bfloat16)
-        copies[k - kdevice].start()
-    for copy in copies[1 + kdevice :]:
-        copy.wait()
-
-
-def make_front(orbitals, points, place):
-    kdevice, slab_size, channels = orbitals.shape
-    npoints = points.shape[1] // 2
-    hbm = pl.BlockSpec(memory_space=pl.ANY)
-    slab = jax.ShapeDtypeStruct((slab_size, channels), jnp.bfloat16)
-    picked = jax.ShapeDtypeStruct((kdevice, npoints, channels), jnp.bfloat16)
+    chosen = one_hot(points_ref, place_ref[0], place_ref[1], slab_size, npoints)
+    for k, slab_ref in ((mine, mine_ref), (1 - mine, other_ref)):
+        picked_ref[k] = pick(chosen, slab_ref[...]).astype(jnp.bfloat16)
+
+
+def make_front(mine, other, points, place):
+    vmem = pl.BlockSpec(memory_space=pltpu.VMEM)
     return pl.pallas_call(
         front_kernel,
-        in_specs=[pl.BlockSpec(memory_space=pltpu.SMEM), hbm, hbm],
-        out_specs=[hbm] * 3,
-        out_shape=[slab, slab, picked],
-        scratch_shapes=[
-            pltpu.VMEM((1, npoints), jnp.int32),
-            pltpu.VMEM(orbitals.shape, jnp.bfloat16),
-            pltpu.VMEM(picked.shape, jnp.bfloat16),
-            pltpu.SemaphoreType.DMA((3 + 2 * kdevice,)),
-        ],
-        compiler_params=pltpu.CompilerParams(vmem_limit_bytes=FRONT_LIMIT),
+        in_specs=[pl.BlockSpec(memory_space=pltpu.SMEM)] + [vmem] * 3,
+        out_specs=vmem,
+        out_shape=jax.ShapeDtypeStruct(
+            (SPLIT, points.shape[1] // 2, mine.shape[1]), jnp.bfloat16
+        ),
+        compiler_params=pltpu.CompilerParams(vmem_limit_bytes=VMEM_LIMIT),
         name="front",
-    )(place, points, orbitals)
+    )(place, points, mine, other)
 
 
 def near_kernel(orbitals_ref, *refs):
     *picked_refs, out_ref = refs
-    groups, _, _, length, slab_size = out_ref.shape
+    groups = out_ref.shape[0]
     rows = sum(picked_ref[0].astype(jnp.float32) for picked_ref in picked_refs)
     for part, turned in enumerate((rows, rotate(rows))):
-        product = lax.dot_general(
-            turned.astype(jnp.bfloat16),
-            orbitals_ref[0],
-            (((1,), (1,)), ((), ())),
-            preferred_element_type=jnp.float32,
-        )
-        out_ref[:, 0, part] = product.reshape(groups, length, slab_size).astype(jnp.bfloat16)
+        out_ref[:, 0, part] = product(turned.astype(jnp.bfloat16), orbitals_ref[0], groups)
 
 
 def make_near(orbitals, shares, groups):
@@ -232,11 +213,13 @@
     groups = lax.axis_size("quarter") * lax.axis_size("inner")
     slabs = lax.axis_size("hi") * lax.axis_size("lo")
     total_k = 2 * groups * kdevice
-    npoints = points.shape[0] // 2
-    here = lax.axis_index("hi") * SPLIT + lax.axis_index("lo")
-    place = jnp.stack([half, here])
-
-    mine, other, share = make_front(orbitals, points.reshape(1, -1), place)
+    points = points.reshape(1, -1)
+    place = jnp.stack([half, lax.axis_index("hi") * SPLIT + lax.axis_index("lo")])
+
+    lo = lax.axis_index("lo")
+    mine = lax.dynamic_index_in_dim(orbitals, lo, 0, keepdims=False)
+    other = lax.dynamic_index_in_dim(orbitals, 1 - lo, 0, keepdims=False)
+    share = make_front(mine, other, points, place)
     shares = [share] + [swap(share, False, x) for x in range(1, slabs)]
     far = [swap(other if x & 1 else mine, True, x) for x in range(slabs)]
 
@@ -245,8 +228,9 @@
         return lax.all_to_all(fields, around, split_axis=0, concat_axis=0, tiled=True)
 
     near_fields = make_near(orbitals, shares, groups)
-    wanted = lax.dynamic_slice_in_dim(points, half * npoints, npoints)
-    starts = jnp.stack([(here ^ x) * slab_size for x in range(slabs)])
+    npoints = points.shape[1] // 2
+    wanted = lax.dynamic_slice_in_dim(points[0], half * npoints, npoints)
+    starts = jnp.stack([(place[1] ^ x) * slab_size for x in range(slabs)])
     rows = wanted[:, None] - starts[None, :]
     near_fields, rows = lax.optimization_barrier((near_fields, rows))
     far_fields = make_far(rows, far, place, groups)

time: 73.1 us -> 64.4 us (0.88)
  Pallas kernels: 24.5 us -> 7.6 us
  waiting for transfers between devices: 28.8 us -> 38.7 us
    pallas_call x1, Pallas kernels: 17.7 us -> 0.87 us  [make_front(): pl.pallas_call(front_kernel, in_specs=[pl.BlockSpec(memory_space=pltpu.SM...]
    ppermute x3, waiting for transfers between devices: 2.8 us -> 11.8 us  [swap(): return lax.ppermute(block, KA + GA, route)]
    unnamed x10 -> x6, local copies, waits for them, and re-layouts: 2.31 us -> 0.68 us
    squeeze x0 -> x1, local copies, waits for them, and re-layouts: none -> 1.08 us  [on_device(): other = lax.dynamic_index_in_dim(orbitals, 1 - lo, 0, keepdims=False)]
    all_to_all x2, waiting for transfers between devices: 26 us -> 26.9 us  [send(): lax.all_to_all(fields, around, split_axis=0, concat_axis=0, tiled=True)]
  transfers between devices with their start and end apart: 5 -> 5, of which waited for: 4 -> 3; matrix products, arithmetic and copies ran while one was open for 1% -> 1% of each run, Pallas kernels for 5% -> 7%
where the time goes in v23:
time: 64.4 us; the launch traced here: 64.1 us
  waiting for transfers between devices  38.7 us (60%)
  starting transfers between devices  15.3 us (24%)
  Pallas kernels  7.6 us (12%)
  local copies, waits for them, and re-layouts  1.91 us (3%)
    all_to_all x2, waiting for transfers between devices, send(): lax.all_to_all(fields, around, split_axis=0, concat_axis=0, tiled=True)  26.9 us
    ppermute x3, waiting for transfers between devices, swap(): return lax.ppermute(block, KA + GA, route)  11.8 us
    all_to_all x2, starting transfers between devices, send(): lax.all_to_all(fields, around, split_axis=0, concat_axis=0, tiled=True)  9.8 us
    ppermute x3, starting transfers between devices, swap(): return lax.ppermute(block, KA + GA, route)  5.54 us
    pallas_call x1, Pallas kernels, make_pairs(): pl.pallas_call(functools.partial(pair_kernel, 1.0 / math.sqrt(2 * half_k)...  2.96 us
    pallas_call x1, Pallas kernels, make_far(): pl.pallas_call(far_kernel, in_specs=[pl.BlockSpec(memory_space=pltpu.SMEM...  2.27 us
    pallas_call x1, Pallas kernels, make_near(): pl.pallas_call(near_kernel, grid=(kdevice,), in_specs=[pl.BlockSpec((1, s...  1.5 us
  transfers between devices with their start and end apart: 5, of which 3 were waited for; matrix products, arithmetic and copies ran while one was open for 1% of the time, Pallas kernels for 7%

profile of v23, /device:TPU:1, one launch (start us, length us, event | category | flops | bytes accessed | tf_op | source)
XLA Modules:
  0.0 64.1 jit_solution(5768748983522080269)
XLA Ops:
  0.0 0.0 copy-start.1
  0.0 1.1 %dynamic-slice_bitcast_fusion = (bf16[512,256]{1,0:T(8,128)(2,1)S(1)}, bf16[512,256]{1,0:T(8,128)(2,1)S(1)}) fusion(bf16[2,512,256]{2,1,0:T(8,128)(2,1)} %orbitals_ref.1, s32[]{:T(128)S(6)} %select_n.43, s32[]{:T(128)S(6)} %select_n.42), kind=kLoop, calls=%fused_computation | loop fusion | bytes 1048584 | tf_op jit(solution)/shard_map/jit(dynamic_index_in_dim)/squeeze | solution.py:221
  1.1 0.0 copy-start
  1.1 4.2 %collective-permute-start.1 = (bf16[512,256]{1,0:T(8,128)(2,1)S(1)}, bf16[512,256]{1,0:T(8,128)(2,1)S(1)}, u32[]{:S(2)}, u32[]{:S(2)}) collective-permute-start(bf16[512,256]{1,0:T(8,128)(2,1)S(1)} %get-tuple-element.14.mine_ref), channel_id=1, source_target_pairs={{0,24},{1,25},{2,26},{3,27},{4,28},{5,29},{6,30},{7,31},{8,16},{9,... | collective-permute-start | bytes 786440 | tf_op jit(solution)/shard_map/ppermute | solution.py:26
  5.3 1.0 %collective-permute-start.2 = (bf16[512,256]{1,0:T(8,128)(2,1)S(1)}, bf16[512,256]{1,0:T(8,128)(2,1)S(1)}, u32[]{:S(2)}, u32[]{:S(2)}) collective-permute-start(bf16[512,256]{1,0:T(8,128)(2,1)S(1)} %get-tuple-element.13.other_ref), channel_id=1, source_target_pairs={{0,25},{1,24},{2,27},{3,26},{4,29},{5,28},{6,31},{7,30},{8,17},{9,... | collective-permute-start | bytes 786440 | tf_op jit(solution)/shard_map/ppermute | solution.py:26
  6.3 0.1 pad_add_fusion.2.place_ref
  6.4 0.0 copy-done.1
  6.4 0.9 %front.1.refs_0_ = bf16[2,256,256]{2,1,0:T(8,128)(2,1)S(1)} custom-call(s32[2]{0:T(128)S(1)} %pad_add_fusion.2.place_ref, s32[1,512]{1,0:T(1,128)S(1)} %bitcast.12, bf16[512,256]{1,0:T(8,128)(2,1)S(1)} %get-tuple-element.14.mine_ref, bf16[512,256]{1,0:T(8,128)(2,1)S(1)} %get-tuple-element.13.other_ref), custom_call_target="tpu_custom_call" | custom-call | tf_op jit(solution)/shard_map/front/pallas_call | solution.py:65
  7.3 0.3 collective-permute-start
  7.6 0.1 pad_add_fusion.3
  7.7 0.1 dynamic_slice.17
  7.7 0.1 broadcast_subtract_fusion.rows_ref
  7.8 11.8 %collective-permute-done.refs_1_ = bf16[2,256,256]{2,1,0:T(8,128)(2,1)S(1)} collective-permute-done((bf16[2,256,256]{2,1,0:T(8,128)(2,1)S(1)}, bf16[2,256,256]{2,1,0:T(8,128)(2,1)S(1)}, u32[]{:S(2)}, u32[]{:S(2)}) %collective-permute-start) | collective-permute-done | bytes 262176 | tf_op jit(solution)/shard_map/ppermute | solution.py:26
  19.7 0.0 copy-done
  19.7 1.5 %near.1 = bf16[8,2,2,32,512]{4,3,2,1,0:T(8,128)(2,1)} custom-call(bf16[2,512,256]{2,1,0:T(8,128)(2,1)S(1)} %copy-done, bf16[2,256,256]{2,1,0:T(8,128)(2,1)S(1)} %front.1.refs_0_, bf16[2,256,256]{2,1,0:T(8,128)(2,1)S(1)} %collective-permute-done.refs_1_), custom_call_target="tpu_custom_call" | custom-call | flops 1000000000 | bytes 3000000 | tf_op jit(solution)/shard_map/near/pallas_call | solution.py:89
  21.2 5.5 %all-to-all-start = ((bf16[16,2,32,512]{3,2,1,0:T(8,128)(2,1)}), bf16[16,2,32,512]{3,2,1,0:T(8,128)(2,1)S(1)}, u32[]{:S(2)}, u32[]{:S(2)}) async-start(bf16[16,2,32,512]{3,2,1,0:T(8,128)(2,1)} %bitcast.7), calls=%async_computation | async-start | bytes 2097152 | tf_op jit(solution)/shard_map/all_to_all | solution.py:228
  26.7 0.0 collective-permute-done.1.refs_0_
  26.7 0.0 collective-permute-done.2.refs_1_
  26.7 2.3 %far.1 = bf16[8,2,2,32,512]{4,3,2,1,0:T(8,128)(2,1)} custom-call(s32[2]{0:T(128)S(1)} %pad_add_fusion.2.place_ref, s32[256,2]{1,0:T(8,128)S(1)} %broadcast_subtract_fusion.rows_ref, bf16[512,256]{1,0:T(8,128)(2,1)S(1)} %collective-permute-done.1.refs_0_, bf16[512,256]{1,0:T(8,128)(2,1)S(1)} %collective-permute-done.2.refs_1_), custom_call_target="tpu_custom_call" | custom-call | flops 60000002048 | bytes 180000000 | tf_op jit(solution)/shard_map/far/pallas_call | solution.py:137
  28.9 11.3 %all-to-all-done.near_ref = bf16[16,2,32,512]{3,2,1,0:T(8,128)(2,1)S(1)} async-done(((bf16[16,2,32,512]{3,2,1,0:T(8,128)(2,1)}), bf16[16,2,32,512]{3,2,1,0:T(8,128)(2,1)S(1)}, u32[]{:S(2)}, u32[]{:S(2)}) %all-to-all-start) | async-done | bytes 1048608 | tf_op jit(solution)/shard_map/all_to_all | solution.py:228
  40.3 4.3 %all-to-all-start.1 = ((bf16[16,2,32,512]{3,2,1,0:T(8,128)(2,1)}), bf16[16,2,32,512]{3,2,1,0:T(8,128)(2,1)S(1)}, u32[]{:S(2)}, u32[]{:S(2)}) async-start(bf16[16,2,32,512]{3,2,1,0:T(8,128)(2,1)} %bitcast.8), calls=%async_computation.1 | async-start | bytes 2097152 | tf_op jit(solution)/shard_map/all_to_all | solution.py:228
  44.6 0.0 copy-start.2
  44.6 0.7 %copy-done.2 = s32[2,32]{1,0:T(2,128)S(1)} copy-done((s32[2,32]{1,0:T(2,128)S(1)}, s32[2,32]{1,0:T(2,128)}, u32[]{:S(2)}) %copy-start.2) | copy-done | bytes 280
  45.3 0.1 pad_add_fusion
  45.4 0.1 compare_select_fusion
  45.4 0.1 fusion.3
  45.5 0.1 pad_add_fusion.1.table_ref
  45.6 15.6 %all-to-all-done.1.far_ref = bf16[16,2,32,512]{3,2,1,0:T(8,128)(2,1)S(1)} async-done(((bf16[16,2,32,512]{3,2,1,0:T(8,128)(2,1)}), bf16[16,2,32,512]{3,2,1,0:T(8,128)(2,1)S(1)}, u32[]{:S(2)}, u32[]{:S(2)}) %all-to-all-start.1) | async-done | bytes 1048608 | tf_op jit(solution)/shard_map/all_to_all | solution.py:228
  61.2 3.0 %pairs.1 = f32[32,2,2,512]{3,2,1,0:T(2,128)} custom-call(s32[2,32]{1,0:T(2,128)S(1)} %pad_add_fusion.1.table_ref, bf16[16,2,32,512]{3,2,1,0:T(8,128)(2,1)S(1)} %all-to-all-done.near_ref, bf16[16,2,32,512]{3,2,1,0:T(8,128)(2,1)S(1)} %all-to-all-done.1.far_ref), custom_call_target="tpu_custom_call" | custom-call | tf_op jit(solution)/shard_map/pairs/pallas_call | solution.py:195
Async XLA Ops:
  0.0 6.4 %copy-start.1 = (s32[512]{0:T(512)S(1)}, s32[512]{0:T(512)}, u32[]{:S(2)}) copy-start(s32[512]{0:T(512)} %param.5) | copy-start | bytes 6148
  1.1 18.6 %copy-start = (bf16[2,512,256]{2,1,0:T(8,128)(2,1)S(1)}, bf16[2,512,256]{2,1,0:T(8,128)(2,1)}, u32[]{:S(2)}) copy-start(bf16[2,512,256]{2,1,0:T(8,128)(2,1)} %orbitals_ref.1) | copy-start | bytes 1572868
  1.1 25.6 %collective-permute-start.1 = (bf16[512,256]{1,0:T(8,128)(2,1)S(1)}, bf16[512,256]{1,0:T(8,128)(2,1)S(1)}, u32[]{:S(2)}, u32[]{:S(2)}) collective-permute-start(bf16[512,256]{1,0:T(8,128)(2,1)S(1)} %get-tuple-element.14.mine_ref), channel_id=1, source_target_pairs={{0,24},{1,25},{2,26},{3,27},{4,28},{5,29},{6,30},{7,31},{8,16},{9,... | collective-permute-start | bytes 786440 | tf_op jit(solution)/shard_map/ppermute | solution.py:26
  5.3 21.4 %collective-permute-start.2 = (bf16[512,256]{1,0:T(8,128)(2,1)S(1)}, bf16[512,256]{1,0:T(8,128)(2,1)S(1)}, u32[]{:S(2)}, u32[]{:S(2)}) collective-permute-start(bf16[512,256]{1,0:T(8,128)(2,1)S(1)} %get-tuple-element.13.other_ref), channel_id=1, source_target_pairs={{0,25},{1,24},{2,27},{3,26},{4,29},{5,28},{6,31},{7,30},{8,17},{9,... | collective-permute-start | bytes 786440 | tf_op jit(solution)/shard_map/ppermute | solution.py:26
  7.3 12.4 %collective-permute-start = (bf16[2,256,256]{2,1,0:T(8,128)(2,1)S(1)}, bf16[2,256,256]{2,1,0:T(8,128)(2,1)S(1)}, u32[]{:S(2)}, u32[]{:S(2)}) collective-permute-start(bf16[2,256,256]{2,1,0:T(8,128)(2,1)S(1)} %front.1.refs_0_), channel_id=1, source_target_pairs={{0,1},{1,0},{2,3},{3,2},{4,5},{5,4},{6,7},{7,6},{8,9},{9,8},{10,11... | collective-permute-start | bytes 786440 | tf_op jit(solution)/shard_map/ppermute | solution.py:26
  21.2 19.1 %all-to-all-start = ((bf16[16,2,32,512]{3,2,1,0:T(8,128)(2,1)}), bf16[16,2,32,512]{3,2,1,0:T(8,128)(2,1)S(1)}, u32[]{:S(2)}, u32[]{:S(2)}) async-start(bf16[16,2,32,512]{3,2,1,0:T(8,128)(2,1)} %bitcast.7), calls=%async_computation | async-start | bytes 2097152 | tf_op jit(solution)/shard_map/all_to_all | solution.py:228
  40.3 20.9 %all-to-all-start.1 = ((bf16[16,2,32,512]{3,2,1,0:T(8,128)(2,1)}), bf16[16,2,32,512]{3,2,1,0:T(8,128)(2,1)S(1)}, u32[]{:S(2)}, u32[]{:S(2)}) async-start(bf16[16,2,32,512]{3,2,1,0:T(8,128)(2,1)} %bitcast.8), calls=%async_computation.1 | async-start | bytes 2097152 | tf_op jit(solution)/shard_map/all_to_all | solution.py:228
  44.6 0.7 %copy-start.2 = (s32[2,32]{1,0:T(2,128)S(1)}, s32[2,32]{1,0:T(2,128)}, u32[]{:S(2)}) copy-start(s32[2,32]{1,0:T(2,128)} %param.4) | copy-start | bytes 772

commit v24 on v23

--- a/solution.py
+++ b/solution.py
@@ -220,6 +220,7 @@
     mine = lax.dynamic_index_in_dim(orbitals, lo, 0, keepdims=False)
     other = lax.dynamic_index_in_dim(orbitals, 1 - lo, 0, keepdims=False)
     share = make_front(mine, other, points, place)
+    share, other = lax.optimization_barrier((share, other))
     shares = [share] + [swap(share, False, x) for x in range(1, slabs)]
     far = [swap(other if x & 1 else mine, True, x) for x in range(slabs)]
 

time: 64.4 us -> 63.6 us (0.988)
  waiting for transfers between devices: 38.7 us -> 36.9 us
  starting transfers between devices: 15.3 us -> 16.4 us
    ppermute x3, waiting for transfers between devices: 11.8 us -> 10 us  [swap(): return lax.ppermute(block, KA + GA, route)]
    all_to_all x2, starting transfers between devices: 9.8 us -> 10.9 us  [send(): lax.all_to_all(fields, around, split_axis=0, concat_axis=0, tiled=True)]
where the time goes in v24:
time: 63.6 us; the launch traced here: 63.3 us
  waiting for transfers between devices  36.9 us (58%)
  starting transfers between devices  16.4 us (26%)
  Pallas kernels  7.6 us (12%)
  local copies, waits for them, and re-layouts  1.91 us (3%)
    all_to_all x2, waiting for transfers between devices, send(): lax.all_to_all(fields, around, split_axis=0, concat_axis=0, tiled=True)  26.9 us
    all_to_all x2, starting transfers between devices, send(): lax.all_to_all(fields, around, split_axis=0, concat_axis=0, tiled=True)  10.9 us
    ppermute x3, waiting for transfers between devices, swap(): return lax.ppermute(block, KA + GA, route)  10 us
    ppermute x3, starting transfers between devices, swap(): return lax.ppermute(block, KA + GA, route)  5.52 us
    pallas_call x1, Pallas kernels, make_pairs(): pl.pallas_call(functools.partial(pair_kernel, 1.0 / math.sqrt(2 * half_k)...  2.96 us
    pallas_call x1, Pallas kernels, make_far(): pl.pallas_call(far_kernel, in_specs=[pl.BlockSpec(memory_space=pltpu.SMEM...  2.27 us
    pallas_call x1, Pallas kernels, make_near(): pl.pallas_call(near_kernel, grid=(kdevice,), in_specs=[pl.BlockSpec((1, s...  1.5 us
  transfers between devices with their start and end apart: 5, of which 3 were waited for; matrix products, arithmetic and copies ran while one was open for 1% of the time, Pallas kernels for 7%

profile of v24, /device:TPU:1, one launch (start us, length us, event | category | flops | bytes accessed | tf_op | source)
XLA Modules:
  0.0 63.3 jit_solution(9557890657911171472)
XLA Ops:
  0.0 0.0 copy-start.1
  0.0 1.1 %dynamic-slice_bitcast_fusion = (bf16[512,256]{1,0:T(8,128)(2,1)S(1)}, bf16[512,256]{1,0:T(8,128)(2,1)S(1)}) fusion(bf16[2,512,256]{2,1,0:T(8,128)(2,1)} %orbitals_ref.1, s32[]{:T(128)S(6)} %select_n.43, s32[]{:T(128)S(6)} %select_n.42), kind=kLoop, calls=%fused_computation | loop fusion | bytes 1048584 | tf_op jit(solution)/shard_map/jit(dynamic_index_in_dim)/squeeze | solution.py:221
  1.1 0.0 copy-start
  1.1 4.2 %collective-permute-start.1 = (bf16[512,256]{1,0:T(8,128)(2,1)S(1)}, bf16[512,256]{1,0:T(8,128)(2,1)S(1)}, u32[]{:S(2)}, u32[]{:S(2)}) collective-permute-start(bf16[512,256]{1,0:T(8,128)(2,1)S(1)} %get-tuple-element.18.mine_ref), channel_id=1, source_target_pairs={{0,24},{1,25},{2,26},{3,27},{4,28},{5,29},{6,30},{7,31},{8,16},{9,... | collective-permute-start | bytes 786440 | tf_op jit(solution)/shard_map/ppermute | solution.py:26
  5.3 0.1 pad_add_fusion.2.place_ref
  5.4 0.0 copy-done.1
  5.4 0.9 %front.1.refs_0_ = bf16[2,256,256]{2,1,0:T(8,128)(2,1)S(1)} custom-call(s32[2]{0:T(128)S(1)} %pad_add_fusion.2.place_ref, s32[1,512]{1,0:T(1,128)S(1)} %bitcast.12, bf16[512,256]{1,0:T(8,128)(2,1)S(1)} %get-tuple-element.18.mine_ref, bf16[512,256]{1,0:T(8,128)(2,1)S(1)} %get-tuple-element.14.other_ref), custom_call_target="tpu_custom_call" | custom-call | tf_op jit(solution)/shard_map/front/pallas_call | solution.py:65
  6.3 1.3 %collective-permute-start = (bf16[2,256,256]{2,1,0:T(8,128)(2,1)S(1)}, bf16[2,256,256]{2,1,0:T(8,128)(2,1)S(1)}, u32[]{:S(2)}, u32[]{:S(2)}) collective-permute-start(bf16[2,256,256]{2,1,0:T(8,128)(2,1)S(1)} %front.1.refs_0_), channel_id=1, source_target_pairs={{0,1},{1,0},{2,3},{3,2},{4,5},{5,4},{6,7},{7,6},{8,9},{9,8},{10,11... | collective-permute-start | bytes 786440 | tf_op jit(solution)/shard_map/ppermute | solution.py:26
  7.6 0.0 collective-permute-start.2
  7.6 0.1 pad_add_fusion.3
  7.6 0.1 dynamic_slice.17
  7.7 0.1 broadcast_subtract_fusion.rows_ref
  7.8 10.0 %collective-permute-done.refs_1_ = bf16[2,256,256]{2,1,0:T(8,128)(2,1)S(1)} collective-permute-done((bf16[2,256,256]{2,1,0:T(8,128)(2,1)S(1)}, bf16[2,256,256]{2,1,0:T(8,128)(2,1)S(1)}, u32[]{:S(2)}, u32[]{:S(2)}) %collective-permute-start) | collective-permute-done | bytes 262176 | tf_op jit(solution)/shard_map/ppermute | solution.py:26
  17.8 0.0 copy-done
  17.8 1.5 %near.1 = bf16[8,2,2,32,512]{4,3,2,1,0:T(8,128)(2,1)} custom-call(bf16[2,512,256]{2,1,0:T(8,128)(2,1)S(1)} %copy-done, bf16[2,256,256]{2,1,0:T(8,128)(2,1)S(1)} %front.1.refs_0_, bf16[2,256,256]{2,1,0:T(8,128)(2,1)S(1)} %collective-permute-done.refs_1_), custom_call_target="tpu_custom_call" | custom-call | flops 1000000000 | bytes 3000000 | tf_op jit(solution)/shard_map/near/pallas_call | solution.py:89
  19.3 6.3 %all-to-all-start = ((bf16[16,2,32,512]{3,2,1,0:T(8,128)(2,1)}), bf16[16,2,32,512]{3,2,1,0:T(8,128)(2,1)S(1)}, u32[]{:S(2)}, u32[]{:S(2)}) async-start(bf16[16,2,32,512]{3,2,1,0:T(8,128)(2,1)} %bitcast.7), calls=%async_computation | async-start | bytes 2097152 | tf_op jit(solution)/shard_map/all_to_all | solution.py:229
  25.6 0.0 collective-permute-done.2.refs_1_
  25.6 0.0 collective-permute-done.1.refs_0_
  25.6 2.3 %far.1 = bf16[8,2,2,32,512]{4,3,2,1,0:T(8,128)(2,1)} custom-call(s32[2]{0:T(128)S(1)} %pad_add_fusion.2.place_ref, s32[256,2]{1,0:T(8,128)S(1)} %broadcast_subtract_fusion.rows_ref, bf16[512,256]{1,0:T(8,128)(2,1)S(1)} %collective-permute-done.1.refs_0_, bf16[512,256]{1,0:T(8,128)(2,1)S(1)} %collective-permute-done.2.refs_1_), custom_call_target="tpu_custom_call" | custom-call | flops 60000002048 | bytes 180000000 | tf_op jit(solution)/shard_map/far/pallas_call | solution.py:137
  27.9 11.3 %all-to-all-done.near_ref = bf16[16,2,32,512]{3,2,1,0:T(8,128)(2,1)S(1)} async-done(((bf16[16,2,32,512]{3,2,1,0:T(8,128)(2,1)}), bf16[16,2,32,512]{3,2,1,0:T(8,128)(2,1)S(1)}, u32[]{:S(2)}, u32[]{:S(2)}) %all-to-all-start) | async-done | bytes 1048608 | tf_op jit(solution)/shard_map/all_to_all | solution.py:229
  39.2 4.6 %all-to-all-start.1 = ((bf16[16,2,32,512]{3,2,1,0:T(8,128)(2,1)}), bf16[16,2,32,512]{3,2,1,0:T(8,128)(2,1)S(1)}, u32[]{:S(2)}, u32[]{:S(2)}) async-start(bf16[16,2,32,512]{3,2,1,0:T(8,128)(2,1)} %bitcast.8), calls=%async_computation.1 | async-start | bytes 2097152 | tf_op jit(solution)/shard_map/all_to_all | solution.py:229
  43.8 0.0 copy-start.2
  43.9 0.7 %copy-done.2 = s32[2,32]{1,0:T(2,128)S(1)} copy-done((s32[2,32]{1,0:T(2,128)S(1)}, s32[2,32]{1,0:T(2,128)}, u32[]{:S(2)}) %copy-start.2) | copy-done | bytes 280
  44.5 0.1 pad_add_fusion
  44.6 0.1 compare_select_fusion
  44.7 0.1 fusion.3
  44.8 0.1 pad_add_fusion.1.table_ref
  44.8 15.5 %all-to-all-done.1.far_ref = bf16[16,2,32,512]{3,2,1,0:T(8,128)(2,1)S(1)} async-done(((bf16[16,2,32,512]{3,2,1,0:T(8,128)(2,1)}), bf16[16,2,32,512]{3,2,1,0:T(8,128)(2,1)S(1)}, u32[]{:S(2)}, u32[]{:S(2)}) %all-to-all-start.1) | async-done | bytes 1048608 | tf_op jit(solution)/shard_map/all_to_all | solution.py:229
  60.4 3.0 %pairs.1 = f32[32,2,2,512]{3,2,1,0:T(2,128)} custom-call(s32[2,32]{1,0:T(2,128)S(1)} %pad_add_fusion.1.table_ref, bf16[16,2,32,512]{3,2,1,0:T(8,128)(2,1)S(1)} %all-to-all-done.near_ref, bf16[16,2,32,512]{3,2,1,0:T(8,128)(2,1)S(1)} %all-to-all-done.1.far_ref), custom_call_target="tpu_custom_call" | custom-call | tf_op jit(solution)/shard_map/pairs/pallas_call | solution.py:195
Async XLA Ops:
  0.0 5.4 %copy-start.1 = (s32[512]{0:T(512)S(1)}, s32[512]{0:T(512)}, u32[]{:S(2)}) copy-start(s32[512]{0:T(512)} %param.5) | copy-start | bytes 6148
  1.1 16.8 %copy-start = (bf16[2,512,256]{2,1,0:T(8,128)(2,1)S(1)}, bf16[2,512,256]{2,1,0:T(8,128)(2,1)}, u32[]{:S(2)}) copy-start(bf16[2,512,256]{2,1,0:T(8,128)(2,1)} %orbitals_ref.1) | copy-start | bytes 1572868
  1.1 24.5 %collective-permute-start.1 = (bf16[512,256]{1,0:T(8,128)(2,1)S(1)}, bf16[512,256]{1,0:T(8,128)(2,1)S(1)}, u32[]{:S(2)}, u32[]{:S(2)}) collective-permute-start(bf16[512,256]{1,0:T(8,128)(2,1)S(1)} %get-tuple-element.18.mine_ref), channel_id=1, source_target_pairs={{0,24},{1,25},{2,26},{3,27},{4,28},{5,29},{6,30},{7,31},{8,16},{9,... | collective-permute-start | bytes 786440 | tf_op jit(solution)/shard_map/ppermute | solution.py:26
  6.3 11.6 %collective-permute-start = (bf16[2,256,256]{2,1,0:T(8,128)(2,1)S(1)}, bf16[2,256,256]{2,1,0:T(8,128)(2,1)S(1)}, u32[]{:S(2)}, u32[]{:S(2)}) collective-permute-start(bf16[2,256,256]{2,1,0:T(8,128)(2,1)S(1)} %front.1.refs_0_), channel_id=1, source_target_pairs={{0,1},{1,0},{2,3},{3,2},{4,5},{5,4},{6,7},{7,6},{8,9},{9,8},{10,11... | collective-permute-start | bytes 786440 | tf_op jit(solution)/shard_map/ppermute | solution.py:26
  7.6 18.1 %collective-permute-start.2 = (bf16[512,256]{1,0:T(8,128)(2,1)S(1)}, bf16[512,256]{1,0:T(8,128)(2,1)S(1)}, u32[]{:S(2)}, u32[]{:S(2)}) collective-permute-start(bf16[512,256]{1,0:T(8,128)(2,1)S(1)} %get-tuple-element.14.other_ref), channel_id=1, source_target_pairs={{0,25},{1,24},{2,27},{3,26},{4,29},{5,28},{6,31},{7,30},{8,17},{9,... | collective-permute-start | bytes 786440 | tf_op jit(solution)/shard_map/ppermute | solution.py:26
  19.3 19.9 %all-to-all-start = ((bf16[16,2,32,512]{3,2,1,0:T(8,128)(2,1)}), bf16[16,2,32,512]{3,2,1,0:T(8,128)(2,1)S(1)}, u32[]{:S(2)}, u32[]{:S(2)}) async-start(bf16[16,2,32,512]{3,2,1,0:T(8,128)(2,1)} %bitcast.7), calls=%async_computation | async-start | bytes 2097152 | tf_op jit(solution)/shard_map/all_to_all | solution.py:229
  39.2 21.1 %all-to-all-start.1 = ((bf16[16,2,32,512]{3,2,1,0:T(8,128)(2,1)}), bf16[16,2,32,512]{3,2,1,0:T(8,128)(2,1)S(1)}, u32[]{:S(2)}, u32[]{:S(2)}) async-start(bf16[16,2,32,512]{3,2,1,0:T(8,128)(2,1)} %bitcast.8), calls=%async_computation.1 | async-start | bytes 2097152 | tf_op jit(solution)/shard_map/all_to_all | solution.py:229
  43.8 0.7 %copy-start.2 = (s32[2,32]{1,0:T(2,128)S(1)}, s32[2,32]{1,0:T(2,128)}, u32[]{:S(2)}) copy-start(s32[2,32]{1,0:T(2,128)} %param.4) | copy-start | bytes 772

commit v25 on v23

--- a/solution.py
+++ b/solution.py
@@ -220,6 +220,7 @@
     mine = lax.dynamic_index_in_dim(orbitals, lo, 0, keepdims=False)
     other = lax.dynamic_index_in_dim(orbitals, 1 - lo, 0, keepdims=False)
     share = make_front(mine, other, points, place)
+    share, mine, other = lax.optimization_barrier((share, mine, other))
     shares = [share] + [swap(share, False, x) for x in range(1, slabs)]
     far = [swap(other if x & 1 else mine, True, x) for x in range(slabs)]
 

time: 64.4 us -> 56.6 us (0.88)
  waiting for transfers between devices: 38.7 us -> 29.9 us
  starting transfers between devices: 15.3 us -> 16.4 us
    ppermute x3, waiting for transfers between devices: 11.8 us -> 4.37 us  [swap(): return lax.ppermute(block, KA + GA, route)]
    all_to_all x2, waiting for transfers between devices: 26.9 us -> 25.5 us  [send(): lax.all_to_all(fields, around, split_axis=0, concat_axis=0, tiled=True)]
    all_to_all x2, starting transfers between devices: 9.8 us -> 10.9 us  [send(): lax.all_to_all(fields, around, split_axis=0, concat_axis=0, tiled=True)]
  transfers between devices with their start and end apart: 5 -> 5, of which waited for: 3 -> 4; matrix products, arithmetic and copies ran while one was open for 1% -> 1% of each run, Pallas kernels for 7% -> 7%
where the time goes in v25:
time: 56.6 us; the launch traced here: 56.3 us
  waiting for transfers between devices  29.9 us (53%)
  starting transfers between devices  16.4 us (29%)
  Pallas kernels  7.6 us (13%)
  local copies, waits for them, and re-layouts  1.91 us (3%)
    all_to_all x2, waiting for transfers between devices, send(): lax.all_to_all(fields, around, split_axis=0, concat_axis=0, tiled=True)  25.5 us
    all_to_all x2, starting transfers between devices, send(): lax.all_to_all(fields, around, split_axis=0, concat_axis=0, tiled=True)  10.9 us
    ppermute x3, starting transfers between devices, swap(): return lax.ppermute(block, KA + GA, route)  5.46 us
    ppermute x3, waiting for transfers between devices, swap(): return lax.ppermute(block, KA + GA, route)  4.37 us
    pallas_call x1, Pallas kernels, make_pairs(): pl.pallas_call(functools.partial(pair_kernel, 1.0 / math.sqrt(2 * half_k)...  2.96 us
    pallas_call x1, Pallas kernels, make_far(): pl.pallas_call(far_kernel, in_specs=[pl.BlockSpec(memory_space=pltpu.SMEM...  2.27 us
    pallas_call x1, Pallas kernels, make_near(): pl.pallas_call(near_kernel, grid=(kdevice,), in_specs=[pl.BlockSpec((1, s...  1.5 us
  transfers between devices with their start and end apart: 5, of which 4 were waited for; matrix products, arithmetic and copies ran while one was open for 1% of the time, Pallas kernels for 7%

profile of v25, /device:TPU:1, one launch (start us, length us, event | category | flops | bytes accessed | tf_op | source)
XLA Modules:
  0.0 56.3 jit_solution(11927521600169321029)
XLA Ops:
  0.0 0.1 pad_add_fusion.2.place_ref
  0.1 0.0 copy-start.1
  0.1 1.1 %dynamic-slice_bitcast_fusion = (bf16[512,256]{1,0:T(8,128)(2,1)S(1)}, bf16[512,256]{1,0:T(8,128)(2,1)S(1)}) fusion(bf16[2,512,256]{2,1,0:T(8,128)(2,1)} %orbitals_ref.1, s32[]{:T(128)S(6)} %select_n.43, s32[]{:T(128)S(6)} %select_n.42), kind=kLoop, calls=%fused_computation | loop fusion | bytes 1048584 | tf_op jit(solution)/shard_map/jit(dynamic_index_in_dim)/squeeze | solution.py:221
  1.2 0.0 copy-start
  1.2 0.0 copy-done.1
  1.2 0.9 %front.1.refs_0_ = bf16[2,256,256]{2,1,0:T(8,128)(2,1)S(1)} custom-call(s32[2]{0:T(128)S(1)} %pad_add_fusion.2.place_ref, s32[1,512]{1,0:T(1,128)S(1)} %bitcast.12, bf16[512,256]{1,0:T(8,128)(2,1)S(1)} %get-tuple-element.15.mine_ref, bf16[512,256]{1,0:T(8,128)(2,1)S(1)} %get-tuple-element.16.other_ref), custom_call_target="tpu_custom_call" | custom-call | tf_op jit(solution)/shard_map/front/pallas_call | solution.py:65
  2.1 2.1 %collective-permute-start = (bf16[2,256,256]{2,1,0:T(8,128)(2,1)S(1)}, bf16[2,256,256]{2,1,0:T(8,128)(2,1)S(1)}, u32[]{:S(2)}, u32[]{:S(2)}) collective-permute-start(bf16[2,256,256]{2,1,0:T(8,128)(2,1)S(1)} %front.1.refs_0_), channel_id=1, source_target_pairs={{0,1},{1,0},{2,3},{3,2},{4,5},{5,4},{6,7},{7,6},{8,9},{9,8},{10,11... | collective-permute-start | bytes 786440 | tf_op jit(solution)/shard_map/ppermute | solution.py:26
  4.2 3.3 %collective-permute-start.1 = (bf16[512,256]{1,0:T(8,128)(2,1)S(1)}, bf16[512,256]{1,0:T(8,128)(2,1)S(1)}, u32[]{:S(2)}, u32[]{:S(2)}) collective-permute-start(bf16[512,256]{1,0:T(8,128)(2,1)S(1)} %get-tuple-element.15.mine_ref), channel_id=1, source_target_pairs={{0,24},{1,25},{2,26},{3,27},{4,28},{5,29},{6,30},{7,31},{8,16},{9,... | collective-permute-start | bytes 786440 | tf_op jit(solution)/shard_map/ppermute | solution.py:26
  7.5 0.0 collective-permute-start.2
  7.5 0.1 pad_add_fusion.3
  7.6 0.1 dynamic_slice.17
  7.7 0.1 broadcast_subtract_fusion.rows_ref
  7.8 2.5 %collective-permute-done.refs_1_ = bf16[2,256,256]{2,1,0:T(8,128)(2,1)S(1)} collective-permute-done((bf16[2,256,256]{2,1,0:T(8,128)(2,1)S(1)}, bf16[2,256,256]{2,1,0:T(8,128)(2,1)S(1)}, u32[]{:S(2)}, u32[]{:S(2)}) %collective-permute-start) | collective-permute-done | bytes 262176 | tf_op jit(solution)/shard_map/ppermute | solution.py:26
  10.2 0.0 copy-done
  10.2 1.5 %near.1 = bf16[8,2,2,32,512]{4,3,2,1,0:T(8,128)(2,1)} custom-call(bf16[2,512,256]{2,1,0:T(8,128)(2,1)S(1)} %copy-done, bf16[2,256,256]{2,1,0:T(8,128)(2,1)S(1)} %front.1.refs_0_, bf16[2,256,256]{2,1,0:T(8,128)(2,1)S(1)} %collective-permute-done.refs_1_), custom_call_target="tpu_custom_call" | custom-call | flops 1000000000 | bytes 3000000 | tf_op jit(solution)/shard_map/near/pallas_call | solution.py:89
  11.7 5.2 %all-to-all-start = ((bf16[16,2,32,512]{3,2,1,0:T(8,128)(2,1)}), bf16[16,2,32,512]{3,2,1,0:T(8,128)(2,1)S(1)}, u32[]{:S(2)}, u32[]{:S(2)}) async-start(bf16[16,2,32,512]{3,2,1,0:T(8,128)(2,1)} %bitcast.7), calls=%async_computation | async-start | bytes 2097152 | tf_op jit(solution)/shard_map/all_to_all | solution.py:229
  17.0 0.0 collective-permute-done.1.refs_0_
  17.0 1.9 %collective-permute-done.2.refs_1_ = bf16[512,256]{1,0:T(8,128)(2,1)S(1)} collective-permute-done((bf16[512,256]{1,0:T(8,128)(2,1)S(1)}, bf16[512,256]{1,0:T(8,128)(2,1)S(1)}, u32[]{:S(2)}, u32[]{:S(2)}) %collective-permute-start.2) | collective-permute-done | bytes 262176 | tf_op jit(solution)/shard_map/ppermute | solution.py:26
  18.9 2.3 %far.1 = bf16[8,2,2,32,512]{4,3,2,1,0:T(8,128)(2,1)} custom-call(s32[2]{0:T(128)S(1)} %pad_add_fusion.2.place_ref, s32[256,2]{1,0:T(8,128)S(1)} %broadcast_subtract_fusion.rows_ref, bf16[512,256]{1,0:T(8,128)(2,1)S(1)} %collective-permute-done.1.refs_0_, bf16[512,256]{1,0:T(8,128)(2,1)S(1)} %collective-permute-done.2.refs_1_), custom_call_target="tpu_custom_call" | custom-call | flops 60000002048 | bytes 180000000 | tf_op jit(solution)/shard_map/far/pallas_call | solution.py:137
  21.2 10.0 %all-to-all-done.near_ref = bf16[16,2,32,512]{3,2,1,0:T(8,128)(2,1)S(1)} async-done(((bf16[16,2,32,512]{3,2,1,0:T(8,128)(2,1)}), bf16[16,2,32,512]{3,2,1,0:T(8,128)(2,1)S(1)}, u32[]{:S(2)}, u32[]{:S(2)}) %all-to-all-start) | async-done | bytes 1048608 | tf_op jit(solution)/shard_map/all_to_all | solution.py:229
  31.1 5.7 %all-to-all-start.1 = ((bf16[16,2,32,512]{3,2,1,0:T(8,128)(2,1)}), bf16[16,2,32,512]{3,2,1,0:T(8,128)(2,1)S(1)}, u32[]{:S(2)}, u32[]{:S(2)}) async-start(bf16[16,2,32,512]{3,2,1,0:T(8,128)(2,1)} %bitcast.8), calls=%async_computation.1 | async-start | bytes 2097152 | tf_op jit(solution)/shard_map/all_to_all | solution.py:229
  36.8 0.0 copy-start.2
  36.8 0.7 %copy-done.2 = s32[2,32]{1,0:T(2,128)S(1)} copy-done((s32[2,32]{1,0:T(2,128)S(1)}, s32[2,32]{1,0:T(2,128)}, u32[]{:S(2)}) %copy-start.2) | copy-done | bytes 280
  37.5 0.1 pad_add_fusion
  37.6 0.1 compare_select_fusion
  37.7 0.1 fusion.3
  37.8 0.1 pad_add_fusion.1.table_ref
  37.8 15.5 %all-to-all-done.1.far_ref = bf16[16,2,32,512]{3,2,1,0:T(8,128)(2,1)S(1)} async-done(((bf16[16,2,32,512]{3,2,1,0:T(8,128)(2,1)}), bf16[16,2,32,512]{3,2,1,0:T(8,128)(2,1)S(1)}, u32[]{:S(2)}, u32[]{:S(2)}) %all-to-all-start.1) | async-done | bytes 1048608 | tf_op jit(solution)/shard_map/all_to_all | solution.py:229
  53.4 3.0 %pairs.1 = f32[32,2,2,512]{3,2,1,0:T(2,128)} custom-call(s32[2,32]{1,0:T(2,128)S(1)} %pad_add_fusion.1.table_ref, bf16[16,2,32,512]{3,2,1,0:T(8,128)(2,1)S(1)} %all-to-all-done.near_ref, bf16[16,2,32,512]{3,2,1,0:T(8,128)(2,1)S(1)} %all-to-all-done.1.far_ref), custom_call_target="tpu_custom_call" | custom-call | tf_op jit(solution)/shard_map/pairs/pallas_call | solution.py:195
Async XLA Ops:
  0.1 1.1 %copy-start.1 = (s32[512]{0:T(512)S(1)}, s32[512]{0:T(512)}, u32[]{:S(2)}) copy-start(s32[512]{0:T(512)} %param.5) | copy-start | bytes 6148
  1.2 9.1 %copy-start = (bf16[2,512,256]{2,1,0:T(8,128)(2,1)S(1)}, bf16[2,512,256]{2,1,0:T(8,128)(2,1)}, u32[]{:S(2)}) copy-start(bf16[2,512,256]{2,1,0:T(8,128)(2,1)} %orbitals_ref.1) | copy-start | bytes 1572868
  2.1 8.2 %collective-permute-start = (bf16[2,256,256]{2,1,0:T(8,128)(2,1)S(1)}, bf16[2,256,256]{2,1,0:T(8,128)(2,1)S(1)}, u32[]{:S(2)}, u32[]{:S(2)}) collective-permute-start(bf16[2,256,256]{2,1,0:T(8,128)(2,1)S(1)} %front.1.refs_0_), channel_id=1, source_target_pairs={{0,1},{1,0},{2,3},{3,2},{4,5},{5,4},{6,7},{7,6},{8,9},{9,8},{10,11... | collective-permute-start | bytes 786440 | tf_op jit(solution)/shard_map/ppermute | solution.py:26
  4.2 12.8 %collective-permute-start.1 = (bf16[512,256]{1,0:T(8,128)(2,1)S(1)}, bf16[512,256]{1,0:T(8,128)(2,1)S(1)}, u32[]{:S(2)}, u32[]{:S(2)}) collective-permute-start(bf16[512,256]{1,0:T(8,128)(2,1)S(1)} %get-tuple-element.15.mine_ref), channel_id=1, source_target_pairs={{0,24},{1,25},{2,26},{3,27},{4,28},{5,29},{6,30},{7,31},{8,16},{9,... | collective-permute-start | bytes 786440 | tf_op jit(solution)/shard_map/ppermute | solution.py:26
  7.5 11.4 %collective-permute-start.2 = (bf16[512,256]{1,0:T(8,128)(2,1)S(1)}, bf16[512,256]{1,0:T(8,128)(2,1)S(1)}, u32[]{:S(2)}, u32[]{:S(2)}) collective-permute-start(bf16[512,256]{1,0:T(8,128)(2,1)S(1)} %get-tuple-element.16.other_ref), channel_id=1, source_target_pairs={{0,25},{1,24},{2,27},{3,26},{4,29},{5,28},{6,31},{7,30},{8,17},{9,... | collective-permute-start | bytes 786440 | tf_op jit(solution)/shard_map/ppermute | solution.py:26
  11.7 19.4 %all-to-all-start = ((bf16[16,2,32,512]{3,2,1,0:T(8,128)(2,1)}), bf16[16,2,32,512]{3,2,1,0:T(8,128)(2,1)S(1)}, u32[]{:S(2)}, u32[]{:S(2)}) async-start(bf16[16,2,32,512]{3,2,1,0:T(8,128)(2,1)} %bitcast.7), calls=%async_computation | async-start | bytes 2097152 | tf_op jit(solution)/shard_map/all_to_all | solution.py:229
  31.1 22.2 %all-to-all-start.1 = ((bf16[16,2,32,512]{3,2,1,0:T(8,128)(2,1)}), bf16[16,2,32,512]{3,2,1,0:T(8,128)(2,1)S(1)}, u32[]{:S(2)}, u32[]{:S(2)}) async-start(bf16[16,2,32,512]{3,2,1,0:T(8,128)(2,1)} %bitcast.8), calls=%async_computation.1 | async-start | bytes 2097152 | tf_op jit(solution)/shard_map/all_to_all | solution.py:229
  36.8 0.7 %copy-start.2 = (s32[2,32]{1,0:T(2,128)S(1)}, s32[2,32]{1,0:T(2,128)}, u32[]{:S(2)}) copy-start(s32[2,32]{1,0:T(2,128)} %param.4) | copy-start | bytes 772

commit v26 on v25

--- a/solution.py
+++ b/solution.py
@@ -101,28 +101,31 @@
     )(orbitals, *shares)
 
 
-def far_kernel(place_ref, rows_ref, *refs):
+def ahead_kernel(rows_ref, slab_ref, picked_ref, chosen_ref):
+    npoints, slabs = rows_ref.shape
+    spot = lax.broadcasted_iota(jnp.int32, (npoints, slab_ref.shape[0]), 1)
+    for number in range(slabs):
+        chosen = (rows_ref[:, number : number + 1] == spot).astype(jnp.float32)
+        chosen = chosen.astype(jnp.bfloat16)
+        if number:
+            chosen_ref[number - 1] = chosen
+        else:
+            picked = jnp.dot(chosen, slab_ref[...], preferred_element_type=jnp.float32)
+            picked_ref[...] = picked.astype(jnp.bfloat16)
+
+
+def far_kernel(place_ref, picked_ref, chosen_ref, *refs):
     *slab_refs, out_ref, parts_ref, sems = refs
     groups, _, _, length, slab_size = out_ref.shape
-    spot = lax.broadcasted_iota(jnp.int32, (rows_ref.shape[0], slab_size), 1)
-    picked = 0.0
-    for number, slab_ref in enumerate(slab_refs):
-        chosen = (rows_ref[:, number : number + 1] == spot).astype(jnp.float32)
-        picked += jnp.dot(
-            chosen.astype(jnp.bfloat16), slab_ref[...], preferred_element_type=jnp.float32
-        )
+    picked = picked_ref[...].astype(jnp.float32)
+    for number, slab_ref in enumerate(slab_refs[1:]):
+        picked += jnp.dot(chosen_ref[number], slab_ref[...], preferred_element_type=jnp.float32)
     turned = [rows.astype(jnp.bfloat16) for rows in (picked, rotate(picked))]
     copies = []
     for number in range(SPLIT):
         for part in range(2):
-            product = lax.dot_general(
-                turned[part],
-                slab_refs[number][...],
-                (((1,), (1,)), ((), ())),
-                preferred_element_type=jnp.float32,
-            )
             place = len(copies)
-            parts_ref[place] = product.reshape(groups, length, slab_size).astype(jnp.bfloat16)
+            parts_ref[place] = product(turned[part], slab_refs[number][...], groups)
             target = out_ref.at[:, place_ref[1] % SPLIT ^ number, part]
             copies.append(pltpu.make_async_copy(parts_ref.at[place], target, sems.at[place]))
             copies[-1].start()
@@ -131,12 +134,25 @@
 
 
 def make_far(rows, slabs, place, groups):
-    slab_size, _ = slabs[0].shape
-    length = rows.shape[0] // groups
+    slab_size, channels = slabs[0].shape
+    npoints, _ = rows.shape
+    length = npoints // groups
     vmem = pl.BlockSpec(memory_space=pltpu.VMEM)
+    picked, chosen = pl.pallas_call(
+        ahead_kernel,
+        in_specs=[vmem] * 2,
+        out_specs=[vmem] * 2,
+        out_shape=[
+            jax.ShapeDtypeStruct((npoints, channels), jnp.bfloat16),
+            jax.ShapeDtypeStruct((len(slabs) - 1, npoints, slab_size), jnp.bfloat16),
+        ],
+        cost_estimate=pl.CostEstimate(flops=1_000_000, bytes_accessed=3_000, transcendentals=0),
+        compiler_params=pltpu.CompilerParams(vmem_limit_bytes=VMEM_LIMIT),
+        name="ahead",
+    )(rows, slabs[0])
     return pl.pallas_call(
         far_kernel,
-        in_specs=[pl.BlockSpec(memory_space=pltpu.SMEM), vmem] + [vmem] * len(slabs),
+        in_specs=[pl.BlockSpec(memory_space=pltpu.SMEM)] + [vmem] * (2 + len(slabs)),
         out_specs=pl.BlockSpec(memory_space=pl.ANY),
         out_shape=jax.ShapeDtypeStruct((groups, SPLIT, 2, length, slab_size), jnp.bfloat16),
         scratch_shapes=[
@@ -148,7 +164,7 @@
         ),
         compiler_params=pltpu.CompilerParams(vmem_limit_bytes=VMEM_LIMIT),
         name="far",
-    )(place, rows, *slabs)
+    )(place, picked, chosen, *slabs)
 
 
 def pair_kernel(scale, table_ref, near_ref, far_ref, out_ref, held_ref, sums_ref, sems):
@@ -157,31 +173,28 @@
     held_ref[: total_k // 2] = near_ref[...].astype(jnp.float32)
     held_ref[total_k // 2 :] = far_ref[...].astype(jnp.float32)
 
-    count, columns = min(16, length), min(256, width)
+    columns = min(256, width)
     copies = []
-    for start in range(0, length, count):
-        rows = pl.ds(start, count)
-        for column in range(0, width, columns):
-            lanes = pl.ds(column, columns)
-
-            def step(k, sums):
-                real, imag = held_ref[k, 0, rows, lanes], held_ref[k, 1, rows, lanes]
-                after = []
-                for transfer in range(transfers):
-                    other = table_ref[transfer, k]
-                    other_real = held_ref[other, 0, rows, lanes]
-                    other_imag = held_ref[other, 1, rows, lanes]
-                    after.append(sums[2 * transfer] + (real * other_real + imag * other_imag))
-                    after.append(sums[2 * transfer + 1] + (imag * other_real - real * other_imag))
-                return tuple(after)
-
-            zero = jnp.zeros((count, columns), jnp.float32)
-            sums = lax.fori_loop(0, total_k, step, (zero,) * (2 * transfers), unroll=4)
-            for place, value in enumerate(sums):
-                sums_ref[rows, place // 2, place % 2, lanes] = value * scale
-        copies.append(
-            pltpu.make_async_copy(sums_ref.at[rows], out_ref.at[rows], sems.at[start // count])
-        )
+    for column in range(0, width, columns):
+        lanes = pl.ds(column, columns)
+
+        def step(k, sums, lanes=lanes):
+            real, imag = held_ref[k, 0, :, lanes], held_ref[k, 1, :, lanes]
+            after = []
+            for transfer in range(transfers):
+                other = table_ref[transfer, k]
+                other_real = held_ref[other, 0, :, lanes]
+                other_imag = held_ref[other, 1, :, lanes]
+                after.append(sums[2 * transfer] + (real * other_real + imag * other_imag))
+                after.append(sums[2 * transfer + 1] + (imag * other_real - real * other_imag))
+            return tuple(after)
+
+        zero = jnp.zeros((length, columns), jnp.float32)
+        sums = lax.fori_loop(0, total_k, step, (zero,) * (2 * transfers), unroll=4)
+        for place, value in enumerate(sums):
+            sums_ref[:, place // 2, place % 2, lanes] = value * scale
+        source, target = sums_ref.at[:, :, :, lanes], out_ref.at[:, :, :, lanes]
+        copies.append(pltpu.make_async_copy(source, target, sems.at[column // columns]))
         copies[-1].start()
     for copy in copies:
         copy.wait()
@@ -200,7 +213,7 @@
         scratch_shapes=[
             pltpu.VMEM((2 * half_k, 2, length, slab_size), jnp.float32),
             pltpu.VMEM(out.shape, jnp.float32),
-            pltpu.SemaphoreType.DMA((length // min(16, length),)),
+            pltpu.SemaphoreType.DMA((slab_size // min(256, slab_size),)),
         ],
         compiler_params=pltpu.CompilerParams(vmem_limit_bytes=VMEM_LIMIT),
         name="pairs",

time: 56.6 us -> 56.5 us (level)
  no operation moved by 1% of the time
where the time goes in v26:
time: 56.5 us; the launch traced here: 56.2 us
  waiting for transfers between devices  29.8 us (53%)
  starting transfers between devices  16.1 us (28%)
  Pallas kernels  7.86 us (14%)
  local copies, waits for them, and re-layouts  1.91 us (3%)
    all_to_all x2, waiting for transfers between devices, send(): lax.all_to_all(fields, around, split_axis=0, concat_axis=0, tiled=True)  25.7 us
    all_to_all x2, starting transfers between devices, send(): lax.all_to_all(fields, around, split_axis=0, concat_axis=0, tiled=True)  10.7 us
    ppermute x3, starting transfers between devices, swap(): return lax.ppermute(block, KA + GA, route)  5.46 us
    ppermute x3, waiting for transfers between devices, swap(): return lax.ppermute(block, KA + GA, route)  4.07 us
    pallas_call x1, Pallas kernels, make_pairs(): pl.pallas_call(functools.partial(pair_kernel, 1.0 / math.sqrt(2 * half_k)...  3.12 us
    pallas_call x1, Pallas kernels, make_far(): pl.pallas_call(far_kernel, in_specs=[pl.BlockSpec(memory_space=pltpu.SMEM...  2.06 us
    pallas_call x1, Pallas kernels, make_near(): pl.pallas_call(near_kernel, grid=(kdevice,), in_specs=[pl.BlockSpec((1, s...  1.53 us
  transfers between devices with their start and end apart: 5, of which 4 were waited for; matrix products, arithmetic and copies ran while one was open for 1% of the time, Pallas kernels for 7%

profile of v26, /device:TPU:1, one launch (start us, length us, event | category | flops | bytes accessed | tf_op | source)
XLA Modules:
  0.0 56.2 jit_solution(17995700937604376523)
XLA Ops:
  0.0 0.1 pad_add_fusion.2.place_ref
  0.1 0.0 copy-start.1
  0.1 1.1 %dynamic-slice_bitcast_fusion = (bf16[512,256]{1,0:T(8,128)(2,1)S(1)}, bf16[512,256]{1,0:T(8,128)(2,1)S(1)}) fusion(bf16[2,512,256]{2,1,0:T(8,128)(2,1)} %orbitals_ref.1, s32[]{:T(128)S(6)} %select_n.43, s32[]{:T(128)S(6)} %select_n.42), kind=kLoop, calls=%fused_computation | loop fusion | bytes 1048584 | tf_op jit(solution)/shard_map/jit(dynamic_index_in_dim)/squeeze | solution.py:234
  1.2 0.0 copy-start
  1.2 0.0 copy-done.1
  1.2 0.9 %front.1.refs_0_ = bf16[2,256,256]{2,1,0:T(8,128)(2,1)S(1)} custom-call(s32[2]{0:T(128)S(1)} %pad_add_fusion.2.place_ref, s32[1,512]{1,0:T(1,128)S(1)} %bitcast.12, bf16[512,256]{1,0:T(8,128)(2,1)S(1)} %get-tuple-element.17.mine_ref, bf16[512,256]{1,0:T(8,128)(2,1)S(1)} %get-tuple-element.20.other_ref), custom_call_target="tpu_custom_call" | custom-call | tf_op jit(solution)/shard_map/front/pallas_call | solution.py:65
  2.1 2.1 %collective-permute-start = (bf16[2,256,256]{2,1,0:T(8,128)(2,1)S(1)}, bf16[2,256,256]{2,1,0:T(8,128)(2,1)S(1)}, u32[]{:S(2)}, u32[]{:S(2)}) collective-permute-start(bf16[2,256,256]{2,1,0:T(8,128)(2,1)S(1)} %front.1.refs_0_), channel_id=1, source_target_pairs={{0,1},{1,0},{2,3},{3,2},{4,5},{5,4},{6,7},{7,6},{8,9},{9,8},{10,11... | collective-permute-start | bytes 786440 | tf_op jit(solution)/shard_map/ppermute | solution.py:26
  4.2 3.3 %collective-permute-start.1 = (bf16[512,256]{1,0:T(8,128)(2,1)S(1)}, bf16[512,256]{1,0:T(8,128)(2,1)S(1)}, u32[]{:S(2)}, u32[]{:S(2)}) collective-permute-start(bf16[512,256]{1,0:T(8,128)(2,1)S(1)} %get-tuple-element.17.mine_ref), channel_id=1, source_target_pairs={{0,24},{1,25},{2,26},{3,27},{4,28},{5,29},{6,30},{7,31},{8,16},{9,... | collective-permute-start | bytes 786440 | tf_op jit(solution)/shard_map/ppermute | solution.py:26
  7.5 0.0 collective-permute-start.2
  7.5 0.1 pad_add_fusion.3
  7.6 0.1 dynamic_slice.17
  7.7 0.1 broadcast_subtract_fusion.rows_ref
  7.8 2.5 %collective-permute-done.refs_1_ = bf16[2,256,256]{2,1,0:T(8,128)(2,1)S(1)} collective-permute-done((bf16[2,256,256]{2,1,0:T(8,128)(2,1)S(1)}, bf16[2,256,256]{2,1,0:T(8,128)(2,1)S(1)}, u32[]{:S(2)}, u32[]{:S(2)}) %collective-permute-start) | collective-permute-done | bytes 262176 | tf_op jit(solution)/shard_map/ppermute | solution.py:26
  10.2 0.0 copy-done
  10.2 1.5 %near.1 = bf16[8,2,2,32,512]{4,3,2,1,0:T(8,128)(2,1)} custom-call(bf16[2,512,256]{2,1,0:T(8,128)(2,1)S(1)} %copy-done, bf16[2,256,256]{2,1,0:T(8,128)(2,1)S(1)} %front.1.refs_0_, bf16[2,256,256]{2,1,0:T(8,128)(2,1)S(1)} %collective-permute-done.refs_1_), custom_call_target="tpu_custom_call" | custom-call | flops 1000000000 | bytes 3000000 | tf_op jit(solution)/shard_map/near/pallas_call | solution.py:89
  11.8 5.2 %all-to-all-start = ((bf16[16,2,32,512]{3,2,1,0:T(8,128)(2,1)}), bf16[16,2,32,512]{3,2,1,0:T(8,128)(2,1)S(1)}, u32[]{:S(2)}, u32[]{:S(2)}) async-start(bf16[16,2,32,512]{3,2,1,0:T(8,128)(2,1)} %bitcast.7), calls=%async_computation | async-start | bytes 2097152 | tf_op jit(solution)/shard_map/all_to_all | solution.py:242
  17.0 0.0 collective-permute-done.1.slab_ref.refs_0_
  17.0 0.3 ahead.1
  17.3 1.6 %collective-permute-done.2.refs_1_ = bf16[512,256]{1,0:T(8,128)(2,1)S(1)} collective-permute-done((bf16[512,256]{1,0:T(8,128)(2,1)S(1)}, bf16[512,256]{1,0:T(8,128)(2,1)S(1)}, u32[]{:S(2)}, u32[]{:S(2)}) %collective-permute-start.2) | collective-permute-done | bytes 262176 | tf_op jit(solution)/shard_map/ppermute | solution.py:26
  18.9 2.1 %far.1 = bf16[8,2,2,32,512]{4,3,2,1,0:T(8,128)(2,1)} custom-call(s32[2]{0:T(128)S(1)} %pad_add_fusion.2.place_ref, bf16[256,256]{1,0:T(8,128)(2,1)S(1)} %get-tuple-element.18.picked_ref, bf16[1,256,512]{2,1,0:T(8,128)(2,1)S(1)} %get-tuple-element.19.chosen_ref, bf16[512,256]{1,0:T(8,128)(2,1)S(1)} %collective-permute-done.1.slab_ref.refs_0_, ...), custom_call_target="tpu_custom_call" | custom-call | flops 60000002048 | bytes 180000000 | tf_op jit(solution)/shard_map/far/pallas_call | solution.py:153
  20.9 10.2 %all-to-all-done.near_ref = bf16[16,2,32,512]{3,2,1,0:T(8,128)(2,1)S(1)} async-done(((bf16[16,2,32,512]{3,2,1,0:T(8,128)(2,1)}), bf16[16,2,32,512]{3,2,1,0:T(8,128)(2,1)S(1)}, u32[]{:S(2)}, u32[]{:S(2)}) %all-to-all-start) | async-done | bytes 1048608 | tf_op jit(solution)/shard_map/all_to_all | solution.py:242
  31.1 5.5 %all-to-all-start.1 = ((bf16[16,2,32,512]{3,2,1,0:T(8,128)(2,1)}), bf16[16,2,32,512]{3,2,1,0:T(8,128)(2,1)S(1)}, u32[]{:S(2)}, u32[]{:S(2)}) async-start(bf16[16,2,32,512]{3,2,1,0:T(8,128)(2,1)} %bitcast.8), calls=%async_computation.1 | async-start | bytes 2097152 | tf_op jit(solution)/shard_map/all_to_all | solution.py:242
  36.6 0.0 copy-start.2
  36.6 0.7 %copy-done.2 = s32[2,32]{1,0:T(2,128)S(1)} copy-done((s32[2,32]{1,0:T(2,128)S(1)}, s32[2,32]{1,0:T(2,128)}, u32[]{:S(2)}) %copy-start.2) | copy-done | bytes 280
  37.3 0.1 pad_add_fusion
  37.3 0.1 compare_select_fusion
  37.4 0.1 fusion.3
  37.5 0.1 pad_add_fusion.1.table_ref
  37.6 15.5 %all-to-all-done.1.far_ref = bf16[16,2,32,512]{3,2,1,0:T(8,128)(2,1)S(1)} async-done(((bf16[16,2,32,512]{3,2,1,0:T(8,128)(2,1)}), bf16[16,2,32,512]{3,2,1,0:T(8,128)(2,1)S(1)}, u32[]{:S(2)}, u32[]{:S(2)}) %all-to-all-start.1) | async-done | bytes 1048608 | tf_op jit(solution)/shard_map/all_to_all | solution.py:242
  53.1 3.1 %pairs.1 = f32[32,2,2,512]{3,2,1,0:T(2,128)} custom-call(s32[2,32]{1,0:T(2,128)S(1)} %pad_add_fusion.1.table_ref, bf16[16,2,32,512]{3,2,1,0:T(8,128)(2,1)S(1)} %all-to-all-done.near_ref, bf16[16,2,32,512]{3,2,1,0:T(8,128)(2,1)S(1)} %all-to-all-done.1.far_ref), custom_call_target="tpu_custom_call" | custom-call | tf_op jit(solution)/shard_map/pairs/pallas_call | solution.py:208
Async XLA Ops:
  0.1 1.1 %copy-start.1 = (s32[512]{0:T(512)S(1)}, s32[512]{0:T(512)}, u32[]{:S(2)}) copy-start(s32[512]{0:T(512)} %param.5) | copy-start | bytes 6148
  1.2 9.1 %copy-start = (bf16[2,512,256]{2,1,0:T(8,128)(2,1)S(1)}, bf16[2,512,256]{2,1,0:T(8,128)(2,1)}, u32[]{:S(2)}) copy-start(bf16[2,512,256]{2,1,0:T(8,128)(2,1)} %orbitals_ref.1) | copy-start | bytes 1572868
  2.1 8.2 %collective-permute-start = (bf16[2,256,256]{2,1,0:T(8,128)(2,1)S(1)}, bf16[2,256,256]{2,1,0:T(8,128)(2,1)S(1)}, u32[]{:S(2)}, u32[]{:S(2)}) collective-permute-start(bf16[2,256,256]{2,1,0:T(8,128)(2,1)S(1)} %front.1.refs_0_), channel_id=1, source_target_pairs={{0,1},{1,0},{2,3},{3,2},{4,5},{5,4},{6,7},{7,6},{8,9},{9,8},{10,11... | collective-permute-start | bytes 786440 | tf_op jit(solution)/shard_map/ppermute | solution.py:26
  4.2 12.8 %collective-permute-start.1 = (bf16[512,256]{1,0:T(8,128)(2,1)S(1)}, bf16[512,256]{1,0:T(8,128)(2,1)S(1)}, u32[]{:S(2)}, u32[]{:S(2)}) collective-permute-start(bf16[512,256]{1,0:T(8,128)(2,1)S(1)} %get-tuple-element.17.mine_ref), channel_id=1, source_target_pairs={{0,24},{1,25},{2,26},{3,27},{4,28},{5,29},{6,30},{7,31},{8,16},{9,... | collective-permute-start | bytes 786440 | tf_op jit(solution)/shard_map/ppermute | solution.py:26
  7.5 11.4 %collective-permute-start.2 = (bf16[512,256]{1,0:T(8,128)(2,1)S(1)}, bf16[512,256]{1,0:T(8,128)(2,1)S(1)}, u32[]{:S(2)}, u32[]{:S(2)}) collective-permute-start(bf16[512,256]{1,0:T(8,128)(2,1)S(1)} %get-tuple-element.20.other_ref), channel_id=1, source_target_pairs={{0,25},{1,24},{2,27},{3,26},{4,29},{5,28},{6,31},{7,30},{8,17},{9,... | collective-permute-start | bytes 786440 | tf_op jit(solution)/shard_map/ppermute | solution.py:26
  11.8 19.4 %all-to-all-start = ((bf16[16,2,32,512]{3,2,1,0:T(8,128)(2,1)}), bf16[16,2,32,512]{3,2,1,0:T(8,128)(2,1)S(1)}, u32[]{:S(2)}, u32[]{:S(2)}) async-start(bf16[16,2,32,512]{3,2,1,0:T(8,128)(2,1)} %bitcast.7), calls=%async_computation | async-start | bytes 2097152 | tf_op jit(solution)/shard_map/all_to_all | solution.py:242
  31.1 22.0 %all-to-all-start.1 = ((bf16[16,2,32,512]{3,2,1,0:T(8,128)(2,1)}), bf16[16,2,32,512]{3,2,1,0:T(8,128)(2,1)S(1)}, u32[]{:S(2)}, u32[]{:S(2)}) async-start(bf16[16,2,32,512]{3,2,1,0:T(8,128)(2,1)} %bitcast.8), calls=%async_computation.1 | async-start | bytes 2097152 | tf_op jit(solution)/shard_map/all_to_all | solution.py:242
  36.6 0.7 %copy-start.2 = (s32[2,32]{1,0:T(2,128)S(1)}, s32[2,32]{1,0:T(2,128)}, u32[]{:S(2)}) copy-start(s32[2,32]{1,0:T(2,128)} %param.4) | copy-start | bytes 772

commit v27 on v23

--- a/solution.py
+++ b/solution.py
@@ -221,6 +221,7 @@
     other = lax.dynamic_index_in_dim(orbitals, 1 - lo, 0, keepdims=False)
     share = make_front(mine, other, points, place)
     shares = [share] + [swap(share, False, x) for x in range(1, slabs)]
+    shares, other = lax.optimization_barrier((shares, other))
     far = [swap(other if x & 1 else mine, True, x) for x in range(slabs)]
 
     def send(fields, around):

time: 64.4 us -> 59.1 us (0.918)
  waiting for transfers between devices: 38.7 us -> 29.5 us
  starting transfers between devices: 15.3 us -> 19.2 us
    ppermute x3, waiting for transfers between devices: 11.8 us -> 2.57 us  [swap(): return lax.ppermute(block, KA + GA, route)]
    ppermute x3, starting transfers between devices: 5.54 us -> 9.64 us  [swap(): return lax.ppermute(block, KA + GA, route)]
  transfers between devices with their start and end apart: 5 -> 5, of which waited for: 3 -> 3; matrix products, arithmetic and copies ran while one was open for 1% -> 1% of each run, Pallas kernels for 7% -> 6%
where the time goes in v27:
time: 59.1 us; the launch traced here: 58.8 us
  waiting for transfers between devices  29.5 us (50%)
  starting transfers between devices  19.2 us (32%)
  Pallas kernels  7.63 us (13%)
  local copies, waits for them, and re-layouts  1.91 us (3%)
    all_to_all x2, waiting for transfers between devices, send(): lax.all_to_all(fields, around, split_axis=0, concat_axis=0, tiled=True)  26.9 us
    ppermute x3, starting transfers between devices, swap(): return lax.ppermute(block, KA + GA, route)  9.64 us
    all_to_all x2, starting transfers between devices, send(): lax.all_to_all(fields, around, split_axis=0, concat_axis=0, tiled=True)  9.61 us
    pallas_call x1, Pallas kernels, make_pairs(): pl.pallas_call(functools.partial(pair_kernel, 1.0 / math.sqrt(2 * half_k)...  2.96 us
    ppermute x3, waiting for transfers between devices, swap(): return lax.ppermute(block, KA + GA, route)  2.57 us
    pallas_call x1, Pallas kernels, make_far(): pl.pallas_call(far_kernel, in_specs=[pl.BlockSpec(memory_space=pltpu.SMEM...  2.27 us
    pallas_call x1, Pallas kernels, make_near(): pl.pallas_call(near_kernel, grid=(kdevice,), in_specs=[pl.BlockSpec((1, s...  1.52 us
  transfers between devices with their start and end apart: 5, of which 3 were waited for; matrix products, arithmetic and copies ran while one was open for 1% of the time, Pallas kernels for 6%

profile of v27, /device:TPU:1, one launch (start us, length us, event | category | flops | bytes accessed | tf_op | source)
XLA Modules:
  0.0 58.8 jit_solution(12403796261211533485)
XLA Ops:
  0.0 0.1 pad_add_fusion.2.place_ref
  0.1 0.0 copy-start.1
  0.1 1.1 %dynamic-slice_bitcast_fusion = (bf16[512,256]{1,0:T(8,128)(2,1)S(1)}, bf16[512,256]{1,0:T(8,128)(2,1)S(1)}) fusion(bf16[2,512,256]{2,1,0:T(8,128)(2,1)} %orbitals_ref.1, s32[]{:T(128)S(6)} %select_n.43, s32[]{:T(128)S(6)} %select_n.42), kind=kLoop, calls=%fused_computation | loop fusion | bytes 1048584 | tf_op jit(solution)/shard_map/jit(dynamic_index_in_dim)/squeeze | solution.py:221
  1.2 0.0 copy-start
  1.2 0.0 copy-done.1
  1.2 0.9 %front.1.refs_0_ = bf16[2,256,256]{2,1,0:T(8,128)(2,1)S(1)} custom-call(s32[2]{0:T(128)S(1)} %pad_add_fusion.2.place_ref, s32[1,512]{1,0:T(1,128)S(1)} %bitcast.12, bf16[512,256]{1,0:T(8,128)(2,1)S(1)} %get-tuple-element.20.mine_ref, bf16[512,256]{1,0:T(8,128)(2,1)S(1)} %get-tuple-element.16.other_ref), custom_call_target="tpu_custom_call" | custom-call | tf_op jit(solution)/shard_map/front/pallas_call | solution.py:65
  2.1 2.1 %collective-permute-start = (bf16[2,256,256]{2,1,0:T(8,128)(2,1)S(1)}, bf16[2,256,256]{2,1,0:T(8,128)(2,1)S(1)}, u32[]{:S(2)}, u32[]{:S(2)}) collective-permute-start(bf16[2,256,256]{2,1,0:T(8,128)(2,1)S(1)} %front.1.refs_0_), channel_id=1, source_target_pairs={{0,1},{1,0},{2,3},{3,2},{4,5},{5,4},{6,7},{7,6},{8,9},{9,8},{10,11... | collective-permute-start | bytes 786440 | tf_op jit(solution)/shard_map/ppermute | solution.py:26
  4.2 3.3 %collective-permute-start.1 = (bf16[512,256]{1,0:T(8,128)(2,1)S(1)}, bf16[512,256]{1,0:T(8,128)(2,1)S(1)}, u32[]{:S(2)}, u32[]{:S(2)}) collective-permute-start(bf16[512,256]{1,0:T(8,128)(2,1)S(1)} %get-tuple-element.20.mine_ref), channel_id=1, source_target_pairs={{0,24},{1,25},{2,26},{3,27},{4,28},{5,29},{6,30},{7,31},{8,16},{9,... | collective-permute-start | bytes 786440 | tf_op jit(solution)/shard_map/ppermute | solution.py:26
  7.5 0.1 dynamic_slice.17
  7.6 0.1 pad_add_fusion.3
  7.7 2.6 %collective-permute-done.refs_1_ = bf16[2,256,256]{2,1,0:T(8,128)(2,1)S(1)} collective-permute-done((bf16[2,256,256]{2,1,0:T(8,128)(2,1)S(1)}, bf16[2,256,256]{2,1,0:T(8,128)(2,1)S(1)}, u32[]{:S(2)}, u32[]{:S(2)}) %collective-permute-start) | collective-permute-done | bytes 262176 | tf_op jit(solution)/shard_map/ppermute | solution.py:26
  10.2 4.2 %collective-permute-start.2 = (bf16[512,256]{1,0:T(8,128)(2,1)S(1)}, bf16[512,256]{1,0:T(8,128)(2,1)S(1)}, u32[]{:S(2)}, u32[]{:S(2)}) collective-permute-start(bf16[512,256]{1,0:T(8,128)(2,1)S(1)} %get-tuple-element.16.other_ref), channel_id=1, source_target_pairs={{0,25},{1,24},{2,27},{3,26},{4,29},{5,28},{6,31},{7,30},{8,17},{9,... | collective-permute-start | bytes 786440 | tf_op jit(solution)/shard_map/ppermute | solution.py:26
  14.4 0.1 broadcast_subtract_fusion.rows_ref
  14.5 0.0 copy-done
  14.5 1.5 %near.1 = bf16[8,2,2,32,512]{4,3,2,1,0:T(8,128)(2,1)} custom-call(bf16[2,512,256]{2,1,0:T(8,128)(2,1)S(1)} %copy-done, bf16[2,256,256]{2,1,0:T(8,128)(2,1)S(1)} %front.1.refs_0_, bf16[2,256,256]{2,1,0:T(8,128)(2,1)S(1)} %collective-permute-done.refs_1_), custom_call_target="tpu_custom_call" | custom-call | flops 1000000000 | bytes 3000000 | tf_op jit(solution)/shard_map/near/pallas_call | solution.py:89
  16.0 5.3 %all-to-all-start = ((bf16[16,2,32,512]{3,2,1,0:T(8,128)(2,1)}), bf16[16,2,32,512]{3,2,1,0:T(8,128)(2,1)S(1)}, u32[]{:S(2)}, u32[]{:S(2)}) async-start(bf16[16,2,32,512]{3,2,1,0:T(8,128)(2,1)} %bitcast.7), calls=%async_computation | async-start | bytes 2097152 | tf_op jit(solution)/shard_map/all_to_all | solution.py:229
  21.3 0.0 collective-permute-done.1.refs_0_
  21.3 0.0 collective-permute-done.2.refs_1_
  21.3 2.3 %far.1 = bf16[8,2,2,32,512]{4,3,2,1,0:T(8,128)(2,1)} custom-call(s32[2]{0:T(128)S(1)} %pad_add_fusion.2.place_ref, s32[256,2]{1,0:T(8,128)S(1)} %broadcast_subtract_fusion.rows_ref, bf16[512,256]{1,0:T(8,128)(2,1)S(1)} %collective-permute-done.1.refs_0_, bf16[512,256]{1,0:T(8,128)(2,1)S(1)} %collective-permute-done.2.refs_1_), custom_call_target="tpu_custom_call" | custom-call | flops 60000002048 | bytes 180000000 | tf_op jit(solution)/shard_map/far/pallas_call | solution.py:137
  23.6 11.3 %all-to-all-done.near_ref = bf16[16,2,32,512]{3,2,1,0:T(8,128)(2,1)S(1)} async-done(((bf16[16,2,32,512]{3,2,1,0:T(8,128)(2,1)}), bf16[16,2,32,512]{3,2,1,0:T(8,128)(2,1)S(1)}, u32[]{:S(2)}, u32[]{:S(2)}) %all-to-all-start) | async-done | bytes 1048608 | tf_op jit(solution)/shard_map/all_to_all | solution.py:229
  34.9 4.3 %all-to-all-start.1 = ((bf16[16,2,32,512]{3,2,1,0:T(8,128)(2,1)}), bf16[16,2,32,512]{3,2,1,0:T(8,128)(2,1)S(1)}, u32[]{:S(2)}, u32[]{:S(2)}) async-start(bf16[16,2,32,512]{3,2,1,0:T(8,128)(2,1)} %bitcast.8), calls=%async_computation.1 | async-start | bytes 2097152 | tf_op jit(solution)/shard_map/all_to_all | solution.py:229
  39.3 0.0 copy-start.2
  39.3 0.7 %copy-done.2 = s32[2,32]{1,0:T(2,128)S(1)} copy-done((s32[2,32]{1,0:T(2,128)S(1)}, s32[2,32]{1,0:T(2,128)}, u32[]{:S(2)}) %copy-start.2) | copy-done | bytes 280
  39.9 0.1 pad_add_fusion
  40.0 0.1 compare_select_fusion
  40.1 0.1 fusion.3
  40.2 0.1 pad_add_fusion.1.table_ref
  40.3 15.6 %all-to-all-done.1.far_ref = bf16[16,2,32,512]{3,2,1,0:T(8,128)(2,1)S(1)} async-done(((bf16[16,2,32,512]{3,2,1,0:T(8,128)(2,1)}), bf16[16,2,32,512]{3,2,1,0:T(8,128)(2,1)S(1)}, u32[]{:S(2)}, u32[]{:S(2)}) %all-to-all-start.1) | async-done | bytes 1048608 | tf_op jit(solution)/shard_map/all_to_all | solution.py:229
  55.8 3.0 %pairs.1 = f32[32,2,2,512]{3,2,1,0:T(2,128)} custom-call(s32[2,32]{1,0:T(2,128)S(1)} %pad_add_fusion.1.table_ref, bf16[16,2,32,512]{3,2,1,0:T(8,128)(2,1)S(1)} %all-to-all-done.near_ref, bf16[16,2,32,512]{3,2,1,0:T(8,128)(2,1)S(1)} %all-to-all-done.1.far_ref), custom_call_target="tpu_custom_call" | custom-call | tf_op jit(solution)/shard_map/pairs/pallas_call | solution.py:195
Async XLA Ops:
  0.1 1.1 %copy-start.1 = (s32[512]{0:T(512)S(1)}, s32[512]{0:T(512)}, u32[]{:S(2)}) copy-start(s32[512]{0:T(512)} %param.5) | copy-start | bytes 6148
  1.2 13.4 %copy-start = (bf16[2,512,256]{2,1,0:T(8,128)(2,1)S(1)}, bf16[2,512,256]{2,1,0:T(8,128)(2,1)}, u32[]{:S(2)}) copy-start(bf16[2,512,256]{2,1,0:T(8,128)(2,1)} %orbitals_ref.1) | copy-start | bytes 1572868
  2.1 8.2 %collective-permute-start = (bf16[2,256,256]{2,1,0:T(8,128)(2,1)S(1)}, bf16[2,256,256]{2,1,0:T(8,128)(2,1)S(1)}, u32[]{:S(2)}, u32[]{:S(2)}) collective-permute-start(bf16[2,256,256]{2,1,0:T(8,128)(2,1)S(1)} %front.1.refs_0_), channel_id=1, source_target_pairs={{0,1},{1,0},{2,3},{3,2},{4,5},{5,4},{6,7},{7,6},{8,9},{9,8},{10,11... | collective-permute-start | bytes 786440 | tf_op jit(solution)/shard_map/ppermute | solution.py:26
  4.2 17.1 %collective-permute-start.1 = (bf16[512,256]{1,0:T(8,128)(2,1)S(1)}, bf16[512,256]{1,0:T(8,128)(2,1)S(1)}, u32[]{:S(2)}, u32[]{:S(2)}) collective-permute-start(bf16[512,256]{1,0:T(8,128)(2,1)S(1)} %get-tuple-element.20.mine_ref), channel_id=1, source_target_pairs={{0,24},{1,25},{2,26},{3,27},{4,28},{5,29},{6,30},{7,31},{8,16},{9,... | collective-permute-start | bytes 786440 | tf_op jit(solution)/shard_map/ppermute | solution.py:26
  10.2 11.1 %collective-permute-start.2 = (bf16[512,256]{1,0:T(8,128)(2,1)S(1)}, bf16[512,256]{1,0:T(8,128)(2,1)S(1)}, u32[]{:S(2)}, u32[]{:S(2)}) collective-permute-start(bf16[512,256]{1,0:T(8,128)(2,1)S(1)} %get-tuple-element.16.other_ref), channel_id=1, source_target_pairs={{0,25},{1,24},{2,27},{3,26},{4,29},{5,28},{6,31},{7,30},{8,17},{9,... | collective-permute-start | bytes 786440 | tf_op jit(solution)/shard_map/ppermute | solution.py:26
  16.0 18.9 %all-to-all-start = ((bf16[16,2,32,512]{3,2,1,0:T(8,128)(2,1)}), bf16[16,2,32,512]{3,2,1,0:T(8,128)(2,1)S(1)}, u32[]{:S(2)}, u32[]{:S(2)}) async-start(bf16[16,2,32,512]{3,2,1,0:T(8,128)(2,1)} %bitcast.7), calls=%async_computation | async-start | bytes 2097152 | tf_op jit(solution)/shard_map/all_to_all | solution.py:229
  34.9 20.9 %all-to-all-start.1 = ((bf16[16,2,32,512]{3,2,1,0:T(8,128)(2,1)}), bf16[16,2,32,512]{3,2,1,0:T(8,128)(2,1)S(1)}, u32[]{:S(2)}, u32[]{:S(2)}) async-start(bf16[16,2,32,512]{3,2,1,0:T(8,128)(2,1)} %bitcast.8), calls=%async_computation.1 | async-start | bytes 2097152 | tf_op jit(solution)/shard_map/all_to_all | solution.py:229
  39.3 0.7 %copy-start.2 = (s32[2,32]{1,0:T(2,128)S(1)}, s32[2,32]{1,0:T(2,128)}, u32[]{:S(2)}) copy-start(s32[2,32]{1,0:T(2,128)} %param.4) | copy-start | bytes 772

commit v28 on v26

--- a/solution.py
+++ b/solution.py
@@ -173,28 +173,31 @@
     held_ref[: total_k // 2] = near_ref[...].astype(jnp.float32)
     held_ref[total_k // 2 :] = far_ref[...].astype(jnp.float32)
 
-    columns = min(256, width)
+    count, columns = min(16, length), min(256, width)
     copies = []
-    for column in range(0, width, columns):
-        lanes = pl.ds(column, columns)
-
-        def step(k, sums, lanes=lanes):
-            real, imag = held_ref[k, 0, :, lanes], held_ref[k, 1, :, lanes]
-            after = []
-            for transfer in range(transfers):
-                other = table_ref[transfer, k]
-                other_real = held_ref[other, 0, :, lanes]
-                other_imag = held_ref[other, 1, :, lanes]
-                after.append(sums[2 * transfer] + (real * other_real + imag * other_imag))
-                after.append(sums[2 * transfer + 1] + (imag * other_real - real * other_imag))
-            return tuple(after)
-
-        zero = jnp.zeros((length, columns), jnp.float32)
-        sums = lax.fori_loop(0, total_k, step, (zero,) * (2 * transfers), unroll=4)
-        for place, value in enumerate(sums):
-            sums_ref[:, place // 2, place % 2, lanes] = value * scale
-        source, target = sums_ref.at[:, :, :, lanes], out_ref.at[:, :, :, lanes]
-        copies.append(pltpu.make_async_copy(source, target, sems.at[column // columns]))
+    for start in range(0, length, count):
+        rows = pl.ds(start, count)
+        for column in range(0, width, columns):
+            lanes = pl.ds(column, columns)
+
+            def step(k, sums):
+                real, imag = held_ref[k, 0, rows, lanes], held_ref[k, 1, rows, lanes]
+                after = []
+                for transfer in range(transfers):
+                    other = table_ref[transfer, k]
+                    other_real = held_ref[other, 0, rows, lanes]
+                    other_imag = held_ref[other, 1, rows, lanes]
+                    after.append(sums[2 * transfer] + (real * other_real + imag * other_imag))
+                    after.append(sums[2 * transfer + 1] + (imag * other_real - real * other_imag))
+                return tuple(after)
+
+            zero = jnp.zeros((count, columns), jnp.float32)
+            sums = lax.fori_loop(0, total_k, step, (zero,) * (2 * transfers), unroll=8)
+            for place, value in enumerate(sums):
+                sums_ref[rows, place // 2, place % 2, lanes] = value * scale
+        copies.append(
+            pltpu.make_async_copy(sums_ref.at[rows], out_ref.at[rows], sems.at[start // count])
+        )
         copies[-1].start()
     for copy in copies:
         copy.wait()
@@ -213,7 +216,7 @@
         scratch_shapes=[
             pltpu.VMEM((2 * half_k, 2, length, slab_size), jnp.float32),
             pltpu.VMEM(out.shape, jnp.float32),
-            pltpu.SemaphoreType.DMA((slab_size // min(256, slab_size),)),
+            pltpu.SemaphoreType.DMA((length // min(16, length),)),
         ],
         compiler_params=pltpu.CompilerParams(vmem_limit_bytes=VMEM_LIMIT),
         name="pairs",

time: 56.5 us -> 56.2 us (level)
  no operation moved by 1% of the time
where the time goes in v28:
time: 56.2 us; the launch traced here: 55.9 us
  waiting for transfers between devices  29.8 us (53%)
  starting transfers between devices  16.1 us (29%)
  Pallas kernels  7.56 us (13%)
  local copies, waits for them, and re-layouts  1.91 us (3%)
    all_to_all x2, waiting for transfers between devices, send(): lax.all_to_all(fields, around, split_axis=0, concat_axis=0, tiled=True)  25.7 us
    all_to_all x2, starting transfers between devices, send(): lax.all_to_all(fields, around, split_axis=0, concat_axis=0, tiled=True)  10.7 us
    ppermute x3, starting transfers between devices, swap(): return lax.ppermute(block, KA + GA, route)  5.46 us
    ppermute x3, waiting for transfers between devices, swap(): return lax.ppermute(block, KA + GA, route)  4.07 us
    pallas_call x1, Pallas kernels, make_pairs(): pl.pallas_call(functools.partial(pair_kernel, 1.0 / math.sqrt(2 * half_k)...  2.83 us
    pallas_call x1, Pallas kernels, make_far(): pl.pallas_call(far_kernel, in_specs=[pl.BlockSpec(memory_space=pltpu.SMEM...  2.06 us
    pallas_call x1, Pallas kernels, make_near(): pl.pallas_call(near_kernel, grid=(kdevice,), in_specs=[pl.BlockSpec((1, s...  1.53 us
  transfers between devices with their start and end apart: 5, of which 4 were waited for; matrix products, arithmetic and copies ran while one was open for 1% of the time, Pallas kernels for 7%

profile of v28, /device:TPU:1, one launch (start us, length us, event | category | flops | bytes accessed | tf_op | source)
XLA Modules:
  0.0 55.9 jit_solution(13315592981693163302)
XLA Ops:
  0.0 0.1 pad_add_fusion.2.place_ref
  0.1 0.0 copy-start.1
  0.1 1.1 %dynamic-slice_bitcast_fusion = (bf16[512,256]{1,0:T(8,128)(2,1)S(1)}, bf16[512,256]{1,0:T(8,128)(2,1)S(1)}) fusion(bf16[2,512,256]{2,1,0:T(8,128)(2,1)} %orbitals_ref.1, s32[]{:T(128)S(6)} %select_n.43, s32[]{:T(128)S(6)} %select_n.42), kind=kLoop, calls=%fused_computation | loop fusion | bytes 1048584 | tf_op jit(solution)/shard_map/jit(dynamic_index_in_dim)/squeeze | solution.py:237
  1.2 0.0 copy-start
  1.2 0.0 copy-done.1
  1.2 0.9 %front.1.refs_0_ = bf16[2,256,256]{2,1,0:T(8,128)(2,1)S(1)} custom-call(s32[2]{0:T(128)S(1)} %pad_add_fusion.2.place_ref, s32[1,512]{1,0:T(1,128)S(1)} %bitcast.12, bf16[512,256]{1,0:T(8,128)(2,1)S(1)} %get-tuple-element.17.mine_ref, bf16[512,256]{1,0:T(8,128)(2,1)S(1)} %get-tuple-element.20.other_ref), custom_call_target="tpu_custom_call" | custom-call | tf_op jit(solution)/shard_map/front/pallas_call | solution.py:65
  2.1 2.1 %collective-permute-start = (bf16[2,256,256]{2,1,0:T(8,128)(2,1)S(1)}, bf16[2,256,256]{2,1,0:T(8,128)(2,1)S(1)}, u32[]{:S(2)}, u32[]{:S(2)}) collective-permute-start(bf16[2,256,256]{2,1,0:T(8,128)(2,1)S(1)} %front.1.refs_0_), channel_id=1, source_target_pairs={{0,1},{1,0},{2,3},{3,2},{4,5},{5,4},{6,7},{7,6},{8,9},{9,8},{10,11... | collective-permute-start | bytes 786440 | tf_op jit(solution)/shard_map/ppermute | solution.py:26
  4.2 3.3 %collective-permute-start.1 = (bf16[512,256]{1,0:T(8,128)(2,1)S(1)}, bf16[512,256]{1,0:T(8,128)(2,1)S(1)}, u32[]{:S(2)}, u32[]{:S(2)}) collective-permute-start(bf16[512,256]{1,0:T(8,128)(2,1)S(1)} %get-tuple-element.17.mine_ref), channel_id=1, source_target_pairs={{0,24},{1,25},{2,26},{3,27},{4,28},{5,29},{6,30},{7,31},{8,16},{9,... | collective-permute-start | bytes 786440 | tf_op jit(solution)/shard_map/ppermute | solution.py:26
  7.5 0.0 collective-permute-start.2
  7.5 0.1 pad_add_fusion.3
  7.6 0.1 dynamic_slice.17
  7.7 0.1 broadcast_subtract_fusion.rows_ref
  7.8 2.5 %collective-permute-done.refs_1_ = bf16[2,256,256]{2,1,0:T(8,128)(2,1)S(1)} collective-permute-done((bf16[2,256,256]{2,1,0:T(8,128)(2,1)S(1)}, bf16[2,256,256]{2,1,0:T(8,128)(2,1)S(1)}, u32[]{:S(2)}, u32[]{:S(2)}) %collective-permute-start) | collective-permute-done | bytes 262176 | tf_op jit(solution)/shard_map/ppermute | solution.py:26
  10.2 0.0 copy-done
  10.2 1.5 %near.1 = bf16[8,2,2,32,512]{4,3,2,1,0:T(8,128)(2,1)} custom-call(bf16[2,512,256]{2,1,0:T(8,128)(2,1)S(1)} %copy-done, bf16[2,256,256]{2,1,0:T(8,128)(2,1)S(1)} %front.1.refs_0_, bf16[2,256,256]{2,1,0:T(8,128)(2,1)S(1)} %collective-permute-done.refs_1_), custom_call_target="tpu_custom_call" | custom-call | flops 1000000000 | bytes 3000000 | tf_op jit(solution)/shard_map/near/pallas_call | solution.py:89
  11.8 5.2 %all-to-all-start = ((bf16[16,2,32,512]{3,2,1,0:T(8,128)(2,1)}), bf16[16,2,32,512]{3,2,1,0:T(8,128)(2,1)S(1)}, u32[]{:S(2)}, u32[]{:S(2)}) async-start(bf16[16,2,32,512]{3,2,1,0:T(8,128)(2,1)} %bitcast.7), calls=%async_computation | async-start | bytes 2097152 | tf_op jit(solution)/shard_map/all_to_all | solution.py:245
  17.0 0.0 collective-permute-done.1.slab_ref.refs_0_
  17.0 0.3 ahead.1
  17.3 1.6 %collective-permute-done.2.refs_1_ = bf16[512,256]{1,0:T(8,128)(2,1)S(1)} collective-permute-done((bf16[512,256]{1,0:T(8,128)(2,1)S(1)}, bf16[512,256]{1,0:T(8,128)(2,1)S(1)}, u32[]{:S(2)}, u32[]{:S(2)}) %collective-permute-start.2) | collective-permute-done | bytes 262176 | tf_op jit(solution)/shard_map/ppermute | solution.py:26
  18.9 2.1 %far.1 = bf16[8,2,2,32,512]{4,3,2,1,0:T(8,128)(2,1)} custom-call(s32[2]{0:T(128)S(1)} %pad_add_fusion.2.place_ref, bf16[256,256]{1,0:T(8,128)(2,1)S(1)} %get-tuple-element.18.picked_ref, bf16[1,256,512]{2,1,0:T(8,128)(2,1)S(1)} %get-tuple-element.19.chosen_ref, bf16[512,256]{1,0:T(8,128)(2,1)S(1)} %collective-permute-done.1.slab_ref.refs_0_, ...), custom_call_target="tpu_custom_call" | custom-call | flops 60000002048 | bytes 180000000 | tf_op jit(solution)/shard_map/far/pallas_call | solution.py:153
  20.9 10.2 %all-to-all-done.near_ref = bf16[16,2,32,512]{3,2,1,0:T(8,128)(2,1)S(1)} async-done(((bf16[16,2,32,512]{3,2,1,0:T(8,128)(2,1)}), bf16[16,2,32,512]{3,2,1,0:T(8,128)(2,1)S(1)}, u32[]{:S(2)}, u32[]{:S(2)}) %all-to-all-start) | async-done | bytes 1048608 | tf_op jit(solution)/shard_map/all_to_all | solution.py:245
  31.1 5.5 %all-to-all-start.1 = ((bf16[16,2,32,512]{3,2,1,0:T(8,128)(2,1)}), bf16[16,2,32,512]{3,2,1,0:T(8,128)(2,1)S(1)}, u32[]{:S(2)}, u32[]{:S(2)}) async-start(bf16[16,2,32,512]{3,2,1,0:T(8,128)(2,1)} %bitcast.8), calls=%async_computation.1 | async-start | bytes 2097152 | tf_op jit(solution)/shard_map/all_to_all | solution.py:245
  36.6 0.0 copy-start.2
  36.6 0.7 %copy-done.2 = s32[2,32]{1,0:T(2,128)S(1)} copy-done((s32[2,32]{1,0:T(2,128)S(1)}, s32[2,32]{1,0:T(2,128)}, u32[]{:S(2)}) %copy-start.2) | copy-done | bytes 280
  37.3 0.1 pad_add_fusion
  37.3 0.1 compare_select_fusion
  37.4 0.1 fusion.3
  37.5 0.1 pad_add_fusion.1.table_ref
  37.6 15.5 %all-to-all-done.1.far_ref = bf16[16,2,32,512]{3,2,1,0:T(8,128)(2,1)S(1)} async-done(((bf16[16,2,32,512]{3,2,1,0:T(8,128)(2,1)}), bf16[16,2,32,512]{3,2,1,0:T(8,128)(2,1)S(1)}, u32[]{:S(2)}, u32[]{:S(2)}) %all-to-all-start.1) | async-done | bytes 1048608 | tf_op jit(solution)/shard_map/all_to_all | solution.py:245
  53.1 2.8 %pairs.1 = f32[32,2,2,512]{3,2,1,0:T(2,128)} custom-call(s32[2,32]{1,0:T(2,128)S(1)} %pad_add_fusion.1.table_ref, bf16[16,2,32,512]{3,2,1,0:T(8,128)(2,1)S(1)} %all-to-all-done.near_ref, bf16[16,2,32,512]{3,2,1,0:T(8,128)(2,1)S(1)} %all-to-all-done.1.far_ref), custom_call_target="tpu_custom_call" | custom-call | tf_op jit(solution)/shard_map/pairs/pallas_call | solution.py:211
Async XLA Ops:
  0.1 1.1 %copy-start.1 = (s32[512]{0:T(512)S(1)}, s32[512]{0:T(512)}, u32[]{:S(2)}) copy-start(s32[512]{0:T(512)} %param.5) | copy-start | bytes 6148
  1.2 9.1 %copy-start = (bf16[2,512,256]{2,1,0:T(8,128)(2,1)S(1)}, bf16[2,512,256]{2,1,0:T(8,128)(2,1)}, u32[]{:S(2)}) copy-start(bf16[2,512,256]{2,1,0:T(8,128)(2,1)} %orbitals_ref.1) | copy-start | bytes 1572868
  2.1 8.2 %collective-permute-start = (bf16[2,256,256]{2,1,0:T(8,128)(2,1)S(1)}, bf16[2,256,256]{2,1,0:T(8,128)(2,1)S(1)}, u32[]{:S(2)}, u32[]{:S(2)}) collective-permute-start(bf16[2,256,256]{2,1,0:T(8,128)(2,1)S(1)} %front.1.refs_0_), channel_id=1, source_target_pairs={{0,1},{1,0},{2,3},{3,2},{4,5},{5,4},{6,7},{7,6},{8,9},{9,8},{10,11... | collective-permute-start | bytes 786440 | tf_op jit(solution)/shard_map/ppermute | solution.py:26
  4.2 12.8 %collective-permute-start.1 = (bf16[512,256]{1,0:T(8,128)(2,1)S(1)}, bf16[512,256]{1,0:T(8,128)(2,1)S(1)}, u32[]{:S(2)}, u32[]{:S(2)}) collective-permute-start(bf16[512,256]{1,0:T(8,128)(2,1)S(1)} %get-tuple-element.17.mine_ref), channel_id=1, source_target_pairs={{0,24},{1,25},{2,26},{3,27},{4,28},{5,29},{6,30},{7,31},{8,16},{9,... | collective-permute-start | bytes 786440 | tf_op jit(solution)/shard_map/ppermute | solution.py:26
  7.5 11.4 %collective-permute-start.2 = (bf16[512,256]{1,0:T(8,128)(2,1)S(1)}, bf16[512,256]{1,0:T(8,128)(2,1)S(1)}, u32[]{:S(2)}, u32[]{:S(2)}) collective-permute-start(bf16[512,256]{1,0:T(8,128)(2,1)S(1)} %get-tuple-element.20.other_ref), channel_id=1, source_target_pairs={{0,25},{1,24},{2,27},{3,26},{4,29},{5,28},{6,31},{7,30},{8,17},{9,... | collective-permute-start | bytes 786440 | tf_op jit(solution)/shard_map/ppermute | solution.py:26
  11.8 19.4 %all-to-all-start = ((bf16[16,2,32,512]{3,2,1,0:T(8,128)(2,1)}), bf16[16,2,32,512]{3,2,1,0:T(8,128)(2,1)S(1)}, u32[]{:S(2)}, u32[]{:S(2)}) async-start(bf16[16,2,32,512]{3,2,1,0:T(8,128)(2,1)} %bitcast.7), calls=%async_computation | async-start | bytes 2097152 | tf_op jit(solution)/shard_map/all_to_all | solution.py:245
  31.1 22.0 %all-to-all-start.1 = ((bf16[16,2,32,512]{3,2,1,0:T(8,128)(2,1)}), bf16[16,2,32,512]{3,2,1,0:T(8,128)(2,1)S(1)}, u32[]{:S(2)}, u32[]{:S(2)}) async-start(bf16[16,2,32,512]{3,2,1,0:T(8,128)(2,1)} %bitcast.8), calls=%async_computation.1 | async-start | bytes 2097152 | tf_op jit(solution)/shard_map/all_to_all | solution.py:245
  36.6 0.7 %copy-start.2 = (s32[2,32]{1,0:T(2,128)S(1)}, s32[2,32]{1,0:T(2,128)}, u32[]{:S(2)}) copy-start(s32[2,32]{1,0:T(2,128)} %param.4) | copy-start | bytes 772

commit v29 on v28

--- a/solution.py
+++ b/solution.py
@@ -14,13 +14,15 @@
 KA, GA = ("half", "quarter", "inner"), ("hi", "lo")
 
 
-def swap(block, mirror, other):
+def swap(block, mirror, other, senders=(0, 1)):
     half, quarter, inner, hi, lo = (lax.axis_size(name) for name in KA + GA)
     slabs = hi * lo
     route = []
     for place in range(half * quarter * inner * slabs):
         kplace, slab = divmod(place, slabs)
         part, within = divmod(kplace, inner)
+        if part // quarter not in senders:
+            continue
         part = half * quarter - 1 - part if mirror else part
         route.append((place, (part * inner + within) * slabs + (slab ^ other)))
     return lax.ppermute(block, KA + GA, route)
@@ -101,8 +103,15 @@
     )(orbitals, *shares)
 
 
-def ahead_kernel(rows_ref, slab_ref, picked_ref, chosen_ref):
+def ahead_kernel(place_ref, rows_ref, *refs):
+    *source_refs, slab_ref, picked_ref, chosen_ref = refs
     npoints, slabs = rows_ref.shape
+    for half, source_ref in enumerate(source_refs):
+
+        @pl.when(place_ref[0] == half)
+        def _(source_ref=source_ref):
+            slab_ref[...] = source_ref[...]
+
     spot = lax.broadcasted_iota(jnp.int32, (npoints, slab_ref.shape[0]), 1)
     for number in range(slabs):
         chosen = (rows_ref[:, number : number + 1] == spot).astype(jnp.float32)
@@ -133,26 +142,27 @@
         copy.wait()
 
 
-def make_far(rows, slabs, place, groups):
+def make_far(rows, firsts, slabs, place, groups):
     slab_size, channels = slabs[0].shape
     npoints, _ = rows.shape
     length = npoints // groups
     vmem = pl.BlockSpec(memory_space=pltpu.VMEM)
-    picked, chosen = pl.pallas_call(
+    first, picked, chosen = pl.pallas_call(
         ahead_kernel,
-        in_specs=[vmem] * 2,
-        out_specs=[vmem] * 2,
+        in_specs=[pl.BlockSpec(memory_space=pltpu.SMEM)] + [vmem] * 3,
+        out_specs=[vmem] * 3,
         out_shape=[
+            jax.ShapeDtypeStruct((slab_size, channels), jnp.bfloat16),
             jax.ShapeDtypeStruct((npoints, channels), jnp.bfloat16),
-            jax.ShapeDtypeStruct((len(slabs) - 1, npoints, slab_size), jnp.bfloat16),
+            jax.ShapeDtypeStruct((len(slabs), npoints, slab_size), jnp.bfloat16),
         ],
         cost_estimate=pl.CostEstimate(flops=1_000_000, bytes_accessed=3_000, transcendentals=0),
         compiler_params=pltpu.CompilerParams(vmem_limit_bytes=VMEM_LIMIT),
         name="ahead",
-    )(rows, slabs[0])
+    )(place, rows, *firsts)
     return pl.pallas_call(
         far_kernel,
-        in_specs=[pl.BlockSpec(memory_space=pltpu.SMEM)] + [vmem] * (2 + len(slabs)),
+        in_specs=[pl.BlockSpec(memory_space=pltpu.SMEM)] + [vmem] * (3 + len(slabs)),
         out_specs=pl.BlockSpec(memory_space=pl.ANY),
         out_shape=jax.ShapeDtypeStruct((groups, SPLIT, 2, length, slab_size), jnp.bfloat16),
         scratch_shapes=[
@@ -164,7 +174,7 @@
         ),
         compiler_params=pltpu.CompilerParams(vmem_limit_bytes=VMEM_LIMIT),
         name="far",
-    )(place, picked, chosen, *slabs)
+    )(place, picked, chosen, first, *slabs)
 
 
 def pair_kernel(scale, table_ref, near_ref, far_ref, out_ref, held_ref, sums_ref, sems):
@@ -235,10 +245,12 @@
     lo = lax.axis_index("lo")
     mine = lax.dynamic_index_in_dim(orbitals, lo, 0, keepdims=False)
     other = lax.dynamic_index_in_dim(orbitals, 1 - lo, 0, keepdims=False)
+    firsts = [swap(mine, True, 0, (1,))]
     share = make_front(mine, other, points, place)
     share, mine, other = lax.optimization_barrier((share, mine, other))
     shares = [share] + [swap(share, False, x) for x in range(1, slabs)]
-    far = [swap(other if x & 1 else mine, True, x) for x in range(slabs)]
+    firsts.append(swap(mine, True, 0, (0,)))
+    far = [swap(other if x & 1 else mine, True, x) for x in range(1, slabs)]
 
     def send(fields, around):
         fields = fields.reshape((-1,) + fields.shape[-3:])
@@ -250,7 +262,7 @@
     starts = jnp.stack([(place[1] ^ x) * slab_size for x in range(slabs)])
     rows = wanted[:, None] - starts[None, :]
     near_fields, rows = lax.optimization_barrier((near_fields, rows))
-    far_fields = make_far(rows, far, place, groups)
+    far_fields = make_far(rows, firsts, far, place, groups)
     near_fields = send(near_fields, ("quarter", "inner"))
     near_fields, far_fields = lax.optimization_barrier((near_fields, far_fields))
     far_fields = send(far_fields, ("quarter", "inner", "lo"))

time: 56.2 us -> 59.3 us (1.055)
  starting transfers between devices: 16.1 us -> 21.2 us
  waiting for transfers between devices: 29.8 us -> 27.1 us
    ppermute x3 -> x4, starting transfers between devices: 5.46 us -> 9.43 us  [swap(): return lax.ppermute(block, KA + GA, route)]
    ppermute x3 -> x4, waiting for transfers between devices: 4.07 us -> 2.21 us  [swap(): return lax.ppermute(block, KA + GA, route)]
    all_to_all x2, starting transfers between devices: 10.7 us -> 11.8 us  [send(): lax.all_to_all(fields, around, split_axis=0, concat_axis=0, tiled=True)]
    all_to_all x2, waiting for transfers between devices: 25.7 us -> 24.9 us  [send(): lax.all_to_all(fields, around, split_axis=0, concat_axis=0, tiled=True)]
  transfers between devices with their start and end apart: 5 -> 6, of which waited for: 4 -> 3; matrix products, arithmetic and copies ran while one was open for 1% -> 1% of each run, Pallas kernels for 7% -> 9%
where the time goes in v29:
time: 59.3 us; the launch traced here: 58.9 us
  waiting for transfers between devices  27.1 us (46%)
  starting transfers between devices  21.2 us (36%)
  Pallas kernels  8.14 us (14%)
  local copies, waits for them, and re-layouts  1.91 us (3%)
    all_to_all x2, waiting for transfers between devices, send(): lax.all_to_all(fields, around, split_axis=0, concat_axis=0, tiled=True)  24.9 us
    all_to_all x2, starting transfers between devices, send(): lax.all_to_all(fields, around, split_axis=0, concat_axis=0, tiled=True)  11.8 us
    ppermute x4, starting transfers between devices, swap(): return lax.ppermute(block, KA + GA, route)  9.43 us
    pallas_call x1, Pallas kernels, make_pairs(): pl.pallas_call(functools.partial(pair_kernel, 1.0 / math.sqrt(2 * half_k)...  2.83 us
    ppermute x4, waiting for transfers between devices, swap(): return lax.ppermute(block, KA + GA, route)  2.21 us
    pallas_call x1, Pallas kernels, make_far(): pl.pallas_call(far_kernel, in_specs=[pl.BlockSpec(memory_space=pltpu.SMEM...  2.06 us
    pallas_call x1, Pallas kernels, make_near(): pl.pallas_call(near_kernel, grid=(kdevice,), in_specs=[pl.BlockSpec((1, s...  1.54 us
  transfers between devices with their start and end apart: 6, of which 3 were waited for; matrix products, arithmetic and copies ran while one was open for 1% of the time, Pallas kernels for 9%

profile of v29, /device:TPU:1, one launch (start us, length us, event | category | flops | bytes accessed | tf_op | source)
XLA Modules:
  0.0 58.9 jit_solution(6086950198107096910)
XLA Ops:
  0.0 0.0 copy-start.1
  0.0 1.1 %dynamic-slice_bitcast_fusion = (bf16[512,256]{1,0:T(8,128)(2,1)S(1)}, bf16[512,256]{1,0:T(8,128)(2,1)S(1)}) fusion(bf16[2,512,256]{2,1,0:T(8,128)(2,1)} %orbitals_ref.1, s32[]{:T(128)S(6)} %select_n.43, s32[]{:T(128)S(6)} %select_n.42), kind=kLoop, calls=%fused_computation | loop fusion | bytes 1048584 | tf_op jit(solution)/shard_map/jit(dynamic_index_in_dim)/squeeze | solution.py:247
  1.1 0.0 copy-start
  1.1 1.4 %collective-permute-start.1 = (bf16[512,256]{1,0:T(8,128)(2,1)S(1)}, bf16[512,256]{1,0:T(8,128)(2,1)S(1)}, u32[]{:S(2)}, u32[]{:S(2)}) collective-permute-start(bf16[512,256]{1,0:T(8,128)(2,1)S(1)} %get-tuple-element.18.mine_ref), channel_id=1, source_target_pairs={{16,8},{17,9},{18,10},{19,11},{20,12},{21,13},{22,14},{23,15},{24,... | collective-permute-start | bytes 786440 | tf_op jit(solution)/shard_map/ppermute | solution.py:28
  2.5 0.1 pad_add_fusion.2.place_ref
  2.6 0.0 copy-done.1
  2.6 0.9 %front.1.refs_0_ = bf16[2,256,256]{2,1,0:T(8,128)(2,1)S(1)} custom-call(s32[2]{0:T(128)S(1)} %pad_add_fusion.2.place_ref, s32[1,512]{1,0:T(1,128)S(1)} %bitcast.12, bf16[512,256]{1,0:T(8,128)(2,1)S(1)} %get-tuple-element.18.mine_ref, bf16[512,256]{1,0:T(8,128)(2,1)S(1)} %get-tuple-element.22.other_ref), custom_call_target="tpu_custom_call" | custom-call | tf_op jit(solution)/shard_map/front/pallas_call | solution.py:67
  3.5 2.1 %collective-permute-start = (bf16[2,256,256]{2,1,0:T(8,128)(2,1)S(1)}, bf16[2,256,256]{2,1,0:T(8,128)(2,1)S(1)}, u32[]{:S(2)}, u32[]{:S(2)}) collective-permute-start(bf16[2,256,256]{2,1,0:T(8,128)(2,1)S(1)} %front.1.refs_0_), channel_id=1, source_target_pairs={{0,1},{1,0},{2,3},{3,2},{4,5},{5,4},{6,7},{7,6},{8,9},{9,8},{10,11... | collective-permute-start | bytes 786440 | tf_op jit(solution)/shard_map/ppermute | solution.py:28
  5.6 5.8 %collective-permute-start.2 = (bf16[512,256]{1,0:T(8,128)(2,1)S(1)}, bf16[512,256]{1,0:T(8,128)(2,1)S(1)}, u32[]{:S(2)}, u32[]{:S(2)}) collective-permute-start(bf16[512,256]{1,0:T(8,128)(2,1)S(1)} %get-tuple-element.18.mine_ref), channel_id=1, source_target_pairs={{0,24},{1,25},{2,26},{3,27},{4,28},{5,29},{6,30},{7,31},{8,16},{9,... | collective-permute-start | bytes 786440 | tf_op jit(solution)/shard_map/ppermute | solution.py:28
  11.4 0.1 collective-permute-start.3
  11.5 0.1 pad_add_fusion.3
  11.6 0.1 dynamic_slice.17
  11.7 0.1 broadcast_subtract_fusion.rows_ref
  11.8 0.0 collective-permute-done.refs_1_
  11.8 0.0 copy-done
  11.8 1.5 %near.1 = bf16[8,2,2,32,512]{4,3,2,1,0:T(8,128)(2,1)} custom-call(bf16[2,512,256]{2,1,0:T(8,128)(2,1)S(1)} %copy-done, bf16[2,256,256]{2,1,0:T(8,128)(2,1)S(1)} %front.1.refs_0_, bf16[2,256,256]{2,1,0:T(8,128)(2,1)S(1)} %collective-permute-done.refs_1_), custom_call_target="tpu_custom_call" | custom-call | flops 1000000000 | bytes 3000000 | tf_op jit(solution)/shard_map/near/pallas_call | solution.py:91
  13.3 5.1 %all-to-all-start = ((bf16[16,2,32,512]{3,2,1,0:T(8,128)(2,1)}), bf16[16,2,32,512]{3,2,1,0:T(8,128)(2,1)S(1)}, u32[]{:S(2)}, u32[]{:S(2)}) async-start(bf16[16,2,32,512]{3,2,1,0:T(8,128)(2,1)} %bitcast.7), calls=%async_computation | async-start | bytes 2097152 | tf_op jit(solution)/shard_map/all_to_all | solution.py:257
  18.4 0.0 collective-permute-done.2.refs_1_
  18.4 0.0 collective-permute-done.1.refs_0_
  18.4 0.8 %ahead.1 = (bf16[512,256]{1,0:T(8,128)(2,1)S(1)}, bf16[256,256]{1,0:T(8,128)(2,1)S(1)}, bf16[1,256,512]{2,1,0:T(8,128)(2,1)S(1)}) custom-call(s32[2]{0:T(128)S(1)} %pad_add_fusion.2.place_ref, s32[256,2]{1,0:T(8,128)S(1)} %broadcast_subtract_fusion.rows_ref, bf16[512,256]{1,0:T(8,128)(2,1)S(1)} %collective-permute-done.1.refs_0_, ...), custom_call_target="tpu_custom_call" | custom-call | flops 1000000 | bytes 3000 | tf_op jit(solution)/shard_map/ahead/pallas_call | solution.py:150
  19.3 2.2 %collective-permute-done.3.refs_1_ = bf16[512,256]{1,0:T(8,128)(2,1)S(1)} collective-permute-done((bf16[512,256]{1,0:T(8,128)(2,1)S(1)}, bf16[512,256]{1,0:T(8,128)(2,1)S(1)}, u32[]{:S(2)}, u32[]{:S(2)}) %collective-permute-start.3) | collective-permute-done | bytes 262176 | tf_op jit(solution)/shard_map/ppermute | solution.py:28
  21.5 2.1 %far.1 = bf16[8,2,2,32,512]{4,3,2,1,0:T(8,128)(2,1)} custom-call(s32[2]{0:T(128)S(1)} %pad_add_fusion.2.place_ref, bf16[256,256]{1,0:T(8,128)(2,1)S(1)} %get-tuple-element.19.picked_ref, bf16[1,256,512]{2,1,0:T(8,128)(2,1)S(1)} %get-tuple-element.20.chosen_ref, bf16[512,256]{1,0:T(8,128)(2,1)S(1)} %get-tuple-element.21.refs_0_, ...), custom_call_target="tpu_custom_call" | custom-call | flops 60000002048 | bytes 180000000 | tf_op jit(solution)/shard_map/far/pallas_call | solution.py:163
  23.5 9.3 %all-to-all-done.near_ref = bf16[16,2,32,512]{3,2,1,0:T(8,128)(2,1)S(1)} async-done(((bf16[16,2,32,512]{3,2,1,0:T(8,128)(2,1)}), bf16[16,2,32,512]{3,2,1,0:T(8,128)(2,1)S(1)}, u32[]{:S(2)}, u32[]{:S(2)}) %all-to-all-start) | async-done | bytes 1048608 | tf_op jit(solution)/shard_map/all_to_all | solution.py:257
  32.8 6.7 %all-to-all-start.1 = ((bf16[16,2,32,512]{3,2,1,0:T(8,128)(2,1)}), bf16[16,2,32,512]{3,2,1,0:T(8,128)(2,1)S(1)}, u32[]{:S(2)}, u32[]{:S(2)}) async-start(bf16[16,2,32,512]{3,2,1,0:T(8,128)(2,1)} %bitcast.8), calls=%async_computation.1 | async-start | bytes 2097152 | tf_op jit(solution)/shard_map/all_to_all | solution.py:257
  39.6 0.0 copy-start.2
  39.6 0.7 %copy-done.2 = s32[2,32]{1,0:T(2,128)S(1)} copy-done((s32[2,32]{1,0:T(2,128)S(1)}, s32[2,32]{1,0:T(2,128)}, u32[]{:S(2)}) %copy-start.2) | copy-done | bytes 280
  40.2 0.1 pad_add_fusion
  40.3 0.1 compare_select_fusion
  40.4 0.1 fusion.3
  40.5 0.1 pad_add_fusion.1.table_ref
  40.6 15.5 %all-to-all-done.1.far_ref = bf16[16,2,32,512]{3,2,1,0:T(8,128)(2,1)S(1)} async-done(((bf16[16,2,32,512]{3,2,1,0:T(8,128)(2,1)}), bf16[16,2,32,512]{3,2,1,0:T(8,128)(2,1)S(1)}, u32[]{:S(2)}, u32[]{:S(2)}) %all-to-all-start.1) | async-done | bytes 1048608 | tf_op jit(solution)/shard_map/all_to_all | solution.py:257
  56.1 2.8 %pairs.1 = f32[32,2,2,512]{3,2,1,0:T(2,128)} custom-call(s32[2,32]{1,0:T(2,128)S(1)} %pad_add_fusion.1.table_ref, bf16[16,2,32,512]{3,2,1,0:T(8,128)(2,1)S(1)} %all-to-all-done.near_ref, bf16[16,2,32,512]{3,2,1,0:T(8,128)(2,1)S(1)} %all-to-all-done.1.far_ref), custom_call_target="tpu_custom_call" | custom-call | tf_op jit(solution)/shard_map/pairs/pallas_call | solution.py:221
Async XLA Ops:
  0.0 2.6 %copy-start.1 = (s32[512]{0:T(512)S(1)}, s32[512]{0:T(512)}, u32[]{:S(2)}) copy-start(s32[512]{0:T(512)} %param.5) | copy-start | bytes 6148
  1.1 10.7 %copy-start = (bf16[2,512,256]{2,1,0:T(8,128)(2,1)S(1)}, bf16[2,512,256]{2,1,0:T(8,128)(2,1)}, u32[]{:S(2)}) copy-start(bf16[2,512,256]{2,1,0:T(8,128)(2,1)} %orbitals_ref.1) | copy-start | bytes 1572868
  1.1 17.3 %collective-permute-start.1 = (bf16[512,256]{1,0:T(8,128)(2,1)S(1)}, bf16[512,256]{1,0:T(8,128)(2,1)S(1)}, u32[]{:S(2)}, u32[]{:S(2)}) collective-permute-start(bf16[512,256]{1,0:T(8,128)(2,1)S(1)} %get-tuple-element.18.mine_ref), channel_id=1, source_target_pairs={{16,8},{17,9},{18,10},{19,11},{20,12},{21,13},{22,14},{23,15},{24,... | collective-permute-start | bytes 786440 | tf_op jit(solution)/shard_map/ppermute | solution.py:28
  3.5 8.3 %collective-permute-start = (bf16[2,256,256]{2,1,0:T(8,128)(2,1)S(1)}, bf16[2,256,256]{2,1,0:T(8,128)(2,1)S(1)}, u32[]{:S(2)}, u32[]{:S(2)}) collective-permute-start(bf16[2,256,256]{2,1,0:T(8,128)(2,1)S(1)} %front.1.refs_0_), channel_id=1, source_target_pairs={{0,1},{1,0},{2,3},{3,2},{4,5},{5,4},{6,7},{7,6},{8,9},{9,8},{10,11... | collective-permute-start | bytes 786440 | tf_op jit(solution)/shard_map/ppermute | solution.py:28
  5.6 12.8 %collective-permute-start.2 = (bf16[512,256]{1,0:T(8,128)(2,1)S(1)}, bf16[512,256]{1,0:T(8,128)(2,1)S(1)}, u32[]{:S(2)}, u32[]{:S(2)}) collective-permute-start(bf16[512,256]{1,0:T(8,128)(2,1)S(1)} %get-tuple-element.18.mine_ref), channel_id=1, source_target_pairs={{0,24},{1,25},{2,26},{3,27},{4,28},{5,29},{6,30},{7,31},{8,16},{9,... | collective-permute-start | bytes 786440 | tf_op jit(solution)/shard_map/ppermute | solution.py:28
  11.4 10.0 %collective-permute-start.3 = (bf16[512,256]{1,0:T(8,128)(2,1)S(1)}, bf16[512,256]{1,0:T(8,128)(2,1)S(1)}, u32[]{:S(2)}, u32[]{:S(2)}) collective-permute-start(bf16[512,256]{1,0:T(8,128)(2,1)S(1)} %get-tuple-element.22.other_ref), channel_id=1, source_target_pairs={{0,25},{1,24},{2,27},{3,26},{4,29},{5,28},{6,31},{7,30},{8,17},{9,... | collective-permute-start | bytes 786440 | tf_op jit(solution)/shard_map/ppermute | solution.py:28
  13.3 19.5 %all-to-all-start = ((bf16[16,2,32,512]{3,2,1,0:T(8,128)(2,1)}), bf16[16,2,32,512]{3,2,1,0:T(8,128)(2,1)S(1)}, u32[]{:S(2)}, u32[]{:S(2)}) async-start(bf16[16,2,32,512]{3,2,1,0:T(8,128)(2,1)} %bitcast.7), calls=%async_computation | async-start | bytes 2097152 | tf_op jit(solution)/shard_map/all_to_all | solution.py:257
  32.8 23.3 %all-to-all-start.1 = ((bf16[16,2,32,512]{3,2,1,0:T(8,128)(2,1)}), bf16[16,2,32,512]{3,2,1,0:T(8,128)(2,1)S(1)}, u32[]{:S(2)}, u32[]{:S(2)}) async-start(bf16[16,2,32,512]{3,2,1,0:T(8,128)(2,1)} %bitcast.8), calls=%async_computation.1 | async-start | bytes 2097152 | tf_op jit(solution)/shard_map/all_to_all | solution.py:257
  39.6 0.7 %copy-start.2 = (s32[2,32]{1,0:T(2,128)S(1)}, s32[2,32]{1,0:T(2,128)}, u32[]{:S(2)}) copy-start(s32[2,32]{1,0:T(2,128)} %param.4) | copy-start | bytes 772

commit v30 on v28

--- a/solution.py
+++ b/solution.py
@@ -39,6 +39,11 @@
     )
 
 
+def crossed(member, groups):
+    quarter, inner = divmod(member, groups // 2)
+    return inner * 2 + quarter
+
+
 def rotate(picked):
     middle = picked.shape[1] // 2
     return jnp.concatenate([-picked[:, middle:], picked[:, :middle]], axis=1)
@@ -79,7 +84,9 @@
     groups = out_ref.shape[0]
     rows = sum(picked_ref[0].astype(jnp.float32) for picked_ref in picked_refs)
     for part, turned in enumerate((rows, rotate(rows))):
-        out_ref[:, 0, part] = product(turned.astype(jnp.bfloat16), orbitals_ref[0], groups)
+        pieces = product(turned.astype(jnp.bfloat16), orbitals_ref[0], groups)
+        for member in range(groups):
+            out_ref[crossed(member, groups), 0, part] = pieces[member]
 
 
 def make_near(orbitals, shares, groups):
@@ -116,7 +123,7 @@
 
 def far_kernel(place_ref, picked_ref, chosen_ref, *refs):
     *slab_refs, out_ref, parts_ref, sems = refs
-    groups, _, _, length, slab_size = out_ref.shape
+    _, groups, _, length, slab_size = out_ref.shape
     picked = picked_ref[...].astype(jnp.float32)
     for number, slab_ref in enumerate(slab_refs[1:]):
         picked += jnp.dot(chosen_ref[number], slab_ref[...], preferred_element_type=jnp.float32)
@@ -126,7 +133,7 @@
         for part in range(2):
             place = len(copies)
             parts_ref[place] = product(turned[part], slab_refs[number][...], groups)
-            target = out_ref.at[:, place_ref[1] % SPLIT ^ number, part]
+            target = out_ref.at[place_ref[1] % SPLIT ^ number, :, part]
             copies.append(pltpu.make_async_copy(parts_ref.at[place], target, sems.at[place]))
             copies[-1].start()
     for copy in copies:
@@ -154,7 +161,7 @@
         far_kernel,
         in_specs=[pl.BlockSpec(memory_space=pltpu.SMEM)] + [vmem] * (2 + len(slabs)),
         out_specs=pl.BlockSpec(memory_space=pl.ANY),
-        out_shape=jax.ShapeDtypeStruct((groups, SPLIT, 2, length, slab_size), jnp.bfloat16),
+        out_shape=jax.ShapeDtypeStruct((SPLIT, groups, 2, length, slab_size), jnp.bfloat16),
         scratch_shapes=[
             pltpu.VMEM((2 * SPLIT, groups, length, slab_size), jnp.bfloat16),
             pltpu.SemaphoreType.DMA((2 * SPLIT,)),
@@ -170,8 +177,13 @@
 def pair_kernel(scale, table_ref, near_ref, far_ref, out_ref, held_ref, sums_ref, sems):
     total_k, _, length, width = held_ref.shape
     transfers = table_ref.shape[0]
-    held_ref[: total_k // 2] = near_ref[...].astype(jnp.float32)
-    held_ref[total_k // 2 :] = far_ref[...].astype(jnp.float32)
+    groups = near_ref.shape[0] // SPLIT
+    for member in range(groups):
+        place = crossed(member, groups) * SPLIT
+        for k in range(SPLIT):
+            held_ref[member * SPLIT + k] = near_ref[place + k].astype(jnp.float32)
+            far = far_ref[k * groups + member]
+            held_ref[total_k // 2 + member * SPLIT + k] = far.astype(jnp.float32)
 
     count, columns = min(16, length), min(256, width)
     copies = []
@@ -251,9 +263,9 @@
     rows = wanted[:, None] - starts[None, :]
     near_fields, rows = lax.optimization_barrier((near_fields, rows))
     far_fields = make_far(rows, far, place, groups)
-    near_fields = send(near_fields, ("quarter", "inner"))
+    near_fields = send(near_fields, ("inner", "quarter"))
     near_fields, far_fields = lax.optimization_barrier((near_fields, far_fields))
-    far_fields = send(far_fields, ("quarter", "inner", "lo"))
+    far_fields = send(far_fields, ("lo", "quarter", "inner"))
 
     def mirrored(kpoints):
         return total_k // 2 + (kpoints + total_k // 4) % (total_k // 2)

time: 56.2 us -> 55.9 us (level); the launches traced: 55.9 us -> 54.8 us
  waiting for transfers between devices: 29.8 us -> 28.9 us
    all_to_all x2, waiting for transfers between devices: 25.7 us -> 24.8 us  [send(): lax.all_to_all(fields, around, split_axis=0, concat_axis=0, tiled=True)]
where the time goes in v30:
time: 55.9 us; the launch traced here: 54.8 us
  waiting for transfers between devices  28.9 us (52%)
  starting transfers between devices  15.9 us (28%)
  Pallas kernels  7.59 us (14%)
  local copies, waits for them, and re-layouts  1.91 us (3%)
    all_to_all x2, waiting for transfers between devices, send(): lax.all_to_all(fields, around, split_axis=0, concat_axis=0, tiled=True)  24.8 us
    all_to_all x2, starting transfers between devices, send(): lax.all_to_all(fields, around, split_axis=0, concat_axis=0, tiled=True)  10.4 us
    ppermute x3, starting transfers between devices, swap(): return lax.ppermute(block, KA + GA, route)  5.46 us
    ppermute x3, waiting for transfers between devices, swap(): return lax.ppermute(block, KA + GA, route)  4.07 us
    pallas_call x1, Pallas kernels, make_pairs(): pl.pallas_call(functools.partial(pair_kernel, 1.0 / math.sqrt(2 * half_k)...  2.83 us
    pallas_call x1, Pallas kernels, make_far(): pl.pallas_call(far_kernel, in_specs=[pl.BlockSpec(memory_space=pltpu.SMEM...  2.09 us
    pallas_call x1, Pallas kernels, make_near(): pl.pallas_call(near_kernel, grid=(kdevice,), in_specs=[pl.BlockSpec((1, s...  1.53 us
  transfers between devices with their start and end apart: 5, of which 4 were waited for; matrix products, arithmetic and copies ran while one was open for 1% of the time, Pallas kernels for 7%

profile of v30, /device:TPU:1, one launch (start us, length us, event | category | flops | bytes accessed | tf_op | source)
XLA Modules:
  0.0 54.8 jit_solution(12716391376741124737)
XLA Ops:
  0.0 0.1 pad_add_fusion.2.place_ref
  0.1 0.0 copy-start.1
  0.1 1.1 %dynamic-slice_bitcast_fusion = (bf16[512,256]{1,0:T(8,128)(2,1)S(1)}, bf16[512,256]{1,0:T(8,128)(2,1)S(1)}) fusion(bf16[2,512,256]{2,1,0:T(8,128)(2,1)} %orbitals_ref.1, s32[]{:T(128)S(6)} %select_n.43, s32[]{:T(128)S(6)} %select_n.42), kind=kLoop, calls=%fused_computation | loop fusion | bytes 1048584 | tf_op jit(solution)/shard_map/jit(dynamic_index_in_dim)/squeeze | solution.py:249
  1.2 0.0 copy-start
  1.2 0.0 copy-done.1
  1.2 0.9 %front.1.refs_0_ = bf16[2,256,256]{2,1,0:T(8,128)(2,1)S(1)} custom-call(s32[2]{0:T(128)S(1)} %pad_add_fusion.2.place_ref, s32[1,512]{1,0:T(1,128)S(1)} %bitcast.12, bf16[512,256]{1,0:T(8,128)(2,1)S(1)} %get-tuple-element.17.mine_ref, bf16[512,256]{1,0:T(8,128)(2,1)S(1)} %get-tuple-element.20.other_ref), custom_call_target="tpu_custom_call" | custom-call | tf_op jit(solution)/shard_map/front/pallas_call | solution.py:70
  2.1 2.1 %collective-permute-start = (bf16[2,256,256]{2,1,0:T(8,128)(2,1)S(1)}, bf16[2,256,256]{2,1,0:T(8,128)(2,1)S(1)}, u32[]{:S(2)}, u32[]{:S(2)}) collective-permute-start(bf16[2,256,256]{2,1,0:T(8,128)(2,1)S(1)} %front.1.refs_0_), channel_id=1, source_target_pairs={{0,1},{1,0},{2,3},{3,2},{4,5},{5,4},{6,7},{7,6},{8,9},{9,8},{10,11... | collective-permute-start | bytes 786440 | tf_op jit(solution)/shard_map/ppermute | solution.py:26
  4.2 3.3 %collective-permute-start.1 = (bf16[512,256]{1,0:T(8,128)(2,1)S(1)}, bf16[512,256]{1,0:T(8,128)(2,1)S(1)}, u32[]{:S(2)}, u32[]{:S(2)}) collective-permute-start(bf16[512,256]{1,0:T(8,128)(2,1)S(1)} %get-tuple-element.17.mine_ref), channel_id=1, source_target_pairs={{0,24},{1,25},{2,26},{3,27},{4,28},{5,29},{6,30},{7,31},{8,16},{9,... | collective-permute-start | bytes 786440 | tf_op jit(solution)/shard_map/ppermute | solution.py:26
  7.5 0.0 collective-permute-start.2
  7.5 0.1 pad_add_fusion.3
  7.6 0.1 dynamic_slice.17
  7.7 0.1 broadcast_subtract_fusion.rows_ref
  7.8 2.5 %collective-permute-done.refs_1_ = bf16[2,256,256]{2,1,0:T(8,128)(2,1)S(1)} collective-permute-done((bf16[2,256,256]{2,1,0:T(8,128)(2,1)S(1)}, bf16[2,256,256]{2,1,0:T(8,128)(2,1)S(1)}, u32[]{:S(2)}, u32[]{:S(2)}) %collective-permute-start) | collective-permute-done | bytes 262176 | tf_op jit(solution)/shard_map/ppermute | solution.py:26
  10.2 0.0 copy-done
  10.2 1.5 %near.1 = bf16[8,2,2,32,512]{4,3,2,1,0:T(8,128)(2,1)} custom-call(bf16[2,512,256]{2,1,0:T(8,128)(2,1)S(1)} %copy-done, bf16[2,256,256]{2,1,0:T(8,128)(2,1)S(1)} %front.1.refs_0_, bf16[2,256,256]{2,1,0:T(8,128)(2,1)S(1)} %collective-permute-done.refs_1_), custom_call_target="tpu_custom_call" | custom-call | flops 1000000000 | bytes 3000000 | tf_op jit(solution)/shard_map/near/pallas_call | solution.py:96
  11.8 5.2 %all-to-all-start = ((bf16[16,2,32,512]{3,2,1,0:T(8,128)(2,1)}), bf16[16,2,32,512]{3,2,1,0:T(8,128)(2,1)S(1)}, u32[]{:S(2)}, u32[]{:S(2)}) async-start(bf16[16,2,32,512]{3,2,1,0:T(8,128)(2,1)} %bitcast.7), calls=%async_computation | async-start | bytes 2097152 | tf_op jit(solution)/shard_map/all_to_all | solution.py:257
  17.0 0.0 collective-permute-done.1.slab_ref.refs_0_
  17.0 0.3 ahead.1
  17.3 1.6 %collective-permute-done.2.refs_1_ = bf16[512,256]{1,0:T(8,128)(2,1)S(1)} collective-permute-done((bf16[512,256]{1,0:T(8,128)(2,1)S(1)}, bf16[512,256]{1,0:T(8,128)(2,1)S(1)}, u32[]{:S(2)}, u32[]{:S(2)}) %collective-permute-start.2) | collective-permute-done | bytes 262176 | tf_op jit(solution)/shard_map/ppermute | solution.py:26
  18.9 2.1 %far.1 = bf16[2,8,2,32,512]{4,3,2,1,0:T(8,128)(2,1)} custom-call(s32[2]{0:T(128)S(1)} %pad_add_fusion.2.place_ref, bf16[256,256]{1,0:T(8,128)(2,1)S(1)} %get-tuple-element.18.picked_ref, bf16[1,256,512]{2,1,0:T(8,128)(2,1)S(1)} %get-tuple-element.19.chosen_ref, bf16[512,256]{1,0:T(8,128)(2,1)S(1)} %collective-permute-done.1.slab_ref.refs_0_, ...), custom_call_target="tpu_custom_call" | custom-call | flops 60000002048 | bytes 180000000 | tf_op jit(solution)/shard_map/far/pallas_call | solution.py:160
  21.0 10.4 %all-to-all-done.near_ref = bf16[16,2,32,512]{3,2,1,0:T(8,128)(2,1)S(1)} async-done(((bf16[16,2,32,512]{3,2,1,0:T(8,128)(2,1)}), bf16[16,2,32,512]{3,2,1,0:T(8,128)(2,1)S(1)}, u32[]{:S(2)}, u32[]{:S(2)}) %all-to-all-start) | async-done | bytes 1048608 | tf_op jit(solution)/shard_map/all_to_all | solution.py:257
  31.4 5.2 %all-to-all-start.1 = ((bf16[16,2,32,512]{3,2,1,0:T(8,128)(2,1)}), bf16[16,2,32,512]{3,2,1,0:T(8,128)(2,1)S(1)}, u32[]{:S(2)}, u32[]{:S(2)}) async-start(bf16[16,2,32,512]{3,2,1,0:T(8,128)(2,1)} %bitcast.8), calls=%async_computation.1 | async-start | bytes 2097152 | tf_op jit(solution)/shard_map/all_to_all | solution.py:257
  36.6 0.0 copy-start.2
  36.6 0.7 %copy-done.2 = s32[2,32]{1,0:T(2,128)S(1)} copy-done((s32[2,32]{1,0:T(2,128)S(1)}, s32[2,32]{1,0:T(2,128)}, u32[]{:S(2)}) %copy-start.2) | copy-done | bytes 280
  37.2 0.1 pad_add_fusion
  37.3 0.1 compare_select_fusion
  37.4 0.1 fusion.3
  37.5 0.1 pad_add_fusion.1.table_ref
  37.6 14.4 %all-to-all-done.1.far_ref = bf16[16,2,32,512]{3,2,1,0:T(8,128)(2,1)S(1)} async-done(((bf16[16,2,32,512]{3,2,1,0:T(8,128)(2,1)}), bf16[16,2,32,512]{3,2,1,0:T(8,128)(2,1)S(1)}, u32[]{:S(2)}, u32[]{:S(2)}) %all-to-all-start.1) | async-done | bytes 1048608 | tf_op jit(solution)/shard_map/all_to_all | solution.py:257
  52.0 2.8 %pairs.1 = f32[32,2,2,512]{3,2,1,0:T(2,128)} custom-call(s32[2,32]{1,0:T(2,128)S(1)} %pad_add_fusion.1.table_ref, bf16[16,2,32,512]{3,2,1,0:T(8,128)(2,1)S(1)} %all-to-all-done.near_ref, bf16[16,2,32,512]{3,2,1,0:T(8,128)(2,1)S(1)} %all-to-all-done.1.far_ref), custom_call_target="tpu_custom_call" | custom-call | tf_op jit(solution)/shard_map/pairs/pallas_call | solution.py:223
Async XLA Ops:
  0.1 1.1 %copy-start.1 = (s32[512]{0:T(512)S(1)}, s32[512]{0:T(512)}, u32[]{:S(2)}) copy-start(s32[512]{0:T(512)} %param.5) | copy-start | bytes 6148
  1.2 9.1 %copy-start = (bf16[2,512,256]{2,1,0:T(8,128)(2,1)S(1)}, bf16[2,512,256]{2,1,0:T(8,128)(2,1)}, u32[]{:S(2)}) copy-start(bf16[2,512,256]{2,1,0:T(8,128)(2,1)} %orbitals_ref.1) | copy-start | bytes 1572868
  2.1 8.2 %collective-permute-start = (bf16[2,256,256]{2,1,0:T(8,128)(2,1)S(1)}, bf16[2,256,256]{2,1,0:T(8,128)(2,1)S(1)}, u32[]{:S(2)}, u32[]{:S(2)}) collective-permute-start(bf16[2,256,256]{2,1,0:T(8,128)(2,1)S(1)} %front.1.refs_0_), channel_id=1, source_target_pairs={{0,1},{1,0},{2,3},{3,2},{4,5},{5,4},{6,7},{7,6},{8,9},{9,8},{10,11... | collective-permute-start | bytes 786440 | tf_op jit(solution)/shard_map/ppermute | solution.py:26
  4.2 12.8 %collective-permute-start.1 = (bf16[512,256]{1,0:T(8,128)(2,1)S(1)}, bf16[512,256]{1,0:T(8,128)(2,1)S(1)}, u32[]{:S(2)}, u32[]{:S(2)}) collective-permute-start(bf16[512,256]{1,0:T(8,128)(2,1)S(1)} %get-tuple-element.17.mine_ref), channel_id=1, source_target_pairs={{0,24},{1,25},{2,26},{3,27},{4,28},{5,29},{6,30},{7,31},{8,16},{9,... | collective-permute-start | bytes 786440 | tf_op jit(solution)/shard_map/ppermute | solution.py:26
  7.5 11.4 %collective-permute-start.2 = (bf16[512,256]{1,0:T(8,128)(2,1)S(1)}, bf16[512,256]{1,0:T(8,128)(2,1)S(1)}, u32[]{:S(2)}, u32[]{:S(2)}) collective-permute-start(bf16[512,256]{1,0:T(8,128)(2,1)S(1)} %get-tuple-element.20.other_ref), channel_id=1, source_target_pairs={{0,25},{1,24},{2,27},{3,26},{4,29},{5,28},{6,31},{7,30},{8,17},{9,... | collective-permute-start | bytes 786440 | tf_op jit(solution)/shard_map/ppermute | solution.py:26
  11.8 19.6 %all-to-all-start = ((bf16[16,2,32,512]{3,2,1,0:T(8,128)(2,1)}), bf16[16,2,32,512]{3,2,1,0:T(8,128)(2,1)S(1)}, u32[]{:S(2)}, u32[]{:S(2)}) async-start(bf16[16,2,32,512]{3,2,1,0:T(8,128)(2,1)} %bitcast.7), calls=%async_computation | async-start | bytes 2097152 | tf_op jit(solution)/shard_map/all_to_all | solution.py:257
  31.4 20.6 %all-to-all-start.1 = ((bf16[16,2,32,512]{3,2,1,0:T(8,128)(2,1)}), bf16[16,2,32,512]{3,2,1,0:T(8,128)(2,1)S(1)}, u32[]{:S(2)}, u32[]{:S(2)}) async-start(bf16[16,2,32,512]{3,2,1,0:T(8,128)(2,1)} %bitcast.8), calls=%async_computation.1 | async-start | bytes 2097152 | tf_op jit(solution)/shard_map/all_to_all | solution.py:257
  36.6 0.7 %copy-start.2 = (s32[2,32]{1,0:T(2,128)S(1)}, s32[2,32]{1,0:T(2,128)}, u32[]{:S(2)}) copy-start(s32[2,32]{1,0:T(2,128)} %param.4) | copy-start | bytes 772

commit v31 on v30

--- a/solution.py
+++ b/solution.py
@@ -44,6 +44,10 @@
     return inner * 2 + quarter
 
 
+def far_place(member, lo, groups):
+    return lo * groups + crossed(member, groups)
+
+
 def rotate(picked):
     middle = picked.shape[1] // 2
     return jnp.concatenate([-picked[:, middle:], picked[:, :middle]], axis=1)
@@ -84,9 +88,7 @@
     groups = out_ref.shape[0]
     rows = sum(picked_ref[0].astype(jnp.float32) for picked_ref in picked_refs)
     for part, turned in enumerate((rows, rotate(rows))):
-        pieces = product(turned.astype(jnp.bfloat16), orbitals_ref[0], groups)
-        for member in range(groups):
-            out_ref[crossed(member, groups), 0, part] = pieces[member]
+        out_ref[:, 0, part] = product(turned.astype(jnp.bfloat16), orbitals_ref[0], groups)
 
 
 def make_near(orbitals, shares, groups):
@@ -132,7 +134,9 @@
     for number in range(SPLIT):
         for part in range(2):
             place = len(copies)
-            parts_ref[place] = product(turned[part], slab_refs[number][...], groups)
+            pieces = product(turned[part], slab_refs[number][...], groups)
+            for member in range(groups):
+                parts_ref[place, crossed(member, groups)] = pieces[member]
             target = out_ref.at[place_ref[1] % SPLIT ^ number, :, part]
             copies.append(pltpu.make_async_copy(parts_ref.at[place], target, sems.at[place]))
             copies[-1].start()
@@ -178,11 +182,10 @@
     total_k, _, length, width = held_ref.shape
     transfers = table_ref.shape[0]
     groups = near_ref.shape[0] // SPLIT
+    held_ref[: total_k // 2] = near_ref[...].astype(jnp.float32)
     for member in range(groups):
-        place = crossed(member, groups) * SPLIT
         for k in range(SPLIT):
-            held_ref[member * SPLIT + k] = near_ref[place + k].astype(jnp.float32)
-            far = far_ref[k * groups + member]
+            far = far_ref[far_place(member, k, groups)]
             held_ref[total_k // 2 + member * SPLIT + k] = far.astype(jnp.float32)
 
     count, columns = min(16, length), min(256, width)
@@ -263,9 +266,9 @@
     rows = wanted[:, None] - starts[None, :]
     near_fields, rows = lax.optimization_barrier((near_fields, rows))
     far_fields = make_far(rows, far, place, groups)
-    near_fields = send(near_fields, ("inner", "quarter"))
+    near_fields = send(near_fields, ("quarter", "inner"))
     near_fields, far_fields = lax.optimization_barrier((near_fields, far_fields))
-    far_fields = send(far_fields, ("lo", "quarter", "inner"))
+    far_fields = send(far_fields, ("lo", "inner", "quarter"))
 
     def mirrored(kpoints):
         return total_k // 2 + (kpoints + total_k // 4) % (total_k // 2)

time: 55.9 us -> 54.7 us (0.979)
  waiting for transfers between devices: 28.9 us -> 27.6 us
    all_to_all x2, waiting for transfers between devices: 24.8 us -> 23.5 us  [send(): lax.all_to_all(fields, around, split_axis=0, concat_axis=0, tiled=True)]
where the time goes in v31:
time: 54.7 us; the launch traced here: 53.8 us
  waiting for transfers between devices  27.6 us (50%)
  starting transfers between devices  16.1 us (29%)
  Pallas kernels  7.59 us (14%)
  local copies, waits for them, and re-layouts  1.91 us (3%)
    all_to_all x2, waiting for transfers between devices, send(): lax.all_to_all(fields, around, split_axis=0, concat_axis=0, tiled=True)  23.5 us
    all_to_all x2, starting transfers between devices, send(): lax.all_to_all(fields, around, split_axis=0, concat_axis=0, tiled=True)  10.7 us
    ppermute x3, starting transfers between devices, swap(): return lax.ppermute(block, KA + GA, route)  5.46 us
    ppermute x3, waiting for transfers between devices, swap(): return lax.ppermute(block, KA + GA, route)  4.07 us
    pallas_call x1, Pallas kernels, make_pairs(): pl.pallas_call(functools.partial(pair_kernel, 1.0 / math.sqrt(2 * half_k)...  2.83 us
    pallas_call x1, Pallas kernels, make_far(): pl.pallas_call(far_kernel, in_specs=[pl.BlockSpec(memory_space=pltpu.SMEM...  2.09 us
    pallas_call x1, Pallas kernels, make_near(): pl.pallas_call(near_kernel, grid=(kdevice,), in_specs=[pl.BlockSpec((1, s...  1.53 us
  transfers between devices with their start and end apart: 5, of which 4 were waited for; matrix products, arithmetic and copies ran while one was open for 1% of the time, Pallas kernels for 7%

profile of v31, /device:TPU:1, one launch (start us, length us, event | category | flops | bytes accessed | tf_op | source)
XLA Modules:
  0.0 53.8 jit_solution(11305117658257156604)
XLA Ops:
  0.0 0.1 pad_add_fusion.2.place_ref
  0.1 0.0 copy-start.1
  0.1 1.1 %dynamic-slice_bitcast_fusion = (bf16[512,256]{1,0:T(8,128)(2,1)S(1)}, bf16[512,256]{1,0:T(8,128)(2,1)S(1)}) fusion(bf16[2,512,256]{2,1,0:T(8,128)(2,1)} %orbitals_ref.1, s32[]{:T(128)S(6)} %select_n.43, s32[]{:T(128)S(6)} %select_n.42), kind=kLoop, calls=%fused_computation | loop fusion | bytes 1048584 | tf_op jit(solution)/shard_map/jit(dynamic_index_in_dim)/squeeze | solution.py:252
  1.2 0.0 copy-start
  1.2 0.0 copy-done.1
  1.2 0.9 %front.1.refs_0_ = bf16[2,256,256]{2,1,0:T(8,128)(2,1)S(1)} custom-call(s32[2]{0:T(128)S(1)} %pad_add_fusion.2.place_ref, s32[1,512]{1,0:T(1,128)S(1)} %bitcast.12, bf16[512,256]{1,0:T(8,128)(2,1)S(1)} %get-tuple-element.17.mine_ref, bf16[512,256]{1,0:T(8,128)(2,1)S(1)} %get-tuple-element.20.other_ref), custom_call_target="tpu_custom_call" | custom-call | tf_op jit(solution)/shard_map/front/pallas_call | solution.py:74
  2.1 2.1 %collective-permute-start = (bf16[2,256,256]{2,1,0:T(8,128)(2,1)S(1)}, bf16[2,256,256]{2,1,0:T(8,128)(2,1)S(1)}, u32[]{:S(2)}, u32[]{:S(2)}) collective-permute-start(bf16[2,256,256]{2,1,0:T(8,128)(2,1)S(1)} %front.1.refs_0_), channel_id=1, source_target_pairs={{0,1},{1,0},{2,3},{3,2},{4,5},{5,4},{6,7},{7,6},{8,9},{9,8},{10,11... | collective-permute-start | bytes 786440 | tf_op jit(solution)/shard_map/ppermute | solution.py:26
  4.2 3.3 %collective-permute-start.1 = (bf16[512,256]{1,0:T(8,128)(2,1)S(1)}, bf16[512,256]{1,0:T(8,128)(2,1)S(1)}, u32[]{:S(2)}, u32[]{:S(2)}) collective-permute-start(bf16[512,256]{1,0:T(8,128)(2,1)S(1)} %get-tuple-element.17.mine_ref), channel_id=1, source_target_pairs={{0,24},{1,25},{2,26},{3,27},{4,28},{5,29},{6,30},{7,31},{8,16},{9,... | collective-permute-start | bytes 786440 | tf_op jit(solution)/shard_map/ppermute | solution.py:26
  7.5 0.0 collective-permute-start.2
  7.5 0.1 pad_add_fusion.3
  7.6 0.1 dynamic_slice.17
  7.7 0.1 broadcast_subtract_fusion.rows_ref
  7.8 2.5 %collective-permute-done.refs_1_ = bf16[2,256,256]{2,1,0:T(8,128)(2,1)S(1)} collective-permute-done((bf16[2,256,256]{2,1,0:T(8,128)(2,1)S(1)}, bf16[2,256,256]{2,1,0:T(8,128)(2,1)S(1)}, u32[]{:S(2)}, u32[]{:S(2)}) %collective-permute-start) | collective-permute-done | bytes 262176 | tf_op jit(solution)/shard_map/ppermute | solution.py:26
  10.2 0.0 copy-done
  10.2 1.5 %near.1 = bf16[8,2,2,32,512]{4,3,2,1,0:T(8,128)(2,1)} custom-call(bf16[2,512,256]{2,1,0:T(8,128)(2,1)S(1)} %copy-done, bf16[2,256,256]{2,1,0:T(8,128)(2,1)S(1)} %front.1.refs_0_, bf16[2,256,256]{2,1,0:T(8,128)(2,1)S(1)} %collective-permute-done.refs_1_), custom_call_target="tpu_custom_call" | custom-call | flops 1000000000 | bytes 3000000 | tf_op jit(solution)/shard_map/near/pallas_call | solution.py:98
  11.8 5.2 %all-to-all-start = ((bf16[16,2,32,512]{3,2,1,0:T(8,128)(2,1)}), bf16[16,2,32,512]{3,2,1,0:T(8,128)(2,1)S(1)}, u32[]{:S(2)}, u32[]{:S(2)}) async-start(bf16[16,2,32,512]{3,2,1,0:T(8,128)(2,1)} %bitcast.7), calls=%async_computation | async-start | bytes 2097152 | tf_op jit(solution)/shard_map/all_to_all | solution.py:260
  17.0 0.0 collective-permute-done.1.slab_ref.refs_0_
  17.0 0.3 ahead.1
  17.3 1.6 %collective-permute-done.2.refs_1_ = bf16[512,256]{1,0:T(8,128)(2,1)S(1)} collective-permute-done((bf16[512,256]{1,0:T(8,128)(2,1)S(1)}, bf16[512,256]{1,0:T(8,128)(2,1)S(1)}, u32[]{:S(2)}, u32[]{:S(2)}) %collective-permute-start.2) | collective-permute-done | bytes 262176 | tf_op jit(solution)/shard_map/ppermute | solution.py:26
  18.9 2.1 %far.1 = bf16[2,8,2,32,512]{4,3,2,1,0:T(8,128)(2,1)} custom-call(s32[2]{0:T(128)S(1)} %pad_add_fusion.2.place_ref, bf16[256,256]{1,0:T(8,128)(2,1)S(1)} %get-tuple-element.18.picked_ref, bf16[1,256,512]{2,1,0:T(8,128)(2,1)S(1)} %get-tuple-element.19.chosen_ref, bf16[512,256]{1,0:T(8,128)(2,1)S(1)} %collective-permute-done.1.slab_ref.refs_0_, ...), custom_call_target="tpu_custom_call" | custom-call | flops 60000002048 | bytes 180000000 | tf_op jit(solution)/shard_map/far/pallas_call | solution.py:164
  21.0 10.1 %all-to-all-done.near_ref = bf16[16,2,32,512]{3,2,1,0:T(8,128)(2,1)S(1)} async-done(((bf16[16,2,32,512]{3,2,1,0:T(8,128)(2,1)}), bf16[16,2,32,512]{3,2,1,0:T(8,128)(2,1)S(1)}, u32[]{:S(2)}, u32[]{:S(2)}) %all-to-all-start) | async-done | bytes 1048608 | tf_op jit(solution)/shard_map/all_to_all | solution.py:260
  31.1 5.5 %all-to-all-start.1 = ((bf16[16,2,32,512]{3,2,1,0:T(8,128)(2,1)}), bf16[16,2,32,512]{3,2,1,0:T(8,128)(2,1)S(1)}, u32[]{:S(2)}, u32[]{:S(2)}) async-start(bf16[16,2,32,512]{3,2,1,0:T(8,128)(2,1)} %bitcast.8), calls=%async_computation.1 | async-start | bytes 2097152 | tf_op jit(solution)/shard_map/all_to_all | solution.py:260
  36.6 0.0 copy-start.2
  36.6 0.7 %copy-done.2 = s32[2,32]{1,0:T(2,128)S(1)} copy-done((s32[2,32]{1,0:T(2,128)S(1)}, s32[2,32]{1,0:T(2,128)}, u32[]{:S(2)}) %copy-start.2) | copy-done | bytes 280
  37.2 0.1 pad_add_fusion
  37.3 0.1 compare_select_fusion
  37.4 0.1 fusion.3
  37.5 0.1 pad_add_fusion.1.table_ref
  37.6 13.4 %all-to-all-done.1.far_ref = bf16[16,2,32,512]{3,2,1,0:T(8,128)(2,1)S(1)} async-done(((bf16[16,2,32,512]{3,2,1,0:T(8,128)(2,1)}), bf16[16,2,32,512]{3,2,1,0:T(8,128)(2,1)S(1)}, u32[]{:S(2)}, u32[]{:S(2)}) %all-to-all-start.1) | async-done | bytes 1048608 | tf_op jit(solution)/shard_map/all_to_all | solution.py:260
  50.9 2.8 %pairs.1 = f32[32,2,2,512]{3,2,1,0:T(2,128)} custom-call(s32[2,32]{1,0:T(2,128)S(1)} %pad_add_fusion.1.table_ref, bf16[16,2,32,512]{3,2,1,0:T(8,128)(2,1)S(1)} %all-to-all-done.near_ref, bf16[16,2,32,512]{3,2,1,0:T(8,128)(2,1)S(1)} %all-to-all-done.1.far_ref), custom_call_target="tpu_custom_call" | custom-call | tf_op jit(solution)/shard_map/pairs/pallas_call | solution.py:226
Async XLA Ops:
  0.1 1.1 %copy-start.1 = (s32[512]{0:T(512)S(1)}, s32[512]{0:T(512)}, u32[]{:S(2)}) copy-start(s32[512]{0:T(512)} %param.5) | copy-start | bytes 6148
  1.2 9.1 %copy-start = (bf16[2,512,256]{2,1,0:T(8,128)(2,1)S(1)}, bf16[2,512,256]{2,1,0:T(8,128)(2,1)}, u32[]{:S(2)}) copy-start(bf16[2,512,256]{2,1,0:T(8,128)(2,1)} %orbitals_ref.1) | copy-start | bytes 1572868
  2.1 8.2 %collective-permute-start = (bf16[2,256,256]{2,1,0:T(8,128)(2,1)S(1)}, bf16[2,256,256]{2,1,0:T(8,128)(2,1)S(1)}, u32[]{:S(2)}, u32[]{:S(2)}) collective-permute-start(bf16[2,256,256]{2,1,0:T(8,128)(2,1)S(1)} %front.1.refs_0_), channel_id=1, source_target_pairs={{0,1},{1,0},{2,3},{3,2},{4,5},{5,4},{6,7},{7,6},{8,9},{9,8},{10,11... | collective-permute-start | bytes 786440 | tf_op jit(solution)/shard_map/ppermute | solution.py:26
  4.2 12.8 %collective-permute-start.1 = (bf16[512,256]{1,0:T(8,128)(2,1)S(1)}, bf16[512,256]{1,0:T(8,128)(2,1)S(1)}, u32[]{:S(2)}, u32[]{:S(2)}) collective-permute-start(bf16[512,256]{1,0:T(8,128)(2,1)S(1)} %get-tuple-element.17.mine_ref), channel_id=1, source_target_pairs={{0,24},{1,25},{2,26},{3,27},{4,28},{5,29},{6,30},{7,31},{8,16},{9,... | collective-permute-start | bytes 786440 | tf_op jit(solution)/shard_map/ppermute | solution.py:26
  7.5 11.4 %collective-permute-start.2 = (bf16[512,256]{1,0:T(8,128)(2,1)S(1)}, bf16[512,256]{1,0:T(8,128)(2,1)S(1)}, u32[]{:S(2)}, u32[]{:S(2)}) collective-permute-start(bf16[512,256]{1,0:T(8,128)(2,1)S(1)} %get-tuple-element.20.other_ref), channel_id=1, source_target_pairs={{0,25},{1,24},{2,27},{3,26},{4,29},{5,28},{6,31},{7,30},{8,17},{9,... | collective-permute-start | bytes 786440 | tf_op jit(solution)/shard_map/ppermute | solution.py:26
  11.8 19.4 %all-to-all-start = ((bf16[16,2,32,512]{3,2,1,0:T(8,128)(2,1)}), bf16[16,2,32,512]{3,2,1,0:T(8,128)(2,1)S(1)}, u32[]{:S(2)}, u32[]{:S(2)}) async-start(bf16[16,2,32,512]{3,2,1,0:T(8,128)(2,1)} %bitcast.7), calls=%async_computation | async-start | bytes 2097152 | tf_op jit(solution)/shard_map/all_to_all | solution.py:260
  31.1 19.8 %all-to-all-start.1 = ((bf16[16,2,32,512]{3,2,1,0:T(8,128)(2,1)}), bf16[16,2,32,512]{3,2,1,0:T(8,128)(2,1)S(1)}, u32[]{:S(2)}, u32[]{:S(2)}) async-start(bf16[16,2,32,512]{3,2,1,0:T(8,128)(2,1)} %bitcast.8), calls=%async_computation.1 | async-start | bytes 2097152 | tf_op jit(solution)/shard_map/all_to_all | solution.py:260
  36.6 0.7 %copy-start.2 = (s32[2,32]{1,0:T(2,128)S(1)}, s32[2,32]{1,0:T(2,128)}, u32[]{:S(2)}) copy-start(s32[2,32]{1,0:T(2,128)} %param.4) | copy-start | bytes 772

commit v32 on v30

--- a/solution.py
+++ b/solution.py
@@ -11,11 +11,14 @@
 
 VMEM_LIMIT = 40 * 1024 * 1024
 SPLIT = 2
-KA, GA = ("half", "quarter", "inner"), ("hi", "lo")
+KA, GA = ("half", "quarter", "ring", "core"), ("hi", "lo")
+NEAR_ORDER = ("core", "quarter", "ring")
+FAR_ORDER = ("core", "lo", "ring", "quarter")
 
 
 def swap(block, mirror, other):
-    half, quarter, inner, hi, lo = (lax.axis_size(name) for name in KA + GA)
+    half, quarter, ring, core, hi, lo = (lax.axis_size(name) for name in KA + GA)
+    inner = ring * core
     slabs = hi * lo
     route = []
     for place in range(half * quarter * inner * slabs):
@@ -39,9 +42,17 @@
     )
 
 
-def crossed(member, groups):
-    quarter, inner = divmod(member, groups // 2)
-    return inner * 2 + quarter
+def sizes(groups):
+    return {"quarter": 2, "ring": groups // 4, "core": 2, "lo": SPLIT}
+
+
+def place_of(member, groups, order, lo=0):
+    ring, core = divmod(member % (groups // 2), 2)
+    at = {"quarter": member // (groups // 2), "ring": ring, "core": core, "lo": lo}
+    place = 0
+    for name in order:
+        place = place * sizes(groups)[name] + at[name]
+    return place
 
 
 def rotate(picked):
@@ -86,7 +97,7 @@
     for part, turned in enumerate((rows, rotate(rows))):
         pieces = product(turned.astype(jnp.bfloat16), orbitals_ref[0], groups)
         for member in range(groups):
-            out_ref[crossed(member, groups), 0, part] = pieces[member]
+            out_ref[place_of(member, groups, NEAR_ORDER), 0, part] = pieces[member]
 
 
 def make_near(orbitals, shares, groups):
@@ -123,7 +134,9 @@
 
 def far_kernel(place_ref, picked_ref, chosen_ref, *refs):
     *slab_refs, out_ref, parts_ref, sems = refs
-    _, groups, _, length, slab_size = out_ref.shape
+    slower, _, faster, _, length, slab_size = out_ref.shape
+    groups = slower * faster
+    order = [name for name in FAR_ORDER if name != "lo"]
     picked = picked_ref[...].astype(jnp.float32)
     for number, slab_ref in enumerate(slab_refs[1:]):
         picked += jnp.dot(chosen_ref[number], slab_ref[...], preferred_element_type=jnp.float32)
@@ -132,8 +145,11 @@
     for number in range(SPLIT):
         for part in range(2):
             place = len(copies)
-            parts_ref[place] = product(turned[part], slab_refs[number][...], groups)
-            target = out_ref.at[place_ref[1] % SPLIT ^ number, :, part]
+            pieces = product(turned[part], slab_refs[number][...], groups)
+            for member in range(groups):
+                at = divmod(place_of(member, groups, order), faster)
+                parts_ref[place, at[0], at[1]] = pieces[member]
+            target = out_ref.at[:, place_ref[1] % SPLIT ^ number, :, part]
             copies.append(pltpu.make_async_copy(parts_ref.at[place], target, sems.at[place]))
             copies[-1].start()
     for copy in copies:
@@ -144,6 +160,8 @@
     slab_size, channels = slabs[0].shape
     npoints, _ = rows.shape
     length = npoints // groups
+    faster = math.prod(sizes(groups)[name] for name in FAR_ORDER[FAR_ORDER.index("lo") + 1 :])
+    around = (groups // faster, faster)
     vmem = pl.BlockSpec(memory_space=pltpu.VMEM)
     picked, chosen = pl.pallas_call(
         ahead_kernel,
@@ -161,9 +179,11 @@
         far_kernel,
         in_specs=[pl.BlockSpec(memory_space=pltpu.SMEM)] + [vmem] * (2 + len(slabs)),
         out_specs=pl.BlockSpec(memory_space=pl.ANY),
-        out_shape=jax.ShapeDtypeStruct((SPLIT, groups, 2, length, slab_size), jnp.bfloat16),
+        out_shape=jax.ShapeDtypeStruct(
+            (around[0], SPLIT, around[1], 2, length, slab_size), jnp.bfloat16
+        ),
         scratch_shapes=[
-            pltpu.VMEM((2 * SPLIT, groups, length, slab_size), jnp.bfloat16),
+            pltpu.VMEM((2 * SPLIT,) + around + (length, slab_size), jnp.bfloat16),
             pltpu.SemaphoreType.DMA((2 * SPLIT,)),
         ],
         cost_estimate=pl.CostEstimate(
@@ -179,10 +199,10 @@
     transfers = table_ref.shape[0]
     groups = near_ref.shape[0] // SPLIT
     for member in range(groups):
-        place = crossed(member, groups) * SPLIT
+        place = place_of(member, groups, NEAR_ORDER) * SPLIT
         for k in range(SPLIT):
             held_ref[member * SPLIT + k] = near_ref[place + k].astype(jnp.float32)
-            far = far_ref[k * groups + member]
+            far = far_ref[place_of(member, groups, FAR_ORDER, k)]
             held_ref[total_k // 2 + member * SPLIT + k] = far.astype(jnp.float32)
 
     count, columns = min(16, length), min(256, width)
@@ -238,7 +258,7 @@
 def on_device(orbitals, minus_table, points):
     kdevice, slab_size, channels = orbitals.shape
     half = lax.axis_index("half")
-    groups = lax.axis_size("quarter") * lax.axis_size("inner")
+    groups = lax.axis_size("quarter") * lax.axis_size("ring") * lax.axis_size("core")
     slabs = lax.axis_size("hi") * lax.axis_size("lo")
     total_k = 2 * groups * kdevice
     points = points.reshape(1, -1)
@@ -263,9 +283,9 @@
     rows = wanted[:, None] - starts[None, :]
     near_fields, rows = lax.optimization_barrier((near_fields, rows))
     far_fields = make_far(rows, far, place, groups)
-    near_fields = send(near_fields, ("inner", "quarter"))
+    near_fields = send(near_fields, NEAR_ORDER)
     near_fields, far_fields = lax.optimization_barrier((near_fields, far_fields))
-    far_fields = send(far_fields, ("lo", "quarter", "inner"))
+    far_fields = send(far_fields, FAR_ORDER)
 
     def mirrored(kpoints):
         return total_k // 2 + (kpoints + total_k // 4) % (total_k // 2)
@@ -279,7 +299,7 @@
 
 def solution(mesh):
     kplaces, slabs = mesh.shape["ka"], mesh.shape["ga"]
-    devices = mesh.devices.reshape(2, 2, kplaces // 4, slabs // SPLIT, SPLIT)
+    devices = mesh.devices.reshape(2, 2, kplaces // 8, 2, slabs // SPLIT, SPLIT)
     finer = Mesh(devices, KA + GA)
     return jax.shard_map(
         on_device,

time: 55.9 us -> 55 us (0.984); the launches traced: 54.8 us -> 54.7 us
  transfers between devices with their start and end apart: 5 -> 5, of which waited for: 4 -> 4; matrix products, arithmetic and copies ran while one was open for 1% -> 1% of each run, Pallas kernels for 7% -> 8%
where the time goes in v32:
time: 55 us; the launch traced here: 54.7 us
  waiting for transfers between devices  28.4 us (52%)
  starting transfers between devices  15.7 us (29%)
  Pallas kernels  8.09 us (15%)
  local copies, waits for them, and re-layouts  1.91 us (3%)
    all_to_all x2, waiting for transfers between devices, send(): lax.all_to_all(fields, around, split_axis=0, concat_axis=0, tiled=True)  24.4 us
    all_to_all x2, starting transfers between devices, send(): lax.all_to_all(fields, around, split_axis=0, concat_axis=0, tiled=True)  10.3 us
    ppermute x3, starting transfers between devices, swap(): return lax.ppermute(block, KA + GA, route)  5.46 us
    ppermute x3, waiting for transfers between devices, swap(): return lax.ppermute(block, KA + GA, route)  4.07 us
    pallas_call x1, Pallas kernels, make_pairs(): pl.pallas_call(functools.partial(pair_kernel, 1.0 / math.sqrt(2 * half_k)...  2.83 us
    pallas_call x1, Pallas kernels, make_far(): pl.pallas_call(far_kernel, in_specs=[pl.BlockSpec(memory_space=pltpu.SMEM...  2.6 us
    pallas_call x1, Pallas kernels, make_near(): pl.pallas_call(near_kernel, grid=(kdevice,), in_specs=[pl.BlockSpec((1, s...  1.53 us
  transfers between devices with their start and end apart: 5, of which 4 were waited for; matrix products, arithmetic and copies ran while one was open for 1% of the time, Pallas kernels for 8%

profile of v32, /device:TPU:1, one launch (start us, length us, event | category | flops | bytes accessed | tf_op | source)
XLA Modules:
  0.0 54.7 jit_solution(15034741170572907366)
XLA Ops:
  0.0 0.1 pad_add_fusion.2.place_ref
  0.1 0.0 copy-start.1
  0.1 1.1 %dynamic-slice_bitcast_fusion = (bf16[512,256]{1,0:T(8,128)(2,1)S(1)}, bf16[512,256]{1,0:T(8,128)(2,1)S(1)}) fusion(bf16[2,512,256]{2,1,0:T(8,128)(2,1)} %orbitals_ref.1, s32[]{:T(128)S(6)} %select_n.43, s32[]{:T(128)S(6)} %select_n.42), kind=kLoop, calls=%fused_computation | loop fusion | bytes 1048584 | tf_op jit(solution)/shard_map/jit(dynamic_index_in_dim)/squeeze | solution.py:269
  1.2 0.0 copy-start
  1.2 0.0 copy-done.1
  1.2 0.9 %front.1.refs_0_ = bf16[2,256,256]{2,1,0:T(8,128)(2,1)S(1)} custom-call(s32[2]{0:T(128)S(1)} %pad_add_fusion.2.place_ref, s32[1,512]{1,0:T(1,128)S(1)} %bitcast.12, bf16[512,256]{1,0:T(8,128)(2,1)S(1)} %get-tuple-element.17.mine_ref, bf16[512,256]{1,0:T(8,128)(2,1)S(1)} %get-tuple-element.20.other_ref), custom_call_target="tpu_custom_call" | custom-call | tf_op jit(solution)/shard_map/front/pallas_call | solution.py:81
  2.1 2.1 %collective-permute-start = (bf16[2,256,256]{2,1,0:T(8,128)(2,1)S(1)}, bf16[2,256,256]{2,1,0:T(8,128)(2,1)S(1)}, u32[]{:S(2)}, u32[]{:S(2)}) collective-permute-start(bf16[2,256,256]{2,1,0:T(8,128)(2,1)S(1)} %front.1.refs_0_), channel_id=1, source_target_pairs={{0,1},{1,0},{2,3},{3,2},{4,5},{5,4},{6,7},{7,6},{8,9},{9,8},{10,11... | collective-permute-start | bytes 786440 | tf_op jit(solution)/shard_map/ppermute | solution.py:29
  4.2 3.3 %collective-permute-start.1 = (bf16[512,256]{1,0:T(8,128)(2,1)S(1)}, bf16[512,256]{1,0:T(8,128)(2,1)S(1)}, u32[]{:S(2)}, u32[]{:S(2)}) collective-permute-start(bf16[512,256]{1,0:T(8,128)(2,1)S(1)} %get-tuple-element.17.mine_ref), channel_id=1, source_target_pairs={{0,24},{1,25},{2,26},{3,27},{4,28},{5,29},{6,30},{7,31},{8,16},{9,... | collective-permute-start | bytes 786440 | tf_op jit(solution)/shard_map/ppermute | solution.py:29
  7.5 0.0 collective-permute-start.2
  7.5 0.1 pad_add_fusion.3
  7.6 0.1 dynamic_slice.17
  7.7 0.1 broadcast_subtract_fusion.rows_ref
  7.8 2.5 %collective-permute-done.refs_1_ = bf16[2,256,256]{2,1,0:T(8,128)(2,1)S(1)} collective-permute-done((bf16[2,256,256]{2,1,0:T(8,128)(2,1)S(1)}, bf16[2,256,256]{2,1,0:T(8,128)(2,1)S(1)}, u32[]{:S(2)}, u32[]{:S(2)}) %collective-permute-start) | collective-permute-done | bytes 262176 | tf_op jit(solution)/shard_map/ppermute | solution.py:29
  10.2 0.0 copy-done
  10.2 1.5 %near.1 = bf16[8,2,2,32,512]{4,3,2,1,0:T(8,128)(2,1)} custom-call(bf16[2,512,256]{2,1,0:T(8,128)(2,1)S(1)} %copy-done, bf16[2,256,256]{2,1,0:T(8,128)(2,1)S(1)} %front.1.refs_0_, bf16[2,256,256]{2,1,0:T(8,128)(2,1)S(1)} %collective-permute-done.refs_1_), custom_call_target="tpu_custom_call" | custom-call | flops 1000000000 | bytes 3000000 | tf_op jit(solution)/shard_map/near/pallas_call | solution.py:107
  11.8 5.2 %all-to-all-start = ((bf16[16,2,32,512]{3,2,1,0:T(8,128)(2,1)}), bf16[16,2,32,512]{3,2,1,0:T(8,128)(2,1)S(1)}, u32[]{:S(2)}, u32[]{:S(2)}) async-start(bf16[16,2,32,512]{3,2,1,0:T(8,128)(2,1)} %bitcast.7), calls=%async_computation | async-start | bytes 2097152 | tf_op jit(solution)/shard_map/all_to_all | solution.py:277
  17.0 0.0 collective-permute-done.1.slab_ref.refs_0_
  17.0 0.3 ahead.1
  17.3 1.6 %collective-permute-done.2.refs_1_ = bf16[512,256]{1,0:T(8,128)(2,1)S(1)} collective-permute-done((bf16[512,256]{1,0:T(8,128)(2,1)S(1)}, bf16[512,256]{1,0:T(8,128)(2,1)S(1)}, u32[]{:S(2)}, u32[]{:S(2)}) %collective-permute-start.2) | collective-permute-done | bytes 262176 | tf_op jit(solution)/shard_map/ppermute | solution.py:29
  18.9 2.6 %far.1 = bf16[2,2,4,2,32,512]{5,4,3,2,1,0:T(8,128)(2,1)} custom-call(s32[2]{0:T(128)S(1)} %pad_add_fusion.2.place_ref, bf16[256,256]{1,0:T(8,128)(2,1)S(1)} %get-tuple-element.18.picked_ref, bf16[1,256,512]{2,1,0:T(8,128)(2,1)S(1)} %get-tuple-element.19.chosen_ref, bf16[512,256]{1,0:T(8,128)(2,1)S(1)} %collective-permute-done.1.slab_ref.refs_0_, ...), custom_call_target="tpu_custom_call" | custom-call | flops 60000002048 | bytes 180000000 | tf_op jit(solution)/shard_map/far/pallas_call | solution.py:178
  21.5 10.5 %all-to-all-done.near_ref = bf16[16,2,32,512]{3,2,1,0:T(8,128)(2,1)S(1)} async-done(((bf16[16,2,32,512]{3,2,1,0:T(8,128)(2,1)}), bf16[16,2,32,512]{3,2,1,0:T(8,128)(2,1)S(1)}, u32[]{:S(2)}, u32[]{:S(2)}) %all-to-all-start) | async-done | bytes 1048608 | tf_op jit(solution)/shard_map/all_to_all | solution.py:277
  32.0 5.0 %all-to-all-start.1 = ((bf16[16,2,32,512]{3,2,1,0:T(8,128)(2,1)}), bf16[16,2,32,512]{3,2,1,0:T(8,128)(2,1)S(1)}, u32[]{:S(2)}, u32[]{:S(2)}) async-start(bf16[16,2,32,512]{3,2,1,0:T(8,128)(2,1)} %bitcast.8), calls=%async_computation.1 | async-start | bytes 2097152 | tf_op jit(solution)/shard_map/all_to_all | solution.py:277
  37.1 0.0 copy-start.2
  37.1 0.7 %copy-done.2 = s32[2,32]{1,0:T(2,128)S(1)} copy-done((s32[2,32]{1,0:T(2,128)S(1)}, s32[2,32]{1,0:T(2,128)}, u32[]{:S(2)}) %copy-start.2) | copy-done | bytes 280
  37.7 0.1 pad_add_fusion
  37.8 0.1 compare_select_fusion
  37.9 0.1 fusion.3
  38.0 0.1 pad_add_fusion.1.table_ref
  38.1 13.8 %all-to-all-done.1.far_ref = bf16[16,2,32,512]{3,2,1,0:T(8,128)(2,1)S(1)} async-done(((bf16[16,2,32,512]{3,2,1,0:T(8,128)(2,1)}), bf16[16,2,32,512]{3,2,1,0:T(8,128)(2,1)S(1)}, u32[]{:S(2)}, u32[]{:S(2)}) %all-to-all-start.1) | async-done | bytes 1048608 | tf_op jit(solution)/shard_map/all_to_all | solution.py:277
  51.9 2.8 %pairs.1 = f32[32,2,2,512]{3,2,1,0:T(2,128)} custom-call(s32[2,32]{1,0:T(2,128)S(1)} %pad_add_fusion.1.table_ref, bf16[16,2,32,512]{3,2,1,0:T(8,128)(2,1)S(1)} %all-to-all-done.near_ref, bf16[16,2,32,512]{3,2,1,0:T(8,128)(2,1)S(1)} %all-to-all-done.1.far_ref), custom_call_target="tpu_custom_call" | custom-call | tf_op jit(solution)/shard_map/pairs/pallas_call | solution.py:243
Async XLA Ops:
  0.1 1.1 %copy-start.1 = (s32[512]{0:T(512)S(1)}, s32[512]{0:T(512)}, u32[]{:S(2)}) copy-start(s32[512]{0:T(512)} %param.5) | copy-start | bytes 6148
  1.2 9.1 %copy-start = (bf16[2,512,256]{2,1,0:T(8,128)(2,1)S(1)}, bf16[2,512,256]{2,1,0:T(8,128)(2,1)}, u32[]{:S(2)}) copy-start(bf16[2,512,256]{2,1,0:T(8,128)(2,1)} %orbitals_ref.1) | copy-start | bytes 1572868
  2.1 8.2 %collective-permute-start = (bf16[2,256,256]{2,1,0:T(8,128)(2,1)S(1)}, bf16[2,256,256]{2,1,0:T(8,128)(2,1)S(1)}, u32[]{:S(2)}, u32[]{:S(2)}) collective-permute-start(bf16[2,256,256]{2,1,0:T(8,128)(2,1)S(1)} %front.1.refs_0_), channel_id=1, source_target_pairs={{0,1},{1,0},{2,3},{3,2},{4,5},{5,4},{6,7},{7,6},{8,9},{9,8},{10,11... | collective-permute-start | bytes 786440 | tf_op jit(solution)/shard_map/ppermute | solution.py:29
  4.2 12.8 %collective-permute-start.1 = (bf16[512,256]{1,0:T(8,128)(2,1)S(1)}, bf16[512,256]{1,0:T(8,128)(2,1)S(1)}, u32[]{:S(2)}, u32[]{:S(2)}) collective-permute-start(bf16[512,256]{1,0:T(8,128)(2,1)S(1)} %get-tuple-element.17.mine_ref), channel_id=1, source_target_pairs={{0,24},{1,25},{2,26},{3,27},{4,28},{5,29},{6,30},{7,31},{8,16},{9,... | collective-permute-start | bytes 786440 | tf_op jit(solution)/shard_map/ppermute | solution.py:29
  7.5 11.4 %collective-permute-start.2 = (bf16[512,256]{1,0:T(8,128)(2,1)S(1)}, bf16[512,256]{1,0:T(8,128)(2,1)S(1)}, u32[]{:S(2)}, u32[]{:S(2)}) collective-permute-start(bf16[512,256]{1,0:T(8,128)(2,1)S(1)} %get-tuple-element.20.other_ref), channel_id=1, source_target_pairs={{0,25},{1,24},{2,27},{3,26},{4,29},{5,28},{6,31},{7,30},{8,17},{9,... | collective-permute-start | bytes 786440 | tf_op jit(solution)/shard_map/ppermute | solution.py:29
  11.8 20.3 %all-to-all-start = ((bf16[16,2,32,512]{3,2,1,0:T(8,128)(2,1)}), bf16[16,2,32,512]{3,2,1,0:T(8,128)(2,1)S(1)}, u32[]{:S(2)}, u32[]{:S(2)}) async-start(bf16[16,2,32,512]{3,2,1,0:T(8,128)(2,1)} %bitcast.7), calls=%async_computation | async-start | bytes 2097152 | tf_op jit(solution)/shard_map/all_to_all | solution.py:277
  32.0 19.9 %all-to-all-start.1 = ((bf16[16,2,32,512]{3,2,1,0:T(8,128)(2,1)}), bf16[16,2,32,512]{3,2,1,0:T(8,128)(2,1)S(1)}, u32[]{:S(2)}, u32[]{:S(2)}) async-start(bf16[16,2,32,512]{3,2,1,0:T(8,128)(2,1)} %bitcast.8), calls=%async_computation.1 | async-start | bytes 2097152 | tf_op jit(solution)/shard_map/all_to_all | solution.py:277
  37.1 0.7 %copy-start.2 = (s32[2,32]{1,0:T(2,128)S(1)}, s32[2,32]{1,0:T(2,128)}, u32[]{:S(2)}) copy-start(s32[2,32]{1,0:T(2,128)} %param.4) | copy-start | bytes 772

commit v33 on v32

--- a/solution.py
+++ b/solution.py
@@ -12,8 +12,8 @@
 VMEM_LIMIT = 40 * 1024 * 1024
 SPLIT = 2
 KA, GA = ("half", "quarter", "ring", "core"), ("hi", "lo")
-NEAR_ORDER = ("core", "quarter", "ring")
-FAR_ORDER = ("core", "lo", "ring", "quarter")
+NEAR_ORDER = ("ring", "quarter", "core")
+FAR_ORDER = ("ring", "core", "lo", "quarter")
 
 
 def swap(block, mirror, other):

time: 55 us -> 55.3 us (level)
  the two profiles are of different devices: /device:TPU:1 before, /device:TPU:0 now
where the time goes in v33:
time: 55.3 us; the launch traced here: 55 us
  waiting for transfers between devices  29.3 us (53%)
  starting transfers between devices  15.1 us (27%)
  Pallas kernels  8.1 us (15%)
  local copies, waits for them, and re-layouts  1.91 us (3%)
    all_to_all x2, waiting for transfers between devices, send(): lax.all_to_all(fields, around, split_axis=0, concat_axis=0, tiled=True)  23 us
    all_to_all x2, starting transfers between devices, send(): lax.all_to_all(fields, around, split_axis=0, concat_axis=0, tiled=True)  8.47 us
    ppermute x3, starting transfers between devices, swap(): return lax.ppermute(block, KA + GA, route)  6.64 us
    ppermute x3, waiting for transfers between devices, swap(): return lax.ppermute(block, KA + GA, route)  6.29 us
    pallas_call x1, Pallas kernels, make_pairs(): pl.pallas_call(functools.partial(pair_kernel, 1.0 / math.sqrt(2 * half_k)...  2.83 us
    pallas_call x1, Pallas kernels, make_far(): pl.pallas_call(far_kernel, in_specs=[pl.BlockSpec(memory_space=pltpu.SMEM...  2.6 us
    pallas_call x1, Pallas kernels, make_near(): pl.pallas_call(near_kernel, grid=(kdevice,), in_specs=[pl.BlockSpec((1, s...  1.53 us
  transfers between devices with their start and end apart: 5, of which 4 were waited for; matrix products, arithmetic and copies ran while one was open for 1% of the time, Pallas kernels for 8%

profile of v33, /device:TPU:0, one launch (start us, length us, event | category | flops | bytes accessed | tf_op | source)
XLA Modules:
  0.0 55.0 jit_solution(1423943802447647810)
XLA Ops:
  0.0 0.1 pad_add_fusion.2.place_ref
  0.1 0.0 copy-start.1
  0.1 1.1 %dynamic-slice_bitcast_fusion = (bf16[512,256]{1,0:T(8,128)(2,1)S(1)}, bf16[512,256]{1,0:T(8,128)(2,1)S(1)}) fusion(bf16[2,512,256]{2,1,0:T(8,128)(2,1)} %orbitals_ref.1, s32[]{:T(128)S(6)} %select_n.43, s32[]{:T(128)S(6)} %select_n.42), kind=kLoop, calls=%fused_computation | loop fusion | bytes 1048584 | tf_op jit(solution)/shard_map/jit(dynamic_index_in_dim)/squeeze | solution.py:269
  1.2 0.0 copy-start
  1.2 0.0 copy-done.1
  1.2 0.9 %front.1.refs_0_ = bf16[2,256,256]{2,1,0:T(8,128)(2,1)S(1)} custom-call(s32[2]{0:T(128)S(1)} %pad_add_fusion.2.place_ref, s32[1,512]{1,0:T(1,128)S(1)} %bitcast.12, bf16[512,256]{1,0:T(8,128)(2,1)S(1)} %get-tuple-element.17.mine_ref, bf16[512,256]{1,0:T(8,128)(2,1)S(1)} %get-tuple-element.20.other_ref), custom_call_target="tpu_custom_call" | custom-call | tf_op jit(solution)/shard_map/front/pallas_call | solution.py:81
  2.1 3.0 %collective-permute-start = (bf16[2,256,256]{2,1,0:T(8,128)(2,1)S(1)}, bf16[2,256,256]{2,1,0:T(8,128)(2,1)S(1)}, u32[]{:S(2)}, u32[]{:S(2)}) collective-permute-start(bf16[2,256,256]{2,1,0:T(8,128)(2,1)S(1)} %front.1.refs_0_), channel_id=1, source_target_pairs={{0,1},{1,0},{2,3},{3,2},{4,5},{5,4},{6,7},{7,6},{8,9},{9,8},{10,11... | collective-permute-start | bytes 786440 | tf_op jit(solution)/shard_map/ppermute | solution.py:29
  5.1 3.6 %collective-permute-start.1 = (bf16[512,256]{1,0:T(8,128)(2,1)S(1)}, bf16[512,256]{1,0:T(8,128)(2,1)S(1)}, u32[]{:S(2)}, u32[]{:S(2)}) collective-permute-start(bf16[512,256]{1,0:T(8,128)(2,1)S(1)} %get-tuple-element.17.mine_ref), channel_id=1, source_target_pairs={{0,24},{1,25},{2,26},{3,27},{4,28},{5,29},{6,30},{7,31},{8,16},{9,... | collective-permute-start | bytes 786440 | tf_op jit(solution)/shard_map/ppermute | solution.py:29
  8.7 0.0 collective-permute-start.2
  8.7 0.1 pad_add_fusion.3
  8.8 0.1 dynamic_slice.17
  8.8 0.1 broadcast_subtract_fusion.rows_ref
  8.9 2.4 %collective-permute-done.refs_1_ = bf16[2,256,256]{2,1,0:T(8,128)(2,1)S(1)} collective-permute-done((bf16[2,256,256]{2,1,0:T(8,128)(2,1)S(1)}, bf16[2,256,256]{2,1,0:T(8,128)(2,1)S(1)}, u32[]{:S(2)}, u32[]{:S(2)}) %collective-permute-start) | collective-permute-done | bytes 262176 | tf_op jit(solution)/shard_map/ppermute | solution.py:29
  11.4 0.0 copy-done
  11.4 1.5 %near.1 = bf16[8,2,2,32,512]{4,3,2,1,0:T(8,128)(2,1)} custom-call(bf16[2,512,256]{2,1,0:T(8,128)(2,1)S(1)} %copy-done, bf16[2,256,256]{2,1,0:T(8,128)(2,1)S(1)} %front.1.refs_0_, bf16[2,256,256]{2,1,0:T(8,128)(2,1)S(1)} %collective-permute-done.refs_1_), custom_call_target="tpu_custom_call" | custom-call | flops 1000000000 | bytes 3000000 | tf_op jit(solution)/shard_map/near/pallas_call | solution.py:107
  12.9 4.0 %all-to-all-start = ((bf16[16,2,32,512]{3,2,1,0:T(8,128)(2,1)}), bf16[16,2,32,512]{3,2,1,0:T(8,128)(2,1)S(1)}, u32[]{:S(2)}, u32[]{:S(2)}) async-start(bf16[16,2,32,512]{3,2,1,0:T(8,128)(2,1)} %bitcast.7), calls=%async_computation | async-start | bytes 2097152 | tf_op jit(solution)/shard_map/all_to_all | solution.py:277
  16.9 0.0 collective-permute-done.1.slab_ref.refs_0_
  16.9 0.3 ahead.1
  17.2 3.8 %collective-permute-done.2.refs_1_ = bf16[512,256]{1,0:T(8,128)(2,1)S(1)} collective-permute-done((bf16[512,256]{1,0:T(8,128)(2,1)S(1)}, bf16[512,256]{1,0:T(8,128)(2,1)S(1)}, u32[]{:S(2)}, u32[]{:S(2)}) %collective-permute-start.2) | collective-permute-done | bytes 262176 | tf_op jit(solution)/shard_map/ppermute | solution.py:29
  21.1 2.6 %far.1 = bf16[4,2,2,2,32,512]{5,4,3,2,1,0:T(8,128)(2,1)} custom-call(s32[2]{0:T(128)S(1)} %pad_add_fusion.2.place_ref, bf16[256,256]{1,0:T(8,128)(2,1)S(1)} %get-tuple-element.18.picked_ref, bf16[1,256,512]{2,1,0:T(8,128)(2,1)S(1)} %get-tuple-element.19.chosen_ref, bf16[512,256]{1,0:T(8,128)(2,1)S(1)} %collective-permute-done.1.slab_ref.refs_0_, ...), custom_call_target="tpu_custom_call" | custom-call | flops 60000002048 | bytes 180000000 | tf_op jit(solution)/shard_map/far/pallas_call | solution.py:178
  23.7 9.0 %all-to-all-done.near_ref = bf16[16,2,32,512]{3,2,1,0:T(8,128)(2,1)S(1)} async-done(((bf16[16,2,32,512]{3,2,1,0:T(8,128)(2,1)}), bf16[16,2,32,512]{3,2,1,0:T(8,128)(2,1)S(1)}, u32[]{:S(2)}, u32[]{:S(2)}) %all-to-all-start) | async-done | bytes 1048608 | tf_op jit(solution)/shard_map/all_to_all | solution.py:277
  32.6 4.5 %all-to-all-start.1 = ((bf16[16,2,32,512]{3,2,1,0:T(8,128)(2,1)}), bf16[16,2,32,512]{3,2,1,0:T(8,128)(2,1)S(1)}, u32[]{:S(2)}, u32[]{:S(2)}) async-start(bf16[16,2,32,512]{3,2,1,0:T(8,128)(2,1)} %bitcast.8), calls=%async_computation.1 | async-start | bytes 2097152 | tf_op jit(solution)/shard_map/all_to_all | solution.py:277
  37.1 0.0 copy-start.2
  37.2 0.7 %copy-done.2 = s32[2,32]{1,0:T(2,128)S(1)} copy-done((s32[2,32]{1,0:T(2,128)S(1)}, s32[2,32]{1,0:T(2,128)}, u32[]{:S(2)}) %copy-start.2) | copy-done | bytes 280
  37.8 0.1 pad_add_fusion
  37.9 0.1 compare_select_fusion
  38.0 0.1 fusion.3
  38.1 0.1 pad_add_fusion.1.table_ref
  38.1 14.0 %all-to-all-done.1.far_ref = bf16[16,2,32,512]{3,2,1,0:T(8,128)(2,1)S(1)} async-done(((bf16[16,2,32,512]{3,2,1,0:T(8,128)(2,1)}), bf16[16,2,32,512]{3,2,1,0:T(8,128)(2,1)S(1)}, u32[]{:S(2)}, u32[]{:S(2)}) %all-to-all-start.1) | async-done | bytes 1048608 | tf_op jit(solution)/shard_map/all_to_all | solution.py:277
  52.2 2.8 %pairs.1 = f32[32,2,2,512]{3,2,1,0:T(2,128)} custom-call(s32[2,32]{1,0:T(2,128)S(1)} %pad_add_fusion.1.table_ref, bf16[16,2,32,512]{3,2,1,0:T(8,128)(2,1)S(1)} %all-to-all-done.near_ref, bf16[16,2,32,512]{3,2,1,0:T(8,128)(2,1)S(1)} %all-to-all-done.1.far_ref), custom_call_target="tpu_custom_call" | custom-call | tf_op jit(solution)/shard_map/pairs/pallas_call | solution.py:243
Async XLA Ops:
  0.1 1.1 %copy-start.1 = (s32[512]{0:T(512)S(1)}, s32[512]{0:T(512)}, u32[]{:S(2)}) copy-start(s32[512]{0:T(512)} %param.5) | copy-start | bytes 6148
  1.2 10.2 %copy-start = (bf16[2,512,256]{2,1,0:T(8,128)(2,1)S(1)}, bf16[2,512,256]{2,1,0:T(8,128)(2,1)}, u32[]{:S(2)}) copy-start(bf16[2,512,256]{2,1,0:T(8,128)(2,1)} %orbitals_ref.1) | copy-start | bytes 1572868
  2.1 9.3 %collective-permute-start = (bf16[2,256,256]{2,1,0:T(8,128)(2,1)S(1)}, bf16[2,256,256]{2,1,0:T(8,128)(2,1)S(1)}, u32[]{:S(2)}, u32[]{:S(2)}) collective-permute-start(bf16[2,256,256]{2,1,0:T(8,128)(2,1)S(1)} %front.1.refs_0_), channel_id=1, source_target_pairs={{0,1},{1,0},{2,3},{3,2},{4,5},{5,4},{6,7},{7,6},{8,9},{9,8},{10,11... | collective-permute-start | bytes 786440 | tf_op jit(solution)/shard_map/ppermute | solution.py:29
  5.1 11.8 %collective-permute-start.1 = (bf16[512,256]{1,0:T(8,128)(2,1)S(1)}, bf16[512,256]{1,0:T(8,128)(2,1)S(1)}, u32[]{:S(2)}, u32[]{:S(2)}) collective-permute-start(bf16[512,256]{1,0:T(8,128)(2,1)S(1)} %get-tuple-element.17.mine_ref), channel_id=1, source_target_pairs={{0,24},{1,25},{2,26},{3,27},{4,28},{5,29},{6,30},{7,31},{8,16},{9,... | collective-permute-start | bytes 786440 | tf_op jit(solution)/shard_map/ppermute | solution.py:29
  8.7 12.4 %collective-permute-start.2 = (bf16[512,256]{1,0:T(8,128)(2,1)S(1)}, bf16[512,256]{1,0:T(8,128)(2,1)S(1)}, u32[]{:S(2)}, u32[]{:S(2)}) collective-permute-start(bf16[512,256]{1,0:T(8,128)(2,1)S(1)} %get-tuple-element.20.other_ref), channel_id=1, source_target_pairs={{0,25},{1,24},{2,27},{3,26},{4,29},{5,28},{6,31},{7,30},{8,17},{9,... | collective-permute-start | bytes 786440 | tf_op jit(solution)/shard_map/ppermute | solution.py:29
  12.9 19.7 %all-to-all-start = ((bf16[16,2,32,512]{3,2,1,0:T(8,128)(2,1)}), bf16[16,2,32,512]{3,2,1,0:T(8,128)(2,1)S(1)}, u32[]{:S(2)}, u32[]{:S(2)}) async-start(bf16[16,2,32,512]{3,2,1,0:T(8,128)(2,1)} %bitcast.7), calls=%async_computation | async-start | bytes 2097152 | tf_op jit(solution)/shard_map/all_to_all | solution.py:277
  32.6 19.5 %all-to-all-start.1 = ((bf16[16,2,32,512]{3,2,1,0:T(8,128)(2,1)}), bf16[16,2,32,512]{3,2,1,0:T(8,128)(2,1)S(1)}, u32[]{:S(2)}, u32[]{:S(2)}) async-start(bf16[16,2,32,512]{3,2,1,0:T(8,128)(2,1)} %bitcast.8), calls=%async_computation.1 | async-start | bytes 2097152 | tf_op jit(solution)/shard_map/all_to_all | solution.py:277
  37.1 0.7 %copy-start.2 = (s32[2,32]{1,0:T(2,128)S(1)}, s32[2,32]{1,0:T(2,128)}, u32[]{:S(2)}) copy-start(s32[2,32]{1,0:T(2,128)} %param.4) | copy-start | bytes 772

commit v34 on v31

--- a/solution.py
+++ b/solution.py
@@ -207,7 +207,7 @@
                 return tuple(after)
 
             zero = jnp.zeros((count, columns), jnp.float32)
-            sums = lax.fori_loop(0, total_k, step, (zero,) * (2 * transfers), unroll=8)
+            sums = lax.fori_loop(0, total_k, step, (zero,) * (2 * transfers), unroll=32)
             for place, value in enumerate(sums):
                 sums_ref[rows, place // 2, place % 2, lanes] = value * scale
         copies.append(

time: 54.7 us -> 54.5 us (level)
  no operation moved by 1% of the time
where the time goes in v34:
time: 54.5 us; the launch traced here: 53.6 us
  waiting for transfers between devices  27.6 us (51%)
  starting transfers between devices  16.1 us (30%)
  Pallas kernels  7.42 us (14%)
  local copies, waits for them, and re-layouts  1.91 us (4%)
    all_to_all x2, waiting for transfers between devices, send(): lax.all_to_all(fields, around, split_axis=0, concat_axis=0, tiled=True)  23.5 us
    all_to_all x2, starting transfers between devices, send(): lax.all_to_all(fields, around, split_axis=0, concat_axis=0, tiled=True)  10.7 us
    ppermute x3, starting transfers between devices, swap(): return lax.ppermute(block, KA + GA, route)  5.46 us
    ppermute x3, waiting for transfers between devices, swap(): return lax.ppermute(block, KA + GA, route)  4.07 us
    pallas_call x1, Pallas kernels, make_pairs(): pl.pallas_call(functools.partial(pair_kernel, 1.0 / math.sqrt(2 * half_k)...  2.66 us
    pallas_call x1, Pallas kernels, make_far(): pl.pallas_call(far_kernel, in_specs=[pl.BlockSpec(memory_space=pltpu.SMEM...  2.09 us
    pallas_call x1, Pallas kernels, make_near(): pl.pallas_call(near_kernel, grid=(kdevice,), in_specs=[pl.BlockSpec((1, s...  1.53 us
  transfers between devices with their start and end apart: 5, of which 4 were waited for; matrix products, arithmetic and copies ran while one was open for 1% of the time, Pallas kernels for 7%

profile of v34, /device:TPU:1, one launch (start us, length us, event | category | flops | bytes accessed | tf_op | source)
XLA Modules:
  0.0 53.6 jit_solution(2928846650636632899)
XLA Ops:
  0.0 0.1 pad_add_fusion.2.place_ref
  0.1 0.0 copy-start.1
  0.1 1.1 %dynamic-slice_bitcast_fusion = (bf16[512,256]{1,0:T(8,128)(2,1)S(1)}, bf16[512,256]{1,0:T(8,128)(2,1)S(1)}) fusion(bf16[2,512,256]{2,1,0:T(8,128)(2,1)} %orbitals_ref.1, s32[]{:T(128)S(6)} %select_n.43, s32[]{:T(128)S(6)} %select_n.42), kind=kLoop, calls=%fused_computation | loop fusion | bytes 1048584 | tf_op jit(solution)/shard_map/jit(dynamic_index_in_dim)/squeeze | solution.py:252
  1.2 0.0 copy-start
  1.2 0.0 copy-done.1
  1.2 0.9 %front.1.refs_0_ = bf16[2,256,256]{2,1,0:T(8,128)(2,1)S(1)} custom-call(s32[2]{0:T(128)S(1)} %pad_add_fusion.2.place_ref, s32[1,512]{1,0:T(1,128)S(1)} %bitcast.12, bf16[512,256]{1,0:T(8,128)(2,1)S(1)} %get-tuple-element.17.mine_ref, bf16[512,256]{1,0:T(8,128)(2,1)S(1)} %get-tuple-element.20.other_ref), custom_call_target="tpu_custom_call" | custom-call | tf_op jit(solution)/shard_map/front/pallas_call | solution.py:74
  2.1 2.1 %collective-permute-start = (bf16[2,256,256]{2,1,0:T(8,128)(2,1)S(1)}, bf16[2,256,256]{2,1,0:T(8,128)(2,1)S(1)}, u32[]{:S(2)}, u32[]{:S(2)}) collective-permute-start(bf16[2,256,256]{2,1,0:T(8,128)(2,1)S(1)} %front.1.refs_0_), channel_id=1, source_target_pairs={{0,1},{1,0},{2,3},{3,2},{4,5},{5,4},{6,7},{7,6},{8,9},{9,8},{10,11... | collective-permute-start | bytes 786440 | tf_op jit(solution)/shard_map/ppermute | solution.py:26
  4.2 3.3 %collective-permute-start.1 = (bf16[512,256]{1,0:T(8,128)(2,1)S(1)}, bf16[512,256]{1,0:T(8,128)(2,1)S(1)}, u32[]{:S(2)}, u32[]{:S(2)}) collective-permute-start(bf16[512,256]{1,0:T(8,128)(2,1)S(1)} %get-tuple-element.17.mine_ref), channel_id=1, source_target_pairs={{0,24},{1,25},{2,26},{3,27},{4,28},{5,29},{6,30},{7,31},{8,16},{9,... | collective-permute-start | bytes 786440 | tf_op jit(solution)/shard_map/ppermute | solution.py:26
  7.5 0.0 collective-permute-start.2
  7.5 0.1 pad_add_fusion.3
  7.6 0.1 dynamic_slice.17
  7.7 0.1 broadcast_subtract_fusion.rows_ref
  7.8 2.5 %collective-permute-done.refs_1_ = bf16[2,256,256]{2,1,0:T(8,128)(2,1)S(1)} collective-permute-done((bf16[2,256,256]{2,1,0:T(8,128)(2,1)S(1)}, bf16[2,256,256]{2,1,0:T(8,128)(2,1)S(1)}, u32[]{:S(2)}, u32[]{:S(2)}) %collective-permute-start) | collective-permute-done | bytes 262176 | tf_op jit(solution)/shard_map/ppermute | solution.py:26
  10.2 0.0 copy-done
  10.2 1.5 %near.1 = bf16[8,2,2,32,512]{4,3,2,1,0:T(8,128)(2,1)} custom-call(bf16[2,512,256]{2,1,0:T(8,128)(2,1)S(1)} %copy-done, bf16[2,256,256]{2,1,0:T(8,128)(2,1)S(1)} %front.1.refs_0_, bf16[2,256,256]{2,1,0:T(8,128)(2,1)S(1)} %collective-permute-done.refs_1_), custom_call_target="tpu_custom_call" | custom-call | flops 1000000000 | bytes 3000000 | tf_op jit(solution)/shard_map/near/pallas_call | solution.py:98
  11.8 5.2 %all-to-all-start = ((bf16[16,2,32,512]{3,2,1,0:T(8,128)(2,1)}), bf16[16,2,32,512]{3,2,1,0:T(8,128)(2,1)S(1)}, u32[]{:S(2)}, u32[]{:S(2)}) async-start(bf16[16,2,32,512]{3,2,1,0:T(8,128)(2,1)} %bitcast.7), calls=%async_computation | async-start | bytes 2097152 | tf_op jit(solution)/shard_map/all_to_all | solution.py:260
  17.0 0.0 collective-permute-done.1.slab_ref.refs_0_
  17.0 0.3 ahead.1
  17.3 1.6 %collective-permute-done.2.refs_1_ = bf16[512,256]{1,0:T(8,128)(2,1)S(1)} collective-permute-done((bf16[512,256]{1,0:T(8,128)(2,1)S(1)}, bf16[512,256]{1,0:T(8,128)(2,1)S(1)}, u32[]{:S(2)}, u32[]{:S(2)}) %collective-permute-start.2) | collective-permute-done | bytes 262176 | tf_op jit(solution)/shard_map/ppermute | solution.py:26
  18.9 2.1 %far.1 = bf16[2,8,2,32,512]{4,3,2,1,0:T(8,128)(2,1)} custom-call(s32[2]{0:T(128)S(1)} %pad_add_fusion.2.place_ref, bf16[256,256]{1,0:T(8,128)(2,1)S(1)} %get-tuple-element.18.picked_ref, bf16[1,256,512]{2,1,0:T(8,128)(2,1)S(1)} %get-tuple-element.19.chosen_ref, bf16[512,256]{1,0:T(8,128)(2,1)S(1)} %collective-permute-done.1.slab_ref.refs_0_, ...), custom_call_target="tpu_custom_call" | custom-call | flops 60000002048 | bytes 180000000 | tf_op jit(solution)/shard_map/far/pallas_call | solution.py:164
  21.0 10.1 %all-to-all-done.near_ref = bf16[16,2,32,512]{3,2,1,0:T(8,128)(2,1)S(1)} async-done(((bf16[16,2,32,512]{3,2,1,0:T(8,128)(2,1)}), bf16[16,2,32,512]{3,2,1,0:T(8,128)(2,1)S(1)}, u32[]{:S(2)}, u32[]{:S(2)}) %all-to-all-start) | async-done | bytes 1048608 | tf_op jit(solution)/shard_map/all_to_all | solution.py:260
  31.1 5.5 %all-to-all-start.1 = ((bf16[16,2,32,512]{3,2,1,0:T(8,128)(2,1)}), bf16[16,2,32,512]{3,2,1,0:T(8,128)(2,1)S(1)}, u32[]{:S(2)}, u32[]{:S(2)}) async-start(bf16[16,2,32,512]{3,2,1,0:T(8,128)(2,1)} %bitcast.8), calls=%async_computation.1 | async-start | bytes 2097152 | tf_op jit(solution)/shard_map/all_to_all | solution.py:260
  36.6 0.0 copy-start.2
  36.6 0.7 %copy-done.2 = s32[2,32]{1,0:T(2,128)S(1)} copy-done((s32[2,32]{1,0:T(2,128)S(1)}, s32[2,32]{1,0:T(2,128)}, u32[]{:S(2)}) %copy-start.2) | copy-done | bytes 280
  37.2 0.1 pad_add_fusion
  37.3 0.1 compare_select_fusion
  37.4 0.1 fusion.3
  37.5 0.1 pad_add_fusion.1.table_ref
  37.6 13.4 %all-to-all-done.1.far_ref = bf16[16,2,32,512]{3,2,1,0:T(8,128)(2,1)S(1)} async-done(((bf16[16,2,32,512]{3,2,1,0:T(8,128)(2,1)}), bf16[16,2,32,512]{3,2,1,0:T(8,128)(2,1)S(1)}, u32[]{:S(2)}, u32[]{:S(2)}) %all-to-all-start.1) | async-done | bytes 1048608 | tf_op jit(solution)/shard_map/all_to_all | solution.py:260
  50.9 2.7 %pairs.1 = f32[32,2,2,512]{3,2,1,0:T(2,128)} custom-call(s32[2,32]{1,0:T(2,128)S(1)} %pad_add_fusion.1.table_ref, bf16[16,2,32,512]{3,2,1,0:T(8,128)(2,1)S(1)} %all-to-all-done.near_ref, bf16[16,2,32,512]{3,2,1,0:T(8,128)(2,1)S(1)} %all-to-all-done.1.far_ref), custom_call_target="tpu_custom_call" | custom-call | tf_op jit(solution)/shard_map/pairs/pallas_call | solution.py:226
Async XLA Ops:
  0.1 1.1 %copy-start.1 = (s32[512]{0:T(512)S(1)}, s32[512]{0:T(512)}, u32[]{:S(2)}) copy-start(s32[512]{0:T(512)} %param.5) | copy-start | bytes 6148
  1.2 9.1 %copy-start = (bf16[2,512,256]{2,1,0:T(8,128)(2,1)S(1)}, bf16[2,512,256]{2,1,0:T(8,128)(2,1)}, u32[]{:S(2)}) copy-start(bf16[2,512,256]{2,1,0:T(8,128)(2,1)} %orbitals_ref.1) | copy-start | bytes 1572868
  2.1 8.2 %collective-permute-start = (bf16[2,256,256]{2,1,0:T(8,128)(2,1)S(1)}, bf16[2,256,256]{2,1,0:T(8,128)(2,1)S(1)}, u32[]{:S(2)}, u32[]{:S(2)}) collective-permute-start(bf16[2,256,256]{2,1,0:T(8,128)(2,1)S(1)} %front.1.refs_0_), channel_id=1, source_target_pairs={{0,1},{1,0},{2,3},{3,2},{4,5},{5,4},{6,7},{7,6},{8,9},{9,8},{10,11... | collective-permute-start | bytes 786440 | tf_op jit(solution)/shard_map/ppermute | solution.py:26
  4.2 12.8 %collective-permute-start.1 = (bf16[512,256]{1,0:T(8,128)(2,1)S(1)}, bf16[512,256]{1,0:T(8,128)(2,1)S(1)}, u32[]{:S(2)}, u32[]{:S(2)}) collective-permute-start(bf16[512,256]{1,0:T(8,128)(2,1)S(1)} %get-tuple-element.17.mine_ref), channel_id=1, source_target_pairs={{0,24},{1,25},{2,26},{3,27},{4,28},{5,29},{6,30},{7,31},{8,16},{9,... | collective-permute-start | bytes 786440 | tf_op jit(solution)/shard_map/ppermute | solution.py:26
  7.5 11.4 %collective-permute-start.2 = (bf16[512,256]{1,0:T(8,128)(2,1)S(1)}, bf16[512,256]{1,0:T(8,128)(2,1)S(1)}, u32[]{:S(2)}, u32[]{:S(2)}) collective-permute-start(bf16[512,256]{1,0:T(8,128)(2,1)S(1)} %get-tuple-element.20.other_ref), channel_id=1, source_target_pairs={{0,25},{1,24},{2,27},{3,26},{4,29},{5,28},{6,31},{7,30},{8,17},{9,... | collective-permute-start | bytes 786440 | tf_op jit(solution)/shard_map/ppermute | solution.py:26
  11.8 19.4 %all-to-all-start = ((bf16[16,2,32,512]{3,2,1,0:T(8,128)(2,1)}), bf16[16,2,32,512]{3,2,1,0:T(8,128)(2,1)S(1)}, u32[]{:S(2)}, u32[]{:S(2)}) async-start(bf16[16,2,32,512]{3,2,1,0:T(8,128)(2,1)} %bitcast.7), calls=%async_computation | async-start | bytes 2097152 | tf_op jit(solution)/shard_map/all_to_all | solution.py:260
  31.1 19.8 %all-to-all-start.1 = ((bf16[16,2,32,512]{3,2,1,0:T(8,128)(2,1)}), bf16[16,2,32,512]{3,2,1,0:T(8,128)(2,1)S(1)}, u32[]{:S(2)}, u32[]{:S(2)}) async-start(bf16[16,2,32,512]{3,2,1,0:T(8,128)(2,1)} %bitcast.8), calls=%async_computation.1 | async-start | bytes 2097152 | tf_op jit(solution)/shard_map/all_to_all | solution.py:260
  36.6 0.7 %copy-start.2 = (s32[2,32]{1,0:T(2,128)S(1)}, s32[2,32]{1,0:T(2,128)}, u32[]{:S(2)}) copy-start(s32[2,32]{1,0:T(2,128)} %param.4) | copy-start | bytes 772

commit v35 on v34

--- a/solution.py
+++ b/solution.py
@@ -60,27 +60,28 @@
     return out.reshape(groups, -1, out.shape[1]).astype(jnp.bfloat16)
 
 
-def front_kernel(place_ref, points_ref, mine_ref, other_ref, picked_ref):
+def front_kernel(points_ref, mine_ref, other_ref, picked_ref):
     slab_size, _ = mine_ref.shape
     _, npoints, _ = picked_ref.shape
-    mine = place_ref[1] % SPLIT
-    chosen = one_hot(points_ref, place_ref[0], place_ref[1], slab_size, npoints)
+    mine = lax.axis_index("lo")
+    here = lax.axis_index("hi") * SPLIT + mine
+    chosen = one_hot(points_ref, lax.axis_index("half"), here, slab_size, npoints)
     for k, slab_ref in ((mine, mine_ref), (1 - mine, other_ref)):
         picked_ref[k] = pick(chosen, slab_ref[...]).astype(jnp.bfloat16)
 
 
-def make_front(mine, other, points, place):
+def make_front(mine, other, points):
     vmem = pl.BlockSpec(memory_space=pltpu.VMEM)
     return pl.pallas_call(
         front_kernel,
-        in_specs=[pl.BlockSpec(memory_space=pltpu.SMEM)] + [vmem] * 3,
+        in_specs=[vmem] * 3,
         out_specs=vmem,
         out_shape=jax.ShapeDtypeStruct(
             (SPLIT, points.shape[1] // 2, mine.shape[1]), jnp.bfloat16
         ),
         compiler_params=pltpu.CompilerParams(vmem_limit_bytes=VMEM_LIMIT),
         name="front",
-    )(place, points, mine, other)
+    )(points, mine, other)
 
 
 def near_kernel(orbitals_ref, *refs):
@@ -123,7 +124,7 @@
             picked_ref[...] = picked.astype(jnp.bfloat16)
 
 
-def far_kernel(place_ref, picked_ref, chosen_ref, *refs):
+def far_kernel(picked_ref, chosen_ref, *refs):
     *slab_refs, out_ref, parts_ref, sems = refs
     _, groups, _, length, slab_size = out_ref.shape
     picked = picked_ref[...].astype(jnp.float32)
@@ -137,14 +138,14 @@
             pieces = product(turned[part], slab_refs[number][...], groups)
             for member in range(groups):
                 parts_ref[place, crossed(member, groups)] = pieces[member]
-            target = out_ref.at[place_ref[1] % SPLIT ^ number, :, part]
+            target = out_ref.at[lax.axis_index("lo") ^ number, :, part]
             copies.append(pltpu.make_async_copy(parts_ref.at[place], target, sems.at[place]))
             copies[-1].start()
     for copy in copies:
         copy.wait()
 
 
-def make_far(rows, slabs, place, groups):
+def make_far(rows, slabs, groups):
     slab_size, channels = slabs[0].shape
     npoints, _ = rows.shape
     length = npoints // groups
@@ -163,7 +164,7 @@
     )(rows, slabs[0])
     return pl.pallas_call(
         far_kernel,
-        in_specs=[pl.BlockSpec(memory_space=pltpu.SMEM)] + [vmem] * (2 + len(slabs)),
+        in_specs=[vmem] * (2 + len(slabs)),
         out_specs=pl.BlockSpec(memory_space=pl.ANY),
         out_shape=jax.ShapeDtypeStruct((SPLIT, groups, 2, length, slab_size), jnp.bfloat16),
         scratch_shapes=[
@@ -175,12 +176,14 @@
         ),
         compiler_params=pltpu.CompilerParams(vmem_limit_bytes=VMEM_LIMIT),
         name="far",
-    )(place, picked, chosen, *slabs)
-
-
-def pair_kernel(scale, table_ref, near_ref, far_ref, out_ref, held_ref, sums_ref, sems):
+    )(picked, chosen, *slabs)
+
+
+def pair_kernel(scale, source_ref, near_ref, far_ref, out_ref, table_ref, held_ref, sums_ref, sems):
     total_k, _, length, width = held_ref.shape
     transfers = table_ref.shape[0]
+    table_copy = pltpu.make_async_copy(source_ref, table_ref, sems.at[sems.shape[0] - 1])
+    table_copy.start()
     groups = near_ref.shape[0] // SPLIT
     held_ref[: total_k // 2] = near_ref[...].astype(jnp.float32)
     for member in range(groups):
@@ -188,6 +191,7 @@
             far = far_ref[far_place(member, k, groups)]
             held_ref[total_k // 2 + member * SPLIT + k] = far.astype(jnp.float32)
 
+    table_copy.wait()
     count, columns = min(16, length), min(256, width)
     copies = []
     for start in range(0, length, count):
@@ -225,13 +229,14 @@
     vmem = pl.BlockSpec(memory_space=pltpu.VMEM)
     return pl.pallas_call(
         functools.partial(pair_kernel, 1.0 / math.sqrt(2 * half_k)),
-        in_specs=[pl.BlockSpec(memory_space=pltpu.SMEM), vmem, vmem],
+        in_specs=[pl.BlockSpec(memory_space=pl.ANY), vmem, vmem],
         out_specs=pl.BlockSpec(memory_space=pl.ANY),
         out_shape=out,
         scratch_shapes=[
+            pltpu.SMEM(table.shape, jnp.int32),
             pltpu.VMEM((2 * half_k, 2, length, slab_size), jnp.float32),
             pltpu.VMEM(out.shape, jnp.float32),
-            pltpu.SemaphoreType.DMA((length // min(16, length),)),
+            pltpu.SemaphoreType.DMA((length // min(16, length) + 1,)),
         ],
         compiler_params=pltpu.CompilerParams(vmem_limit_bytes=VMEM_LIMIT),
         name="pairs",
@@ -245,12 +250,12 @@
     slabs = lax.axis_size("hi") * lax.axis_size("lo")
     total_k = 2 * groups * kdevice
     points = points.reshape(1, -1)
-    place = jnp.stack([half, lax.axis_index("hi") * SPLIT + lax.axis_index("lo")])
+    here = lax.axis_index("hi") * SPLIT + lax.axis_index("lo")
 
     lo = lax.axis_index("lo")
     mine = lax.dynamic_index_in_dim(orbitals, lo, 0, keepdims=False)
     other = lax.dynamic_index_in_dim(orbitals, 1 - lo, 0, keepdims=False)
-    share = make_front(mine, other, points, place)
+    share = make_front(mine, other, points)
     share, mine, other = lax.optimization_barrier((share, mine, other))
     shares = [share] + [swap(share, False, x) for x in range(1, slabs)]
     far = [swap(other if x & 1 else mine, True, x) for x in range(slabs)]
@@ -262,10 +267,10 @@
     near_fields = make_near(orbitals, shares, groups)
     npoints = points.shape[1] // 2
     wanted = lax.dynamic_slice_in_dim(points[0], half * npoints, npoints)
-    starts = jnp.stack([(place[1] ^ x) * slab_size for x in range(slabs)])
+    starts = jnp.stack([(here ^ x) * slab_size for x in range(slabs)])
     rows = wanted[:, None] - starts[None, :]
     near_fields, rows = lax.optimization_barrier((near_fields, rows))
-    far_fields = make_far(rows, far, place, groups)
+    far_fields = make_far(rows, far, groups)
     near_fields = send(near_fields, ("quarter", "inner"))
     near_fields, far_fields = lax.optimization_barrier((near_fields, far_fields))
     far_fields = send(far_fields, ("lo", "inner", "quarter"))

time: 54.5 us -> 54.1 us (level)
    pallas_call x2, Pallas kernels: 2.96 us -> 1.88 us  [the longest x1 1.55 us: make_far(): pl.pallas_call(far_kernel, in_specs=[vmem] * (2 + len(slabs)), out_specs=...]
    pallas_call x1, Pallas kernels: 2.66 us -> 3.36 us  [make_pairs(): pl.pallas_call(functools.partial(pair_kernel, 1.0 / math.sqrt(2 * half_k)...]
  transfers between devices with their start and end apart: 5 -> 5, of which waited for: 4 -> 4; matrix products, arithmetic and copies ran while one was open for 1% -> 1% of each run, Pallas kernels for 7% -> 6%
where the time goes in v35:
time: 54.1 us; the launch traced here: 53.2 us
  waiting for transfers between devices  28.1 us (52%)
  starting transfers between devices  15.6 us (29%)
  Pallas kernels  7.05 us (13%)
  local copies, waits for them, and re-layouts  1.91 us (4%)
    all_to_all x2, waiting for transfers between devices, send(): lax.all_to_all(fields, around, split_axis=0, concat_axis=0, tiled=True)  24.1 us
    all_to_all x2, starting transfers between devices, send(): lax.all_to_all(fields, around, split_axis=0, concat_axis=0, tiled=True)  10.1 us
    ppermute x3, starting transfers between devices, swap(): return lax.ppermute(block, KA + GA, route)  5.46 us
    ppermute x3, waiting for transfers between devices, swap(): return lax.ppermute(block, KA + GA, route)  4.07 us
    pallas_call x1, Pallas kernels, make_pairs(): pl.pallas_call(functools.partial(pair_kernel, 1.0 / math.sqrt(2 * half_k)...  3.36 us
    pallas_call x1, Pallas kernels, make_far(): pl.pallas_call(far_kernel, in_specs=[vmem] * (2 + len(slabs)), out_specs=...  1.55 us
    pallas_call x1, Pallas kernels, make_near(): pl.pallas_call(near_kernel, grid=(kdevice,), in_specs=[pl.BlockSpec((1, s...  1.53 us
  transfers between devices with their start and end apart: 5, of which 4 were waited for; matrix products, arithmetic and copies ran while one was open for 1% of the time, Pallas kernels for 6%

profile of v35, /device:TPU:1, one launch (start us, length us, event | category | flops | bytes accessed | tf_op | source)
XLA Modules:
  0.0 53.2 jit_solution(12778632556125211385)
XLA Ops:
  0.0 0.0 copy-start.1
  0.0 1.1 %dynamic-slice_bitcast_fusion = (bf16[512,256]{1,0:T(8,128)(2,1)S(1)}, bf16[512,256]{1,0:T(8,128)(2,1)S(1)}) fusion(bf16[2,512,256]{2,1,0:T(8,128)(2,1)} %orbitals_ref.1, s32[]{:T(128)S(6)} %select_n.43, s32[]{:T(128)S(6)} %select_n.42), kind=kLoop, calls=%fused_computation | loop fusion | bytes 1048584 | tf_op jit(solution)/shard_map/jit(dynamic_index_in_dim)/squeeze | solution.py:257
  1.1 0.0 copy-start
  1.1 0.0 copy-done.1
  1.1 0.3 front.1.refs_0_
  1.4 2.1 %collective-permute-start = (bf16[2,256,256]{2,1,0:T(8,128)(2,1)S(1)}, bf16[2,256,256]{2,1,0:T(8,128)(2,1)S(1)}, u32[]{:S(2)}, u32[]{:S(2)}) collective-permute-start(bf16[2,256,256]{2,1,0:T(8,128)(2,1)S(1)} %front.1.refs_0_), channel_id=1, source_target_pairs={{0,1},{1,0},{2,3},{3,2},{4,5},{5,4},{6,7},{7,6},{8,9},{9,8},{10,11... | collective-permute-start | bytes 786440 | tf_op jit(solution)/shard_map/ppermute | solution.py:26
  3.6 3.3 %collective-permute-start.1 = (bf16[512,256]{1,0:T(8,128)(2,1)S(1)}, bf16[512,256]{1,0:T(8,128)(2,1)S(1)}, u32[]{:S(2)}, u32[]{:S(2)}) collective-permute-start(bf16[512,256]{1,0:T(8,128)(2,1)S(1)} %get-tuple-element.17.mine_ref), channel_id=1, source_target_pairs={{0,24},{1,25},{2,26},{3,27},{4,28},{5,29},{6,30},{7,31},{8,16},{9,... | collective-permute-start | bytes 786440 | tf_op jit(solution)/shard_map/ppermute | solution.py:26
  6.9 0.0 collective-permute-start.2
  6.9 0.1 pad_add_fusion.2
  7.0 0.1 dynamic_slice.17
  7.1 0.1 broadcast_subtract_fusion.rows_ref
  7.2 2.5 %collective-permute-done.refs_1_ = bf16[2,256,256]{2,1,0:T(8,128)(2,1)S(1)} collective-permute-done((bf16[2,256,256]{2,1,0:T(8,128)(2,1)S(1)}, bf16[2,256,256]{2,1,0:T(8,128)(2,1)S(1)}, u32[]{:S(2)}, u32[]{:S(2)}) %collective-permute-start) | collective-permute-done | bytes 262176 | tf_op jit(solution)/shard_map/ppermute | solution.py:26
  9.6 0.0 copy-done
  9.6 1.5 %near.1 = bf16[8,2,2,32,512]{4,3,2,1,0:T(8,128)(2,1)} custom-call(bf16[2,512,256]{2,1,0:T(8,128)(2,1)S(1)} %copy-done, bf16[2,256,256]{2,1,0:T(8,128)(2,1)S(1)} %front.1.refs_0_, bf16[2,256,256]{2,1,0:T(8,128)(2,1)S(1)} %collective-permute-done.refs_1_), custom_call_target="tpu_custom_call" | custom-call | flops 1000000000 | bytes 3000000 | tf_op jit(solution)/shard_map/near/pallas_call | solution.py:99
  11.2 5.2 %all-to-all-start = ((bf16[16,2,32,512]{3,2,1,0:T(8,128)(2,1)}), bf16[16,2,32,512]{3,2,1,0:T(8,128)(2,1)S(1)}, u32[]{:S(2)}, u32[]{:S(2)}) async-start(bf16[16,2,32,512]{3,2,1,0:T(8,128)(2,1)} %bitcast.5), calls=%async_computation | async-start | bytes 2097152 | tf_op jit(solution)/shard_map/all_to_all | solution.py:265
  16.4 0.0 collective-permute-done.1.slab_ref.refs_0_
  16.4 0.3 ahead.1
  16.7 1.6 %collective-permute-done.2.refs_1_ = bf16[512,256]{1,0:T(8,128)(2,1)S(1)} collective-permute-done((bf16[512,256]{1,0:T(8,128)(2,1)S(1)}, bf16[512,256]{1,0:T(8,128)(2,1)S(1)}, u32[]{:S(2)}, u32[]{:S(2)}) %collective-permute-start.2) | collective-permute-done | bytes 262176 | tf_op jit(solution)/shard_map/ppermute | solution.py:26
  18.3 1.5 %far.1 = bf16[2,8,2,32,512]{4,3,2,1,0:T(8,128)(2,1)} custom-call(bf16[256,256]{1,0:T(8,128)(2,1)S(1)} %get-tuple-element.18.picked_ref, bf16[1,256,512]{2,1,0:T(8,128)(2,1)S(1)} %get-tuple-element.19.chosen_ref, bf16[512,256]{1,0:T(8,128)(2,1)S(1)} %collective-permute-done.1.slab_ref.refs_0_, bf16[512,256]{1,0:T(8,128)(2,1)S(1)} %collective-permute-done.2.refs_1_), custom_call_target="tpu_custom_call" | custom-call | flops 60000002048 | bytes 180000000 | tf_op jit(solution)/shard_map/far/pallas_call | solution.py:165
  19.8 10.7 %all-to-all-done.near_ref = bf16[16,2,32,512]{3,2,1,0:T(8,128)(2,1)S(1)} async-done(((bf16[16,2,32,512]{3,2,1,0:T(8,128)(2,1)}), bf16[16,2,32,512]{3,2,1,0:T(8,128)(2,1)S(1)}, u32[]{:S(2)}, u32[]{:S(2)}) %all-to-all-start) | async-done | bytes 1048608 | tf_op jit(solution)/shard_map/all_to_all | solution.py:265
  30.5 4.9 %all-to-all-start.1 = ((bf16[16,2,32,512]{3,2,1,0:T(8,128)(2,1)}), bf16[16,2,32,512]{3,2,1,0:T(8,128)(2,1)S(1)}, u32[]{:S(2)}, u32[]{:S(2)}) async-start(bf16[16,2,32,512]{3,2,1,0:T(8,128)(2,1)} %bitcast.6), calls=%async_computation.1 | async-start | bytes 2097152 | tf_op jit(solution)/shard_map/all_to_all | solution.py:265
  35.4 0.0 copy-start.2
  35.4 0.7 %copy-done.2 = s32[2,32]{1,0:T(2,128)S(1)} copy-done((s32[2,32]{1,0:T(2,128)S(1)}, s32[2,32]{1,0:T(2,128)}, u32[]{:S(2)}) %copy-start.2) | copy-done | bytes 280
  36.1 0.1 pad_add_fusion
  36.2 0.1 compare_select_fusion
  36.3 0.1 fusion.3
  36.3 0.1 pad_add_fusion.1.source_ref
  36.4 13.4 %all-to-all-done.1.far_ref = bf16[16,2,32,512]{3,2,1,0:T(8,128)(2,1)S(1)} async-done(((bf16[16,2,32,512]{3,2,1,0:T(8,128)(2,1)}), bf16[16,2,32,512]{3,2,1,0:T(8,128)(2,1)S(1)}, u32[]{:S(2)}, u32[]{:S(2)}) %all-to-all-start.1) | async-done | bytes 1048608 | tf_op jit(solution)/shard_map/all_to_all | solution.py:265
  49.8 3.4 %pairs.1 = f32[32,2,2,512]{3,2,1,0:T(2,128)} custom-call(s32[2,32]{1,0:T(2,128)S(1)} %pad_add_fusion.1.source_ref, bf16[16,2,32,512]{3,2,1,0:T(8,128)(2,1)S(1)} %all-to-all-done.near_ref, bf16[16,2,32,512]{3,2,1,0:T(8,128)(2,1)S(1)} %all-to-all-done.1.far_ref), custom_call_target="tpu_custom_call" | custom-call | tf_op jit(solution)/shard_map/pairs/pallas_call | solution.py:230
Async XLA Ops:
  0.0 1.1 %copy-start.1 = (s32[512]{0:T(512)S(1)}, s32[512]{0:T(512)}, u32[]{:S(2)}) copy-start(s32[512]{0:T(512)} %param.5) | copy-start | bytes 6148
  1.1 8.5 %copy-start = (bf16[2,512,256]{2,1,0:T(8,128)(2,1)S(1)}, bf16[2,512,256]{2,1,0:T(8,128)(2,1)}, u32[]{:S(2)}) copy-start(bf16[2,512,256]{2,1,0:T(8,128)(2,1)} %orbitals_ref.1) | copy-start | bytes 1572868
  1.4 8.2 %collective-permute-start = (bf16[2,256,256]{2,1,0:T(8,128)(2,1)S(1)}, bf16[2,256,256]{2,1,0:T(8,128)(2,1)S(1)}, u32[]{:S(2)}, u32[]{:S(2)}) collective-permute-start(bf16[2,256,256]{2,1,0:T(8,128)(2,1)S(1)} %front.1.refs_0_), channel_id=1, source_target_pairs={{0,1},{1,0},{2,3},{3,2},{4,5},{5,4},{6,7},{7,6},{8,9},{9,8},{10,11... | collective-permute-start | bytes 786440 | tf_op jit(solution)/shard_map/ppermute | solution.py:26
  3.6 12.8 %collective-permute-start.1 = (bf16[512,256]{1,0:T(8,128)(2,1)S(1)}, bf16[512,256]{1,0:T(8,128)(2,1)S(1)}, u32[]{:S(2)}, u32[]{:S(2)}) collective-permute-start(bf16[512,256]{1,0:T(8,128)(2,1)S(1)} %get-tuple-element.17.mine_ref), channel_id=1, source_target_pairs={{0,24},{1,25},{2,26},{3,27},{4,28},{5,29},{6,30},{7,31},{8,16},{9,... | collective-permute-start | bytes 786440 | tf_op jit(solution)/shard_map/ppermute | solution.py:26
  6.9 11.4 %collective-permute-start.2 = (bf16[512,256]{1,0:T(8,128)(2,1)S(1)}, bf16[512,256]{1,0:T(8,128)(2,1)S(1)}, u32[]{:S(2)}, u32[]{:S(2)}) collective-permute-start(bf16[512,256]{1,0:T(8,128)(2,1)S(1)} %get-tuple-element.20.other_ref), channel_id=1, source_target_pairs={{0,25},{1,24},{2,27},{3,26},{4,29},{5,28},{6,31},{7,30},{8,17},{9,... | collective-permute-start | bytes 786440 | tf_op jit(solution)/shard_map/ppermute | solution.py:26
  11.2 19.4 %all-to-all-start = ((bf16[16,2,32,512]{3,2,1,0:T(8,128)(2,1)}), bf16[16,2,32,512]{3,2,1,0:T(8,128)(2,1)S(1)}, u32[]{:S(2)}, u32[]{:S(2)}) async-start(bf16[16,2,32,512]{3,2,1,0:T(8,128)(2,1)} %bitcast.5), calls=%async_computation | async-start | bytes 2097152 | tf_op jit(solution)/shard_map/all_to_all | solution.py:265
  30.5 19.3 %all-to-all-start.1 = ((bf16[16,2,32,512]{3,2,1,0:T(8,128)(2,1)}), bf16[16,2,32,512]{3,2,1,0:T(8,128)(2,1)S(1)}, u32[]{:S(2)}, u32[]{:S(2)}) async-start(bf16[16,2,32,512]{3,2,1,0:T(8,128)(2,1)} %bitcast.6), calls=%async_computation.1 | async-start | bytes 2097152 | tf_op jit(solution)/shard_map/all_to_all | solution.py:265
  35.4 0.7 %copy-start.2 = (s32[2,32]{1,0:T(2,128)S(1)}, s32[2,32]{1,0:T(2,128)}, u32[]{:S(2)}) copy-start(s32[2,32]{1,0:T(2,128)} %param.4) | copy-start | bytes 772

commit v36 on v35

--- a/solution.py
+++ b/solution.py
@@ -179,19 +179,19 @@
     )(picked, chosen, *slabs)
 
 
-def pair_kernel(scale, source_ref, near_ref, far_ref, out_ref, table_ref, held_ref, sums_ref, sems):
+def pair_kernel(scale, table_ref, near_ref, far_ref, out_ref, held_ref, sums_ref, sems):
     total_k, _, length, width = held_ref.shape
     transfers = table_ref.shape[0]
-    table_copy = pltpu.make_async_copy(source_ref, table_ref, sems.at[sems.shape[0] - 1])
-    table_copy.start()
+    table = table_ref[...]
+    shifts = [lax.rem(total_k - table[transfer, 0], total_k) for transfer in range(transfers)]
     groups = near_ref.shape[0] // SPLIT
     held_ref[: total_k // 2] = near_ref[...].astype(jnp.float32)
     for member in range(groups):
         for k in range(SPLIT):
             far = far_ref[far_place(member, k, groups)]
-            held_ref[total_k // 2 + member * SPLIT + k] = far.astype(jnp.float32)
-
-    table_copy.wait()
+            place = (member * SPLIT + k + total_k // 4) % (total_k // 2)
+            held_ref[total_k // 2 + place] = far.astype(jnp.float32)
+
     count, columns = min(16, length), min(256, width)
     copies = []
     for start in range(0, length, count):
@@ -203,7 +203,7 @@
                 real, imag = held_ref[k, 0, rows, lanes], held_ref[k, 1, rows, lanes]
                 after = []
                 for transfer in range(transfers):
-                    other = table_ref[transfer, k]
+                    other = lax.rem(k + total_k - shifts[transfer], total_k)
                     other_real = held_ref[other, 0, rows, lanes]
                     other_imag = held_ref[other, 1, rows, lanes]
                     after.append(sums[2 * transfer] + (real * other_real + imag * other_imag))
@@ -229,14 +229,13 @@
     vmem = pl.BlockSpec(memory_space=pltpu.VMEM)
     return pl.pallas_call(
         functools.partial(pair_kernel, 1.0 / math.sqrt(2 * half_k)),
-        in_specs=[pl.BlockSpec(memory_space=pl.ANY), vmem, vmem],
+        in_specs=[vmem, vmem, vmem],
         out_specs=pl.BlockSpec(memory_space=pl.ANY),
         out_shape=out,
         scratch_shapes=[
-            pltpu.SMEM(table.shape, jnp.int32),
             pltpu.VMEM((2 * half_k, 2, length, slab_size), jnp.float32),
             pltpu.VMEM(out.shape, jnp.float32),
-            pltpu.SemaphoreType.DMA((length // min(16, length) + 1,)),
+            pltpu.SemaphoreType.DMA((length // min(16, length),)),
         ],
         compiler_params=pltpu.CompilerParams(vmem_limit_bytes=VMEM_LIMIT),
         name="pairs",
@@ -274,15 +273,7 @@
     near_fields = send(near_fields, ("quarter", "inner"))
     near_fields, far_fields = lax.optimization_barrier((near_fields, far_fields))
     far_fields = send(far_fields, ("lo", "inner", "quarter"))
-
-    def mirrored(kpoints):
-        return total_k // 2 + (kpoints + total_k // 4) % (total_k // 2)
-
-    turn = half * (total_k // 2)
-    table = (jnp.roll(minus_table, -turn, axis=1) - turn) % total_k
-    table = jnp.where(table < total_k // 2, table, mirrored(table))
-    first, third, fourth = jnp.split(table, (total_k // 2, 3 * total_k // 4), axis=1)
-    return make_pairs(near_fields, far_fields, jnp.concatenate([first, fourth, third], axis=1))
+    return make_pairs(near_fields, far_fields, minus_table)
 
 
 def solution(mesh):

time: 54.1 us -> 59.9 us (1.11); the launches traced: 53.2 us -> 59.6 us
  blocking collectives: 0 us -> 17.9 us
  waiting for transfers between devices: 28.1 us -> 19 us
  Pallas kernels: 7.05 us -> 5.6 us
  local copies, waits for them, and re-layouts: 1.91 us -> 1.16 us
    all_to_all x0 -> x1, blocking collectives: none -> 17.9 us  [send(): lax.all_to_all(fields, around, split_axis=0, concat_axis=0, tiled=True)]
    all_to_all x2 -> x1, waiting for transfers between devices: 24.1 us -> 11.9 us  [send(): lax.all_to_all(fields, around, split_axis=0, concat_axis=0, tiled=True)]
    ppermute x3, waiting for transfers between devices: 4.07 us -> 7.06 us  [swap(): return lax.ppermute(block, KA + GA, route)]
    pallas_call x1, Pallas kernels: 3.36 us -> 2.12 us  [make_pairs(): pl.pallas_call(functools.partial(pair_kernel, 1.0 / math.sqrt(2 * half_k)...]
    unnamed x6, local copies, waits for them, and re-layouts: 0.68 us -> 0.01 us
    all_to_all x2 -> x1, starting transfers between devices: 10.1 us -> 10.3 us  [send(): lax.all_to_all(fields, around, split_axis=0, concat_axis=0, tiled=True)]
  transfers between devices with their start and end apart: 5 -> 4, of which waited for: 4 -> 2; matrix products, arithmetic and copies ran while one was open for 1% -> 0% of each run, Pallas kernels for 6% -> 5%
where the time goes in v36:
time: 59.9 us; the launch traced here: 59.6 us
  waiting for transfers between devices  19 us (32%)
  blocking collectives  17.9 us (30%)
  starting transfers between devices  15.7 us (26%)
  Pallas kernels  5.6 us (9%)
  local copies, waits for them, and re-layouts  1.16 us (2%)
    all_to_all x1, blocking collectives, send(): lax.all_to_all(fields, around, split_axis=0, concat_axis=0, tiled=True)  17.9 us
    all_to_all x1, waiting for transfers between devices, send(): lax.all_to_all(fields, around, split_axis=0, concat_axis=0, tiled=True)  11.9 us
    all_to_all x1, starting transfers between devices, send(): lax.all_to_all(fields, around, split_axis=0, concat_axis=0, tiled=True)  10.3 us
    ppermute x3, waiting for transfers between devices, swap(): return lax.ppermute(block, KA + GA, route)  7.06 us
    ppermute x3, starting transfers between devices, swap(): return lax.ppermute(block, KA + GA, route)  5.48 us
    pallas_call x1, Pallas kernels, make_pairs(): pl.pallas_call(functools.partial(pair_kernel, 1.0 / math.sqrt(2 * half_k)...  2.12 us
    pallas_call x1, Pallas kernels, make_near(): pl.pallas_call(near_kernel, grid=(kdevice,), in_specs=[pl.BlockSpec((1, s...  1.48 us
    pallas_call x1, Pallas kernels, make_far(): pl.pallas_call(far_kernel, in_specs=[vmem] * (2 + len(slabs)), out_specs=...  1.39 us
  transfers between devices with their start and end apart: 4, of which 2 were waited for; matrix products, arithmetic and copies ran while one was open for 0% of the time, Pallas kernels for 5%

profile of v36, /device:TPU:1, one launch (start us, length us, event | category | flops | bytes accessed | tf_op | source)
XLA Modules:
  0.0 59.6 jit_solution(8044235173630714582)
XLA Ops:
  0.0 0.0 copy-start.1
  0.0 1.1 %dynamic-slice_bitcast_fusion = (bf16[512,256]{1,0:T(8,128)(2,1)S(1)}, bf16[512,256]{1,0:T(8,128)(2,1)S(1)}) fusion(bf16[2,512,256]{2,1,0:T(8,128)(2,1)} %orbitals_ref.1, s32[]{:T(128)S(6)} %select_n.11, s32[]{:T(128)S(6)} %select_n.10), kind=kLoop, calls=%fused_computation | loop fusion | bytes 1048584 | tf_op jit(solution)/shard_map/jit(dynamic_index_in_dim)/squeeze | solution.py:256
  1.1 0.0 copy-start
  1.1 0.0 copy-done.1
  1.1 0.3 front.1.refs_0_
  1.4 4.2 %collective-permute-start.1 = (bf16[512,256]{1,0:T(8,128)(2,1)S(1)}, bf16[512,256]{1,0:T(8,128)(2,1)S(1)}, u32[]{:S(2)}, u32[]{:S(2)}) collective-permute-start(bf16[512,256]{1,0:T(8,128)(2,1)S(1)} %get-tuple-element.17.mine_ref), channel_id=1, source_target_pairs={{0,24},{1,25},{2,26},{3,27},{4,28},{5,29},{6,30},{7,31},{8,16},{9,... | collective-permute-start | bytes 786440 | tf_op jit(solution)/shard_map/ppermute | solution.py:26
  5.7 1.0 %collective-permute-start.2 = (bf16[512,256]{1,0:T(8,128)(2,1)S(1)}, bf16[512,256]{1,0:T(8,128)(2,1)S(1)}, u32[]{:S(2)}, u32[]{:S(2)}) collective-permute-start(bf16[512,256]{1,0:T(8,128)(2,1)S(1)} %get-tuple-element.20.other_ref), channel_id=1, source_target_pairs={{0,25},{1,24},{2,27},{3,26},{4,29},{5,28},{6,31},{7,30},{8,17},{9,... | collective-permute-start | bytes 786440 | tf_op jit(solution)/shard_map/ppermute | solution.py:26
  6.7 0.2 collective-permute-start
  6.9 0.1 pad_add_fusion
  7.0 0.1 dynamic_slice.12
  7.1 0.1 broadcast_subtract_fusion.rows_ref
  7.2 7.1 %collective-permute-done.refs_1_ = bf16[2,256,256]{2,1,0:T(8,128)(2,1)S(1)} collective-permute-done((bf16[2,256,256]{2,1,0:T(8,128)(2,1)S(1)}, bf16[2,256,256]{2,1,0:T(8,128)(2,1)S(1)}, u32[]{:S(2)}, u32[]{:S(2)}) %collective-permute-start) | collective-permute-done | bytes 262176 | tf_op jit(solution)/shard_map/ppermute | solution.py:26
  14.2 0.0 copy-done
  14.2 1.5 %near.1 = bf16[8,2,2,32,512]{4,3,2,1,0:T(8,128)(2,1)} custom-call(bf16[2,512,256]{2,1,0:T(8,128)(2,1)S(1)} %copy-done, bf16[2,256,256]{2,1,0:T(8,128)(2,1)S(1)} %front.1.refs_0_, bf16[2,256,256]{2,1,0:T(8,128)(2,1)S(1)} %collective-permute-done.refs_1_), custom_call_target="tpu_custom_call" | custom-call | flops 1000000000 | bytes 3000000 | tf_op jit(solution)/shard_map/near/pallas_call | solution.py:99
  15.7 10.3 %all-to-all-start = ((bf16[16,2,32,512]{3,2,1,0:T(8,128)(2,1)}), bf16[16,2,32,512]{3,2,1,0:T(8,128)(2,1)S(1)}, u32[]{:S(2)}, u32[]{:S(2)}) async-start(bf16[16,2,32,512]{3,2,1,0:T(8,128)(2,1)} %bitcast.5), calls=%async_computation | async-start | bytes 2097152 | tf_op jit(solution)/shard_map/all_to_all | solution.py:264
  26.0 0.0 collective-permute-done.1.slab_ref.refs_0_
  26.0 0.3 ahead.1
  26.3 0.0 collective-permute-done.2.refs_1_
  26.3 1.4 %far.1 = bf16[2,8,2,32,512]{4,3,2,1,0:T(8,128)(2,1)S(1)} custom-call(bf16[256,256]{1,0:T(8,128)(2,1)S(1)} %get-tuple-element.18.picked_ref, bf16[1,256,512]{2,1,0:T(8,128)(2,1)S(1)} %get-tuple-element.19.chosen_ref, bf16[512,256]{1,0:T(8,128)(2,1)S(1)} %collective-permute-done.1.slab_ref.refs_0_, bf16[512,256]{1,0:T(8,128)(2,1)S(1)} %collective-permute-done.2.refs_1_), custom_call_target="tpu_custom_call" | custom-call | flops 60000002048 | bytes 180000000 | tf_op jit(solution)/shard_map/far/pallas_call | solution.py:165
  27.7 11.9 %all-to-all-done.near_ref = bf16[16,2,32,512]{3,2,1,0:T(8,128)(2,1)S(1)} async-done(((bf16[16,2,32,512]{3,2,1,0:T(8,128)(2,1)}), bf16[16,2,32,512]{3,2,1,0:T(8,128)(2,1)S(1)}, u32[]{:S(2)}, u32[]{:S(2)}) %all-to-all-start) | async-done | bytes 1048608 | tf_op jit(solution)/shard_map/all_to_all | solution.py:264
  39.6 0.0 copy-start.2
  39.6 17.9 %all_to_all.10.far_ref = bf16[16,2,32,512]{3,2,1,0:T(8,128)(2,1)S(1)} all-to-all(bf16[16,2,32,512]{3,2,1,0:T(8,128)(2,1)S(1)} %bitcast.9), channel_id=1, replica_groups=mesh['half'=2,'quarter'=2,'inner'=4,'hi'=1,'lo'=2] {'lo','inner','quarter'}, dimensions={0} | all-to-all | bytes 2097152 | tf_op jit(solution)/shard_map/all_to_all | solution.py:264
  57.5 0.0 copy-done.2
  57.5 2.1 %pairs.1 = f32[32,2,2,512]{3,2,1,0:T(2,128)} custom-call(s32[2,32]{1,0:T(2,128)S(1)} %copy-done.2, bf16[16,2,32,512]{3,2,1,0:T(8,128)(2,1)S(1)} %all-to-all-done.near_ref, bf16[16,2,32,512]{3,2,1,0:T(8,128)(2,1)S(1)} %all_to_all.10.far_ref), custom_call_target="tpu_custom_call" | custom-call | tf_op jit(solution)/shard_map/pairs/pallas_call | solution.py:230
Async XLA Ops:
  0.0 1.1 %copy-start.1 = (s32[512]{0:T(512)S(1)}, s32[512]{0:T(512)}, u32[]{:S(2)}) copy-start(s32[512]{0:T(512)} %param.5) | copy-start | bytes 6148
  1.1 13.2 %copy-start = (bf16[2,512,256]{2,1,0:T(8,128)(2,1)S(1)}, bf16[2,512,256]{2,1,0:T(8,128)(2,1)}, u32[]{:S(2)}) copy-start(bf16[2,512,256]{2,1,0:T(8,128)(2,1)} %orbitals_ref.1) | copy-start | bytes 1572868
  1.4 24.5 %collective-permute-start.1 = (bf16[512,256]{1,0:T(8,128)(2,1)S(1)}, bf16[512,256]{1,0:T(8,128)(2,1)S(1)}, u32[]{:S(2)}, u32[]{:S(2)}) collective-permute-start(bf16[512,256]{1,0:T(8,128)(2,1)S(1)} %get-tuple-element.17.mine_ref), channel_id=1, source_target_pairs={{0,24},{1,25},{2,26},{3,27},{4,28},{5,29},{6,30},{7,31},{8,16},{9,... | collective-permute-start | bytes 786440 | tf_op jit(solution)/shard_map/ppermute | solution.py:26
  5.7 20.6 %collective-permute-start.2 = (bf16[512,256]{1,0:T(8,128)(2,1)S(1)}, bf16[512,256]{1,0:T(8,128)(2,1)S(1)}, u32[]{:S(2)}, u32[]{:S(2)}) collective-permute-start(bf16[512,256]{1,0:T(8,128)(2,1)S(1)} %get-tuple-element.20.other_ref), channel_id=1, source_target_pairs={{0,25},{1,24},{2,27},{3,26},{4,29},{5,28},{6,31},{7,30},{8,17},{9,... | collective-permute-start | bytes 786440 | tf_op jit(solution)/shard_map/ppermute | solution.py:26
  6.7 7.5 %collective-permute-start = (bf16[2,256,256]{2,1,0:T(8,128)(2,1)S(1)}, bf16[2,256,256]{2,1,0:T(8,128)(2,1)S(1)}, u32[]{:S(2)}, u32[]{:S(2)}) collective-permute-start(bf16[2,256,256]{2,1,0:T(8,128)(2,1)S(1)} %front.1.refs_0_), channel_id=1, source_target_pairs={{0,1},{1,0},{2,3},{3,2},{4,5},{5,4},{6,7},{7,6},{8,9},{9,8},{10,11... | collective-permute-start | bytes 786440 | tf_op jit(solution)/shard_map/ppermute | solution.py:26
  15.7 23.9 %all-to-all-start = ((bf16[16,2,32,512]{3,2,1,0:T(8,128)(2,1)}), bf16[16,2,32,512]{3,2,1,0:T(8,128)(2,1)S(1)}, u32[]{:S(2)}, u32[]{:S(2)}) async-start(bf16[16,2,32,512]{3,2,1,0:T(8,128)(2,1)} %bitcast.5), calls=%async_computation | async-start | bytes 2097152 | tf_op jit(solution)/shard_map/all_to_all | solution.py:264
  39.6 17.9 %copy-start.2 = (s32[2,32]{1,0:T(2,128)S(1)}, s32[2,32]{1,0:T(2,128)}, u32[]{:S(2)}) copy-start(s32[2,32]{1,0:T(2,128)} %table_ref.1) | copy-start | bytes 772

commit v37 on v36

--- a/solution.py
+++ b/solution.py
@@ -183,7 +183,11 @@
     total_k, _, length, width = held_ref.shape
     transfers = table_ref.shape[0]
     table = table_ref[...]
-    shifts = [lax.rem(total_k - table[transfer, 0], total_k) for transfer in range(transfers)]
+    shifts = []
+    for transfer in range(transfers):
+        place = table[transfer, 0]
+        far_place_of = total_k // 2 + lax.rem(place + total_k // 4, total_k // 2)
+        shifts.append(total_k - jnp.where(place < total_k // 2, place, far_place_of))
     groups = near_ref.shape[0] // SPLIT
     held_ref[: total_k // 2] = near_ref[...].astype(jnp.float32)
     for member in range(groups):
@@ -273,7 +277,15 @@
     near_fields = send(near_fields, ("quarter", "inner"))
     near_fields, far_fields = lax.optimization_barrier((near_fields, far_fields))
     far_fields = send(far_fields, ("lo", "inner", "quarter"))
-    return make_pairs(near_fields, far_fields, minus_table)
+
+    def mirrored(kpoints):
+        return total_k // 2 + (kpoints + total_k // 4) % (total_k // 2)
+
+    turn = half * (total_k // 2)
+    table = (jnp.roll(minus_table, -turn, axis=1) - turn) % total_k
+    table = jnp.where(table < total_k // 2, table, mirrored(table))
+    first, third, fourth = jnp.split(table, (total_k // 2, 3 * total_k // 4), axis=1)
+    return make_pairs(near_fields, far_fields, jnp.concatenate([first, fourth, third], axis=1))
 
 
 def solution(mesh):

time: 59.9 us -> 52.8 us (0.88)
  blocking collectives: 17.9 us -> 0 us
  waiting for transfers between devices: 19 us -> 28.1 us
  local copies, waits for them, and re-layouts: 1.16 us -> 1.91 us
    all_to_all x1 -> x0, blocking collectives: 17.9 us -> none  [send(): lax.all_to_all(fields, around, split_axis=0, concat_axis=0, tiled=True)]
    all_to_all x1 -> x2, waiting for transfers between devices: 11.9 us -> 24.1 us  [send(): lax.all_to_all(fields, around, split_axis=0, concat_axis=0, tiled=True)]
    ppermute x3, waiting for transfers between devices: 7.06 us -> 4.07 us  [swap(): return lax.ppermute(block, KA + GA, route)]
    unnamed x6, local copies, waits for them, and re-layouts: 0.01 us -> 0.68 us
    all_to_all x1 -> x2, starting transfers between devices: 10.3 us -> 10.1 us  [send(): lax.all_to_all(fields, around, split_axis=0, concat_axis=0, tiled=True)]
  transfers between devices with their start and end apart: 4 -> 5, of which waited for: 2 -> 4; matrix products, arithmetic and copies ran while one was open for 0% -> 1% of each run, Pallas kernels for 5% -> 6%
where the time goes in v37:
time: 52.8 us; the launch traced here: 51.9 us
  waiting for transfers between devices  28.1 us (53%)
  starting transfers between devices  15.6 us (30%)
  Pallas kernels  5.8 us (11%)
  local copies, waits for them, and re-layouts  1.91 us (4%)
    all_to_all x2, waiting for transfers between devices, send(): lax.all_to_all(fields, around, split_axis=0, concat_axis=0, tiled=True)  24.1 us
    all_to_all x2, starting transfers between devices, send(): lax.all_to_all(fields, around, split_axis=0, concat_axis=0, tiled=True)  10.1 us
    ppermute x3, starting transfers between devices, swap(): return lax.ppermute(block, KA + GA, route)  5.46 us
    ppermute x3, waiting for transfers between devices, swap(): return lax.ppermute(block, KA + GA, route)  4.07 us
    pallas_call x1, Pallas kernels, make_pairs(): pl.pallas_call(functools.partial(pair_kernel, 1.0 / math.sqrt(2 * half_k)...  2.11 us
    pallas_call x1, Pallas kernels, make_far(): pl.pallas_call(far_kernel, in_specs=[vmem] * (2 + len(slabs)), out_specs=...  1.55 us
    pallas_call x1, Pallas kernels, make_near(): pl.pallas_call(near_kernel, grid=(kdevice,), in_specs=[pl.BlockSpec((1, s...  1.53 us
    squeeze x1, local copies, waits for them, and re-layouts, on_device(): other = lax.dynamic_index_in_dim(orbitals, 1 - lo, 0, keepdims=False)  1.08 us
  transfers between devices with their start and end apart: 5, of which 4 were waited for; matrix products, arithmetic and copies ran while one was open for 1% of the time, Pallas kernels for 6%

profile of v37, /device:TPU:1, one launch (start us, length us, event | category | flops | bytes accessed | tf_op | source)
XLA Modules:
  0.0 51.9 jit_solution(16973935818711155160)
XLA Ops:
  0.0 0.0 copy-start.1
  0.0 1.1 %dynamic-slice_bitcast_fusion = (bf16[512,256]{1,0:T(8,128)(2,1)S(1)}, bf16[512,256]{1,0:T(8,128)(2,1)S(1)}) fusion(bf16[2,512,256]{2,1,0:T(8,128)(2,1)} %orbitals_ref.1, s32[]{:T(128)S(6)} %select_n.43, s32[]{:T(128)S(6)} %select_n.42), kind=kLoop, calls=%fused_computation | loop fusion | bytes 1048584 | tf_op jit(solution)/shard_map/jit(dynamic_index_in_dim)/squeeze | solution.py:260
  1.1 0.0 copy-start
  1.1 0.0 copy-done.1
  1.1 0.3 front.1.refs_0_
  1.4 2.1 %collective-permute-start = (bf16[2,256,256]{2,1,0:T(8,128)(2,1)S(1)}, bf16[2,256,256]{2,1,0:T(8,128)(2,1)S(1)}, u32[]{:S(2)}, u32[]{:S(2)}) collective-permute-start(bf16[2,256,256]{2,1,0:T(8,128)(2,1)S(1)} %front.1.refs_0_), channel_id=1, source_target_pairs={{0,1},{1,0},{2,3},{3,2},{4,5},{5,4},{6,7},{7,6},{8,9},{9,8},{10,11... | collective-permute-start | bytes 786440 | tf_op jit(solution)/shard_map/ppermute | solution.py:26
  3.6 3.3 %collective-permute-start.1 = (bf16[512,256]{1,0:T(8,128)(2,1)S(1)}, bf16[512,256]{1,0:T(8,128)(2,1)S(1)}, u32[]{:S(2)}, u32[]{:S(2)}) collective-permute-start(bf16[512,256]{1,0:T(8,128)(2,1)S(1)} %get-tuple-element.17.mine_ref), channel_id=1, source_target_pairs={{0,24},{1,25},{2,26},{3,27},{4,28},{5,29},{6,30},{7,31},{8,16},{9,... | collective-permute-start | bytes 786440 | tf_op jit(solution)/shard_map/ppermute | solution.py:26
  6.9 0.0 collective-permute-start.2
  6.9 0.1 pad_add_fusion.2
  7.0 0.1 dynamic_slice.17
  7.1 0.1 broadcast_subtract_fusion.rows_ref
  7.2 2.5 %collective-permute-done.refs_1_ = bf16[2,256,256]{2,1,0:T(8,128)(2,1)S(1)} collective-permute-done((bf16[2,256,256]{2,1,0:T(8,128)(2,1)S(1)}, bf16[2,256,256]{2,1,0:T(8,128)(2,1)S(1)}, u32[]{:S(2)}, u32[]{:S(2)}) %collective-permute-start) | collective-permute-done | bytes 262176 | tf_op jit(solution)/shard_map/ppermute | solution.py:26
  9.6 0.0 copy-done
  9.6 1.5 %near.1 = bf16[8,2,2,32,512]{4,3,2,1,0:T(8,128)(2,1)} custom-call(bf16[2,512,256]{2,1,0:T(8,128)(2,1)S(1)} %copy-done, bf16[2,256,256]{2,1,0:T(8,128)(2,1)S(1)} %front.1.refs_0_, bf16[2,256,256]{2,1,0:T(8,128)(2,1)S(1)} %collective-permute-done.refs_1_), custom_call_target="tpu_custom_call" | custom-call | flops 1000000000 | bytes 3000000 | tf_op jit(solution)/shard_map/near/pallas_call | solution.py:99
  11.2 5.2 %all-to-all-start = ((bf16[16,2,32,512]{3,2,1,0:T(8,128)(2,1)}), bf16[16,2,32,512]{3,2,1,0:T(8,128)(2,1)S(1)}, u32[]{:S(2)}, u32[]{:S(2)}) async-start(bf16[16,2,32,512]{3,2,1,0:T(8,128)(2,1)} %bitcast.5), calls=%async_computation | async-start | bytes 2097152 | tf_op jit(solution)/shard_map/all_to_all | solution.py:268
  16.4 0.0 collective-permute-done.1.slab_ref.refs_0_
  16.4 0.3 ahead.1
  16.7 1.6 %collective-permute-done.2.refs_1_ = bf16[512,256]{1,0:T(8,128)(2,1)S(1)} collective-permute-done((bf16[512,256]{1,0:T(8,128)(2,1)S(1)}, bf16[512,256]{1,0:T(8,128)(2,1)S(1)}, u32[]{:S(2)}, u32[]{:S(2)}) %collective-permute-start.2) | collective-permute-done | bytes 262176 | tf_op jit(solution)/shard_map/ppermute | solution.py:26
  18.3 1.5 %far.1 = bf16[2,8,2,32,512]{4,3,2,1,0:T(8,128)(2,1)} custom-call(bf16[256,256]{1,0:T(8,128)(2,1)S(1)} %get-tuple-element.18.picked_ref, bf16[1,256,512]{2,1,0:T(8,128)(2,1)S(1)} %get-tuple-element.19.chosen_ref, bf16[512,256]{1,0:T(8,128)(2,1)S(1)} %collective-permute-done.1.slab_ref.refs_0_, bf16[512,256]{1,0:T(8,128)(2,1)S(1)} %collective-permute-done.2.refs_1_), custom_call_target="tpu_custom_call" | custom-call | flops 60000002048 | bytes 180000000 | tf_op jit(solution)/shard_map/far/pallas_call | solution.py:165
  19.8 10.7 %all-to-all-done.near_ref = bf16[16,2,32,512]{3,2,1,0:T(8,128)(2,1)S(1)} async-done(((bf16[16,2,32,512]{3,2,1,0:T(8,128)(2,1)}), bf16[16,2,32,512]{3,2,1,0:T(8,128)(2,1)S(1)}, u32[]{:S(2)}, u32[]{:S(2)}) %all-to-all-start) | async-done | bytes 1048608 | tf_op jit(solution)/shard_map/all_to_all | solution.py:268
  30.5 4.9 %all-to-all-start.1 = ((bf16[16,2,32,512]{3,2,1,0:T(8,128)(2,1)}), bf16[16,2,32,512]{3,2,1,0:T(8,128)(2,1)S(1)}, u32[]{:S(2)}, u32[]{:S(2)}) async-start(bf16[16,2,32,512]{3,2,1,0:T(8,128)(2,1)} %bitcast.6), calls=%async_computation.1 | async-start | bytes 2097152 | tf_op jit(solution)/shard_map/all_to_all | solution.py:268
  35.4 0.0 copy-start.2
  35.4 0.7 %copy-done.2 = s32[2,32]{1,0:T(2,128)S(1)} copy-done((s32[2,32]{1,0:T(2,128)S(1)}, s32[2,32]{1,0:T(2,128)}, u32[]{:S(2)}) %copy-start.2) | copy-done | bytes 280
  36.1 0.1 pad_add_fusion
  36.2 0.1 compare_select_fusion
  36.3 0.1 fusion.3
  36.3 0.1 pad_add_fusion.1.table_ref
  36.4 13.4 %all-to-all-done.1.far_ref = bf16[16,2,32,512]{3,2,1,0:T(8,128)(2,1)S(1)} async-done(((bf16[16,2,32,512]{3,2,1,0:T(8,128)(2,1)}), bf16[16,2,32,512]{3,2,1,0:T(8,128)(2,1)S(1)}, u32[]{:S(2)}, u32[]{:S(2)}) %all-to-all-start.1) | async-done | bytes 1048608 | tf_op jit(solution)/shard_map/all_to_all | solution.py:268
  49.8 2.1 %pairs.1 = f32[32,2,2,512]{3,2,1,0:T(2,128)} custom-call(s32[2,32]{1,0:T(2,128)S(1)} %pad_add_fusion.1.table_ref, bf16[16,2,32,512]{3,2,1,0:T(8,128)(2,1)S(1)} %all-to-all-done.near_ref, bf16[16,2,32,512]{3,2,1,0:T(8,128)(2,1)S(1)} %all-to-all-done.1.far_ref), custom_call_target="tpu_custom_call" | custom-call | tf_op jit(solution)/shard_map/pairs/pallas_call | solution.py:234
Async XLA Ops:
  0.0 1.1 %copy-start.1 = (s32[512]{0:T(512)S(1)}, s32[512]{0:T(512)}, u32[]{:S(2)}) copy-start(s32[512]{0:T(512)} %param.5) | copy-start | bytes 6148
  1.1 8.5 %copy-start = (bf16[2,512,256]{2,1,0:T(8,128)(2,1)S(1)}, bf16[2,512,256]{2,1,0:T(8,128)(2,1)}, u32[]{:S(2)}) copy-start(bf16[2,512,256]{2,1,0:T(8,128)(2,1)} %orbitals_ref.1) | copy-start | bytes 1572868
  1.4 8.2 %collective-permute-start = (bf16[2,256,256]{2,1,0:T(8,128)(2,1)S(1)}, bf16[2,256,256]{2,1,0:T(8,128)(2,1)S(1)}, u32[]{:S(2)}, u32[]{:S(2)}) collective-permute-start(bf16[2,256,256]{2,1,0:T(8,128)(2,1)S(1)} %front.1.refs_0_), channel_id=1, source_target_pairs={{0,1},{1,0},{2,3},{3,2},{4,5},{5,4},{6,7},{7,6},{8,9},{9,8},{10,11... | collective-permute-start | bytes 786440 | tf_op jit(solution)/shard_map/ppermute | solution.py:26
  3.6 12.8 %collective-permute-start.1 = (bf16[512,256]{1,0:T(8,128)(2,1)S(1)}, bf16[512,256]{1,0:T(8,128)(2,1)S(1)}, u32[]{:S(2)}, u32[]{:S(2)}) collective-permute-start(bf16[512,256]{1,0:T(8,128)(2,1)S(1)} %get-tuple-element.17.mine_ref), channel_id=1, source_target_pairs={{0,24},{1,25},{2,26},{3,27},{4,28},{5,29},{6,30},{7,31},{8,16},{9,... | collective-permute-start | bytes 786440 | tf_op jit(solution)/shard_map/ppermute | solution.py:26
  6.9 11.4 %collective-permute-start.2 = (bf16[512,256]{1,0:T(8,128)(2,1)S(1)}, bf16[512,256]{1,0:T(8,128)(2,1)S(1)}, u32[]{:S(2)}, u32[]{:S(2)}) collective-permute-start(bf16[512,256]{1,0:T(8,128)(2,1)S(1)} %get-tuple-element.20.other_ref), channel_id=1, source_target_pairs={{0,25},{1,24},{2,27},{3,26},{4,29},{5,28},{6,31},{7,30},{8,17},{9,... | collective-permute-start | bytes 786440 | tf_op jit(solution)/shard_map/ppermute | solution.py:26
  11.2 19.4 %all-to-all-start = ((bf16[16,2,32,512]{3,2,1,0:T(8,128)(2,1)}), bf16[16,2,32,512]{3,2,1,0:T(8,128)(2,1)S(1)}, u32[]{:S(2)}, u32[]{:S(2)}) async-start(bf16[16,2,32,512]{3,2,1,0:T(8,128)(2,1)} %bitcast.5), calls=%async_computation | async-start | bytes 2097152 | tf_op jit(solution)/shard_map/all_to_all | solution.py:268
  30.5 19.3 %all-to-all-start.1 = ((bf16[16,2,32,512]{3,2,1,0:T(8,128)(2,1)}), bf16[16,2,32,512]{3,2,1,0:T(8,128)(2,1)S(1)}, u32[]{:S(2)}, u32[]{:S(2)}) async-start(bf16[16,2,32,512]{3,2,1,0:T(8,128)(2,1)} %bitcast.6), calls=%async_computation.1 | async-start | bytes 2097152 | tf_op jit(solution)/shard_map/all_to_all | solution.py:268
  35.4 0.7 %copy-start.2 = (s32[2,32]{1,0:T(2,128)S(1)}, s32[2,32]{1,0:T(2,128)}, u32[]{:S(2)}) copy-start(s32[2,32]{1,0:T(2,128)} %param.4) | copy-start | bytes 772

commit v38 on v36

--- a/solution.py
+++ b/solution.py
@@ -104,7 +104,7 @@
         out_specs=pl.BlockSpec((groups, 1, 2, length, slab_size), lambda k: (0, k, 0, 0, 0)),
         out_shape=jax.ShapeDtypeStruct((groups, kdevice, 2, length, slab_size), jnp.bfloat16),
         cost_estimate=pl.CostEstimate(
-            flops=1_000_000_000, bytes_accessed=3_000_000, transcendentals=0
+            flops=3_000_000_000, bytes_accessed=9_000_000, transcendentals=0
         ),
         compiler_params=pltpu.CompilerParams(vmem_limit_bytes=VMEM_LIMIT),
         name="near",

time: 59.9 us -> 59.9 us (level)
  no operation moved by 1% of the time
where the time goes in v38:
time: 59.9 us; the launch traced here: 59.6 us
  waiting for transfers between devices  19 us (32%)
  blocking collectives  17.9 us (30%)
  starting transfers between devices  15.7 us (26%)
  Pallas kernels  5.6 us (9%)
  local copies, waits for them, and re-layouts  1.16 us (2%)
    all_to_all x1, blocking collectives, send(): lax.all_to_all(fields, around, split_axis=0, concat_axis=0, tiled=True)  17.9 us
    all_to_all x1, waiting for transfers between devices, send(): lax.all_to_all(fields, around, split_axis=0, concat_axis=0, tiled=True)  11.9 us
    all_to_all x1, starting transfers between devices, send(): lax.all_to_all(fields, around, split_axis=0, concat_axis=0, tiled=True)  10.3 us
    ppermute x3, waiting for transfers between devices, swap(): return lax.ppermute(block, KA + GA, route)  7.06 us
    ppermute x3, starting transfers between devices, swap(): return lax.ppermute(block, KA + GA, route)  5.48 us
    pallas_call x1, Pallas kernels, make_pairs(): pl.pallas_call(functools.partial(pair_kernel, 1.0 / math.sqrt(2 * half_k)...  2.12 us
    pallas_call x1, Pallas kernels, make_near(): pl.pallas_call(near_kernel, grid=(kdevice,), in_specs=[pl.BlockSpec((1, s...  1.48 us
    pallas_call x1, Pallas kernels, make_far(): pl.pallas_call(far_kernel, in_specs=[vmem] * (2 + len(slabs)), out_specs=...  1.39 us
  transfers between devices with their start and end apart: 4, of which 2 were waited for; matrix products, arithmetic and copies ran while one was open for 0% of the time, Pallas kernels for 5%

profile of v38, /device:TPU:1, one launch (start us, length us, event | category | flops | bytes accessed | tf_op | source)
XLA Modules:
  0.0 59.6 jit_solution(8044235173630714582)
XLA Ops:
  0.0 0.0 copy-start.1
  0.0 1.1 %dynamic-slice_bitcast_fusion = (bf16[512,256]{1,0:T(8,128)(2,1)S(1)}, bf16[512,256]{1,0:T(8,128)(2,1)S(1)}) fusion(bf16[2,512,256]{2,1,0:T(8,128)(2,1)} %orbitals_ref.1, s32[]{:T(128)S(6)} %select_n.11, s32[]{:T(128)S(6)} %select_n.10), kind=kLoop, calls=%fused_computation | loop fusion | bytes 1048584 | tf_op jit(solution)/shard_map/jit(dynamic_index_in_dim)/squeeze | solution.py:256
  1.1 0.0 copy-start
  1.1 0.0 copy-done.1
  1.1 0.3 front.1.refs_0_
  1.4 4.2 %collective-permute-start.1 = (bf16[512,256]{1,0:T(8,128)(2,1)S(1)}, bf16[512,256]{1,0:T(8,128)(2,1)S(1)}, u32[]{:S(2)}, u32[]{:S(2)}) collective-permute-start(bf16[512,256]{1,0:T(8,128)(2,1)S(1)} %get-tuple-element.17.mine_ref), channel_id=1, source_target_pairs={{0,24},{1,25},{2,26},{3,27},{4,28},{5,29},{6,30},{7,31},{8,16},{9,... | collective-permute-start | bytes 786440 | tf_op jit(solution)/shard_map/ppermute | solution.py:26
  5.7 1.0 %collective-permute-start.2 = (bf16[512,256]{1,0:T(8,128)(2,1)S(1)}, bf16[512,256]{1,0:T(8,128)(2,1)S(1)}, u32[]{:S(2)}, u32[]{:S(2)}) collective-permute-start(bf16[512,256]{1,0:T(8,128)(2,1)S(1)} %get-tuple-element.20.other_ref), channel_id=1, source_target_pairs={{0,25},{1,24},{2,27},{3,26},{4,29},{5,28},{6,31},{7,30},{8,17},{9,... | collective-permute-start | bytes 786440 | tf_op jit(solution)/shard_map/ppermute | solution.py:26
  6.7 0.2 collective-permute-start
  6.9 0.1 pad_add_fusion
  7.0 0.1 dynamic_slice.12
  7.1 0.1 broadcast_subtract_fusion.rows_ref
  7.2 7.1 %collective-permute-done.refs_1_ = bf16[2,256,256]{2,1,0:T(8,128)(2,1)S(1)} collective-permute-done((bf16[2,256,256]{2,1,0:T(8,128)(2,1)S(1)}, bf16[2,256,256]{2,1,0:T(8,128)(2,1)S(1)}, u32[]{:S(2)}, u32[]{:S(2)}) %collective-permute-start) | collective-permute-done | bytes 262176 | tf_op jit(solution)/shard_map/ppermute | solution.py:26
  14.2 0.0 copy-done
  14.2 1.5 %near.1 = bf16[8,2,2,32,512]{4,3,2,1,0:T(8,128)(2,1)} custom-call(bf16[2,512,256]{2,1,0:T(8,128)(2,1)S(1)} %copy-done, bf16[2,256,256]{2,1,0:T(8,128)(2,1)S(1)} %front.1.refs_0_, bf16[2,256,256]{2,1,0:T(8,128)(2,1)S(1)} %collective-permute-done.refs_1_), custom_call_target="tpu_custom_call" | custom-call | flops 3000000000 | bytes 9000000 | tf_op jit(solution)/shard_map/near/pallas_call | solution.py:99
  15.7 10.3 %all-to-all-start = ((bf16[16,2,32,512]{3,2,1,0:T(8,128)(2,1)}), bf16[16,2,32,512]{3,2,1,0:T(8,128)(2,1)S(1)}, u32[]{:S(2)}, u32[]{:S(2)}) async-start(bf16[16,2,32,512]{3,2,1,0:T(8,128)(2,1)} %bitcast.5), calls=%async_computation | async-start | bytes 2097152 | tf_op jit(solution)/shard_map/all_to_all | solution.py:264
  26.0 0.0 collective-permute-done.1.slab_ref.refs_0_
  26.0 0.3 ahead.1
  26.3 0.0 collective-permute-done.2.refs_1_
  26.3 1.4 %far.1 = bf16[2,8,2,32,512]{4,3,2,1,0:T(8,128)(2,1)S(1)} custom-call(bf16[256,256]{1,0:T(8,128)(2,1)S(1)} %get-tuple-element.18.picked_ref, bf16[1,256,512]{2,1,0:T(8,128)(2,1)S(1)} %get-tuple-element.19.chosen_ref, bf16[512,256]{1,0:T(8,128)(2,1)S(1)} %collective-permute-done.1.slab_ref.refs_0_, bf16[512,256]{1,0:T(8,128)(2,1)S(1)} %collective-permute-done.2.refs_1_), custom_call_target="tpu_custom_call" | custom-call | flops 60000002048 | bytes 180000000 | tf_op jit(solution)/shard_map/far/pallas_call | solution.py:165
  27.7 11.9 %all-to-all-done.near_ref = bf16[16,2,32,512]{3,2,1,0:T(8,128)(2,1)S(1)} async-done(((bf16[16,2,32,512]{3,2,1,0:T(8,128)(2,1)}), bf16[16,2,32,512]{3,2,1,0:T(8,128)(2,1)S(1)}, u32[]{:S(2)}, u32[]{:S(2)}) %all-to-all-start) | async-done | bytes 1048608 | tf_op jit(solution)/shard_map/all_to_all | solution.py:264
  39.6 0.0 copy-start.2
  39.6 17.9 %all_to_all.10.far_ref = bf16[16,2,32,512]{3,2,1,0:T(8,128)(2,1)S(1)} all-to-all(bf16[16,2,32,512]{3,2,1,0:T(8,128)(2,1)S(1)} %bitcast.9), channel_id=1, replica_groups=mesh['half'=2,'quarter'=2,'inner'=4,'hi'=1,'lo'=2] {'lo','inner','quarter'}, dimensions={0} | all-to-all | bytes 2097152 | tf_op jit(solution)/shard_map/all_to_all | solution.py:264
  57.5 0.0 copy-done.2
  57.5 2.1 %pairs.1 = f32[32,2,2,512]{3,2,1,0:T(2,128)} custom-call(s32[2,32]{1,0:T(2,128)S(1)} %copy-done.2, bf16[16,2,32,512]{3,2,1,0:T(8,128)(2,1)S(1)} %all-to-all-done.near_ref, bf16[16,2,32,512]{3,2,1,0:T(8,128)(2,1)S(1)} %all_to_all.10.far_ref), custom_call_target="tpu_custom_call" | custom-call | tf_op jit(solution)/shard_map/pairs/pallas_call | solution.py:230
Async XLA Ops:
  0.0 1.1 %copy-start.1 = (s32[512]{0:T(512)S(1)}, s32[512]{0:T(512)}, u32[]{:S(2)}) copy-start(s32[512]{0:T(512)} %param.5) | copy-start | bytes 6148
  1.1 13.2 %copy-start = (bf16[2,512,256]{2,1,0:T(8,128)(2,1)S(1)}, bf16[2,512,256]{2,1,0:T(8,128)(2,1)}, u32[]{:S(2)}) copy-start(bf16[2,512,256]{2,1,0:T(8,128)(2,1)} %orbitals_ref.1) | copy-start | bytes 1572868
  1.4 24.5 %collective-permute-start.1 = (bf16[512,256]{1,0:T(8,128)(2,1)S(1)}, bf16[512,256]{1,0:T(8,128)(2,1)S(1)}, u32[]{:S(2)}, u32[]{:S(2)}) collective-permute-start(bf16[512,256]{1,0:T(8,128)(2,1)S(1)} %get-tuple-element.17.mine_ref), channel_id=1, source_target_pairs={{0,24},{1,25},{2,26},{3,27},{4,28},{5,29},{6,30},{7,31},{8,16},{9,... | collective-permute-start | bytes 786440 | tf_op jit(solution)/shard_map/ppermute | solution.py:26
  5.7 20.6 %collective-permute-start.2 = (bf16[512,256]{1,0:T(8,128)(2,1)S(1)}, bf16[512,256]{1,0:T(8,128)(2,1)S(1)}, u32[]{:S(2)}, u32[]{:S(2)}) collective-permute-start(bf16[512,256]{1,0:T(8,128)(2,1)S(1)} %get-tuple-element.20.other_ref), channel_id=1, source_target_pairs={{0,25},{1,24},{2,27},{3,26},{4,29},{5,28},{6,31},{7,30},{8,17},{9,... | collective-permute-start | bytes 786440 | tf_op jit(solution)/shard_map/ppermute | solution.py:26
  6.7 7.5 %collective-permute-start = (bf16[2,256,256]{2,1,0:T(8,128)(2,1)S(1)}, bf16[2,256,256]{2,1,0:T(8,128)(2,1)S(1)}, u32[]{:S(2)}, u32[]{:S(2)}) collective-permute-start(bf16[2,256,256]{2,1,0:T(8,128)(2,1)S(1)} %front.1.refs_0_), channel_id=1, source_target_pairs={{0,1},{1,0},{2,3},{3,2},{4,5},{5,4},{6,7},{7,6},{8,9},{9,8},{10,11... | collective-permute-start | bytes 786440 | tf_op jit(solution)/shard_map/ppermute | solution.py:26
  15.7 23.9 %all-to-all-start = ((bf16[16,2,32,512]{3,2,1,0:T(8,128)(2,1)}), bf16[16,2,32,512]{3,2,1,0:T(8,128)(2,1)S(1)}, u32[]{:S(2)}, u32[]{:S(2)}) async-start(bf16[16,2,32,512]{3,2,1,0:T(8,128)(2,1)} %bitcast.5), calls=%async_computation | async-start | bytes 2097152 | tf_op jit(solution)/shard_map/all_to_all | solution.py:264
  39.6 17.9 %copy-start.2 = (s32[2,32]{1,0:T(2,128)S(1)}, s32[2,32]{1,0:T(2,128)}, u32[]{:S(2)}) copy-start(s32[2,32]{1,0:T(2,128)} %table_ref.1) | copy-start | bytes 772

commit v39 on v37

--- a/solution.py
+++ b/solution.py
@@ -274,10 +274,6 @@
     rows = wanted[:, None] - starts[None, :]
     near_fields, rows = lax.optimization_barrier((near_fields, rows))
     far_fields = make_far(rows, far, groups)
-    near_fields = send(near_fields, ("quarter", "inner"))
-    near_fields, far_fields = lax.optimization_barrier((near_fields, far_fields))
-    far_fields = send(far_fields, ("lo", "inner", "quarter"))
-
     def mirrored(kpoints):
         return total_k // 2 + (kpoints + total_k // 4) % (total_k // 2)
 
@@ -285,7 +281,12 @@
     table = (jnp.roll(minus_table, -turn, axis=1) - turn) % total_k
     table = jnp.where(table < total_k // 2, table, mirrored(table))
     first, third, fourth = jnp.split(table, (total_k // 2, 3 * total_k // 4), axis=1)
-    return make_pairs(near_fields, far_fields, jnp.concatenate([first, fourth, third], axis=1))
+    table = jnp.concatenate([first, fourth, third], axis=1)
+
+    near_fields = send(near_fields, ("quarter", "inner"))
+    near_fields, far_fields, table = lax.optimization_barrier((near_fields, far_fields, table))
+    far_fields = send(far_fields, ("lo", "inner", "quarter"))
+    return make_pairs(near_fields, far_fields, table)
 
 
 def solution(mesh):

time: 52.8 us -> 59.8 us (1.13)
  blocking collectives: 0 us -> 17.7 us
  waiting for transfers between devices: 28.1 us -> 18.1 us
    all_to_all x0 -> x1, blocking collectives: none -> 17.7 us  [send(): lax.all_to_all(fields, around, split_axis=0, concat_axis=0, tiled=True)]
    all_to_all x2 -> x1, waiting for transfers between devices: 24.1 us -> 11.9 us  [send(): lax.all_to_all(fields, around, split_axis=0, concat_axis=0, tiled=True)]
    ppermute x3, waiting for transfers between devices: 4.07 us -> 6.14 us  [swap(): return lax.ppermute(block, KA + GA, route)]
    all_to_all x2 -> x1, starting transfers between devices: 10.1 us -> 10.3 us  [send(): lax.all_to_all(fields, around, split_axis=0, concat_axis=0, tiled=True)]
  transfers between devices with their start and end apart: 5 -> 4, of which waited for: 4 -> 2; matrix products, arithmetic and copies ran while one was open for 1% -> 1% of each run, Pallas kernels for 6% -> 5%
where the time goes in v39:
time: 59.8 us; the launch traced here: 59.5 us
  waiting for transfers between devices  18.1 us (30%)
  blocking collectives  17.7 us (30%)
  starting transfers between devices  15.7 us (26%)
  Pallas kernels  5.61 us (9%)
  local copies, waits for them, and re-layouts  1.84 us (3%)
    all_to_all x1, blocking collectives, send(): lax.all_to_all(fields, around, split_axis=0, concat_axis=0, tiled=True)  17.7 us
    all_to_all x1, waiting for transfers between devices, send(): lax.all_to_all(fields, around, split_axis=0, concat_axis=0, tiled=True)  11.9 us
    all_to_all x1, starting transfers between devices, send(): lax.all_to_all(fields, around, split_axis=0, concat_axis=0, tiled=True)  10.3 us
    ppermute x3, waiting for transfers between devices, swap(): return lax.ppermute(block, KA + GA, route)  6.14 us
    ppermute x3, starting transfers between devices, swap(): return lax.ppermute(block, KA + GA, route)  5.48 us
    pallas_call x1, Pallas kernels, make_pairs(): pl.pallas_call(functools.partial(pair_kernel, 1.0 / math.sqrt(2 * half_k)...  2.11 us
    pallas_call x1, Pallas kernels, make_near(): pl.pallas_call(near_kernel, grid=(kdevice,), in_specs=[pl.BlockSpec((1, s...  1.5 us
    pallas_call x1, Pallas kernels, make_far(): pl.pallas_call(far_kernel, in_specs=[vmem] * (2 + len(slabs)), out_specs=...  1.39 us
  transfers between devices with their start and end apart: 4, of which 2 were waited for; matrix products, arithmetic and copies ran while one was open for 1% of the time, Pallas kernels for 5%

profile of v39, /device:TPU:1, one launch (start us, length us, event | category | flops | bytes accessed | tf_op | source)
XLA Modules:
  0.0 59.5 jit_solution(7533169450340876499)
XLA Ops:
  0.0 0.0 copy-start.1
  0.0 1.1 %dynamic-slice_bitcast_fusion = (bf16[512,256]{1,0:T(8,128)(2,1)S(1)}, bf16[512,256]{1,0:T(8,128)(2,1)S(1)}) fusion(bf16[2,512,256]{2,1,0:T(8,128)(2,1)} %orbitals_ref.1, s32[]{:T(128)S(6)} %select_n.38, s32[]{:T(128)S(6)} %select_n.37), kind=kLoop, calls=%fused_computation | loop fusion | bytes 1048584 | tf_op jit(solution)/shard_map/jit(dynamic_index_in_dim)/squeeze | solution.py:260
  1.1 0.0 copy-start
  1.1 0.0 copy-done.1
  1.1 0.3 front.1.refs_0_
  1.4 4.2 %collective-permute-start.1 = (bf16[512,256]{1,0:T(8,128)(2,1)S(1)}, bf16[512,256]{1,0:T(8,128)(2,1)S(1)}, u32[]{:S(2)}, u32[]{:S(2)}) collective-permute-start(bf16[512,256]{1,0:T(8,128)(2,1)S(1)} %get-tuple-element.18.mine_ref), channel_id=1, source_target_pairs={{0,24},{1,25},{2,26},{3,27},{4,28},{5,29},{6,30},{7,31},{8,16},{9,... | collective-permute-start | bytes 786440 | tf_op jit(solution)/shard_map/ppermute | solution.py:26
  5.7 1.0 %collective-permute-start.2 = (bf16[512,256]{1,0:T(8,128)(2,1)S(1)}, bf16[512,256]{1,0:T(8,128)(2,1)S(1)}, u32[]{:S(2)}, u32[]{:S(2)}) collective-permute-start(bf16[512,256]{1,0:T(8,128)(2,1)S(1)} %get-tuple-element.21.other_ref), channel_id=1, source_target_pairs={{0,25},{1,24},{2,27},{3,26},{4,29},{5,28},{6,31},{7,30},{8,17},{9,... | collective-permute-start | bytes 786440 | tf_op jit(solution)/shard_map/ppermute | solution.py:26
  6.7 0.2 collective-permute-start
  6.9 0.0 copy-start.2
  6.9 0.1 dynamic_slice.16
  7.0 0.6 %copy-done.2 = s32[2,32]{1,0:T(2,128)S(1)} copy-done((s32[2,32]{1,0:T(2,128)S(1)}, s32[2,32]{1,0:T(2,128)}, u32[]{:S(2)}) %copy-start.2) | copy-done | bytes 280
  7.6 0.1 pad_add_fusion
  7.7 0.1 pad_add_fusion.2
  7.8 0.1 compare_select_fusion
  7.8 0.1 broadcast_subtract_fusion.rows_ref
  7.9 0.1 fusion.3
  8.0 0.1 pad_add_fusion.1.table_ref
  8.1 6.1 %collective-permute-done.refs_1_ = bf16[2,256,256]{2,1,0:T(8,128)(2,1)S(1)} collective-permute-done((bf16[2,256,256]{2,1,0:T(8,128)(2,1)S(1)}, bf16[2,256,256]{2,1,0:T(8,128)(2,1)S(1)}, u32[]{:S(2)}, u32[]{:S(2)}) %collective-permute-start) | collective-permute-done | bytes 262176 | tf_op jit(solution)/shard_map/ppermute | solution.py:26
  14.2 0.0 copy-done
  14.2 1.5 %near.1 = bf16[8,2,2,32,512]{4,3,2,1,0:T(8,128)(2,1)} custom-call(bf16[2,512,256]{2,1,0:T(8,128)(2,1)S(1)} %copy-done, bf16[2,256,256]{2,1,0:T(8,128)(2,1)S(1)} %front.1.refs_0_, bf16[2,256,256]{2,1,0:T(8,128)(2,1)S(1)} %collective-permute-done.refs_1_), custom_call_target="tpu_custom_call" | custom-call | flops 1000000000 | bytes 3000000 | tf_op jit(solution)/shard_map/near/pallas_call | solution.py:99
  15.7 10.3 %all-to-all-start = ((bf16[16,2,32,512]{3,2,1,0:T(8,128)(2,1)}), bf16[16,2,32,512]{3,2,1,0:T(8,128)(2,1)S(1)}, u32[]{:S(2)}, u32[]{:S(2)}) async-start(bf16[16,2,32,512]{3,2,1,0:T(8,128)(2,1)} %bitcast.5), calls=%async_computation | async-start | bytes 2097152 | tf_op jit(solution)/shard_map/all_to_all | solution.py:268
  26.0 0.0 collective-permute-done.1.slab_ref.refs_0_
  26.0 0.3 ahead.1
  26.3 0.0 collective-permute-done.2.refs_1_
  26.3 1.4 %far.1 = bf16[2,8,2,32,512]{4,3,2,1,0:T(8,128)(2,1)S(1)} custom-call(bf16[256,256]{1,0:T(8,128)(2,1)S(1)} %get-tuple-element.19.picked_ref, bf16[1,256,512]{2,1,0:T(8,128)(2,1)S(1)} %get-tuple-element.20.chosen_ref, bf16[512,256]{1,0:T(8,128)(2,1)S(1)} %collective-permute-done.1.slab_ref.refs_0_, bf16[512,256]{1,0:T(8,128)(2,1)S(1)} %collective-permute-done.2.refs_1_), custom_call_target="tpu_custom_call" | custom-call | flops 60000002048 | bytes 180000000 | tf_op jit(solution)/shard_map/far/pallas_call | solution.py:165
  27.7 11.9 %all-to-all-done.near_ref = bf16[16,2,32,512]{3,2,1,0:T(8,128)(2,1)S(1)} async-done(((bf16[16,2,32,512]{3,2,1,0:T(8,128)(2,1)}), bf16[16,2,32,512]{3,2,1,0:T(8,128)(2,1)S(1)}, u32[]{:S(2)}, u32[]{:S(2)}) %all-to-all-start) | async-done | bytes 1048608 | tf_op jit(solution)/shard_map/all_to_all | solution.py:268
  39.6 17.7 %all_to_all.10.far_ref = bf16[16,2,32,512]{3,2,1,0:T(8,128)(2,1)S(1)} all-to-all(bf16[16,2,32,512]{3,2,1,0:T(8,128)(2,1)S(1)} %bitcast.10), channel_id=1, replica_groups=mesh['half'=2,'quarter'=2,'inner'=4,'hi'=1,'lo'=2] {'lo','inner','quarter'}, dimensions={0} | all-to-all | bytes 2097152 | tf_op jit(solution)/shard_map/all_to_all | solution.py:268
  57.4 2.1 %pairs.1 = f32[32,2,2,512]{3,2,1,0:T(2,128)} custom-call(s32[2,32]{1,0:T(2,128)S(1)} %pad_add_fusion.1.table_ref, bf16[16,2,32,512]{3,2,1,0:T(8,128)(2,1)S(1)} %all-to-all-done.near_ref, bf16[16,2,32,512]{3,2,1,0:T(8,128)(2,1)S(1)} %all_to_all.10.far_ref), custom_call_target="tpu_custom_call" | custom-call | tf_op jit(solution)/shard_map/pairs/pallas_call | solution.py:234
Async XLA Ops:
  0.0 1.1 %copy-start.1 = (s32[512]{0:T(512)S(1)}, s32[512]{0:T(512)}, u32[]{:S(2)}) copy-start(s32[512]{0:T(512)} %param.5) | copy-start | bytes 6148
  1.1 13.2 %copy-start = (bf16[2,512,256]{2,1,0:T(8,128)(2,1)S(1)}, bf16[2,512,256]{2,1,0:T(8,128)(2,1)}, u32[]{:S(2)}) copy-start(bf16[2,512,256]{2,1,0:T(8,128)(2,1)} %orbitals_ref.1) | copy-start | bytes 1572868
  1.4 24.6 %collective-permute-start.1 = (bf16[512,256]{1,0:T(8,128)(2,1)S(1)}, bf16[512,256]{1,0:T(8,128)(2,1)S(1)}, u32[]{:S(2)}, u32[]{:S(2)}) collective-permute-start(bf16[512,256]{1,0:T(8,128)(2,1)S(1)} %get-tuple-element.18.mine_ref), channel_id=1, source_target_pairs={{0,24},{1,25},{2,26},{3,27},{4,28},{5,29},{6,30},{7,31},{8,16},{9,... | collective-permute-start | bytes 786440 | tf_op jit(solution)/shard_map/ppermute | solution.py:26
  5.7 20.6 %collective-permute-start.2 = (bf16[512,256]{1,0:T(8,128)(2,1)S(1)}, bf16[512,256]{1,0:T(8,128)(2,1)S(1)}, u32[]{:S(2)}, u32[]{:S(2)}) collective-permute-start(bf16[512,256]{1,0:T(8,128)(2,1)S(1)} %get-tuple-element.21.other_ref), channel_id=1, source_target_pairs={{0,25},{1,24},{2,27},{3,26},{4,29},{5,28},{6,31},{7,30},{8,17},{9,... | collective-permute-start | bytes 786440 | tf_op jit(solution)/shard_map/ppermute | solution.py:26
  6.7 7.5 %collective-permute-start = (bf16[2,256,256]{2,1,0:T(8,128)(2,1)S(1)}, bf16[2,256,256]{2,1,0:T(8,128)(2,1)S(1)}, u32[]{:S(2)}, u32[]{:S(2)}) collective-permute-start(bf16[2,256,256]{2,1,0:T(8,128)(2,1)S(1)} %front.1.refs_0_), channel_id=1, source_target_pairs={{0,1},{1,0},{2,3},{3,2},{4,5},{5,4},{6,7},{7,6},{8,9},{9,8},{10,11... | collective-permute-start | bytes 786440 | tf_op jit(solution)/shard_map/ppermute | solution.py:26
  6.9 0.7 %copy-start.2 = (s32[2,32]{1,0:T(2,128)S(1)}, s32[2,32]{1,0:T(2,128)}, u32[]{:S(2)}) copy-start(s32[2,32]{1,0:T(2,128)} %param.4) | copy-start | bytes 772
  15.7 23.9 %all-to-all-start = ((bf16[16,2,32,512]{3,2,1,0:T(8,128)(2,1)}), bf16[16,2,32,512]{3,2,1,0:T(8,128)(2,1)S(1)}, u32[]{:S(2)}, u32[]{:S(2)}) async-start(bf16[16,2,32,512]{3,2,1,0:T(8,128)(2,1)} %bitcast.5), calls=%async_computation | async-start | bytes 2097152 | tf_op jit(solution)/shard_map/all_to_all | solution.py:268

commit v40 on v38

--- a/solution.py
+++ b/solution.py
@@ -104,7 +104,7 @@
         out_specs=pl.BlockSpec((groups, 1, 2, length, slab_size), lambda k: (0, k, 0, 0, 0)),
         out_shape=jax.ShapeDtypeStruct((groups, kdevice, 2, length, slab_size), jnp.bfloat16),
         cost_estimate=pl.CostEstimate(
-            flops=3_000_000_000, bytes_accessed=9_000_000, transcendentals=0
+            flops=10_000_000_000, bytes_accessed=30_000_000, transcendentals=0
         ),
         compiler_params=pltpu.CompilerParams(vmem_limit_bytes=VMEM_LIMIT),
         name="near",

time: 59.9 us -> 59.9 us (level)
  no operation moved by 1% of the time
where the time goes in v40:
time: 59.9 us; the launch traced here: 59.6 us
  waiting for transfers between devices  19 us (32%)
  blocking collectives  17.9 us (30%)
  starting transfers between devices  15.7 us (26%)
  Pallas kernels  5.6 us (9%)
  local copies, waits for them, and re-layouts  1.16 us (2%)
    all_to_all x1, blocking collectives, send(): lax.all_to_all(fields, around, split_axis=0, concat_axis=0, tiled=True)  17.9 us
    all_to_all x1, waiting for transfers between devices, send(): lax.all_to_all(fields, around, split_axis=0, concat_axis=0, tiled=True)  11.9 us
    all_to_all x1, starting transfers between devices, send(): lax.all_to_all(fields, around, split_axis=0, concat_axis=0, tiled=True)  10.3 us
    ppermute x3, waiting for transfers between devices, swap(): return lax.ppermute(block, KA + GA, route)  7.06 us
    ppermute x3, starting transfers between devices, swap(): return lax.ppermute(block, KA + GA, route)  5.48 us
    pallas_call x1, Pallas kernels, make_pairs(): pl.pallas_call(functools.partial(pair_kernel, 1.0 / math.sqrt(2 * half_k)...  2.12 us
    pallas_call x1, Pallas kernels, make_near(): pl.pallas_call(near_kernel, grid=(kdevice,), in_specs=[pl.BlockSpec((1, s...  1.48 us
    pallas_call x1, Pallas kernels, make_far(): pl.pallas_call(far_kernel, in_specs=[vmem] * (2 + len(slabs)), out_specs=...  1.39 us
  transfers between devices with their start and end apart: 4, of which 2 were waited for; matrix products, arithmetic and copies ran while one was open for 0% of the time, Pallas kernels for 5%

profile of v40, /device:TPU:1, one launch (start us, length us, event | category | flops | bytes accessed | tf_op | source)
XLA Modules:
  0.0 59.6 jit_solution(8044235173630714582)
XLA Ops:
  0.0 0.0 copy-start.1
  0.0 1.1 %dynamic-slice_bitcast_fusion = (bf16[512,256]{1,0:T(8,128)(2,1)S(1)}, bf16[512,256]{1,0:T(8,128)(2,1)S(1)}) fusion(bf16[2,512,256]{2,1,0:T(8,128)(2,1)} %orbitals_ref.1, s32[]{:T(128)S(6)} %select_n.11, s32[]{:T(128)S(6)} %select_n.10), kind=kLoop, calls=%fused_computation | loop fusion | bytes 1048584 | tf_op jit(solution)/shard_map/jit(dynamic_index_in_dim)/squeeze | solution.py:256
  1.1 0.0 copy-start
  1.1 0.0 copy-done.1
  1.1 0.3 front.1.refs_0_
  1.4 4.2 %collective-permute-start.1 = (bf16[512,256]{1,0:T(8,128)(2,1)S(1)}, bf16[512,256]{1,0:T(8,128)(2,1)S(1)}, u32[]{:S(2)}, u32[]{:S(2)}) collective-permute-start(bf16[512,256]{1,0:T(8,128)(2,1)S(1)} %get-tuple-element.17.mine_ref), channel_id=1, source_target_pairs={{0,24},{1,25},{2,26},{3,27},{4,28},{5,29},{6,30},{7,31},{8,16},{9,... | collective-permute-start | bytes 786440 | tf_op jit(solution)/shard_map/ppermute | solution.py:26
  5.7 1.0 %collective-permute-start.2 = (bf16[512,256]{1,0:T(8,128)(2,1)S(1)}, bf16[512,256]{1,0:T(8,128)(2,1)S(1)}, u32[]{:S(2)}, u32[]{:S(2)}) collective-permute-start(bf16[512,256]{1,0:T(8,128)(2,1)S(1)} %get-tuple-element.20.other_ref), channel_id=1, source_target_pairs={{0,25},{1,24},{2,27},{3,26},{4,29},{5,28},{6,31},{7,30},{8,17},{9,... | collective-permute-start | bytes 786440 | tf_op jit(solution)/shard_map/ppermute | solution.py:26
  6.7 0.2 collective-permute-start
  6.9 0.1 pad_add_fusion
  7.0 0.1 dynamic_slice.12
  7.1 0.1 broadcast_subtract_fusion.rows_ref
  7.2 7.1 %collective-permute-done.refs_1_ = bf16[2,256,256]{2,1,0:T(8,128)(2,1)S(1)} collective-permute-done((bf16[2,256,256]{2,1,0:T(8,128)(2,1)S(1)}, bf16[2,256,256]{2,1,0:T(8,128)(2,1)S(1)}, u32[]{:S(2)}, u32[]{:S(2)}) %collective-permute-start) | collective-permute-done | bytes 262176 | tf_op jit(solution)/shard_map/ppermute | solution.py:26
  14.2 0.0 copy-done
  14.2 1.5 %near.1 = bf16[8,2,2,32,512]{4,3,2,1,0:T(8,128)(2,1)} custom-call(bf16[2,512,256]{2,1,0:T(8,128)(2,1)S(1)} %copy-done, bf16[2,256,256]{2,1,0:T(8,128)(2,1)S(1)} %front.1.refs_0_, bf16[2,256,256]{2,1,0:T(8,128)(2,1)S(1)} %collective-permute-done.refs_1_), custom_call_target="tpu_custom_call" | custom-call | flops 10000000000 | bytes 30000000 | tf_op jit(solution)/shard_map/near/pallas_call | solution.py:99
  15.7 10.3 %all-to-all-start = ((bf16[16,2,32,512]{3,2,1,0:T(8,128)(2,1)}), bf16[16,2,32,512]{3,2,1,0:T(8,128)(2,1)S(1)}, u32[]{:S(2)}, u32[]{:S(2)}) async-start(bf16[16,2,32,512]{3,2,1,0:T(8,128)(2,1)} %bitcast.5), calls=%async_computation | async-start | bytes 2097152 | tf_op jit(solution)/shard_map/all_to_all | solution.py:264
  26.0 0.0 collective-permute-done.1.slab_ref.refs_0_
  26.0 0.3 ahead.1
  26.3 0.0 collective-permute-done.2.refs_1_
  26.3 1.4 %far.1 = bf16[2,8,2,32,512]{4,3,2,1,0:T(8,128)(2,1)S(1)} custom-call(bf16[256,256]{1,0:T(8,128)(2,1)S(1)} %get-tuple-element.18.picked_ref, bf16[1,256,512]{2,1,0:T(8,128)(2,1)S(1)} %get-tuple-element.19.chosen_ref, bf16[512,256]{1,0:T(8,128)(2,1)S(1)} %collective-permute-done.1.slab_ref.refs_0_, bf16[512,256]{1,0:T(8,128)(2,1)S(1)} %collective-permute-done.2.refs_1_), custom_call_target="tpu_custom_call" | custom-call | flops 60000002048 | bytes 180000000 | tf_op jit(solution)/shard_map/far/pallas_call | solution.py:165
  27.7 11.9 %all-to-all-done.near_ref = bf16[16,2,32,512]{3,2,1,0:T(8,128)(2,1)S(1)} async-done(((bf16[16,2,32,512]{3,2,1,0:T(8,128)(2,1)}), bf16[16,2,32,512]{3,2,1,0:T(8,128)(2,1)S(1)}, u32[]{:S(2)}, u32[]{:S(2)}) %all-to-all-start) | async-done | bytes 1048608 | tf_op jit(solution)/shard_map/all_to_all | solution.py:264
  39.6 0.0 copy-start.2
  39.6 17.9 %all_to_all.10.far_ref = bf16[16,2,32,512]{3,2,1,0:T(8,128)(2,1)S(1)} all-to-all(bf16[16,2,32,512]{3,2,1,0:T(8,128)(2,1)S(1)} %bitcast.9), channel_id=1, replica_groups=mesh['half'=2,'quarter'=2,'inner'=4,'hi'=1,'lo'=2] {'lo','inner','quarter'}, dimensions={0} | all-to-all | bytes 2097152 | tf_op jit(solution)/shard_map/all_to_all | solution.py:264
  57.5 0.0 copy-done.2
  57.5 2.1 %pairs.1 = f32[32,2,2,512]{3,2,1,0:T(2,128)} custom-call(s32[2,32]{1,0:T(2,128)S(1)} %copy-done.2, bf16[16,2,32,512]{3,2,1,0:T(8,128)(2,1)S(1)} %all-to-all-done.near_ref, bf16[16,2,32,512]{3,2,1,0:T(8,128)(2,1)S(1)} %all_to_all.10.far_ref), custom_call_target="tpu_custom_call" | custom-call | tf_op jit(solution)/shard_map/pairs/pallas_call | solution.py:230
Async XLA Ops:
  0.0 1.1 %copy-start.1 = (s32[512]{0:T(512)S(1)}, s32[512]{0:T(512)}, u32[]{:S(2)}) copy-start(s32[512]{0:T(512)} %param.5) | copy-start | bytes 6148
  1.1 13.2 %copy-start = (bf16[2,512,256]{2,1,0:T(8,128)(2,1)S(1)}, bf16[2,512,256]{2,1,0:T(8,128)(2,1)}, u32[]{:S(2)}) copy-start(bf16[2,512,256]{2,1,0:T(8,128)(2,1)} %orbitals_ref.1) | copy-start | bytes 1572868
  1.4 24.5 %collective-permute-start.1 = (bf16[512,256]{1,0:T(8,128)(2,1)S(1)}, bf16[512,256]{1,0:T(8,128)(2,1)S(1)}, u32[]{:S(2)}, u32[]{:S(2)}) collective-permute-start(bf16[512,256]{1,0:T(8,128)(2,1)S(1)} %get-tuple-element.17.mine_ref), channel_id=1, source_target_pairs={{0,24},{1,25},{2,26},{3,27},{4,28},{5,29},{6,30},{7,31},{8,16},{9,... | collective-permute-start | bytes 786440 | tf_op jit(solution)/shard_map/ppermute | solution.py:26
  5.7 20.6 %collective-permute-start.2 = (bf16[512,256]{1,0:T(8,128)(2,1)S(1)}, bf16[512,256]{1,0:T(8,128)(2,1)S(1)}, u32[]{:S(2)}, u32[]{:S(2)}) collective-permute-start(bf16[512,256]{1,0:T(8,128)(2,1)S(1)} %get-tuple-element.20.other_ref), channel_id=1, source_target_pairs={{0,25},{1,24},{2,27},{3,26},{4,29},{5,28},{6,31},{7,30},{8,17},{9,... | collective-permute-start | bytes 786440 | tf_op jit(solution)/shard_map/ppermute | solution.py:26
  6.7 7.5 %collective-permute-start = (bf16[2,256,256]{2,1,0:T(8,128)(2,1)S(1)}, bf16[2,256,256]{2,1,0:T(8,128)(2,1)S(1)}, u32[]{:S(2)}, u32[]{:S(2)}) collective-permute-start(bf16[2,256,256]{2,1,0:T(8,128)(2,1)S(1)} %front.1.refs_0_), channel_id=1, source_target_pairs={{0,1},{1,0},{2,3},{3,2},{4,5},{5,4},{6,7},{7,6},{8,9},{9,8},{10,11... | collective-permute-start | bytes 786440 | tf_op jit(solution)/shard_map/ppermute | solution.py:26
  15.7 23.9 %all-to-all-start = ((bf16[16,2,32,512]{3,2,1,0:T(8,128)(2,1)}), bf16[16,2,32,512]{3,2,1,0:T(8,128)(2,1)S(1)}, u32[]{:S(2)}, u32[]{:S(2)}) async-start(bf16[16,2,32,512]{3,2,1,0:T(8,128)(2,1)} %bitcast.5), calls=%async_computation | async-start | bytes 2097152 | tf_op jit(solution)/shard_map/all_to_all | solution.py:264
  39.6 17.9 %copy-start.2 = (s32[2,32]{1,0:T(2,128)S(1)}, s32[2,32]{1,0:T(2,128)}, u32[]{:S(2)}) copy-start(s32[2,32]{1,0:T(2,128)} %table_ref.1) | copy-start | bytes 772

commit v41 on v36

--- a/solution.py
+++ b/solution.py
@@ -256,8 +256,8 @@
     other = lax.dynamic_index_in_dim(orbitals, 1 - lo, 0, keepdims=False)
     share = make_front(mine, other, points)
     share, mine, other = lax.optimization_barrier((share, mine, other))
+    far = [swap(other if x & 1 else mine, True, x) for x in range(slabs)]
     shares = [share] + [swap(share, False, x) for x in range(1, slabs)]
-    far = [swap(other if x & 1 else mine, True, x) for x in range(slabs)]
 
     def send(fields, around):
         fields = fields.reshape((-1,) + fields.shape[-3:])

time: 59.9 us -> 59.9 us (level)
  no operation moved by 1% of the time
where the time goes in v41:
time: 59.9 us; the launch traced here: 59.6 us
  waiting for transfers between devices  19 us (32%)
  blocking collectives  17.9 us (30%)
  starting transfers between devices  15.7 us (26%)
  Pallas kernels  5.6 us (9%)
  local copies, waits for them, and re-layouts  1.16 us (2%)
    all_to_all x1, blocking collectives, send(): lax.all_to_all(fields, around, split_axis=0, concat_axis=0, tiled=True)  17.9 us
    all_to_all x1, waiting for transfers between devices, send(): lax.all_to_all(fields, around, split_axis=0, concat_axis=0, tiled=True)  11.9 us
    all_to_all x1, starting transfers between devices, send(): lax.all_to_all(fields, around, split_axis=0, concat_axis=0, tiled=True)  10.3 us
    ppermute x3, waiting for transfers between devices, swap(): return lax.ppermute(block, KA + GA, route)  7.06 us
    ppermute x3, starting transfers between devices, swap(): return lax.ppermute(block, KA + GA, route)  5.48 us
    pallas_call x1, Pallas kernels, make_pairs(): pl.pallas_call(functools.partial(pair_kernel, 1.0 / math.sqrt(2 * half_k)...  2.12 us
    pallas_call x1, Pallas kernels, make_near(): pl.pallas_call(near_kernel, grid=(kdevice,), in_specs=[pl.BlockSpec((1, s...  1.48 us
    pallas_call x1, Pallas kernels, make_far(): pl.pallas_call(far_kernel, in_specs=[vmem] * (2 + len(slabs)), out_specs=...  1.39 us
  transfers between devices with their start and end apart: 4, of which 2 were waited for; matrix products, arithmetic and copies ran while one was open for 0% of the time, Pallas kernels for 5%

profile of v41, /device:TPU:1, one launch (start us, length us, event | category | flops | bytes accessed | tf_op | source)
XLA Modules:
  0.0 59.6 jit_solution(8044235173630714582)
XLA Ops:
  0.0 0.0 copy-start.1
  0.0 1.1 %dynamic-slice_bitcast_fusion = (bf16[512,256]{1,0:T(8,128)(2,1)S(1)}, bf16[512,256]{1,0:T(8,128)(2,1)S(1)}) fusion(bf16[2,512,256]{2,1,0:T(8,128)(2,1)} %orbitals_ref.1, s32[]{:T(128)S(6)} %select_n.11, s32[]{:T(128)S(6)} %select_n.10), kind=kLoop, calls=%fused_computation | loop fusion | bytes 1048584 | tf_op jit(solution)/shard_map/jit(dynamic_index_in_dim)/squeeze | solution.py:256
  1.1 0.0 copy-start
  1.1 0.0 copy-done.1
  1.1 0.3 front.1.refs_0_
  1.4 4.2 %collective-permute-start.1 = (bf16[512,256]{1,0:T(8,128)(2,1)S(1)}, bf16[512,256]{1,0:T(8,128)(2,1)S(1)}, u32[]{:S(2)}, u32[]{:S(2)}) collective-permute-start(bf16[512,256]{1,0:T(8,128)(2,1)S(1)} %get-tuple-element.17.mine_ref), channel_id=1, source_target_pairs={{0,24},{1,25},{2,26},{3,27},{4,28},{5,29},{6,30},{7,31},{8,16},{9,... | collective-permute-start | bytes 786440 | tf_op jit(solution)/shard_map/ppermute | solution.py:26
  5.7 1.0 %collective-permute-start.2 = (bf16[512,256]{1,0:T(8,128)(2,1)S(1)}, bf16[512,256]{1,0:T(8,128)(2,1)S(1)}, u32[]{:S(2)}, u32[]{:S(2)}) collective-permute-start(bf16[512,256]{1,0:T(8,128)(2,1)S(1)} %get-tuple-element.20.other_ref), channel_id=1, source_target_pairs={{0,25},{1,24},{2,27},{3,26},{4,29},{5,28},{6,31},{7,30},{8,17},{9,... | collective-permute-start | bytes 786440 | tf_op jit(solution)/shard_map/ppermute | solution.py:26
  6.7 0.2 collective-permute-start
  6.9 0.1 pad_add_fusion
  7.0 0.1 dynamic_slice.12
  7.1 0.1 broadcast_subtract_fusion.rows_ref
  7.2 7.1 %collective-permute-done.refs_1_ = bf16[2,256,256]{2,1,0:T(8,128)(2,1)S(1)} collective-permute-done((bf16[2,256,256]{2,1,0:T(8,128)(2,1)S(1)}, bf16[2,256,256]{2,1,0:T(8,128)(2,1)S(1)}, u32[]{:S(2)}, u32[]{:S(2)}) %collective-permute-start) | collective-permute-done | bytes 262176 | tf_op jit(solution)/shard_map/ppermute | solution.py:26
  14.2 0.0 copy-done
  14.2 1.5 %near.1 = bf16[8,2,2,32,512]{4,3,2,1,0:T(8,128)(2,1)} custom-call(bf16[2,512,256]{2,1,0:T(8,128)(2,1)S(1)} %copy-done, bf16[2,256,256]{2,1,0:T(8,128)(2,1)S(1)} %front.1.refs_0_, bf16[2,256,256]{2,1,0:T(8,128)(2,1)S(1)} %collective-permute-done.refs_1_), custom_call_target="tpu_custom_call" | custom-call | flops 1000000000 | bytes 3000000 | tf_op jit(solution)/shard_map/near/pallas_call | solution.py:99
  15.7 10.3 %all-to-all-start = ((bf16[16,2,32,512]{3,2,1,0:T(8,128)(2,1)}), bf16[16,2,32,512]{3,2,1,0:T(8,128)(2,1)S(1)}, u32[]{:S(2)}, u32[]{:S(2)}) async-start(bf16[16,2,32,512]{3,2,1,0:T(8,128)(2,1)} %bitcast.5), calls=%async_computation | async-start | bytes 2097152 | tf_op jit(solution)/shard_map/all_to_all | solution.py:264
  26.0 0.0 collective-permute-done.1.slab_ref.refs_0_
  26.0 0.3 ahead.1
  26.3 0.0 collective-permute-done.2.refs_1_
  26.3 1.4 %far.1 = bf16[2,8,2,32,512]{4,3,2,1,0:T(8,128)(2,1)S(1)} custom-call(bf16[256,256]{1,0:T(8,128)(2,1)S(1)} %get-tuple-element.18.picked_ref, bf16[1,256,512]{2,1,0:T(8,128)(2,1)S(1)} %get-tuple-element.19.chosen_ref, bf16[512,256]{1,0:T(8,128)(2,1)S(1)} %collective-permute-done.1.slab_ref.refs_0_, bf16[512,256]{1,0:T(8,128)(2,1)S(1)} %collective-permute-done.2.refs_1_), custom_call_target="tpu_custom_call" | custom-call | flops 60000002048 | bytes 180000000 | tf_op jit(solution)/shard_map/far/pallas_call | solution.py:165
  27.7 11.9 %all-to-all-done.near_ref = bf16[16,2,32,512]{3,2,1,0:T(8,128)(2,1)S(1)} async-done(((bf16[16,2,32,512]{3,2,1,0:T(8,128)(2,1)}), bf16[16,2,32,512]{3,2,1,0:T(8,128)(2,1)S(1)}, u32[]{:S(2)}, u32[]{:S(2)}) %all-to-all-start) | async-done | bytes 1048608 | tf_op jit(solution)/shard_map/all_to_all | solution.py:264
  39.6 0.0 copy-start.2
  39.6 17.9 %all_to_all.10.far_ref = bf16[16,2,32,512]{3,2,1,0:T(8,128)(2,1)S(1)} all-to-all(bf16[16,2,32,512]{3,2,1,0:T(8,128)(2,1)S(1)} %bitcast.9), channel_id=1, replica_groups=mesh['half'=2,'quarter'=2,'inner'=4,'hi'=1,'lo'=2] {'lo','inner','quarter'}, dimensions={0} | all-to-all | bytes 2097152 | tf_op jit(solution)/shard_map/all_to_all | solution.py:264
  57.5 0.0 copy-done.2
  57.5 2.1 %pairs.1 = f32[32,2,2,512]{3,2,1,0:T(2,128)} custom-call(s32[2,32]{1,0:T(2,128)S(1)} %copy-done.2, bf16[16,2,32,512]{3,2,1,0:T(8,128)(2,1)S(1)} %all-to-all-done.near_ref, bf16[16,2,32,512]{3,2,1,0:T(8,128)(2,1)S(1)} %all_to_all.10.far_ref), custom_call_target="tpu_custom_call" | custom-call | tf_op jit(solution)/shard_map/pairs/pallas_call | solution.py:230
Async XLA Ops:
  0.0 1.1 %copy-start.1 = (s32[512]{0:T(512)S(1)}, s32[512]{0:T(512)}, u32[]{:S(2)}) copy-start(s32[512]{0:T(512)} %param.5) | copy-start | bytes 6148
  1.1 13.2 %copy-start = (bf16[2,512,256]{2,1,0:T(8,128)(2,1)S(1)}, bf16[2,512,256]{2,1,0:T(8,128)(2,1)}, u32[]{:S(2)}) copy-start(bf16[2,512,256]{2,1,0:T(8,128)(2,1)} %orbitals_ref.1) | copy-start | bytes 1572868
  1.4 24.5 %collective-permute-start.1 = (bf16[512,256]{1,0:T(8,128)(2,1)S(1)}, bf16[512,256]{1,0:T(8,128)(2,1)S(1)}, u32[]{:S(2)}, u32[]{:S(2)}) collective-permute-start(bf16[512,256]{1,0:T(8,128)(2,1)S(1)} %get-tuple-element.17.mine_ref), channel_id=1, source_target_pairs={{0,24},{1,25},{2,26},{3,27},{4,28},{5,29},{6,30},{7,31},{8,16},{9,... | collective-permute-start | bytes 786440 | tf_op jit(solution)/shard_map/ppermute | solution.py:26
  5.7 20.6 %collective-permute-start.2 = (bf16[512,256]{1,0:T(8,128)(2,1)S(1)}, bf16[512,256]{1,0:T(8,128)(2,1)S(1)}, u32[]{:S(2)}, u32[]{:S(2)}) collective-permute-start(bf16[512,256]{1,0:T(8,128)(2,1)S(1)} %get-tuple-element.20.other_ref), channel_id=1, source_target_pairs={{0,25},{1,24},{2,27},{3,26},{4,29},{5,28},{6,31},{7,30},{8,17},{9,... | collective-permute-start | bytes 786440 | tf_op jit(solution)/shard_map/ppermute | solution.py:26
  6.7 7.5 %collective-permute-start = (bf16[2,256,256]{2,1,0:T(8,128)(2,1)S(1)}, bf16[2,256,256]{2,1,0:T(8,128)(2,1)S(1)}, u32[]{:S(2)}, u32[]{:S(2)}) collective-permute-start(bf16[2,256,256]{2,1,0:T(8,128)(2,1)S(1)} %front.1.refs_0_), channel_id=1, source_target_pairs={{0,1},{1,0},{2,3},{3,2},{4,5},{5,4},{6,7},{7,6},{8,9},{9,8},{10,11... | collective-permute-start | bytes 786440 | tf_op jit(solution)/shard_map/ppermute | solution.py:26
  15.7 23.9 %all-to-all-start = ((bf16[16,2,32,512]{3,2,1,0:T(8,128)(2,1)}), bf16[16,2,32,512]{3,2,1,0:T(8,128)(2,1)S(1)}, u32[]{:S(2)}, u32[]{:S(2)}) async-start(bf16[16,2,32,512]{3,2,1,0:T(8,128)(2,1)} %bitcast.5), calls=%async_computation | async-start | bytes 2097152 | tf_op jit(solution)/shard_map/all_to_all | solution.py:264
  39.6 17.9 %copy-start.2 = (s32[2,32]{1,0:T(2,128)S(1)}, s32[2,32]{1,0:T(2,128)}, u32[]{:S(2)}) copy-start(s32[2,32]{1,0:T(2,128)} %table_ref.1) | copy-start | bytes 772
